TPU v7x, 32 devices: a whole 2x2x4 slice. The times are simulated.
32 devices in a mesh: gx: 4 (over y, x), gy: 4 (over z), gz: 2 (over core).
Axes of the slice: x: 2, y: 2, z: 4, core: 2. Of those that a mesh axis runs over, the one named last changes fastest.
Arguments:
- features: bfloat16 [32, 16, 8, 512], P('gx', 'gy', 'gz'), may hold values from -31 to 31, as said below
- grad_y: bfloat16 [32, 16, 8, 512], P('gx', 'gy', 'gz'), may hold values from -6 to 6
- attn_out: bfloat16 [32, 16, 8, 512], P('gx', 'gy', 'gz'), may hold values from -3 to 3
- w_query: bfloat16 [512, 512], P('gz'), may hold values from -0.25 to 0.25
- w_key: bfloat16 [512, 512], P('gz'), may hold values from -0.25 to 0.25
- w_value: bfloat16 [512, 512], P('gz'), may hold values from -0.25 to 0.25
- w_out: bfloat16 [512, 512], P('gz'), may hold values from -0.25 to 0.25
Outputs:
- grad_x: bfloat16 [32, 16, 8, 512], P('gx', 'gy', 'gz')
- grad_query: float32 [512, 512], P('gz')
- grad_key: float32 [512, 512], P('gz')
- grad_value: float32 [512, 512], P('gz')
- grad_out: float32 [512, 512], P('gz')
Inputs may be any that keep to these rules, and one draw needn't show every extreme that they name: features of the patch tokens.
All inputs are finite; a program needn't handle non-finite values.
Results may differ from a plain program's by a relative error of at most 0.018.
Values may be sent and summed in bfloat16 or wider, within the bound.
No kernel may reach another device: no remote copies, remote signals or barrier semaphores. Data moves between devices by JAX's collectives and lax.ppermute only.
A program may use at most 64 MiB of HBM per device.

v0:
```python
import math

import jax
import jax.numpy as jnp
from jax import lax
from jax.sharding import PartitionSpec as P

HEADS = 8


def from_partner(block, axis, distance):
    count = lax.axis_size(axis)
    route = []
    for low in range(count):
        high = low | 1 << distance
        if high != low and high < count:
            route += [(low, high), (high, low)]
    return lax.ppermute(block, axis, route)


def shifted(value, axis, steps):
    count = lax.axis_size(axis)
    pairs = [(source, (source + steps) % count) for source in range(count)]
    return lax.ppermute(value, axis, pairs)


def channel_part(stacked, start, count):
    return lax.dynamic_slice_in_dim(stacked, start, count, stacked.ndim - 1)


def ordered_join(first_bit, own_part, other_part, axis):
    lower = jnp.where(first_bit == 0, own_part, other_part)
    upper = jnp.where(first_bit == 0, other_part, own_part)
    return jnp.concatenate([lower, upper], axis=axis)


def transpose_dot(left, right):
    return lax.dot_general(
        left, right, (((1,), (1,)), ((), ())), preferred_element_type=jnp.float32
    )


def token_dot(left, right):
    return lax.dot_general(
        left, right, (((0,), (0,)), ((), ())), preferred_element_type=jnp.float32
    )


def on_device(features, grad_y, attn_out, w_query, w_key, w_value, w_out):
    block_edge, half_y, half_z, width = features.shape
    local_tokens = block_edge * half_y * half_z
    block_tokens = block_edge**3
    half_width = width // 2
    quarter = width // 4
    head_dim = width // HEADS
    group_heads = HEADS // 4
    score_scale = 1.0 / math.sqrt(head_dim)
    z_bit = lax.axis_index("gz") % 2
    y_bit = lax.axis_index("gy") % 2
    full_query, full_key, full_value, full_out = (
        lax.all_gather(w_query, "gz", axis=0, tiled=True),
        lax.all_gather(w_key, "gz", axis=0, tiled=True),
        lax.all_gather(w_value, "gz", axis=0, tiled=True),
        lax.all_gather(w_out, "gz", axis=0, tiled=True),
    )
    feature_rows = features.reshape(local_tokens, width)
    dy_rows = grad_y.reshape(local_tokens, width)
    saved_rows = attn_out.reshape(local_tokens, width)
    out_term = token_dot(saved_rows, dy_rows)
    query = jnp.dot(feature_rows, full_query, preferred_element_type=jnp.float32).astype(
        jnp.bfloat16
    )
    key_rows = jnp.dot(feature_rows, full_key, preferred_element_type=jnp.float32).astype(
        jnp.bfloat16
    )
    value_rows = jnp.dot(feature_rows, full_value, preferred_element_type=jnp.float32).astype(
        jnp.bfloat16
    )
    out_grad = transpose_dot(dy_rows, full_out).astype(jnp.bfloat16)
    stacked = jnp.stack([query, key_rows, value_rows, out_grad, saved_rows]).reshape(
        5, block_edge, half_y, half_z, width
    )
    kept_part = channel_part(stacked, z_bit * half_width, half_width)
    sent_part = channel_part(stacked, (1 - z_bit) * half_width, half_width)
    came_part = from_partner(sent_part, "gz", 0)
    by_z = ordered_join(z_bit, kept_part, came_part, 3)
    kept_part = channel_part(by_z, y_bit * quarter, quarter)
    sent_part = channel_part(by_z, (1 - y_bit) * quarter, quarter)
    came_part = from_partner(sent_part, "gy", 0)
    whole_block = ordered_join(y_bit, kept_part, came_part, 2).reshape(5, block_tokens, quarter)
    query_heads = whole_block[0].reshape(block_tokens, group_heads, head_dim)
    grad_heads = whole_block[3].reshape(block_tokens, group_heads, head_dim)
    products = whole_block[3].astype(jnp.float32) * whole_block[4].astype(jnp.float32)
    row_delta = jnp.sum(products.reshape(block_tokens, group_heads, head_dim), axis=2).T
    own_pair = whole_block[1:3]
    key_list = [own_pair]
    for offset in (1, -1):
        key_list.append(shifted(own_pair, "gx", offset))
    for offset in (2, -2):
        key_list.append(shifted(own_pair, "gy", offset))
    for offset in (2, -2):
        key_list.append(shifted(own_pair, "gz", offset))
    nearby = jnp.stack(key_list)

    def first_pass(carry, key_value):
        row_top, row_total = carry
        key_heads = key_value[0].reshape(block_tokens, group_heads, head_dim)
        scores = (
            jnp.einsum("qhd,khd->hqk", query_heads, key_heads, preferred_element_type=jnp.float32)
            * score_scale
        )
        new_top = jnp.maximum(row_top, jnp.max(scores, axis=2))
        row_total = row_total * jnp.exp(row_top - new_top) + jnp.sum(
            jnp.exp(scores - new_top[:, :, None]), axis=2
        )
        return ((new_top, row_total), None)

    start_top = jnp.full((group_heads, block_tokens), -jnp.inf, jnp.float32)
    start_total = jnp.zeros((group_heads, block_tokens), jnp.float32)
    stats, unused = lax.scan(first_pass, (start_top, start_total), nearby)
    log_total = stats[0] + jnp.log(stats[1])

    def second_pass(query_grad, key_value):
        key_heads = key_value[0].reshape(block_tokens, group_heads, head_dim)
        value_heads = key_value[1].reshape(block_tokens, group_heads, head_dim)
        scores = (
            jnp.einsum("qhd,khd->hqk", query_heads, key_heads, preferred_element_type=jnp.float32)
            * score_scale
        )
        attn_prob = jnp.exp(scores - log_total[:, :, None]).astype(jnp.bfloat16)
        prob_grad = jnp.einsum(
            "qhd,khd->hqk", grad_heads, value_heads, preferred_element_type=jnp.float32
        )
        score_grad = (
            attn_prob.astype(jnp.float32) * (prob_grad - row_delta[:, :, None]) * score_scale
        ).astype(jnp.bfloat16)
        query_grad = query_grad + jnp.einsum(
            "hqk,khd->qhd", score_grad, key_heads, preferred_element_type=jnp.float32
        )
        key_grad = jnp.einsum(
            "hqk,qhd->khd", score_grad, query_heads, preferred_element_type=jnp.float32
        )
        value_grad = jnp.einsum(
            "hqk,qhd->khd", attn_prob, grad_heads, preferred_element_type=jnp.float32
        )
        key_grad = key_grad.astype(jnp.bfloat16).reshape(block_tokens, quarter)
        value_grad = value_grad.astype(jnp.bfloat16).reshape(block_tokens, quarter)
        return (query_grad, jnp.stack([key_grad, value_grad]))

    start_grad = jnp.zeros((block_tokens, group_heads, head_dim), jnp.float32)
    query_block_grad, partials = lax.scan(second_pass, start_grad, nearby)
    summed = partials[0].astype(jnp.float32)
    for slot_index, offset in ((1, -1), (2, 1)):
        summed = summed + shifted(partials[slot_index], "gx", offset).astype(jnp.float32)
    for slot_index, offset in ((3, -2), (4, 2)):
        summed = summed + shifted(partials[slot_index], "gy", offset).astype(jnp.float32)
    for slot_index, offset in ((5, -2), (6, 2)):
        summed = summed + shifted(partials[slot_index], "gz", offset).astype(jnp.float32)
    pair_grads = summed.astype(jnp.bfloat16)
    query_part = query_block_grad.reshape(block_tokens, quarter).astype(jnp.bfloat16)
    block_grads = jnp.concatenate([query_part[None], pair_grads]).reshape(
        3, block_edge, block_edge, block_edge, quarter
    )
    kept_part = lax.dynamic_slice_in_dim(block_grads, y_bit * half_y, half_y, 2)
    sent_part = lax.dynamic_slice_in_dim(block_grads, (1 - y_bit) * half_y, half_y, 2)
    came_part = from_partner(sent_part, "gy", 0)
    by_y = ordered_join(y_bit, kept_part, came_part, 4)
    kept_part = lax.dynamic_slice_in_dim(by_y, z_bit * half_z, half_z, 3)
    sent_part = lax.dynamic_slice_in_dim(by_y, (1 - z_bit) * half_z, half_z, 3)
    came_part = from_partner(sent_part, "gz", 0)
    local_grads = ordered_join(z_bit, kept_part, came_part, 4).reshape(3, local_tokens, width)
    grad_x = transpose_dot(local_grads[0], full_query) + transpose_dot(local_grads[1], full_key)
    grad_x = grad_x + transpose_dot(local_grads[2], full_value)
    grad_x = grad_x.astype(jnp.bfloat16).reshape(features.shape)
    query_term = token_dot(feature_rows, local_grads[0])
    key_term = token_dot(feature_rows, local_grads[1])
    value_term = token_dot(feature_rows, local_grads[2])
    query_shard, key_shard, value_shard, out_shard = (
        lax.psum_scatter(
            query_term.astype(jnp.bfloat16), "gz", scatter_dimension=0, tiled=True
        ).astype(jnp.float32),
        lax.psum_scatter(
            key_term.astype(jnp.bfloat16), "gz", scatter_dimension=0, tiled=True
        ).astype(jnp.float32),
        lax.psum_scatter(
            value_term.astype(jnp.bfloat16), "gz", scatter_dimension=0, tiled=True
        ).astype(jnp.float32),
        lax.psum_scatter(
            out_term.astype(jnp.bfloat16), "gz", scatter_dimension=0, tiled=True
        ).astype(jnp.float32),
    )
    grad_query, grad_key, grad_value, grad_out = lax.psum(
        (query_shard, key_shard, value_shard, out_shard), ("gx", "gy")
    )
    return (grad_x, grad_query, grad_key, grad_value, grad_out)


def solution(mesh):
    return jax.shard_map(
        on_device,
        mesh=mesh,
        in_specs=(
            P("gx", "gy", "gz", None),
            P("gx", "gy", "gz", None),
            P("gx", "gy", "gz", None),
            P("gz", None),
            P("gz", None),
            P("gz", None),
            P("gz", None),
        ),
        out_specs=(
            P("gx", "gy", "gz", None),
            P("gz", None),
            P("gz", None),
            P("gz", None),
            P("gz", None),
        ),
        check_vma=False,
    )
```

profile of v0, /device:TPU:0, one launch (start us, length us, event | category | flops | bytes accessed | tf_op | source)
XLA Modules:
  0.0 277.2 jit_solution(6498246052747530004)
XLA Ops:
  9.2 2.6 all_gather.12
  12.1 2.3 all_gather.13
  15.5 2.2 all_gather.14
  18.8 2.2 all_gather.15
  22.2 1.3 collective-permute-done
  24.0 3.0 %collective-permute-start.1 = (bf16[5,8,4,8,128]{4,3,2,1,0:T(8,128)(2,1)S(1)}, bf16[5,8,4,8,128]{4,3,2,1,0:T(8,128)(2,1)S(1)}, u32[]{:S(2)}, u32[]{:S(2)}) collective-permute-start(bf16[5,8,4,8,128]{4,3,2,1,0:T(8,128)(2,1)S(1)} %fusion.16), channel_id=1, source_target_pairs={{0,2},{2,0},{4,6},{6,4},{1,3},{3,1},{5,7},{7,5},{8,10},{10,8},{12,... | collective-permute-start | bytes 983048 | tf_op jit(solution)/shard_map/ppermute | solution.py:18
  27.0 8.0 %collective-permute-done.1 = bf16[5,8,4,8,128]{4,3,2,1,0:T(8,128)(2,1)S(1)} collective-permute-done((bf16[5,8,4,8,128]{4,3,2,1,0:T(8,128)(2,1)S(1)}, bf16[5,8,4,8,128]{4,3,2,1,0:T(8,128)(2,1)S(1)}, u32[]{:S(2)}, u32[]{:S(2)}) %collective-permute-start.1) | collective-permute-done | bytes 327712 | tf_op jit(solution)/shard_map/ppermute | solution.py:18
  35.5 2.8 %collective-permute-start.4 = (bf16[2,512,128]{2,1,0:T(8,128)(2,1)S(1)}, bf16[2,512,128]{2,1,0:T(8,128)(2,1)S(1)}, u32[]{:S(2)}, u32[]{:S(2)}) collective-permute-start(bf16[2,512,128]{2,1,0:T(8,128)(2,1)S(1)} %bitcast.156), channel_id=1, source_target_pairs={{0,4},{2,6},{4,0},{6,2},{1,5},{3,7},{5,1},{7,3},{8,12},{10,14},{12... | collective-permute-start | bytes 786440 | tf_op jit(solution)/shard_map/ppermute | solution.py:24
  38.3 2.5 collective-permute-start.3
  43.1 9.0 %collective-permute-done.2 = bf16[2,512,128]{2,1,0:T(8,128)(2,1)S(1)} collective-permute-done((bf16[2,512,128]{2,1,0:T(8,128)(2,1)S(1)}, bf16[2,512,128]{2,1,0:T(8,128)(2,1)S(1)}, u32[]{:S(2)}, u32[]{:S(2)}) %collective-permute-start.2) | collective-permute-done | bytes 262176 | tf_op jit(solution)/shard_map/ppermute | solution.py:24
  56.5 2.7 copy.42
  59.2 6.7 %while.26 = (s32[]{:T(128)}, f32[2,512]{1,0:T(2,128)S(1)}, f32[2,512]{1,0:T(2,128)S(1)}, bf16[7,2,512,128]{2,3,1,0:T(8,128)(2,1)S(1)}, bf16[512,2,64]{0,2,1:T(8,128)(2,1)S(1)}, /*index=5*/s32[]{:T(128)}, s32[]{:T(128)}) while((s32[]{:T(128)}, f32[2,512]{1,0:T(2,128)S(1)}, f32[2,512]{1,0:T(2,128)S(1)}, ...), condition=%wide.region_3.4_spmd.clone, body=%wide.region_0.3_spmd.clone.sunk | while | flops 69735424 | bytes 4771940 | solution.py:120
  65.9 22.7 %while.27 = (s32[]{:T(128)}, f32[512,2,64]{0,2,1:T(8,128)S(1)}, bf16[7,2,512,128]{3,2,1,0:T(8,128)(2,1)}, bf16[7,2,512,128]{2,3,1,0:T(8,128)(2,1)S(1)}, bf16[512...) while((s32[]{:T(128)}, f32[512,2,64]{0,2,1:T(8,128)S(1)}, ...), condition=%wide.region_6.7_spmd.clone, body=%wide.region_5.6_spmd.clone.sunk | while | flops 340131840 | bytes 10100887 | solution.py:151
  88.6 1.4 slice_bitcast_fusion.5
  90.0 1.5 collective-permute-start.6
  92.0 2.6 collective-permute-start.8
  95.1 3.0 %collective-permute-done.6 = bf16[2,512,128]{2,1,0:T(8,128)(2,1)S(1)} collective-permute-done((bf16[2,512,128]{2,1,0:T(8,128)(2,1)S(1)}, bf16[2,512,128]{2,1,0:T(8,128)(2,1)S(1)}, u32[]{:S(2)}, u32[]{:S(2)}) %collective-permute-start.6) | collective-permute-done | bytes 262176 | tf_op jit(solution)/shard_map/ppermute | solution.py:24
  99.3 11.7 %collective-permute-done.9 = bf16[2,512,128]{2,1,0:T(8,128)(2,1)S(1)} collective-permute-done((bf16[2,512,128]{2,1,0:T(8,128)(2,1)S(1)}, bf16[2,512,128]{2,1,0:T(8,128)(2,1)S(1)}, u32[]{:S(2)}, u32[]{:S(2)}) %collective-permute-start.9) | collective-permute-done | bytes 262176 | tf_op jit(solution)/shard_map/ppermute | solution.py:24
  111.0 4.5 %collective-permute-done.8 = bf16[2,512,128]{2,1,0:T(8,128)(2,1)} collective-permute-done((bf16[2,512,128]{2,1,0:T(8,128)(2,1)S(1)}, bf16[2,512,128]{2,1,0:T(8,128)(2,1)}, u32[]{:S(2)}, u32[]{:S(2)}) %collective-permute-start.8) | collective-permute-done | bytes 262176 | tf_op jit(solution)/shard_map/ppermute | solution.py:24
  115.5 1.4 fusion.15
  117.1 1.2 fusion.5
  118.4 4.4 %collective-permute-done.12 = bf16[3,8,4,8,128]{4,3,2,1,0:T(8,128)(2,1)S(1)} collective-permute-done((bf16[3,8,4,8,128]{4,3,2,1,0:T(8,128)(2,1)S(1)}, bf16[3,8,4,8,128]{4,3,2,1,0:T(8,128)(2,1)S(1)}, u32[]{:S(2)}, u32[]{:S(2)}) %collective-permute-start.12) | collective-permute-done | bytes 196640 | tf_op jit(solution)/shard_map/ppermute | solution.py:18
  123.1 1.4 collective-permute-done.13
  125.0 1.1 fusion.8
  126.2 1.1 fusion.7
  127.4 1.1 fusion.6
  130.3 6.4 %reduce-scatter.9.cloned.1.call-done = bf16[256,512]{0,1:T(8,128)(2,1)} async-done(((bf16[512,512]{0,1:T(8,128)(2,1)}), bf16[256,512]{0,1:T(8,128)(2,1)}) %reduce-scatter.9.cloned.1.call-update) | async-done | bytes 262160 | tf_op jit(solution)/shard_map/reduce_scatter | solution.py:185
  136.7 12.0 %reduce-scatter.7.cloned.1.call-done = bf16[256,512]{0,1:T(8,128)(2,1)} async-done(((bf16[512,512]{0,1:T(8,128)(2,1)}), bf16[256,512]{0,1:T(8,128)(2,1)}) %reduce-scatter.7.cloned.1.call-update) | async-done | bytes 262160 | tf_op jit(solution)/shard_map/reduce_scatter | solution.py:182
  148.6 11.9 %reduce-scatter.5.cloned.1.call-done = bf16[256,512]{0,1:T(8,128)(2,1)} async-done(((bf16[512,512]{0,1:T(8,128)(2,1)}), bf16[256,512]{0,1:T(8,128)(2,1)}) %reduce-scatter.5.cloned.1.call-update) | async-done | bytes 262160 | tf_op jit(solution)/shard_map/reduce_scatter | solution.py:179
  160.5 107.1 %all-reduce.2 = (f32[256,512]{0,1:T(8,128)S(1)}, f32[256,512]{0,1:T(8,128)S(1)}, f32[256,512]{0,1:T(8,128)S(1)}, f32[256,512]{1,0:T(8,128)}) all-reduce(bf16[256,512]{0,1:T(8,128)(2,1)} %reduce-scatter.5.cloned.1.call-done, bf16[256,512]{0,1:T(8,128)(2,1)} %reduce-scatter.7.cloned.1.call-done, ...), channel_id=1, replica_groups=mesh['gx'=4,'gy'=4,'gz'=2] {'gx','gy'}, use_global_device_ids=true, to_apply=%region_8.9 | all-reduce | flops 524288 | bytes 3145728 | tf_op jit(solution)/shard_map/psum | solution.py:192
  267.7 1.0 copy.54
  268.6 1.0 copy.55
  (207 shorter events, 47.7 us)
Async XLA Ops:
  7.2 4.9 %copy-start.4 = (bf16[256,512]{1,0:T(8,128)(2,1)S(1)}, bf16[256,512]{1,0:T(8,128)(2,1)}, u32[]{:S(2)}) copy-start(bf16[256,512]{1,0:T(8,128)(2,1)} %param.15) | copy-start | bytes 786436
  7.2 121.4 %reduce-scatter.11.cloned.1.call-start = ((), (), s32[]{:S(2)}) async-start(), calls=%async_computation.7 | async-start | bytes 786432 | tf_op jit(solution)/shard_map/reduce_scatter | solution.py:188
  9.2 6.3 %copy-start.5 = (bf16[256,512]{1,0:T(8,128)(2,1)S(1)}, bf16[256,512]{1,0:T(8,128)(2,1)}, u32[]{:S(2)}) copy-start(bf16[256,512]{1,0:T(8,128)(2,1)} %param.16) | copy-start | bytes 786436
  12.1 6.7 %copy-start.6 = (bf16[256,512]{1,0:T(8,128)(2,1)S(1)}, bf16[256,512]{1,0:T(8,128)(2,1)}, u32[]{:S(2)}) copy-start(bf16[256,512]{1,0:T(8,128)(2,1)} %param.17) | copy-start | bytes 786436
  14.4 0.8 copy-start
  17.6 0.8 copy-start.2
  18.4 3.1 %copy-start.9 = (bf16[8,4,4,512]{3,2,1,0:T(4,128)(2,1)S(1)}, bf16[8,4,4,512]{3,2,1,0:T(4,128)(2,1)}, u32[]{:S(2)}) copy-start(bf16[8,4,4,512]{3,2,1,0:T(4,128)(2,1)} %param.13) | copy-start | bytes 393220
  21.7 1.7 collective-permute-start
  24.0 11.0 %collective-permute-start.1 = (bf16[5,8,4,8,128]{4,3,2,1,0:T(8,128)(2,1)S(1)}, bf16[5,8,4,8,128]{4,3,2,1,0:T(8,128)(2,1)S(1)}, u32[]{:S(2)}, u32[]{:S(2)}) collective-permute-start(bf16[5,8,4,8,128]{4,3,2,1,0:T(8,128)(2,1)S(1)} %fusion.16), channel_id=1, source_target_pairs={{0,2},{2,0},{4,6},{6,4},{1,3},{3,1},{5,7},{7,5},{8,10},{10,8},{12,... | collective-permute-start | bytes 983048 | tf_op jit(solution)/shard_map/ppermute | solution.py:18
  35.5 19.6 %collective-permute-start.5 = (bf16[2,512,128]{2,1,0:T(8,128)(2,1)S(1)}, bf16[2,512,128]{2,1,0:T(8,128)(2,1)S(1)}, u32[]{:S(2)}, u32[]{:S(2)}) collective-permute-start(bf16[2,512,128]{2,1,0:T(8,128)(2,1)S(1)} %bitcast.155), channel_id=1, source_target_pairs={{0,0},{1,1},{2,2},{3,3},{4,4},{5,5},{6,6},{7,7},{8,8},{9,9},{10,10... | collective-permute-start | bytes 786440 | tf_op jit(solution)/shard_map/ppermute | solution.py:24
  35.5 18.1 %collective-permute-start.4 = (bf16[2,512,128]{2,1,0:T(8,128)(2,1)S(1)}, bf16[2,512,128]{2,1,0:T(8,128)(2,1)S(1)}, u32[]{:S(2)}, u32[]{:S(2)}) collective-permute-start(bf16[2,512,128]{2,1,0:T(8,128)(2,1)S(1)} %bitcast.156), channel_id=1, source_target_pairs={{0,4},{2,6},{4,0},{6,2},{1,5},{3,7},{5,1},{7,3},{8,12},{10,14},{12... | collective-permute-start | bytes 786440 | tf_op jit(solution)/shard_map/ppermute | solution.py:24
  38.3 14.5 %collective-permute-start.3 = (bf16[2,512,128]{2,1,0:T(8,128)(2,1)S(1)}, bf16[2,512,128]{2,1,0:T(8,128)(2,1)S(1)}, u32[]{:S(2)}, u32[]{:S(2)}) collective-permute-start(bf16[2,512,128]{2,1,0:T(8,128)(2,1)S(1)} %bitcast.157), channel_id=1, source_target_pairs={{0,24},{8,0},{16,8},{24,16},{1,25},{9,1},{17,9},{25,17},{2,26},{10... | collective-permute-start | bytes 786440 | tf_op jit(solution)/shard_map/ppermute | solution.py:24
  40.8 11.4 %collective-permute-start.2 = (bf16[2,512,128]{2,1,0:T(8,128)(2,1)S(1)}, bf16[2,512,128]{2,1,0:T(8,128)(2,1)S(1)}, u32[]{:S(2)}, u32[]{:S(2)}) collective-permute-start(bf16[2,512,128]{2,1,0:T(8,128)(2,1)S(1)} %bitcast.158), channel_id=1, source_target_pairs={{0,8},{8,16},{16,24},{24,0},{1,9},{9,17},{17,25},{25,1},{2,10},{10... | collective-permute-start | bytes 786440 | tf_op jit(solution)/shard_map/ppermute | solution.py:24
  90.0 8.1 %collective-permute-start.6 = (bf16[2,512,128]{2,1,0:T(8,128)(2,1)S(1)}, bf16[2,512,128]{2,1,0:T(8,128)(2,1)S(1)}, u32[]{:S(2)}, u32[]{:S(2)}) collective-permute-start(bf16[2,512,128]{2,1,0:T(8,128)(2,1)S(1)} %get-tuple-element.200), channel_id=1, source_target_pairs={{0,24},{8,0},{16,8},{24,16},{1,25},{9,1},{17,9},{25,17},{2,26},{10... | collective-permute-start | bytes 786440 | tf_op jit(solution)/shard_map/ppermute | solution.py:24
  91.5 7.7 %collective-permute-start.10 = (bf16[2,512,128]{2,1,0:T(8,128)(2,1)S(1)}, bf16[2,512,128]{2,1,0:T(8,128)(2,1)S(1)}, u32[]{:S(2)}, u32[]{:S(2)}) collective-permute-start(bf16[2,512,128]{2,1,0:T(8,128)(2,1)S(1)} %get-tuple-element.201), channel_id=1, source_target_pairs={{0,0},{1,1},{2,2},{3,3},{4,4},{5,5},{6,6},{7,7},{8,8},{9,9},{10,10... | collective-permute-start | bytes 786440 | tf_op jit(solution)/shard_map/ppermute | solution.py:24
  91.6 19.4 %collective-permute-start.9 = (bf16[2,512,128]{2,1,0:T(8,128)(2,1)S(1)}, bf16[2,512,128]{2,1,0:T(8,128)(2,1)S(1)}, u32[]{:S(2)}, u32[]{:S(2)}) collective-permute-start(bf16[2,512,128]{2,1,0:T(8,128)(2,1)S(1)} %get-tuple-element.202), channel_id=1, source_target_pairs={{0,4},{2,6},{4,0},{6,2},{1,5},{3,7},{5,1},{7,3},{8,12},{10,14},{12... | collective-permute-start | bytes 786440 | tf_op jit(solution)/shard_map/ppermute | solution.py:24
  92.0 23.6 %collective-permute-start.8 = (bf16[2,512,128]{2,1,0:T(8,128)(2,1)S(1)}, bf16[2,512,128]{2,1,0:T(8,128)(2,1)}, u32[]{:S(2)}, u32[]{:S(2)}) collective-permute-start(bf16[2,512,128]{2,1,0:T(8,128)(2,1)S(1)} %get-tuple-element.203), channel_id=1, source_target_pairs={{0,4},{2,6},{4,0},{6,2},{1,5},{3,7},{5,1},{7,3},{8,12},{10,14},{12... | collective-permute-start | bytes 786440 | tf_op jit(solution)/shard_map/ppermute | solution.py:24
  94.5 21.0 %collective-permute-start.7 = (bf16[2,512,128]{2,1,0:T(8,128)(2,1)S(1)}, bf16[2,512,128]{2,1,0:T(8,128)(2,1)}, u32[]{:S(2)}, u32[]{:S(2)}) collective-permute-start(bf16[2,512,128]{2,1,0:T(8,128)(2,1)S(1)} %get-tuple-element.204), channel_id=1, source_target_pairs={{0,8},{8,16},{16,24},{24,0},{1,9},{9,17},{17,25},{25,1},{2,10},{10... | collective-permute-start | bytes 786440 | tf_op jit(solution)/shard_map/ppermute | solution.py:24
  98.2 17.3 %collective-permute-start.11 = (bf16[2,512,128]{2,1,0:T(8,128)(2,1)S(1)}, bf16[2,512,128]{2,1,0:T(8,128)(2,1)}, u32[]{:S(2)}, u32[]{:S(2)}) collective-permute-start(bf16[2,512,128]{2,1,0:T(8,128)(2,1)S(1)} %get-tuple-element.205), channel_id=1, source_target_pairs={{0,0},{1,1},{2,2},{3,3},{4,4},{5,5},{6,6},{7,7},{8,8},{9,9},{10,10... | collective-permute-start | bytes 786440 | tf_op jit(solution)/shard_map/ppermute | solution.py:24
  98.9 18.2 %copy-start.8 = (bf16[8,4,4,512]{3,2,1,0:T(4,128)(2,1)S(1)}, bf16[8,4,4,512]{3,2,1,0:T(4,128)(2,1)}, u32[]{:S(2)}) copy-start(bf16[8,4,4,512]{3,2,1,0:T(4,128)(2,1)} %param.12) | copy-start | bytes 393220
  99.1 18.0 %copy-start.10 = (bf16[8,4,4,512]{3,2,1,0:T(4,128)(2,1)S(1)}, bf16[8,4,4,512]{3,2,1,0:T(4,128)(2,1)}, u32[]{:S(2)}) copy-start(bf16[8,4,4,512]{3,2,1,0:T(4,128)(2,1)} %param.13) | copy-start | bytes 393220
  117.0 5.8 %collective-permute-start.12 = (bf16[3,8,4,8,128]{4,3,2,1,0:T(8,128)(2,1)S(1)}, bf16[3,8,4,8,128]{4,3,2,1,0:T(8,128)(2,1)S(1)}, u32[]{:S(2)}, u32[]{:S(2)}) collective-permute-start(bf16[3,8,4,8,128]{4,3,2,1,0:T(8,128)(2,1)S(1)} %fusion.19), channel_id=1, source_target_pairs={{0,2},{2,0},{4,6},{6,4},{1,3},{3,1},{5,7},{7,5},{8,10},{10,8},{12,... | collective-permute-start | bytes 589832 | tf_op jit(solution)/shard_map/ppermute | solution.py:18
  118.3 18.3 %reduce-scatter.9.cloned.1.call-start = ((), (), s32[]{:S(2)}) async-start(), calls=%async_computation.6 | async-start | bytes 786432 | tf_op jit(solution)/shard_map/reduce_scatter | solution.py:185
  123.0 1.5 collective-permute-start.13
  126.1 22.5 %reduce-scatter.7.cloned.1.call-start = ((), (), s32[]{:S(2)}) async-start(), calls=%async_computation.5 | async-start | bytes 786432 | tf_op jit(solution)/shard_map/reduce_scatter | solution.py:182
  126.2 2.7 copy-start.1
  127.3 33.2 %reduce-scatter.5.cloned.1.call-start = ((), (), s32[]{:S(2)}) async-start(), calls=%async_computation.4 | async-start | bytes 786432 | tf_op jit(solution)/shard_map/reduce_scatter | solution.py:179
  127.4 1.9 copy-start.3
  128.6 31.9 %copy-start.7 = (bf16[256,512]{1,0:T(8,128)(2,1)S(1)}, bf16[256,512]{1,0:T(8,128)(2,1)}, u32[]{:S(2)}) copy-start(bf16[256,512]{1,0:T(8,128)(2,1)} %reduce-scatter.11.cloned.1.call-done) | copy-start | bytes 786436
Sparse Core Ops, SparseCore 0:
  118.4 6.6 reduce-scatter.10
  127.5 9.1 reduce-scatter.8
  139.5 9.0 reduce-scatter.6
  151.4 9.1 reduce-scatter.4
where the time goes:
time: 278 us; the launch traced here: 277 us
  blocking collectives  116 us (42%)
  waiting for transfers between devices  73.7 us (27%)
  matrix products  25.7 us (9%)
  local copies, waits for them, and re-layouts  24.9 us (9%)
  starting transfers between devices  14.8 us (5%)
  between operations  14.3 us (5%)
  other arithmetic  6.6 us (2%)
    psum x1, blocking collectives, on_device(): lax.psum((query_shard, key_shard, value_shard, out_shard), ('gx', 'gy'))  107 us
    ppermute x10, waiting for transfers between devices, shifted(): return lax.ppermute(value, axis, pairs)  28.3 us
    ppermute x4, waiting for transfers between devices, from_partner(): return lax.ppermute(block, axis, route)  15.1 us
    unnamed x39, local copies, waits for them, and re-layouts  12.3 us
    reduce_scatter x1, waiting for transfers between devices, on_device(): lax.psum_scatter(key_term.astype(jnp.bfloat16), 'gz', scatter_dimension=0...  12 us
    reduce_scatter x1, waiting for transfers between devices, on_device(): lax.psum_scatter(query_term.astype(jnp.bfloat16), 'gz', scatter_dimension...  11.9 us
    ppermute x10, starting transfers between devices, shifted(): return lax.ppermute(value, axis, pairs)  11.1 us
    reduce_scatter x1, waiting for transfers between devices, on_device(): lax.psum_scatter(value_term.astype(jnp.bfloat16), 'gz', scatter_dimension...  6.37 us
  transfers between devices with their start and end apart: 18, of which 11 were waited for; matrix products, arithmetic and copies ran while one was open for 4% of the time, Pallas kernels for 0%

commit v1 on v0

v1 whole, which is shorter than its diff:
```python
import functools
import math

import jax
import jax.numpy as jnp
from jax import lax
from jax.experimental import pallas as pl
from jax.experimental.pallas import tpu as pltpu
from jax.sharding import PartitionSpec as P

HEADS = 8
PART = 128
BF = jnp.bfloat16
F32 = jnp.float32
VMEM_BYTES = 52 * 1024 * 1024


def from_partner(block, axis):
    route = [(index, index ^ 1) for index in range(lax.axis_size(axis))]
    return lax.ppermute(block, axis, route)


def shifted(value, axis, steps):
    count = lax.axis_size(axis)
    return lax.ppermute(value, axis, [(source, (source + steps) % count) for source in range(count)])


def plane_swap(value, flip_x, flip_y):
    count_x, count_y = lax.axis_size("gx"), lax.axis_size("gy")
    route = []
    for at_x in range(count_x):
        for at_y in range(count_y):
            route.append((at_x * count_y + at_y, (at_x ^ flip_x) * count_y + (at_y ^ flip_y)))
    return lax.ppermute(value, ("gx", "gy"), route)


def dot_nn(left, right):
    return lax.dot_general(left, right, (((1,), (0,)), ((), ())), preferred_element_type=F32)


def dot_nt(left, right):
    return lax.dot_general(left, right, (((1,), (1,)), ((), ())), preferred_element_type=F32)


def dot_tn(left, right):
    return lax.dot_general(left, right, (((0,), (0,)), ((), ())), preferred_element_type=F32)


def columns(start):
    return pl.ds(pl.multiple_of(start, PART), PART)


def call(kernel, out_shape, args, scratch=(), flops=1e6, moved=1e6, exps=0):
    return pl.pallas_call(
        kernel,
        out_shape=out_shape,
        scratch_shapes=list(scratch),
        compiler_params=pltpu.CompilerParams(vmem_limit_bytes=VMEM_BYTES),
        cost_estimate=pl.CostEstimate(
            flops=int(flops), bytes_accessed=int(moved), transcendentals=int(exps)
        ),
    )(*args)


def shape_of(dims, dtype=BF):
    return jax.ShapeDtypeStruct(dims, dtype)


def pack_kernel(feat_ref, dy_ref, saved_ref, pair_ref, own_ref):
    y_bit = lax.axis_index("gy") % 2
    z_bit = lax.axis_index("gz") % 2
    tokens, width = feat_ref.shape
    last = 2 * width + PART
    for out in (pair_ref, own_ref):
        out[:, PART : PART + width] = feat_ref[...]
        out[:, PART + width : last] = dy_ref[...]
    pair_ref[:, 0:PART] = saved_ref[:, columns((z_bit * 2 + 1 - y_bit) * PART)]
    pair_ref[:, last:] = saved_ref[:, columns(((1 - z_bit) * 2 + 1 - y_bit) * PART)]
    own_ref[:, 0:PART] = saved_ref[:, columns(((1 - z_bit) * 2 + y_bit) * PART)]
    own_ref[:, last:] = saved_ref[:, columns((z_bit * 2 + y_bit) * PART)]


def project_kernel(
    own_half, own, core, pair, far, wq0, wq1, wk0, wk1, wv0, wv1, wout,
    q_ref, kv_ref, do_ref, w_cols,
):
    y_bit = lax.axis_index("gy") % 2
    z_bit = lax.axis_index("gz") % 2
    half = z_bit if own_half else z_bit * 0
    group = columns((z_bit * 2 + y_bit) * PART)
    half_rows = wq0.shape[0]
    width = 2 * half_rows
    for at, (first, second) in enumerate(((wq0, wq1), (wk0, wk1), (wv0, wv1))):
        spot = slice(at * PART, (at + 1) * PART)
        w_cols[pl.ds(pl.multiple_of(half * half_rows, half_rows), half_rows), spot] = first[:, group]
        w_cols[pl.ds(pl.multiple_of((1 - half) * half_rows, half_rows), half_rows), spot] = second[:, group]
    w_rows = wout[pl.ds(pl.multiple_of(y_bit * PART, PART), PART), :]
    for at, source in enumerate((own, core, pair, far)):
        rows = slice(at * PART, (at + 1) * PART)
        made = dot_nn(source[:, PART : PART + width], w_cols[...])
        q_ref[rows, :] = made[:, 0:PART].astype(BF) * jnp.asarray(1.0 / math.sqrt(width // HEADS), BF)
        kv_ref[rows, :] = made[:, PART:].astype(BF)
        do_ref[rows, :] = dot_nt(source[:, PART + width : PART + 2 * width], w_rows).astype(BF)


def early_kernel(own, core, pair, far, do_ref, delta_ref, feat_t_ref, o_ref, saved, dys):
    z_bit = lax.axis_index("gz") % 2
    width = (own.shape[1] - 2 * PART) // 2
    half = width // 2
    last = PART + 2 * width
    for at, (source, spot) in enumerate(((own, last), (core, 0), (pair, 0), (far, last))):
        rows = slice(at * PART, (at + 1) * PART)
        saved[rows, :] = source[:, spot : spot + PART]
        dys[rows, :] = source[:, PART + width : last]
        wanted = source[:, pl.ds(pl.multiple_of(PART + z_bit * half, PART), half)]
        feat_t_ref[:, rows] = wanted.astype(F32).T.astype(BF)
    head_dim = width // HEADS
    products = (do_ref[...].astype(F32) * saved[...].astype(F32)).T
    delta_ref[0:1, :] = jnp.sum(products[0:head_dim], axis=0, keepdims=True)
    delta_ref[1:2, :] = jnp.sum(products[head_dim:PART], axis=0, keepdims=True)
    out = dot_nn(saved[...].astype(F32).T.astype(BF), dys[...]).astype(BF)
    for at in range(8):
        low = out[at * 16 : (at + 1) * 16, :]
        o_ref[at * 32 : at * 32 + 16, :] = low[:, 0:half]
        o_ref[at * 32 + 16 : at * 32 + 32, :] = low[:, half:]


def attention_kernel(times, q_ref, do_ref, delta_ref, *refs):
    count = len(times)
    kvs = refs[:count]
    dq_ref = refs[count]
    dkvs = refs[count + 1 : 2 * count + 1]
    kv_s, e_s, top_s, total_s, f_s, fcol_s, dq_s, dkv_s = refs[2 * count + 1 :]
    tokens = q_ref.shape[0]
    head_dim = PART // 2
    for at in range(count):
        kv_s[at] = kvs[at][...]
    lane = lax.broadcasted_iota(jnp.int32, (tokens, PART), 1)
    low = lane < head_dim
    query = q_ref[...]
    grad = do_ref[...]
    none = jnp.zeros_like(query)
    q_heads = (jnp.where(low, query, none), jnp.where(low, none, query))
    g_heads = (jnp.where(low, grad, none), jnp.where(low, none, grad))

    def first(at, carry):
        keys = kv_s[at, :, 0:PART]
        for head in range(2):
            scores = dot_nt(keys, q_heads[head])
            top = jnp.max(scores, axis=0, keepdims=True)
            grown = jnp.exp(scores - top)
            e_s[2 * at + head] = grown.astype(BF)
            top_s[pl.ds(2 * at + head, 1), :] = top
            total_s[pl.ds(2 * at + head, 1), :] = jnp.sum(grown, axis=0, keepdims=True)
        return carry

    lax.fori_loop(0, count, first, 0)
    for head in range(2):
        tops = [top_s[2 * at + head : 2 * at + head + 1, :] for at in range(count)]
        most = functools.reduce(jnp.maximum, tops)
        lifts = [jnp.exp(top - most) for top in tops]
        total = functools.reduce(
            jnp.add,
            [
                times[at] * lifts[at] * total_s[2 * at + head : 2 * at + head + 1, :]
                for at in range(count)
            ],
        )
        for at in range(count):
            part = lifts[at] / total
            f_s[2 * at + head : 2 * at + head + 1, :] = part * times[at]
            top_s[2 * at + head : 2 * at + head + 1, :] = part
    turned = top_s[...].T
    for at in range(count):
        fcol_s[at] = jnp.where(low, turned[:, 2 * at : 2 * at + 1], turned[:, 2 * at + 1 : 2 * at + 2])
    dq_s[...] = jnp.zeros_like(dq_s)
    delta = delta_ref[...]

    def second(at, carry):
        keys = kv_s[at, :, 0:PART]
        values = kv_s[at, :, PART:]
        keys_t = keys.astype(F32).T.astype(BF)
        scale = fcol_s[at]
        query_f = (query.astype(F32) * scale).astype(BF)
        grad_f = (grad.astype(F32) * scale).astype(BF)
        dk = jnp.zeros((tokens, PART), F32)
        dv = jnp.zeros((tokens, PART), F32)
        for head in range(2):
            mine = low if head == 0 else jnp.logical_not(low)
            grown = e_s[2 * at + head]
            dprob = dot_nt(values, g_heads[head])
            dscore = (grown.astype(F32) * (dprob - delta[head : head + 1, :])).astype(BF)
            dv = dv + dot_nn(grown, jnp.where(mine, grad_f, none))
            dk = dk + dot_nn(dscore, jnp.where(mine, query_f, none))
            spot = slice(head * head_dim, (head + 1) * head_dim)
            dq_s[spot, :] = dq_s[spot, :] + dot_nn(keys_t[spot, :], dscore) * f_s[
                pl.ds(2 * at + head, 1), :
            ]
        dkv_s[at, :, 0:PART] = dk.astype(BF)
        dkv_s[at, :, PART:] = dv.astype(BF)
        return carry

    lax.fori_loop(0, count, second, 0)
    for at in range(count):
        dkvs[at][...] = dkv_s[at]
    dq_ref[...] = (dq_s[...].T * (1.0 / math.sqrt(head_dim))).astype(BF)


def collect_kernel(times, dq_ref, *refs):
    count = len(times)
    out = refs[count]
    total = times[0] * refs[0][...].astype(F32)
    for at in range(1, count):
        total = total + times[at] * refs[at][...].astype(F32)
    out[:, 0:PART] = dq_ref[...]
    out[:, PART:] = total.astype(BF)


def weight_kernel(chunks, own, core, feat_t, o_ref, pair_ref, mine_ref, *refs):
    outs, (grads, held) = refs[:chunks], refs[chunks:]
    z_bit = lax.axis_index("gz") % 2
    tokens = own.shape[0]
    for at in range(3):
        source = slice(at * PART, (at + 1) * PART)
        own_at = columns(at * 2 * PART + z_bit * PART)
        core_at = columns(at * 2 * PART + (1 - z_bit) * PART)
        grads[:, own_at] = own[:, source]
        for low in range(4):
            grads[low * PART : (low + 1) * PART, core_at] = core[
                (low ^ 1) * PART : ((low ^ 1) + 1) * PART, source
            ]
    mine_ref[...] = grads[0:PART, :]
    pair_ref[...] = grads[2 * PART : 3 * PART, :]
    wide = grads.shape[1]
    held[:, 0:wide] = dot_nn(feat_t[...], grads[...]).astype(BF)
    held[:, wide:] = o_ref[...]
    rows = held.shape[0] // chunks
    place = (lax.axis_index("gx") * 2 + lax.axis_index("gy") // 2) if chunks > 1 else 0
    for at in range(chunks):
        if chunks > 1:
            spot = (lax.axis_index("gx") ^ (at // 2)) * 2 + ((lax.axis_index("gy") // 2) ^ (at % 2))
            outs[at][...] = held[pl.ds(pl.multiple_of(spot * rows, rows), rows), :]
        else:
            outs[at][...] = held[...]


def grad_x_kernel(own_half, mine, pair, wq0, wq1, wk0, wk1, wv0, wv1, out, full):
    y_bit = lax.axis_index("gy") % 2
    z_bit = lax.axis_index("gz") % 2
    half = z_bit if own_half else z_bit * 0
    width = wq0.shape[1]
    half_rows = wq0.shape[0]
    for at in range(3):
        for side in range(2):
            spot = slice((at * 2 + side) * PART, (at * 2 + side + 1) * PART)
            base = at * width + side * 2 * PART
            full[:, columns(base + y_bit * PART)] = mine[:, spot]
            full[:, columns(base + (1 - y_bit) * PART)] = pair[:, spot]
    for at, sources in ((half, (wq0, wk0, wv0)), (1 - half, (wq1, wk1, wv1))):
        total = functools.reduce(
            jnp.add,
            [dot_nt(full[:, n * width : (n + 1) * width], sources[n][...]) for n in range(3)],
        )
        out[:, pl.ds(pl.multiple_of(at * half_rows, PART), half_rows)] = total.astype(BF)


def sum_kernel(*refs):
    total = refs[0][...].astype(F32)
    for ref in refs[1:-1]:
        total = total + ref[...].astype(F32)
    refs[-1][...] = total.astype(BF)


def spread_kernel(*refs):
    outs = refs[4:]
    at_x = lax.axis_index("gx")
    at_y = lax.axis_index("gy")
    rows, wide = refs[0].shape[1:]
    half = 2 * PART
    for flip_x in range(4):
        for flip_y in range(4):
            piece = refs[flip_x][flip_y].astype(F32)
            their_y = at_y ^ flip_y
            place = (at_x ^ flip_x) * 2 + their_y // 2
            bit = their_y % 2
            spot = pl.ds(pl.multiple_of(place * rows, rows), rows)
            for at in range(3):
                for side in range(2):
                    outs[at][spot, columns(side * half + bit * PART)] = piece[
                        :, (at * 2 + side) * PART : (at * 2 + side + 1) * PART
                    ]
            low = piece[:, 6 * PART :]
            spot = pl.ds(pl.multiple_of(bit * PART + place * (rows // 2), rows // 2), rows // 2)
            outs[3][spot, 0:half] = low[0 : rows // 2]
            outs[3][spot, half:] = low[rows // 2 :]


def on_device(features, grad_y, attn_out, w_query, w_key, w_value, w_out):
    width = features.shape[-1]
    half = width // 2
    tokens = features.shape[0] * features.shape[1] * features.shape[2]
    block_tokens = 4 * tokens
    count_x, count_y, count_z = lax.axis_size("gx"), lax.axis_size("gy"), lax.axis_size("gz")
    z_bit = lax.axis_index("gz") % 2
    y_bit = lax.axis_index("gy") % 2

    own_half = count_z == 2
    if own_half:
        pairs = []
        for weight in (w_query, w_key, w_value):
            pairs += [weight, from_partner(weight, "gz")]
        out_rows = w_out
    else:
        pairs = []
        for weight in (w_query, w_key, w_value):
            whole = lax.all_gather(weight, "gz", axis=0, tiled=True)
            pairs += [whole[:half], whole[half:]]
        whole = lax.all_gather(w_out, "gz", axis=0, tiled=True)
        out_rows = lax.dynamic_slice_in_dim(whole, z_bit * half, half, 0)

    message = shape_of((tokens, 2 * width + 2 * PART))
    pair_message, own = call(
        pack_kernel,
        (message, message),
        [value.reshape(tokens, width) for value in (features, grad_y, attn_out)],
    )
    pair = from_partner(pair_message, "gy")
    core = from_partner(own, "gz")
    far = from_partner(pair, "gz")
    query, own_kv, out_grad = call(
        functools.partial(project_kernel, own_half),
        (
            shape_of((block_tokens, PART)),
            shape_of((block_tokens, 2 * PART)),
            shape_of((block_tokens, PART)),
        ),
        [own, core, pair, far, *pairs, out_rows],
        scratch=[pltpu.VMEM((width, 3 * PART), BF)],
        flops=2 * block_tokens * width * 4 * PART,
    )

    times = [1]
    routes = []
    for axis, step, blocks in (("gx", 1, count_x), ("gy", 2, count_y // 2), ("gz", 2, count_z // 2)):
        if blocks == 1:
            times[0] += 2
        elif blocks == 2:
            routes.append((axis, step))
            times.append(2)
        else:
            routes += [(axis, step), (axis, -step)]
            times += [1, 1]
    near = [own_kv] + [shifted(own_kv, axis, step) for axis, step in routes]
    count = len(times)
    delta, feat_t, out_term = call(
        early_kernel,
        (
            shape_of((2, block_tokens), F32),
            shape_of((half, block_tokens)),
            shape_of((half, half)),
        ),
        [own, core, pair, far, out_grad],
        scratch=[pltpu.VMEM((block_tokens, PART), BF), pltpu.VMEM((block_tokens, width), BF)],
        flops=2 * block_tokens * width * PART,
    )
    rows = -(-2 * count // 8) * 8
    dq, *partials = call(
        functools.partial(attention_kernel, tuple(float(n) for n in times)),
        (
            shape_of((block_tokens, PART)),
            *[shape_of((block_tokens, 2 * PART)) for n in range(count)],
        ),
        [query, out_grad, delta, *near],
        scratch=[
            pltpu.VMEM((count, block_tokens, 2 * PART), BF),
            pltpu.VMEM((2 * count, block_tokens, block_tokens), BF),
            pltpu.VMEM((rows, block_tokens), F32),
            pltpu.VMEM((rows, block_tokens), F32),
            pltpu.VMEM((rows, block_tokens), F32),
            pltpu.VMEM((count, block_tokens, PART), F32),
            pltpu.VMEM((PART, block_tokens), F32),
            pltpu.VMEM((count, block_tokens, 2 * PART), BF),
        ],
        flops=2 * 2 * 5 * count * block_tokens * block_tokens * PART,
        exps=2 * count * block_tokens * block_tokens,
    )
    back = [partials[0]]
    for partial, (axis, step) in zip(partials[1:], routes):
        back.append(shifted(partial, axis, -step))
    grads = call(
        functools.partial(collect_kernel, tuple(float(n) for n in times)),
        shape_of((block_tokens, 3 * PART)),
        [dq, *back],
    )
    core_grads = from_partner(grads, "gz")
    planned = count_x == 4 and count_y == 4 and count_z == 2
    chunks = 8 if planned else 1
    piece = shape_of((half // chunks, 8 * PART))
    pair_out, mine, *pieces = call(
        functools.partial(weight_kernel, chunks),
        (shape_of((tokens, 6 * PART)), shape_of((tokens, 6 * PART)), *[piece] * chunks),
        [grads, core_grads, feat_t, out_term],
        scratch=[pltpu.VMEM((block_tokens, 6 * PART), BF), pltpu.VMEM((half, 8 * PART), BF)],
        flops=2 * block_tokens * half * 6 * PART,
    )
    pair_in = from_partner(pair_out, "gy")
    if planned:
        terms = [pieces[0]]
        for at in range(1, 8):
            terms.append(plane_swap(pieces[at], at // 2, 2 * (at % 2)))
        total = call(sum_kernel, piece, terms)
        line = jnp.stack([total] + [plane_swap(total, 0, flip) for flip in (1, 2, 3)])
        plane = [line] + [plane_swap(line, flip, 0) for flip in (1, 2, 3)]
        weights = call(spread_kernel, tuple([shape_of((half, width), F32)] * 4), plane)
    else:
        terms = pieces[0].astype(F32)
        stacked = jnp.zeros((4, width, width), F32)
        for at in range(3):
            for side in range(2):
                tile = terms[:, (at * 2 + side) * PART : (at * 2 + side + 1) * PART]
                stacked = lax.dynamic_update_slice(
                    stacked, tile[None], (at, z_bit * half, side * half + y_bit * PART)
                )
        tile = terms[:, 6 * PART :].reshape(8, 2, 16, half).transpose(0, 2, 1, 3).reshape(PART, width)
        stacked = lax.dynamic_update_slice(
            stacked, tile[None], (3, z_bit * half + y_bit * PART, 0)
        )
        stacked = lax.psum(stacked, ("gx", "gy", "gz"))
        held = w_query.shape[0]
        stacked = lax.dynamic_slice_in_dim(stacked, lax.axis_index("gz") * held, held, 1)
        weights = [stacked[at] for at in range(4)]
    grad_x = call(
        functools.partial(grad_x_kernel, own_half),
        shape_of((tokens, width)),
        [mine, pair_in, *pairs],
        scratch=[pltpu.VMEM((tokens, 3 * width), BF)],
        flops=2 * tokens * 3 * width * width,
    ).reshape(features.shape)
    return (grad_x, *weights)


def solution(mesh):
    return jax.shard_map(
        on_device,
        mesh=mesh,
        in_specs=(
            P("gx", "gy", "gz", None),
            P("gx", "gy", "gz", None),
            P("gx", "gy", "gz", None),
            P("gz", None),
            P("gz", None),
            P("gz", None),
            P("gz", None),
        ),
        out_specs=(
            P("gx", "gy", "gz", None),
            P("gz", None),
            P("gz", None),
            P("gz", None),
            P("gz", None),
        ),
        check_vma=False,
    )
```

time: 278 us -> 105 us (0.38)
  blocking collectives: 116 us -> 0 us
  waiting for transfers between devices: 73.7 us -> 46.1 us
  matrix products: 25.7 us -> 0 us
  Pallas kernels: 0 us -> 17.7 us
  starting transfers between devices: 14.8 us -> 32 us
  local copies, waits for them, and re-layouts: 24.9 us -> 7.93 us
  between operations: 14.3 us -> 0.82 us
  other arithmetic: 6.6 us -> 0.04 us
    psum x1 -> x0, blocking collectives: 107 us -> none  [on_device(): lax.psum((query_shard, key_shard, value_shard, out_shard), ('gx', 'gy'))]
    reduce_scatter x4 -> x0, waiting for transfers between devices: 30.3 us -> none  [the longest x1 12 us: on_device(): lax.psum_scatter(key_term.astype(jnp.bfloat16), 'gz', scatter_dimension=0...]
    dot_general x53 -> x0, matrix products: 25.7 us -> none  [the longest x4 4.56 us: token_dot(): lax.dot_general(left, right, (((0,), (0,)), ((), ())), preferred_element_...]
    pallas_call x0 -> x9, Pallas kernels: none -> 17.7 us  [call(): pl.pallas_call(kernel, out_shape=out_shape, scratch_shapes=list(scratch),...]
    ppermute x10 -> x19, starting transfers between devices: 11.1 us -> 27.3 us  [the longest x13 19.6 us: plane_swap(): return lax.ppermute(value, ('gx', 'gy'), route)]
    all_gather x4 -> x0, blocking collectives: 9.28 us -> none  [the longest x1 2.6 us: on_device(): lax.all_gather(w_query, 'gz', axis=0, tiled=True)]
    dynamic_update_slice x14 -> x0, local copies, waits for them, and re-layouts: 6.24 us -> none  [on_device(): query_block_grad, partials = lax.scan(second_pass, start_grad, nearby)]
    unnamed x39 -> x34, local copies, waits for them, and re-layouts: 12.3 us -> 6.18 us
  transfers between devices with their start and end apart: 18 -> 27, of which waited for: 11 -> 18; matrix products, arithmetic and copies ran while one was open for 4% -> 1% of each run, Pallas kernels for 0% -> 2%
where the time goes in v1:
time: 105 us
  waiting for transfers between devices  46.1 us (44%)
  starting transfers between devices  32 us (30%)
  Pallas kernels  17.7 us (17%)
  local copies, waits for them, and re-layouts  7.93 us (8%)
    ppermute x6, waiting for transfers between devices, shifted(): lax.ppermute(value, axis, [(source, (source + steps) % count) for source...  20.8 us
    ppermute x13, starting transfers between devices, plane_swap(): return lax.ppermute(value, ('gx', 'gy'), route)  19.6 us
    pallas_call x9, Pallas kernels, call(): pl.pallas_call(kernel, out_shape=out_shape, scratch_shapes=list(scratch),...  17.7 us
    ppermute x8, waiting for transfers between devices, from_partner(): return lax.ppermute(block, axis, route)  16.2 us
    ppermute x13, waiting for transfers between devices, plane_swap(): return lax.ppermute(value, ('gx', 'gy'), route)  9.05 us
    ppermute x6, starting transfers between devices, shifted(): lax.ppermute(value, axis, [(source, (source + steps) % count) for source...  7.69 us
    unnamed x34, local copies, waits for them, and re-layouts  6.18 us
    ppermute x8, starting transfers between devices, from_partner(): return lax.ppermute(block, axis, route)  4.75 us
  transfers between devices with their start and end apart: 27, of which 18 were waited for; matrix products, arithmetic and copies ran while one was open for 1% of the time, Pallas kernels for 2%

profile of v1, /device:TPU:0, one launch (start us, length us, event | category | flops | bytes accessed | tf_op | source)
XLA Modules:
  0.0 104.6 jit_solution(7297376500405570280)
XLA Ops:
  0.7 1.0 reshape.22.feat_ref
  1.8 3.1 %collective-permute-start.1 = (bf16[128,1280]{1,0:T(8,128)(2,1)S(1)}, bf16[128,1280]{1,0:T(8,128)(2,1)S(1)}, u32[]{:S(2)}, u32[]{:S(2)}) collective-permute-start(bf16[128,1280]{1,0:T(8,128)(2,1)S(1)} %get-tuple-element.33), channel_id=1, source_target_pairs={{0,2},{2,0},{4,6},{6,4},{1,3},{3,1},{5,7},{7,5},{8,10},{10,8},{12,... | collective-permute-start | bytes 983048 | tf_op jit(solution)/shard_map/ppermute | solution.py:20
  4.9 7.7 %collective-permute-done.1.pair = bf16[128,1280]{1,0:T(8,128)(2,1)S(1)} collective-permute-done((bf16[128,1280]{1,0:T(8,128)(2,1)S(1)}, bf16[128,1280]{1,0:T(8,128)(2,1)S(1)}, u32[]{:S(2)}, u32[]{:S(2)}) %collective-permute-start.1) | collective-permute-done | bytes 327712 | tf_op jit(solution)/shard_map/ppermute | solution.py:20
  16.9 2.1 %shard_map.111 = (bf16[512,128]{1,0:T(8,128)(2,1)S(1)}, bf16[512,256]{1,0:T(8,128)(2,1)S(1)}, bf16[512,128]{1,0:T(8,128)(2,1)S(1)}) custom-call(bf16[128,1280]{1,0:T(8,128)(2,1)} %copy-done, bf16[128,1280]{1,0:T(8,128)(2,1)} %copy-done.4, bf16[128,1280]{1,0:T(8,128)(2,1)} %copy-done.2, bf16[128,1280]{1,0:T(8,128)(2,1)} %copy-done.6, ...), custom_call_target="tpu_custom_call" | custom-call | flops 268435456 | bytes 1000000 | tf_op jit(solution)/shard_map/pallas_call | solution.py:54
  19.0 2.8 %collective-permute-start.8 = (bf16[512,256]{1,0:T(8,128)(2,1)S(1)}, bf16[512,256]{1,0:T(8,128)(2,1)S(1)}, u32[]{:S(2)}, u32[]{:S(2)}) collective-permute-start(bf16[512,256]{1,0:T(8,128)(2,1)S(1)} %get-tuple-element.37.refs_0_), channel_id=1, source_target_pairs={{0,4},{2,6},{4,0},{6,2},{1,5},{3,7},{5,1},{7,3},{8,12},{10,14},{12... | collective-permute-start | bytes 786440 | tf_op jit(solution)/shard_map/ppermute | solution.py:25
  21.8 2.5 %collective-permute-start.7 = (bf16[512,256]{1,0:T(8,128)(2,1)S(1)}, bf16[512,256]{1,0:T(8,128)(2,1)S(1)}, u32[]{:S(2)}, u32[]{:S(2)}) collective-permute-start(bf16[512,256]{1,0:T(8,128)(2,1)S(1)} %get-tuple-element.37.refs_0_), channel_id=1, source_target_pairs={{0,24},{8,0},{16,8},{24,16},{1,25},{9,1},{17,9},{25,17},{2,26},{10... | collective-permute-start | bytes 786440 | tf_op jit(solution)/shard_map/ppermute | solution.py:25
  28.5 5.5 %collective-permute-done.8.refs_3_ = bf16[512,256]{1,0:T(8,128)(2,1)S(1)} collective-permute-done((bf16[512,256]{1,0:T(8,128)(2,1)S(1)}, bf16[512,256]{1,0:T(8,128)(2,1)S(1)}, u32[]{:S(2)}, u32[]{:S(2)}) %collective-permute-start.8) | collective-permute-done | bytes 262176 | tf_op jit(solution)/shard_map/ppermute | solution.py:25
  34.1 2.4 %collective-permute-done.6.refs_1_ = bf16[512,256]{1,0:T(8,128)(2,1)S(1)} collective-permute-done((bf16[512,256]{1,0:T(8,128)(2,1)S(1)}, bf16[512,256]{1,0:T(8,128)(2,1)S(1)}, u32[]{:S(2)}, u32[]{:S(2)}) %collective-permute-start.6) | collective-permute-done | bytes 262176 | tf_op jit(solution)/shard_map/ppermute | solution.py:25
  36.5 10.4 %shard_map.113 = (bf16[512,128]{1,0:T(8,128)(2,1)S(1)}, bf16[512,256]{1,0:T(8,128)(2,1)S(1)}, bf16[512,256]{1,0:T(8,128)(2,1)S(1)}, bf16[512,256]{1,0:T(8,128)(2,1)S(1)}, bf16[512,256]{1,0:T(8,128)(2,1)S(1)}) custom-call(bf16[512,128]{1,0:T(8,128)(2,1)S(1)} %get-tuple-element.34.q_ref, bf16[512,128]{1,0:T(8,128)(2,1)S(1)} %get-tuple-element.35.do_ref, ...), custom_call_target="tpu_custom_call" | custom-call | flops 2684354560 | bytes 1000000 | tf_op jit(solution)/shard_map/pallas_call | solution.py:54
  46.9 1.5 %collective-permute-start.9 = (bf16[512,256]{1,0:T(8,128)(2,1)S(1)}, bf16[512,256]{1,0:T(8,128)(2,1)S(1)}, u32[]{:S(2)}, u32[]{:S(2)}) collective-permute-start(bf16[512,256]{1,0:T(8,128)(2,1)S(1)} %get-tuple-element.40), channel_id=1, source_target_pairs={{0,24},{8,0},{16,8},{24,16},{1,25},{9,1},{17,9},{25,17},{2,26},{10... | collective-permute-start | bytes 786440 | tf_op jit(solution)/shard_map/ppermute | solution.py:25
  49.3 6.9 %collective-permute-done.9.refs_1_ = bf16[512,256]{1,0:T(8,128)(2,1)S(1)} collective-permute-done((bf16[512,256]{1,0:T(8,128)(2,1)S(1)}, bf16[512,256]{1,0:T(8,128)(2,1)S(1)}, u32[]{:S(2)}, u32[]{:S(2)}) %collective-permute-start.9) | collective-permute-done | bytes 262176 | tf_op jit(solution)/shard_map/ppermute | solution.py:25
  56.2 3.5 %collective-permute-done.10.refs_2_ = bf16[512,256]{1,0:T(8,128)(2,1)S(1)} collective-permute-done((bf16[512,256]{1,0:T(8,128)(2,1)S(1)}, bf16[512,256]{1,0:T(8,128)(2,1)S(1)}, u32[]{:S(2)}, u32[]{:S(2)}) %collective-permute-start.10) | collective-permute-done | bytes 262176 | tf_op jit(solution)/shard_map/ppermute | solution.py:25
  59.7 2.4 %collective-permute-done.11.refs_3_ = bf16[512,256]{1,0:T(8,128)(2,1)S(1)} collective-permute-done((bf16[512,256]{1,0:T(8,128)(2,1)S(1)}, bf16[512,256]{1,0:T(8,128)(2,1)S(1)}, u32[]{:S(2)}, u32[]{:S(2)}) %collective-permute-start.11) | collective-permute-done | bytes 262176 | tf_op jit(solution)/shard_map/ppermute | solution.py:25
  62.4 1.7 %collective-permute-done.12.core = bf16[512,384]{1,0:T(8,128)(2,1)S(1)} collective-permute-done((bf16[512,384]{1,0:T(8,128)(2,1)S(1)}, bf16[512,384]{1,0:T(8,128)(2,1)S(1)}, u32[]{:S(2)}, u32[]{:S(2)}) %collective-permute-start.12) | collective-permute-done | bytes 393248 | tf_op jit(solution)/shard_map/ppermute | solution.py:20
  64.8 1.6 %shard_map.115 = (bf16[128,768]{1,0:T(8,128)(2,1)S(1)}, bf16[128,768]{1,0:T(8,128)(2,1)S(1)}, bf16[32,1024]{1,0:T(8,128)(2,1)S(1)}, bf16[32,1024]{1,0:T(8,128)(2...) custom-call(bf16[512,384]{1,0:T(8,128)(2,1)S(1)} %shard_map.114.own,, ...), custom_call_target="tpu_custom_call" | custom-call | flops 201326592 | bytes 1000000 | tf_op jit(solution)/shard_map/pallas_call | solution.py:54
  66.5 2.5 %collective-permute-start.15 = (bf16[32,1024]{1,0:T(8,128)(2,1)S(1)}, bf16[32,1024]{1,0:T(8,128)(2,1)S(1)}, u32[]{:S(2)}, u32[]{:S(2)}) collective-permute-start(bf16[32,1024]{1,0:T(8,128)(2,1)S(1)} %get-tuple-element.49), channel_id=1, source_target_pairs={{0,8},{2,10},{4,12},{6,14},{8,0},{10,2},{12,4},{14,6},{16,24},{18,... | collective-permute-start | bytes 196616 | tf_op jit(solution)/shard_map/ppermute | solution.py:34
  68.9 2.3 %collective-permute-start.16 = (bf16[32,1024]{1,0:T(8,128)(2,1)S(1)}, bf16[32,1024]{1,0:T(8,128)(2,1)S(1)}, u32[]{:S(2)}, u32[]{:S(2)}) collective-permute-start(bf16[32,1024]{1,0:T(8,128)(2,1)S(1)} %get-tuple-element.50), channel_id=1, source_target_pairs={{0,12},{2,14},{4,8},{6,10},{8,4},{10,6},{12,0},{14,2},{16,28},{18,... | collective-permute-start | bytes 196616 | tf_op jit(solution)/shard_map/ppermute | solution.py:34
  72.1 1.2 %collective-permute-start.18 = (bf16[32,1024]{1,0:T(8,128)(2,1)S(1)}, bf16[32,1024]{1,0:T(8,128)(2,1)S(1)}, u32[]{:S(2)}, u32[]{:S(2)}) collective-permute-start(bf16[32,1024]{1,0:T(8,128)(2,1)S(1)} %get-tuple-element.52), channel_id=1, source_target_pairs={{0,20},{2,22},{4,16},{6,18},{8,28},{10,30},{12,24},{14,26},{16,4},... | collective-permute-start | bytes 196616 | tf_op jit(solution)/shard_map/ppermute | solution.py:34
  73.3 1.5 %collective-permute-start.19 = (bf16[32,1024]{1,0:T(8,128)(2,1)S(1)}, bf16[32,1024]{1,0:T(8,128)(2,1)S(1)}, u32[]{:S(2)}, u32[]{:S(2)}) collective-permute-start(bf16[32,1024]{1,0:T(8,128)(2,1)S(1)} %get-tuple-element.53), channel_id=1, source_target_pairs={{0,24},{2,26},{4,28},{6,30},{8,16},{10,18},{12,20},{14,22},{16,8},... | collective-permute-start | bytes 196616 | tf_op jit(solution)/shard_map/ppermute | solution.py:34
  74.7 3.2 %collective-permute-start.20 = (bf16[32,1024]{1,0:T(8,128)(2,1)S(1)}, bf16[32,1024]{1,0:T(8,128)(2,1)S(1)}, u32[]{:S(2)}, u32[]{:S(2)}) collective-permute-start(bf16[32,1024]{1,0:T(8,128)(2,1)S(1)} %get-tuple-element.54), channel_id=1, source_target_pairs={{0,28},{2,30},{4,24},{6,26},{8,20},{10,22},{12,16},{14,18},{16,12}... | collective-permute-start | bytes 196616 | tf_op jit(solution)/shard_map/ppermute | solution.py:34
  78.9 2.8 %collective-permute-done.20.refs_7_ = bf16[32,1024]{1,0:T(8,128)(2,1)S(1)} collective-permute-done((bf16[32,1024]{1,0:T(8,128)(2,1)S(1)}, bf16[32,1024]{1,0:T(8,128)(2,1)S(1)}, u32[]{:S(2)}, u32[]{:S(2)}) %collective-permute-start.20) | collective-permute-done | bytes 65568 | tf_op jit(solution)/shard_map/ppermute | solution.py:34
  81.8 2.0 %collective-permute-start.23 = (bf16[32,1024]{1,0:T(8,128)(2,1)S(1)}, bf16[32,1024]{1,0:T(8,128)(2,1)S(1)}, u32[]{:S(2)}, u32[]{:S(2)}) collective-permute-start(bf16[32,1024]{1,0:T(8,128)(2,1)S(1)} %shard_map.117), channel_id=1, source_target_pairs={{0,6},{2,4},{4,2},{6,0},{8,14},{10,12},{12,10},{14,8},{16,22},{18,... | collective-permute-start | bytes 196616 | tf_op jit(solution)/shard_map/ppermute | solution.py:34
  83.8 1.3 %collective-permute-start.22 = (bf16[32,1024]{1,0:T(8,128)(2,1)S(1)}, bf16[32,1024]{1,0:T(8,128)(2,1)S(1)}, u32[]{:S(2)}, u32[]{:S(2)}) collective-permute-start(bf16[32,1024]{1,0:T(8,128)(2,1)S(1)} %shard_map.117), channel_id=1, source_target_pairs={{0,4},{2,6},{4,0},{6,2},{8,12},{10,14},{12,8},{14,10},{16,20},{18,... | collective-permute-start | bytes 196616 | tf_op jit(solution)/shard_map/ppermute | solution.py:34
  85.1 1.2 %collective-permute-start.21 = (bf16[32,1024]{1,0:T(8,128)(2,1)S(1)}, bf16[32,1024]{1,0:T(8,128)(2,1)S(1)}, u32[]{:S(2)}, u32[]{:S(2)}) collective-permute-start(bf16[32,1024]{1,0:T(8,128)(2,1)S(1)} %shard_map.117), channel_id=1, source_target_pairs={{0,2},{2,0},{4,6},{6,4},{8,10},{10,8},{12,14},{14,12},{16,18},{18,... | collective-permute-start | bytes 196616 | tf_op jit(solution)/shard_map/ppermute | solution.py:34
  86.2 1.8 %collective-permute-done.23 = bf16[32,1024]{1,0:T(8,128)(2,1)S(1)} collective-permute-done((bf16[32,1024]{1,0:T(8,128)(2,1)S(1)}, bf16[32,1024]{1,0:T(8,128)(2,1)S(1)}, u32[]{:S(2)}, u32[]{:S(2)}) %collective-permute-start.23) | collective-permute-done | bytes 65568 | tf_op jit(solution)/shard_map/ppermute | solution.py:34
  88.0 1.3 %collective-permute-done.22 = bf16[32,1024]{1,0:T(8,128)(2,1)S(1)} collective-permute-done((bf16[32,1024]{1,0:T(8,128)(2,1)S(1)}, bf16[32,1024]{1,0:T(8,128)(2,1)S(1)}, u32[]{:S(2)}, u32[]{:S(2)}) %collective-permute-start.22) | collective-permute-done | bytes 65568 | tf_op jit(solution)/shard_map/ppermute | solution.py:34
  90.0 1.2 %collective-permute-start.26 = (bf16[4,32,1024]{2,1,0:T(8,128)(2,1)S(1)}, bf16[4,32,1024]{2,1,0:T(8,128)(2,1)S(1)}, u32[]{:S(2)}, u32[]{:S(2)}) collective-permute-start(bf16[4,32,1024]{2,1,0:T(8,128)(2,1)S(1)} %pad_maximum_fusion.refs_0_), channel_id=1, source_target_pairs={{0,24},{2,26},{4,28},{6,30},{8,16},{10,18},{12,20},{14,22},{16,8},... | collective-permute-start | bytes 786440 | tf_op jit(solution)/shard_map/ppermute | solution.py:34
  92.1 1.5 %collective-permute-start.24 = (bf16[4,32,1024]{2,1,0:T(8,128)(2,1)S(1)}, bf16[4,32,1024]{2,1,0:T(8,128)(2,1)S(1)}, u32[]{:S(2)}, u32[]{:S(2)}) collective-permute-start(bf16[4,32,1024]{2,1,0:T(8,128)(2,1)S(1)} %pad_maximum_fusion.refs_0_), channel_id=1, source_target_pairs={{0,8},{2,10},{4,12},{6,14},{8,0},{10,2},{12,4},{14,6},{16,24},{18,... | collective-permute-start | bytes 786440 | tf_op jit(solution)/shard_map/ppermute | solution.py:34
  94.1 5.1 %collective-permute-done.13.pair = bf16[128,768]{1,0:T(8,128)(2,1)S(1)} collective-permute-done((bf16[128,768]{1,0:T(8,128)(2,1)S(1)}, bf16[128,768]{1,0:T(8,128)(2,1)S(1)}, u32[]{:S(2)}, u32[]{:S(2)}) %collective-permute-start.13) | collective-permute-done | bytes 196640 | tf_op jit(solution)/shard_map/ppermute | solution.py:20
  99.2 1.6 %shard_map.116 = bf16[128,512]{1,0:T(8,128)(2,1)S(1)} custom-call(bf16[128,768]{1,0:T(8,128)(2,1)S(1)} %get-tuple-element.45.mine, bf16[128,768]{1,0:T(8,128)(2,1)S(1)} %collective-permute-done.13.pair, bf16[256,512]{1,0:T(8,128)(2,1)S(1)} %copy-done.8, bf16[256,512]{1,0:T(8,128)(2,1)S(1)} %collective-permute-done.3.wq1, bf16[256,512]{1,0:T(8,128)(2,1)S(1)} %copy-done.9, ...), custom_call_target="tpu_custom_call" | custom-call | flops 201326592 | bytes 1000000 | tf_op jit(solution)/shard_map/pallas_call | solution.py:54
  101.5 1.5 %collective-permute-done.25.refs_2_ = bf16[4,32,1024]{2,1,0:T(8,128)(2,1)S(1)} collective-permute-done((bf16[4,32,1024]{2,1,0:T(8,128)(2,1)S(1)}, bf16[4,32,1024]{2,1,0:T(8,128)(2,1)S(1)}, u32[]{:S(2)}, u32[]{:S(2)}) %collective-permute-start.25) | collective-permute-done | bytes 262176 | tf_op jit(solution)/shard_map/ppermute | solution.py:34
  103.1 1.5 %shard_map.118 = (f32[256,512]{1,0:T(8,128)}, f32[256,512]{1,0:T(8,128)}, f32[256,512]{1,0:T(8,128)}, f32[256,512]{1,0:T(8,128)}) custom-call(bf16[4,32,1024]{2,1,0:T(8,128)(2,1)S(1)} %pad_maximum_fusion.refs_0_, bf16[4,32,1024]{2,1,0:T(8,128)(2,1)S(1)} %collective-permute-done.24.refs_1_, bf16[4,32,1024]{2,1,0:T(8,128)(2,1)S(1)} %collective-permute-done.25.refs_2_, ...), custom_call_target="tpu_custom_call" | custom-call | flops 1000000 | bytes 1000000 | tf_op jit(solution)/shard_map/pallas_call | solution.py:54
  (70 shorter events, 15.5 us)
Async XLA Ops:
  1.6 11.6 %copy-start.10 = (bf16[256,512]{1,0:T(8,128)(2,1)S(1)}, bf16[256,512]{1,0:T(8,128)(2,1)}, u32[]{:S(2)}) copy-start(bf16[256,512]{1,0:T(8,128)(2,1)} %wv0.3) | copy-start | bytes 786436
  1.7 11.5 %copy-start.9 = (bf16[256,512]{1,0:T(8,128)(2,1)S(1)}, bf16[256,512]{1,0:T(8,128)(2,1)}, u32[]{:S(2)}) copy-start(bf16[256,512]{1,0:T(8,128)(2,1)} %wk0.3) | copy-start | bytes 786436
  1.8 10.9 %copy-start.8 = (bf16[256,512]{1,0:T(8,128)(2,1)S(1)}, bf16[256,512]{1,0:T(8,128)(2,1)}, u32[]{:S(2)}) copy-start(bf16[256,512]{1,0:T(8,128)(2,1)} %wq0.3) | copy-start | bytes 786436
  1.8 13.6 %copy-start = (bf16[128,1280]{1,0:T(8,128)(2,1)}, bf16[128,1280]{1,0:T(8,128)(2,1)S(1)}, u32[]{:S(2)}) copy-start(bf16[128,1280]{1,0:T(8,128)(2,1)S(1)} %get-tuple-element.32.own) | copy-start | bytes 983044
  1.8 10.8 %collective-permute-start.1 = (bf16[128,1280]{1,0:T(8,128)(2,1)S(1)}, bf16[128,1280]{1,0:T(8,128)(2,1)S(1)}, u32[]{:S(2)}, u32[]{:S(2)}) collective-permute-start(bf16[128,1280]{1,0:T(8,128)(2,1)S(1)} %get-tuple-element.33), channel_id=1, source_target_pairs={{0,2},{2,0},{4,6},{6,4},{1,3},{3,1},{5,7},{7,5},{8,10},{10,8},{12,... | collective-permute-start | bytes 983048 | tf_op jit(solution)/shard_map/ppermute | solution.py:20
  4.9 10.5 %collective-permute-start = (bf16[128,1280]{1,0:T(8,128)(2,1)S(1)}, bf16[128,1280]{1,0:T(8,128)(2,1)S(1)}, u32[]{:S(2)}, u32[]{:S(2)}) collective-permute-start(bf16[128,1280]{1,0:T(8,128)(2,1)S(1)} %get-tuple-element.32.own), channel_id=1, source_target_pairs={{0,1},{1,0},{2,3},{3,2},{4,5},{5,4},{6,7},{7,6},{8,9},{9,8},{10,11... | collective-permute-start | bytes 983048 | tf_op jit(solution)/shard_map/ppermute | solution.py:20
  12.6 2.8 %copy-start.2 = (bf16[128,1280]{1,0:T(8,128)(2,1)}, bf16[128,1280]{1,0:T(8,128)(2,1)S(1)}, u32[]{:S(2)}) copy-start(bf16[128,1280]{1,0:T(8,128)(2,1)S(1)} %collective-permute-done.1.pair) | copy-start | bytes 983044
  12.6 2.8 %collective-permute-start.2 = (bf16[128,1280]{1,0:T(8,128)(2,1)S(1)}, bf16[128,1280]{1,0:T(8,128)(2,1)S(1)}, u32[]{:S(2)}, u32[]{:S(2)}) collective-permute-start(bf16[128,1280]{1,0:T(8,128)(2,1)S(1)} %collective-permute-done.1.pair), channel_id=1, source_target_pairs={{0,1},{1,0},{2,3},{3,2},{4,5},{5,4},{6,7},{7,6},{8,9},{9,8},{10,11... | collective-permute-start | bytes 983048 | tf_op jit(solution)/shard_map/ppermute | solution.py:20
  12.7 2.0 %collective-permute-start.3 = (bf16[256,512]{1,0:T(8,128)(2,1)S(1)}, bf16[256,512]{1,0:T(8,128)(2,1)S(1)}, u32[]{:S(2)}, u32[]{:S(2)}) collective-permute-start(bf16[256,512]{1,0:T(8,128)(2,1)S(1)} %copy-done.8), channel_id=1, source_target_pairs={{0,1},{1,0},{2,3},{3,2},{4,5},{5,4},{6,7},{7,6},{8,9},{9,8},{10,11... | collective-permute-start | bytes 786440 | tf_op jit(solution)/shard_map/ppermute | solution.py:20
  13.2 1.9 %collective-permute-start.4 = (bf16[256,512]{1,0:T(8,128)(2,1)S(1)}, bf16[256,512]{1,0:T(8,128)(2,1)S(1)}, u32[]{:S(2)}, u32[]{:S(2)}) collective-permute-start(bf16[256,512]{1,0:T(8,128)(2,1)S(1)} %copy-done.9), channel_id=1, source_target_pairs={{0,1},{1,0},{2,3},{3,2},{4,5},{5,4},{6,7},{7,6},{8,9},{9,8},{10,11... | collective-permute-start | bytes 786440 | tf_op jit(solution)/shard_map/ppermute | solution.py:20
  13.2 2.2 %collective-permute-start.5 = (bf16[256,512]{1,0:T(8,128)(2,1)S(1)}, bf16[256,512]{1,0:T(8,128)(2,1)S(1)}, u32[]{:S(2)}, u32[]{:S(2)}) collective-permute-start(bf16[256,512]{1,0:T(8,128)(2,1)S(1)} %copy-done.10), channel_id=1, source_target_pairs={{0,1},{1,0},{2,3},{3,2},{4,5},{5,4},{6,7},{7,6},{8,9},{9,8},{10,11... | collective-permute-start | bytes 786440 | tf_op jit(solution)/shard_map/ppermute | solution.py:20
  19.0 15.0 %collective-permute-start.8 = (bf16[512,256]{1,0:T(8,128)(2,1)S(1)}, bf16[512,256]{1,0:T(8,128)(2,1)S(1)}, u32[]{:S(2)}, u32[]{:S(2)}) collective-permute-start(bf16[512,256]{1,0:T(8,128)(2,1)S(1)} %get-tuple-element.37.refs_0_), channel_id=1, source_target_pairs={{0,4},{2,6},{4,0},{6,2},{1,5},{3,7},{5,1},{7,3},{8,12},{10,14},{12... | collective-permute-start | bytes 786440 | tf_op jit(solution)/shard_map/ppermute | solution.py:25
  21.8 12.2 %collective-permute-start.7 = (bf16[512,256]{1,0:T(8,128)(2,1)S(1)}, bf16[512,256]{1,0:T(8,128)(2,1)S(1)}, u32[]{:S(2)}, u32[]{:S(2)}) collective-permute-start(bf16[512,256]{1,0:T(8,128)(2,1)S(1)} %get-tuple-element.37.refs_0_), channel_id=1, source_target_pairs={{0,24},{8,0},{16,8},{24,16},{1,25},{9,1},{17,9},{25,17},{2,26},{10... | collective-permute-start | bytes 786440 | tf_op jit(solution)/shard_map/ppermute | solution.py:25
  24.3 12.2 %collective-permute-start.6 = (bf16[512,256]{1,0:T(8,128)(2,1)S(1)}, bf16[512,256]{1,0:T(8,128)(2,1)S(1)}, u32[]{:S(2)}, u32[]{:S(2)}) collective-permute-start(bf16[512,256]{1,0:T(8,128)(2,1)S(1)} %get-tuple-element.37.refs_0_), channel_id=1, source_target_pairs={{0,8},{8,16},{16,24},{24,0},{1,9},{9,17},{17,25},{25,1},{2,10},{10... | collective-permute-start | bytes 786440 | tf_op jit(solution)/shard_map/ppermute | solution.py:25
  46.9 9.3 %collective-permute-start.9 = (bf16[512,256]{1,0:T(8,128)(2,1)S(1)}, bf16[512,256]{1,0:T(8,128)(2,1)S(1)}, u32[]{:S(2)}, u32[]{:S(2)}) collective-permute-start(bf16[512,256]{1,0:T(8,128)(2,1)S(1)} %get-tuple-element.40), channel_id=1, source_target_pairs={{0,24},{8,0},{16,8},{24,16},{1,25},{9,1},{17,9},{25,17},{2,26},{10... | collective-permute-start | bytes 786440 | tf_op jit(solution)/shard_map/ppermute | solution.py:25
  48.3 11.3 %collective-permute-start.10 = (bf16[512,256]{1,0:T(8,128)(2,1)S(1)}, bf16[512,256]{1,0:T(8,128)(2,1)S(1)}, u32[]{:S(2)}, u32[]{:S(2)}) collective-permute-start(bf16[512,256]{1,0:T(8,128)(2,1)S(1)} %get-tuple-element.41), channel_id=1, source_target_pairs={{0,8},{8,16},{16,24},{24,0},{1,9},{9,17},{17,25},{25,1},{2,10},{10... | collective-permute-start | bytes 786440 | tf_op jit(solution)/shard_map/ppermute | solution.py:25
  48.9 13.2 %collective-permute-start.11 = (bf16[512,256]{1,0:T(8,128)(2,1)S(1)}, bf16[512,256]{1,0:T(8,128)(2,1)S(1)}, u32[]{:S(2)}, u32[]{:S(2)}) collective-permute-start(bf16[512,256]{1,0:T(8,128)(2,1)S(1)} %get-tuple-element.42), channel_id=1, source_target_pairs={{0,4},{2,6},{4,0},{6,2},{1,5},{3,7},{5,1},{7,3},{8,12},{10,14},{12... | collective-permute-start | bytes 786440 | tf_op jit(solution)/shard_map/ppermute | solution.py:25
  62.3 1.8 %collective-permute-start.12 = (bf16[512,384]{1,0:T(8,128)(2,1)S(1)}, bf16[512,384]{1,0:T(8,128)(2,1)S(1)}, u32[]{:S(2)}, u32[]{:S(2)}) collective-permute-start(bf16[512,384]{1,0:T(8,128)(2,1)S(1)} %shard_map.114.own), channel_id=1, source_target_pairs={{0,1},{1,0},{2,3},{3,2},{4,5},{5,4},{6,7},{7,6},{8,9},{9,8},{10,11... | collective-permute-start | bytes 1179656 | tf_op jit(solution)/shard_map/ppermute | solution.py:20
  66.4 6.8 %collective-permute-start.14 = (bf16[32,1024]{1,0:T(8,128)(2,1)S(1)}, bf16[32,1024]{1,0:T(8,128)(2,1)S(1)}, u32[]{:S(2)}, u32[]{:S(2)}) collective-permute-start(bf16[32,1024]{1,0:T(8,128)(2,1)S(1)} %get-tuple-element.48), channel_id=1, source_target_pairs={{0,4},{2,6},{4,0},{6,2},{8,12},{10,14},{12,8},{14,10},{16,20},{18,... | collective-permute-start | bytes 196616 | tf_op jit(solution)/shard_map/ppermute | solution.py:34
  66.5 8.2 %collective-permute-start.15 = (bf16[32,1024]{1,0:T(8,128)(2,1)S(1)}, bf16[32,1024]{1,0:T(8,128)(2,1)S(1)}, u32[]{:S(2)}, u32[]{:S(2)}) collective-permute-start(bf16[32,1024]{1,0:T(8,128)(2,1)S(1)} %get-tuple-element.49), channel_id=1, source_target_pairs={{0,8},{2,10},{4,12},{6,14},{8,0},{10,2},{12,4},{14,6},{16,24},{18,... | collective-permute-start | bytes 196616 | tf_op jit(solution)/shard_map/ppermute | solution.py:34
  68.9 9.0 %collective-permute-start.16 = (bf16[32,1024]{1,0:T(8,128)(2,1)S(1)}, bf16[32,1024]{1,0:T(8,128)(2,1)S(1)}, u32[]{:S(2)}, u32[]{:S(2)}) collective-permute-start(bf16[32,1024]{1,0:T(8,128)(2,1)S(1)} %get-tuple-element.50), channel_id=1, source_target_pairs={{0,12},{2,14},{4,8},{6,10},{8,4},{10,6},{12,0},{14,2},{16,28},{18,... | collective-permute-start | bytes 196616 | tf_op jit(solution)/shard_map/ppermute | solution.py:34
  71.2 6.8 %collective-permute-start.17 = (bf16[32,1024]{1,0:T(8,128)(2,1)S(1)}, bf16[32,1024]{1,0:T(8,128)(2,1)S(1)}, u32[]{:S(2)}, u32[]{:S(2)}) collective-permute-start(bf16[32,1024]{1,0:T(8,128)(2,1)S(1)} %get-tuple-element.51), channel_id=1, source_target_pairs={{0,16},{2,18},{4,20},{6,22},{8,24},{10,26},{12,28},{14,30},{16,0},... | collective-permute-start | bytes 196616 | tf_op jit(solution)/shard_map/ppermute | solution.py:34
  72.1 6.8 %collective-permute-start.18 = (bf16[32,1024]{1,0:T(8,128)(2,1)S(1)}, bf16[32,1024]{1,0:T(8,128)(2,1)S(1)}, u32[]{:S(2)}, u32[]{:S(2)}) collective-permute-start(bf16[32,1024]{1,0:T(8,128)(2,1)S(1)} %get-tuple-element.52), channel_id=1, source_target_pairs={{0,20},{2,22},{4,16},{6,18},{8,28},{10,30},{12,24},{14,26},{16,4},... | collective-permute-start | bytes 196616 | tf_op jit(solution)/shard_map/ppermute | solution.py:34
  73.3 5.7 %collective-permute-start.19 = (bf16[32,1024]{1,0:T(8,128)(2,1)S(1)}, bf16[32,1024]{1,0:T(8,128)(2,1)S(1)}, u32[]{:S(2)}, u32[]{:S(2)}) collective-permute-start(bf16[32,1024]{1,0:T(8,128)(2,1)S(1)} %get-tuple-element.53), channel_id=1, source_target_pairs={{0,24},{2,26},{4,28},{6,30},{8,16},{10,18},{12,20},{14,22},{16,8},... | collective-permute-start | bytes 196616 | tf_op jit(solution)/shard_map/ppermute | solution.py:34
  74.7 7.0 %collective-permute-start.20 = (bf16[32,1024]{1,0:T(8,128)(2,1)S(1)}, bf16[32,1024]{1,0:T(8,128)(2,1)S(1)}, u32[]{:S(2)}, u32[]{:S(2)}) collective-permute-start(bf16[32,1024]{1,0:T(8,128)(2,1)S(1)} %get-tuple-element.54), channel_id=1, source_target_pairs={{0,28},{2,30},{4,24},{6,26},{8,20},{10,22},{12,16},{14,18},{16,12}... | collective-permute-start | bytes 196616 | tf_op jit(solution)/shard_map/ppermute | solution.py:34
  81.8 6.2 %collective-permute-start.23 = (bf16[32,1024]{1,0:T(8,128)(2,1)S(1)}, bf16[32,1024]{1,0:T(8,128)(2,1)S(1)}, u32[]{:S(2)}, u32[]{:S(2)}) collective-permute-start(bf16[32,1024]{1,0:T(8,128)(2,1)S(1)} %shard_map.117), channel_id=1, source_target_pairs={{0,6},{2,4},{4,2},{6,0},{8,14},{10,12},{12,10},{14,8},{16,22},{18,... | collective-permute-start | bytes 196616 | tf_op jit(solution)/shard_map/ppermute | solution.py:34
  83.8 5.5 %collective-permute-start.22 = (bf16[32,1024]{1,0:T(8,128)(2,1)S(1)}, bf16[32,1024]{1,0:T(8,128)(2,1)S(1)}, u32[]{:S(2)}, u32[]{:S(2)}) collective-permute-start(bf16[32,1024]{1,0:T(8,128)(2,1)S(1)} %shard_map.117), channel_id=1, source_target_pairs={{0,4},{2,6},{4,0},{6,2},{8,12},{10,14},{12,8},{14,10},{16,20},{18,... | collective-permute-start | bytes 196616 | tf_op jit(solution)/shard_map/ppermute | solution.py:34
  85.1 4.9 %collective-permute-start.21 = (bf16[32,1024]{1,0:T(8,128)(2,1)S(1)}, bf16[32,1024]{1,0:T(8,128)(2,1)S(1)}, u32[]{:S(2)}, u32[]{:S(2)}) collective-permute-start(bf16[32,1024]{1,0:T(8,128)(2,1)S(1)} %shard_map.117), channel_id=1, source_target_pairs={{0,2},{2,0},{4,6},{6,4},{8,10},{10,8},{12,14},{14,12},{16,18},{18,... | collective-permute-start | bytes 196616 | tf_op jit(solution)/shard_map/ppermute | solution.py:34
  90.0 11.5 %collective-permute-start.26 = (bf16[4,32,1024]{2,1,0:T(8,128)(2,1)S(1)}, bf16[4,32,1024]{2,1,0:T(8,128)(2,1)S(1)}, u32[]{:S(2)}, u32[]{:S(2)}) collective-permute-start(bf16[4,32,1024]{2,1,0:T(8,128)(2,1)S(1)} %pad_maximum_fusion.refs_0_), channel_id=1, source_target_pairs={{0,24},{2,26},{4,28},{6,30},{8,16},{10,18},{12,20},{14,22},{16,8},... | collective-permute-start | bytes 786440 | tf_op jit(solution)/shard_map/ppermute | solution.py:34
  91.2 11.8 %collective-permute-start.25 = (bf16[4,32,1024]{2,1,0:T(8,128)(2,1)S(1)}, bf16[4,32,1024]{2,1,0:T(8,128)(2,1)S(1)}, u32[]{:S(2)}, u32[]{:S(2)}) collective-permute-start(bf16[4,32,1024]{2,1,0:T(8,128)(2,1)S(1)} %pad_maximum_fusion.refs_0_), channel_id=1, source_target_pairs={{0,16},{2,18},{4,20},{6,22},{8,24},{10,26},{12,28},{14,30},{16,0},... | collective-permute-start | bytes 786440 | tf_op jit(solution)/shard_map/ppermute | solution.py:34
  92.1 11.1 %collective-permute-start.24 = (bf16[4,32,1024]{2,1,0:T(8,128)(2,1)S(1)}, bf16[4,32,1024]{2,1,0:T(8,128)(2,1)S(1)}, u32[]{:S(2)}, u32[]{:S(2)}) collective-permute-start(bf16[4,32,1024]{2,1,0:T(8,128)(2,1)S(1)} %pad_maximum_fusion.refs_0_), channel_id=1, source_target_pairs={{0,8},{2,10},{4,12},{6,14},{8,0},{10,2},{12,4},{14,6},{16,24},{18,... | collective-permute-start | bytes 786440 | tf_op jit(solution)/shard_map/ppermute | solution.py:34
  93.5 5.7 %collective-permute-start.13 = (bf16[128,768]{1,0:T(8,128)(2,1)S(1)}, bf16[128,768]{1,0:T(8,128)(2,1)S(1)}, u32[]{:S(2)}, u32[]{:S(2)}) collective-permute-start(bf16[128,768]{1,0:T(8,128)(2,1)S(1)} %get-tuple-element.46), channel_id=1, source_target_pairs={{0,2},{2,0},{4,6},{6,4},{1,3},{3,1},{5,7},{7,5},{8,10},{10,8},{12,... | collective-permute-start | bytes 589832 | tf_op jit(solution)/shard_map/ppermute | solution.py:20
  (12 other events, 13.8 us)

commit v2 on v1

v2 whole, which is shorter than its diff:
```python
import functools
import math

import jax
import jax.numpy as jnp
from jax import lax
from jax.experimental import pallas as pl
from jax.experimental.pallas import tpu as pltpu
from jax.sharding import PartitionSpec as P

HEADS = 8
PART = 128
BF = jnp.bfloat16
F32 = jnp.float32
VMEM_BYTES = 32 * 1024 * 1024


def from_partner(block, axis):
    route = [(index, index ^ 1) for index in range(lax.axis_size(axis))]
    return lax.ppermute(block, axis, route)


def shifted(value, axis, steps):
    count = lax.axis_size(axis)
    return lax.ppermute(value, axis, [(source, (source + steps) % count) for source in range(count)])


def plane_swap(value, flip_x, flip_y):
    count_x, count_y = lax.axis_size("gx"), lax.axis_size("gy")
    route = []
    for at_x in range(count_x):
        for at_y in range(count_y):
            route.append((at_x * count_y + at_y, (at_x ^ flip_x) * count_y + (at_y ^ flip_y)))
    return lax.ppermute(value, ("gx", "gy"), route)


def dot_nn(left, right):
    return lax.dot_general(left, right, (((1,), (0,)), ((), ())), preferred_element_type=F32)


def dot_nt(left, right):
    return lax.dot_general(left, right, (((1,), (1,)), ((), ())), preferred_element_type=F32)


def dot_tn(left, right):
    return lax.dot_general(left, right, (((0,), (0,)), ((), ())), preferred_element_type=F32)


def columns(start):
    return pl.ds(pl.multiple_of(start, PART), PART)


def call(kernel, out_shape, args, scratch=(), flops=1e6, moved=1e6, exps=0):
    return pl.pallas_call(
        kernel,
        out_shape=out_shape,
        scratch_shapes=list(scratch),
        compiler_params=pltpu.CompilerParams(vmem_limit_bytes=VMEM_BYTES),
        cost_estimate=pl.CostEstimate(
            flops=int(flops), bytes_accessed=int(moved), transcendentals=int(exps)
        ),
    )(*args)


def shape_of(dims, dtype=BF):
    return jax.ShapeDtypeStruct(dims, dtype)


def pack_kernel(dy_ref, saved_ref, pair_ref, own_ref):
    y_bit = lax.axis_index("gy") % 2
    z_bit = lax.axis_index("gz") % 2
    last = PART + dy_ref.shape[1]
    for out in (pair_ref, own_ref):
        out[:, PART:last] = dy_ref[...]
    pair_ref[:, 0:PART] = saved_ref[:, columns((z_bit * 2 + 1 - y_bit) * PART)]
    pair_ref[:, last:] = saved_ref[:, columns(((1 - z_bit) * 2 + 1 - y_bit) * PART)]
    own_ref[:, 0:PART] = saved_ref[:, columns(((1 - z_bit) * 2 + y_bit) * PART)]
    own_ref[:, last:] = saved_ref[:, columns((z_bit * 2 + y_bit) * PART)]


def project_kernel(
    own_half, own, core, pair, far, wq0, wq1, wk0, wk1, wv0, wv1, q_ref, k_ref, v_ref, w_cols
):
    y_bit = lax.axis_index("gy") % 2
    z_bit = lax.axis_index("gz") % 2
    half = z_bit if own_half else z_bit * 0
    group = columns((z_bit * 2 + y_bit) * PART)
    half_rows = wq0.shape[0]
    width = 2 * half_rows
    for at, (first, second) in enumerate(((wq0, wq1), (wk0, wk1), (wv0, wv1))):
        spot = slice(at * PART, (at + 1) * PART)
        w_cols[pl.ds(pl.multiple_of(half * half_rows, half_rows), half_rows), spot] = first[:, group]
        w_cols[pl.ds(pl.multiple_of((1 - half) * half_rows, half_rows), half_rows), spot] = second[:, group]
    for at, source in enumerate((own, core, pair, far)):
        rows = slice(at * PART, (at + 1) * PART)
        made = dot_nn(source[...], w_cols[...])
        q_ref[rows, :] = made[:, 0:PART].astype(BF) * jnp.asarray(1.0 / math.sqrt(width // HEADS), BF)
        k_ref[rows, :] = made[:, PART : 2 * PART].astype(BF)
        v_ref[rows, :] = made[:, 2 * PART :].astype(BF)


def early_kernel(
    f_own, f_core, f_pair, f_far, own, core, pair, far, wout,
    do_ref, delta_ref, feat_t_ref, o_ref, saved, dys,
):
    y_bit = lax.axis_index("gy") % 2
    z_bit = lax.axis_index("gz") % 2
    width = f_own.shape[1]
    half = width // 2
    last = PART + width
    for at, (source, spot) in enumerate(((own, last), (core, 0), (pair, 0), (far, last))):
        rows = slice(at * PART, (at + 1) * PART)
        saved[rows, :] = source[:, spot : spot + PART]
        dys[rows, :] = source[:, PART:last]
    for at, source in enumerate((f_own, f_core, f_pair, f_far)):
        wanted = source[:, pl.ds(pl.multiple_of(z_bit * half, PART), half)]
        feat_t_ref[:, at * PART : (at + 1) * PART] = wanted.astype(F32).T.astype(BF)
    w_rows = wout[pl.ds(pl.multiple_of(y_bit * PART, PART), PART), :]
    out_grad = dot_nt(dys[...], w_rows).astype(BF)
    do_ref[...] = out_grad
    head_dim = width // HEADS
    products = (out_grad.astype(F32) * saved[...].astype(F32)).T
    delta_ref[0:1, :] = jnp.sum(products[0:head_dim], axis=0, keepdims=True)
    delta_ref[1:2, :] = jnp.sum(products[head_dim:PART], axis=0, keepdims=True)
    out = dot_nn(saved[...].astype(F32).T.astype(BF), dys[...]).astype(BF)
    for at in range(4):
        low = out[at * 32 : (at + 1) * 32, :]
        o_ref[at * 64 : at * 64 + 32, :] = low[:, 0:half]
        o_ref[at * 64 + 32 : at * 64 + 64, :] = low[:, half:]


def by_head(value):
    low = lax.broadcasted_iota(jnp.int32, value.shape, 1) < PART // 2
    none = jnp.zeros_like(value)
    return (jnp.where(low, value, none), jnp.where(low, none, value))


def row_scale(table, at, tokens):
    low = lax.broadcasted_iota(jnp.int32, (tokens, PART), 1) < PART // 2
    return jnp.where(low, table[:, 2 * at : 2 * at + 1], table[:, 2 * at + 1 : 2 * at + 2])


def score_kernel(times, q_ref, do_ref, *refs):
    count = len(times)
    keys_in = refs[:count]
    e_ref, part_ref = refs[count : count + 2]
    dvs = refs[count + 2 : 2 * count + 2]
    keys_s, top_s, total_s, fcol_s, dv_s = refs[2 * count + 2 :]
    tokens = q_ref.shape[0]
    for at in range(count):
        keys_s[at] = keys_in[at][...]
    q_heads = by_head(q_ref[...])

    def first(at, carry):
        keys = keys_s[at]
        for head in range(2):
            scores = dot_nt(keys, q_heads[head])
            top = jnp.max(scores, axis=0, keepdims=True)
            grown = jnp.exp(scores - top)
            e_ref[2 * at + head] = grown.astype(BF)
            top_s[pl.ds(2 * at + head, 1), :] = top
            total_s[pl.ds(2 * at + head, 1), :] = jnp.sum(grown, axis=0, keepdims=True)
        return carry

    lax.fori_loop(0, count, first, 0)
    for head in range(2):
        tops = [top_s[2 * at + head : 2 * at + head + 1, :] for at in range(count)]
        most = functools.reduce(jnp.maximum, tops)
        lifts = [jnp.exp(top - most) for top in tops]
        total = functools.reduce(
            jnp.add,
            [
                times[at] * lifts[at] * total_s[2 * at + head : 2 * at + head + 1, :]
                for at in range(count)
            ],
        )
        for at in range(count):
            part_ref[2 * at + head : 2 * at + head + 1, :] = lifts[at] / total
    if part_ref.shape[0] > 2 * count:
        part_ref[2 * count :, :] = jnp.zeros((part_ref.shape[0] - 2 * count, tokens), F32)
    turned = part_ref[...].T
    for at in range(count):
        fcol_s[at] = row_scale(turned, at, tokens)
    grad = do_ref[...].astype(F32)

    def second(at, carry):
        g_heads = by_head((grad * fcol_s[at]).astype(BF))
        dv_s[at] = (dot_nn(e_ref[2 * at], g_heads[0]) + dot_nn(e_ref[2 * at + 1], g_heads[1])).astype(BF)
        return carry

    lax.fori_loop(0, count, second, 0)
    for at in range(count):
        dvs[at][...] = dv_s[at]


def gradient_kernel(times, q_ref, do_ref, delta_ref, e_ref, part_ref, *refs):
    count = len(times)
    keys_in, values_in = refs[:count], refs[count : 2 * count]
    dq_ref = refs[2 * count]
    dks = refs[2 * count + 1 : 3 * count + 1]
    keys_s, values_s, f_s, fcol_s, dq_s, dk_s = refs[3 * count + 1 :]
    tokens = q_ref.shape[0]
    head_dim = PART // 2
    turned = part_ref[...].T
    for at in range(count):
        keys_s[at] = keys_in[at][...]
        values_s[at] = values_in[at][...]
        fcol_s[at] = row_scale(turned, at, tokens)
        f_s[2 * at : 2 * at + 2, :] = part_ref[2 * at : 2 * at + 2, :] * times[at]
    g_heads = by_head(do_ref[...])
    query = q_ref[...].astype(F32)
    delta = delta_ref[...]
    dq_s[...] = jnp.zeros_like(dq_s)

    def step(at, carry):
        keys_t = keys_s[at].astype(F32).T.astype(BF)
        values = values_s[at]
        q_heads = by_head((query * fcol_s[at]).astype(BF))
        dk = jnp.zeros((tokens, PART), F32)
        for head in range(2):
            dprob = dot_nt(values, g_heads[head])
            dscore = (e_ref[2 * at + head].astype(F32) * (dprob - delta[head : head + 1, :])).astype(BF)
            dk = dk + dot_nn(dscore, q_heads[head])
            spot = slice(head * head_dim, (head + 1) * head_dim)
            dq_s[spot, :] = dq_s[spot, :] + dot_nn(keys_t[spot, :], dscore) * f_s[
                pl.ds(2 * at + head, 1), :
            ]
        dk_s[at] = dk.astype(BF)
        return carry

    lax.fori_loop(0, count, step, 0)
    for at in range(count):
        dks[at][...] = dk_s[at]
    dq_ref[...] = (dq_s[...].T * (1.0 / math.sqrt(head_dim))).astype(BF)


def combined(times, refs):
    total = times[0] * refs[0][...].astype(F32)
    for time, ref in zip(times[1:], refs[1:]):
        total = total + time * ref[...].astype(F32)
    return total.astype(BF)


def collect_values_kernel(times, dq_ref, *refs):
    refs[-1][:, 0:PART] = dq_ref[...]
    refs[-1][:, PART:] = combined(times, refs[:-1])


def collect_keys_kernel(times, *refs):
    refs[-1][...] = combined(times, refs[:-1])


def place_grads(grads, own, core, count):
    z_bit = lax.axis_index("gz") % 2
    for at in range(count):
        source = slice(at * PART, (at + 1) * PART)
        grads[:, columns(at * 2 * PART + z_bit * PART)] = own[:, source]
        core_at = columns(at * 2 * PART + (1 - z_bit) * PART)
        for low in range(4):
            grads[low * PART : (low + 1) * PART, core_at] = core[
                (low ^ 1) * PART : ((low ^ 1) + 1) * PART, source
            ]


def weight_early_kernel(own, core, feat_t, o_ref, held_ref, rows_ref, grads):
    place_grads(grads, own, core, 2)
    wide = grads.shape[1]
    held_ref[:, 0:wide] = dot_nn(feat_t[...], grads[...]).astype(BF)
    held_ref[:, wide:] = o_ref[...]
    rows_ref[0] = grads[0:PART, :]
    rows_ref[1] = grads[2 * PART : 3 * PART, :]


def weight_late_kernel(chunks, own, core, feat_t, held_ref, rows_ref, pair_ref, mine_ref, *refs):
    outs, (grads, made) = refs[:chunks], refs[chunks:]
    place_grads(grads, own, core, 1)
    early = rows_ref.shape[2]
    mine_ref[:, 0:early] = rows_ref[0]
    mine_ref[:, early:] = grads[0:PART, :]
    pair_ref[:, 0:early] = rows_ref[1]
    pair_ref[:, early:] = grads[2 * PART : 3 * PART, :]
    made[...] = dot_nn(feat_t[...], grads[...]).astype(BF)
    rows = made.shape[0] // chunks
    wide = held_ref.shape[1]
    for at in range(chunks):
        spot = pl.ds(0, rows)
        if chunks > 1:
            spot = pl.ds(pl.multiple_of((lax.axis_index("gx") ^ at) * rows, rows), rows)
        outs[at][:, 0:wide] = held_ref[spot, :]
        outs[at][:, wide:] = made[spot, :]


def grad_x_kernel(own_half, mine, pair, wq0, wq1, wk0, wk1, wv0, wv1, out, full):
    y_bit = lax.axis_index("gy") % 2
    z_bit = lax.axis_index("gz") % 2
    half = z_bit if own_half else z_bit * 0
    width = wq0.shape[1]
    half_rows = wq0.shape[0]
    for at in range(3):
        for side in range(2):
            spot = slice((at * 2 + side) * PART, (at * 2 + side + 1) * PART)
            base = at * width + side * 2 * PART
            full[:, columns(base + y_bit * PART)] = mine[:, spot]
            full[:, columns(base + (1 - y_bit) * PART)] = pair[:, spot]
    for at, sources in ((half, (wq0, wv0, wk0)), (1 - half, (wq1, wv1, wk1))):
        total = functools.reduce(
            jnp.add,
            [dot_nt(full[:, n * width : (n + 1) * width], sources[n][...]) for n in range(3)],
        )
        out[:, pl.ds(pl.multiple_of(at * half_rows, PART), half_rows)] = total.astype(BF)


def sum_kernel(*refs):
    total = refs[0][...].astype(F32)
    for ref in refs[1:-1]:
        total = total + ref[...].astype(F32)
    refs[-1][...] = total.astype(BF)


def spread_kernel(*refs):
    pieces, outs = refs[:8], refs[8:]
    half = 2 * PART
    rows = pieces[0].shape[0]
    for at, piece in enumerate(pieces):
        place = lax.axis_index("gx") ^ (at // 2)
        bit = (lax.axis_index("gy") % 2) ^ (at % 2)
        spot = pl.ds(pl.multiple_of(place * rows, rows), rows)
        for base, out in ((0, outs[0]), (3, outs[1]), (1, outs[2])):
            for side in range(2):
                source = slice((base * 2 + side) * PART, (base * 2 + side + 1) * PART)
                out[spot, columns(side * half + bit * PART)] = piece[:, source].astype(F32)
        spot = pl.ds(pl.multiple_of(bit * PART + place * (rows // 2), rows // 2), rows // 2)
        outs[3][spot, 0:half] = piece[0 : rows // 2, 2 * half : 3 * half].astype(F32)
        outs[3][spot, half:] = piece[rows // 2 :, 2 * half : 3 * half].astype(F32)


def on_device(features, grad_y, attn_out, w_query, w_key, w_value, w_out):
    width = features.shape[-1]
    half = width // 2
    tokens = features.shape[0] * features.shape[1] * features.shape[2]
    block_tokens = 4 * tokens
    count_x, count_y, count_z = lax.axis_size("gx"), lax.axis_size("gy"), lax.axis_size("gz")
    z_bit = lax.axis_index("gz") % 2
    y_bit = lax.axis_index("gy") % 2

    own_half = count_z == 2
    if own_half:
        pairs = []
        for weight in (w_query, w_key, w_value):
            pairs += [weight, from_partner(weight, "gz")]
        out_rows = w_out
    else:
        pairs = []
        for weight in (w_query, w_key, w_value):
            whole = lax.all_gather(weight, "gz", axis=0, tiled=True)
            pairs += [whole[:half], whole[half:]]
        whole = lax.all_gather(w_out, "gz", axis=0, tiled=True)
        out_rows = lax.dynamic_slice_in_dim(whole, z_bit * half, half, 0)

    message = shape_of((tokens, width + 2 * PART))
    feat = features.reshape(tokens, width)
    feat_pair = from_partner(feat, "gy")
    feat_core = from_partner(feat, "gz")
    feat_pair, feat_core, *pairs = lax.optimization_barrier((feat_pair, feat_core, *pairs))
    feat_far = from_partner(feat_pair, "gz")
    feats = [feat, feat_core, feat_pair, feat_far]
    column = shape_of((block_tokens, PART))
    query, own_keys, own_values = call(
        functools.partial(project_kernel, own_half),
        (column, column, column),
        [*feats, *pairs],
        scratch=[pltpu.VMEM((width, 3 * PART), BF)],
        flops=2 * block_tokens * width * 3 * PART,
    )
    pair_message, own = call(
        pack_kernel,
        (message, message),
        [value.reshape(tokens, width) for value in (grad_y, attn_out)],
    )
    pair = from_partner(pair_message, "gy")
    core = from_partner(own, "gz")
    far = from_partner(pair, "gz")

    times = [1.0]
    routes = []
    for axis, step, blocks in (("gx", 1, count_x), ("gy", 2, count_y // 2), ("gz", 2, count_z // 2)):
        if blocks == 1:
            times[0] += 2.0
        elif blocks == 2:
            routes.append((axis, step))
            times.append(2.0)
        else:
            routes += [(axis, step), (axis, -step)]
            times += [1.0, 1.0]
    times = tuple(times)
    count = len(times)
    keys = [own_keys] + [shifted(own_keys, axis, step) for axis, step in routes]
    values = [own_values] + [shifted(own_values, axis, step) for axis, step in routes]
    out_grad, delta, feat_t, out_term = call(
        early_kernel,
        (
            column,
            shape_of((2, block_tokens), F32),
            shape_of((half, block_tokens)),
            shape_of((half, half)),
        ),
        [*feats, own, core, pair, far, out_rows],
        scratch=[pltpu.VMEM((block_tokens, PART), BF), pltpu.VMEM((block_tokens, width), BF)],
        flops=4 * block_tokens * width * PART,
    )
    rows = -(-2 * count // 8) * 8
    pixels = 2 * count * block_tokens * block_tokens
    grown, parts, *dvs = call(
        functools.partial(score_kernel, times),
        (
            shape_of((2 * count, block_tokens, block_tokens)),
            shape_of((rows, block_tokens), F32),
            *[column] * count,
        ),
        [query, out_grad, *keys],
        scratch=[
            pltpu.VMEM((count, block_tokens, PART), BF),
            pltpu.VMEM((rows, block_tokens), F32),
            pltpu.VMEM((rows, block_tokens), F32),
            pltpu.VMEM((count, block_tokens, PART), F32),
            pltpu.VMEM((count, block_tokens, PART), BF),
        ],
        flops=4 * pixels * PART,
        moved=2 * pixels,
        exps=pixels,
    )
    dv_back = [dvs[0]]
    for partial, (axis, step) in zip(dvs[1:], routes):
        dv_back.append(shifted(partial, axis, -step))
    dq, *dks = call(
        functools.partial(gradient_kernel, times),
        (column, *[column] * count),
        [query, out_grad, delta, grown, parts, *keys, *values],
        scratch=[
            pltpu.VMEM((count, block_tokens, PART), BF),
            pltpu.VMEM((count, block_tokens, PART), BF),
            pltpu.VMEM((rows, block_tokens), F32),
            pltpu.VMEM((count, block_tokens, PART), F32),
            pltpu.VMEM((PART, block_tokens), F32),
            pltpu.VMEM((count, block_tokens, PART), BF),
        ],
        flops=6 * pixels * PART,
        moved=2 * pixels,
    )
    dk_back = [dks[0]]
    for partial, (axis, step) in zip(dks[1:], routes):
        dk_back.append(shifted(partial, axis, -step))
    early = call(
        functools.partial(collect_values_kernel, times),
        shape_of((block_tokens, 2 * PART)),
        [dq, *dv_back],
    )
    early_core = from_partner(early, "gz")
    planned = count_x == 4 and count_y == 4 and count_z == 2
    chunks = 4 if planned else 1
    piece = shape_of((half // chunks, 8 * PART))
    held, early_rows = call(
        weight_early_kernel,
        (shape_of((half, 6 * PART)), shape_of((2, tokens, 4 * PART))),
        [early, early_core, feat_t, out_term],
        scratch=[pltpu.VMEM((block_tokens, 4 * PART), BF)],
        flops=2 * block_tokens * half * 4 * PART,
    )
    late = call(functools.partial(collect_keys_kernel, times), column, dk_back)
    late_core = from_partner(late, "gz")
    pair_out, mine, *pieces = call(
        functools.partial(weight_late_kernel, chunks),
        (shape_of((tokens, 6 * PART)), shape_of((tokens, 6 * PART)), *[piece] * chunks),
        [late, late_core, feat_t, held, early_rows],
        scratch=[pltpu.VMEM((block_tokens, 2 * PART), BF), pltpu.VMEM((half, 2 * PART), BF)],
        flops=2 * block_tokens * half * 2 * PART,
    )
    pair_in = from_partner(pair_out, "gy")
    if planned:
        terms = [pieces[0]] + [plane_swap(pieces[at], at, 0) for at in (1, 2, 3)]
        total = call(sum_kernel, piece, terms)
        total = call(sum_kernel, piece, [total, plane_swap(total, 0, 2)])
        by_x, by_y, by_z = plane_swap(total, 1, 0), plane_swap(total, 2, 0), plane_swap(total, 0, 1)
        by_xy, by_xz = plane_swap(by_y, 1, 0), plane_swap(by_x, 0, 1)
        by_yz, by_xyz = plane_swap(by_z, 2, 0), plane_swap(by_z, 3, 0)
        weights = call(
            spread_kernel,
            tuple([shape_of((half, width), F32)] * 4),
            [total, by_z, by_x, by_xz, by_y, by_yz, by_xy, by_xyz],
        )
    else:
        terms = pieces[0].astype(F32)
        stacked = jnp.zeros((4, width, width), F32)
        for base, at in ((0, 0), (3, 1), (1, 2)):
            for side in range(2):
                tile = terms[:, (base * 2 + side) * PART : (base * 2 + side + 1) * PART]
                stacked = lax.dynamic_update_slice(
                    stacked, tile[None], (at, z_bit * half, side * half + y_bit * PART)
                )
        tile = terms[:, 4 * PART : 6 * PART].reshape(4, 2, 32, half)
        tile = tile.transpose(0, 2, 1, 3).reshape(PART, width)
        stacked = lax.dynamic_update_slice(
            stacked, tile[None], (3, z_bit * half + y_bit * PART, 0)
        )
        stacked = lax.psum(stacked, ("gx", "gy", "gz"))
        held_rows = w_query.shape[0]
        stacked = lax.dynamic_slice_in_dim(stacked, lax.axis_index("gz") * held_rows, held_rows, 1)
        weights = [stacked[at] for at in range(4)]
    grad_x = call(
        functools.partial(grad_x_kernel, own_half),
        shape_of((tokens, width)),
        [mine, pair_in, *pairs],
        scratch=[pltpu.VMEM((tokens, 3 * width), BF)],
        flops=2 * tokens * 3 * width * width,
    ).reshape(features.shape)
    return (grad_x, *weights)


def solution(mesh):
    return jax.shard_map(
        on_device,
        mesh=mesh,
        in_specs=(
            P("gx", "gy", "gz", None),
            P("gx", "gy", "gz", None),
            P("gx", "gy", "gz", None),
            P("gz", None),
            P("gz", None),
            P("gz", None),
            P("gz", None),
        ),
        out_specs=(
            P("gx", "gy", "gz", None),
            P("gz", None),
            P("gz", None),
            P("gz", None),
            P("gz", None),
        ),
        check_vma=False,
    )
```

time: 105 us -> 98.8 us (0.941)
  waiting for transfers between devices: 46.1 us -> 42.8 us
  Pallas kernels: 17.7 us -> 16.1 us
    ppermute x13 -> x11, starting transfers between devices: 19.6 us -> 8.6 us  [plane_swap(): return lax.ppermute(value, ('gx', 'gy'), route)]
    ppermute x13 -> x11, waiting for transfers between devices: 9.05 us -> 19.3 us  [plane_swap(): return lax.ppermute(value, ('gx', 'gy'), route)]
    ppermute x6 -> x12, starting transfers between devices: 7.69 us -> 15.9 us  [shifted(): lax.ppermute(value, axis, [(source, (source + steps) % count) for source...]
    ppermute x8 -> x12, waiting for transfers between devices: 16.2 us -> 9.46 us  [from_partner(): return lax.ppermute(block, axis, route)]
    ppermute x6 -> x12, waiting for transfers between devices: 20.8 us -> 14 us  [shifted(): lax.ppermute(value, axis, [(source, (source + steps) % count) for source...]
    unnamed x34 -> x14, local copies, waits for them, and re-layouts: 6.18 us -> 3.82 us
    ppermute x8 -> x12, starting transfers between devices: 4.75 us -> 6.98 us  [from_partner(): return lax.ppermute(block, axis, route)]
    pallas_call x9 -> x13, Pallas kernels: 17.7 us -> 16.1 us  [call(): pl.pallas_call(kernel, out_shape=out_shape, scratch_shapes=list(scratch),...]
  transfers between devices with their start and end apart: 27 -> 35, of which waited for: 18 -> 16; matrix products, arithmetic and copies ran while one was open for 1% -> 4% of each run, Pallas kernels for 2% -> 14%
where the time goes in v2:
time: 98.8 us; the launch traced here: 98.5 us
  waiting for transfers between devices  42.8 us (43%)
  starting transfers between devices  31.4 us (32%)
  Pallas kernels  16.1 us (16%)
  local copies, waits for them, and re-layouts  7.33 us (7%)
    ppermute x11, waiting for transfers between devices, plane_swap(): return lax.ppermute(value, ('gx', 'gy'), route)  19.3 us
    pallas_call x13, Pallas kernels, call(): pl.pallas_call(kernel, out_shape=out_shape, scratch_shapes=list(scratch),...  16.1 us
    ppermute x12, starting transfers between devices, shifted(): lax.ppermute(value, axis, [(source, (source + steps) % count) for source...  15.9 us
    ppermute x12, waiting for transfers between devices, shifted(): lax.ppermute(value, axis, [(source, (source + steps) % count) for source...  14 us
    ppermute x12, waiting for transfers between devices, from_partner(): return lax.ppermute(block, axis, route)  9.46 us
    ppermute x11, starting transfers between devices, plane_swap(): return lax.ppermute(value, ('gx', 'gy'), route)  8.6 us
    ppermute x12, starting transfers between devices, from_partner(): return lax.ppermute(block, axis, route)  6.98 us
    unnamed x14, local copies, waits for them, and re-layouts  3.82 us
  transfers between devices with their start and end apart: 35, of which 16 were waited for; matrix products, arithmetic and copies ran while one was open for 4% of the time, Pallas kernels for 14%

profile of v2, /device:TPU:0, one launch (start us, length us, event | category | flops | bytes accessed | tf_op | source)
XLA Modules:
  0.0 98.5 jit_solution(8161317197276590297)
XLA Ops:
  2.7 3.0 %collective-permute-start = (bf16[128,512]{1,0:T(8,128)(2,1)S(1)}, bf16[128,512]{1,0:T(8,128)(2,1)S(1)}, u32[]{:S(2)}, u32[]{:S(2)}) collective-permute-start(bf16[128,512]{1,0:T(8,128)(2,1)S(1)} %reshape.22.own.f_own), channel_id=1, source_target_pairs={{0,2},{2,0},{4,6},{6,4},{1,3},{3,1},{5,7},{7,5},{8,10},{10,8},{12,... | collective-permute-start | bytes 393224 | tf_op jit(solution)/shard_map/ppermute | solution.py:20
  7.8 1.7 %collective-permute-done.pair.f_pair = bf16[128,512]{1,0:T(8,128)(2,1)S(1)} collective-permute-done((bf16[128,512]{1,0:T(8,128)(2,1)S(1)}, bf16[128,512]{1,0:T(8,128)(2,1)S(1)}, u32[]{:S(2)}, u32[]{:S(2)}) %collective-permute-start) | collective-permute-done | bytes 131104 | tf_op jit(solution)/shard_map/ppermute | solution.py:20
  10.1 4.3 %collective-permute-done.7.pair = bf16[128,768]{1,0:T(8,128)(2,1)S(1)} collective-permute-done((bf16[128,768]{1,0:T(8,128)(2,1)S(1)}, bf16[128,768]{1,0:T(8,128)(2,1)S(1)}, u32[]{:S(2)}, u32[]{:S(2)}) %collective-permute-start.7) | collective-permute-done | bytes 196640 | tf_op jit(solution)/shard_map/ppermute | solution.py:20
  15.3 0.9 copy-done.2
  16.3 0.9 copy-done.4
  17.8 2.7 %collective-permute-start.11 = (bf16[512,128]{1,0:T(8,128)(2,1)S(1)}, bf16[512,128]{1,0:T(8,128)(2,1)S(1)}, u32[]{:S(2)}, u32[]{:S(2)}) collective-permute-start(bf16[512,128]{1,0:T(8,128)(2,1)S(1)} %get-tuple-element.58.refs_0_), channel_id=1, source_target_pairs={{0,4},{2,6},{4,0},{6,2},{1,5},{3,7},{5,1},{7,3},{8,12},{10,14},{12... | collective-permute-start | bytes 393224 | tf_op jit(solution)/shard_map/ppermute | solution.py:25
  20.4 2.4 %collective-permute-start.10 = (bf16[512,128]{1,0:T(8,128)(2,1)S(1)}, bf16[512,128]{1,0:T(8,128)(2,1)S(1)}, u32[]{:S(2)}, u32[]{:S(2)}) collective-permute-start(bf16[512,128]{1,0:T(8,128)(2,1)S(1)} %get-tuple-element.58.refs_0_), channel_id=1, source_target_pairs={{0,24},{8,0},{16,8},{24,16},{1,25},{9,1},{17,9},{25,17},{2,26},{10... | collective-permute-start | bytes 393224 | tf_op jit(solution)/shard_map/ppermute | solution.py:25
  23.2 2.9 %collective-permute-start.13 = (bf16[512,128]{1,0:T(8,128)(2,1)S(1)}, bf16[512,128]{1,0:T(8,128)(2,1)S(1)}, u32[]{:S(2)}, u32[]{:S(2)}) collective-permute-start(bf16[512,128]{1,0:T(8,128)(2,1)S(1)} %get-tuple-element.61.refs_4_), channel_id=1, source_target_pairs={{0,24},{8,0},{16,8},{24,16},{1,25},{9,1},{17,9},{25,17},{2,26},{10... | collective-permute-start | bytes 393224 | tf_op jit(solution)/shard_map/ppermute | solution.py:25
  26.1 4.5 %collective-permute-done.11.refs_3_ = bf16[512,128]{1,0:T(8,128)(2,1)S(1)} collective-permute-done((bf16[512,128]{1,0:T(8,128)(2,1)S(1)}, bf16[512,128]{1,0:T(8,128)(2,1)S(1)}, u32[]{:S(2)}, u32[]{:S(2)}) %collective-permute-start.11) | collective-permute-done | bytes 131104 | tf_op jit(solution)/shard_map/ppermute | solution.py:25
  30.6 1.5 %collective-permute-start.12 = (bf16[512,128]{1,0:T(8,128)(2,1)S(1)}, bf16[512,128]{1,0:T(8,128)(2,1)S(1)}, u32[]{:S(2)}, u32[]{:S(2)}) collective-permute-start(bf16[512,128]{1,0:T(8,128)(2,1)S(1)} %get-tuple-element.61.refs_4_), channel_id=1, source_target_pairs={{0,8},{8,16},{16,24},{24,0},{1,9},{9,17},{17,25},{25,1},{2,10},{10... | collective-permute-start | bytes 393224 | tf_op jit(solution)/shard_map/ppermute | solution.py:25
  33.6 6.0 %shard_map.113 = (bf16[8,512,512]{2,1,0:T(8,128)(2,1)S(1)}, f32[8,512]{1,0:T(8,128)S(1)}, bf16[512,128]{1,0:T(8,128)(2,1)S(1)}, bf16[512,128]{1,0:T(8,128)(2,1)S...) custom-call(bf16[512,128]{1,0:T(8,128)(2,1)S(1)} %get-tuple-element.53.q_ref, ...), custom_call_target="tpu_custom_call" | custom-call | flops 1073741824 | bytes 4194304 | tf_op jit(solution)/shard_map/pallas_call | solution.py:54
  39.6 1.5 %collective-permute-start.19 = (bf16[512,128]{1,0:T(8,128)(2,1)S(1)}, bf16[512,128]{1,0:T(8,128)(2,1)S(1)}, u32[]{:S(2)}, u32[]{:S(2)}) collective-permute-start(bf16[512,128]{1,0:T(8,128)(2,1)S(1)} %get-tuple-element.69), channel_id=1, source_target_pairs={{0,24},{8,0},{16,8},{24,16},{1,25},{9,1},{17,9},{25,17},{2,26},{10... | collective-permute-start | bytes 393224 | tf_op jit(solution)/shard_map/ppermute | solution.py:25
  41.7 5.8 %shard_map.114 = (bf16[512,128]{1,0:T(8,128)(2,1)S(1)}, bf16[512,128]{1,0:T(8,128)(2,1)S(1)}, bf16[512,128]{1,0:T(8,128)(2,1)S(1)}, bf16[512,128]{1,0:T(8,128)(2,1)S(1)}, bf16[512,128]{1,0:T(8,128)(2,1)S(1)}) custom-call(bf16[512,128]{1,0:T(8,128)(2,1)S(1)} %get-tuple-element.53.q_ref, bf16[512,128]{1,0:T(8,128)(2,1)S(1)} %get-tuple-element.56.do_ref, ...), custom_call_target="tpu_custom_call" | custom-call | flops 1610612736 | bytes 4194304 | tf_op jit(solution)/shard_map/pallas_call | solution.py:54
  47.6 1.5 %collective-permute-done.21.refs_3_ = bf16[512,128]{1,0:T(8,128)(2,1)S(1)} collective-permute-done((bf16[512,128]{1,0:T(8,128)(2,1)S(1)}, bf16[512,128]{1,0:T(8,128)(2,1)S(1)}, u32[]{:S(2)}, u32[]{:S(2)}) %collective-permute-start.21) | collective-permute-done | bytes 131104 | tf_op jit(solution)/shard_map/ppermute | solution.py:25
  49.3 2.6 %collective-permute-start.15 = (bf16[512,128]{1,0:T(8,128)(2,1)S(1)}, bf16[512,128]{1,0:T(8,128)(2,1)S(1)}, u32[]{:S(2)}, u32[]{:S(2)}) collective-permute-start(bf16[512,128]{1,0:T(8,128)(2,1)S(1)} %get-tuple-element.63), channel_id=1, source_target_pairs={{0,24},{8,0},{16,8},{24,16},{1,25},{9,1},{17,9},{25,17},{2,26},{10... | collective-permute-start | bytes 393224 | tf_op jit(solution)/shard_map/ppermute | solution.py:25
  52.0 1.2 %collective-permute-start.17 = (bf16[512,128]{1,0:T(8,128)(2,1)S(1)}, bf16[512,128]{1,0:T(8,128)(2,1)S(1)}, u32[]{:S(2)}, u32[]{:S(2)}) collective-permute-start(bf16[512,128]{1,0:T(8,128)(2,1)S(1)} %get-tuple-element.65), channel_id=1, source_target_pairs={{0,4},{2,6},{4,0},{6,2},{1,5},{3,7},{5,1},{7,3},{8,12},{10,14},{12... | collective-permute-start | bytes 393224 | tf_op jit(solution)/shard_map/ppermute | solution.py:25
  53.2 3.1 %collective-permute-done.15.refs_1_ = bf16[512,128]{1,0:T(8,128)(2,1)S(1)} collective-permute-done((bf16[512,128]{1,0:T(8,128)(2,1)S(1)}, bf16[512,128]{1,0:T(8,128)(2,1)S(1)}, u32[]{:S(2)}, u32[]{:S(2)}) %collective-permute-start.15) | collective-permute-done | bytes 131104 | tf_op jit(solution)/shard_map/ppermute | solution.py:25
  56.3 2.6 %collective-permute-done.16.refs_2_ = bf16[512,128]{1,0:T(8,128)(2,1)S(1)} collective-permute-done((bf16[512,128]{1,0:T(8,128)(2,1)S(1)}, bf16[512,128]{1,0:T(8,128)(2,1)S(1)}, u32[]{:S(2)}, u32[]{:S(2)}) %collective-permute-start.16) | collective-permute-done | bytes 131104 | tf_op jit(solution)/shard_map/ppermute | solution.py:25
  58.8 2.4 %collective-permute-done.17.refs_3_ = bf16[512,128]{1,0:T(8,128)(2,1)S(1)} collective-permute-done((bf16[512,128]{1,0:T(8,128)(2,1)S(1)}, bf16[512,128]{1,0:T(8,128)(2,1)S(1)}, u32[]{:S(2)}, u32[]{:S(2)}) %collective-permute-start.17) | collective-permute-done | bytes 131104 | tf_op jit(solution)/shard_map/ppermute | solution.py:25
  63.0 2.7 %collective-permute-start.24 = (bf16[64,1024]{1,0:T(8,128)(2,1)S(1)}, bf16[64,1024]{1,0:T(8,128)(2,1)S(1)}, u32[]{:S(2)}, u32[]{:S(2)}) collective-permute-start(bf16[64,1024]{1,0:T(8,128)(2,1)S(1)} %get-tuple-element.78), channel_id=1, source_target_pairs={{0,8},{2,10},{4,12},{6,14},{8,0},{10,2},{12,4},{14,6},{16,24},{18,... | collective-permute-start | bytes 393224 | tf_op jit(solution)/shard_map/ppermute | solution.py:34
  66.3 1.0 %collective-permute-start.26 = (bf16[64,1024]{1,0:T(8,128)(2,1)S(1)}, bf16[64,1024]{1,0:T(8,128)(2,1)S(1)}, u32[]{:S(2)}, u32[]{:S(2)}) collective-permute-start(bf16[64,1024]{1,0:T(8,128)(2,1)S(1)} %get-tuple-element.80), channel_id=1, source_target_pairs={{0,24},{2,26},{4,28},{6,30},{8,16},{10,18},{12,20},{14,22},{16,8},... | collective-permute-start | bytes 393224 | tf_op jit(solution)/shard_map/ppermute | solution.py:34
  67.3 2.4 %collective-permute-done.24.refs_1_ = bf16[64,1024]{1,0:T(8,128)(2,1)S(1)} collective-permute-done((bf16[64,1024]{1,0:T(8,128)(2,1)S(1)}, bf16[64,1024]{1,0:T(8,128)(2,1)S(1)}, u32[]{:S(2)}, u32[]{:S(2)}) %collective-permute-start.24) | collective-permute-done | bytes 131104 | tf_op jit(solution)/shard_map/ppermute | solution.py:34
  69.7 4.2 %collective-permute-done.25.refs_2_ = bf16[64,1024]{1,0:T(8,128)(2,1)S(1)} collective-permute-done((bf16[64,1024]{1,0:T(8,128)(2,1)S(1)}, bf16[64,1024]{1,0:T(8,128)(2,1)S(1)}, u32[]{:S(2)}, u32[]{:S(2)}) %collective-permute-start.25) | collective-permute-done | bytes 131104 | tf_op jit(solution)/shard_map/ppermute | solution.py:34
  74.0 7.2 %collective-permute-done.27.refs_1_ = bf16[64,1024]{1,0:T(8,128)(2,1)S(1)} collective-permute-done((bf16[64,1024]{1,0:T(8,128)(2,1)S(1)}, bf16[64,1024]{1,0:T(8,128)(2,1)S(1)}, u32[]{:S(2)}, u32[]{:S(2)}) %collective-permute-start.27) | collective-permute-done | bytes 131104 | tf_op jit(solution)/shard_map/ppermute | solution.py:34
  81.3 2.0 %collective-permute-start.29 = (bf16[64,1024]{1,0:T(8,128)(2,1)S(1)}, bf16[64,1024]{1,0:T(8,128)(2,1)S(1)}, u32[]{:S(2)}, u32[]{:S(2)}) collective-permute-start(bf16[64,1024]{1,0:T(8,128)(2,1)S(1)} %shard_map.121.refs_0_), channel_id=1, source_target_pairs={{0,8},{2,10},{4,12},{6,14},{8,0},{10,2},{12,4},{14,6},{16,24},{18,... | collective-permute-start | bytes 393224 | tf_op jit(solution)/shard_map/ppermute | solution.py:34
  83.3 2.0 %collective-permute-start.23 = (bf16[128,768]{1,0:T(8,128)(2,1)S(1)}, bf16[128,768]{1,0:T(8,128)(2,1)S(1)}, u32[]{:S(2)}, u32[]{:S(2)}) collective-permute-start(bf16[128,768]{1,0:T(8,128)(2,1)S(1)} %get-tuple-element.76), channel_id=1, source_target_pairs={{0,2},{2,0},{4,6},{6,4},{1,3},{3,1},{5,7},{7,5},{8,10},{10,8},{12,... | collective-permute-start | bytes 589832 | tf_op jit(solution)/shard_map/ppermute | solution.py:20
  85.3 1.1 %collective-permute-done.31.refs_4_ = bf16[64,1024]{1,0:T(8,128)(2,1)S(1)} collective-permute-done((bf16[64,1024]{1,0:T(8,128)(2,1)S(1)}, bf16[64,1024]{1,0:T(8,128)(2,1)S(1)}, u32[]{:S(2)}, u32[]{:S(2)}) %collective-permute-start.31) | collective-permute-done | bytes 131104 | tf_op jit(solution)/shard_map/ppermute | solution.py:34
  87.2 2.6 %collective-permute-done.28.refs_1_ = bf16[64,1024]{1,0:T(8,128)(2,1)S(1)} collective-permute-done((bf16[64,1024]{1,0:T(8,128)(2,1)S(1)}, bf16[64,1024]{1,0:T(8,128)(2,1)S(1)}, u32[]{:S(2)}, u32[]{:S(2)}) %collective-permute-start.28) | collective-permute-done | bytes 131104 | tf_op jit(solution)/shard_map/ppermute | solution.py:34
  89.7 1.4 %collective-permute-start.34 = (bf16[64,1024]{1,0:T(8,128)(2,1)S(1)}, bf16[64,1024]{1,0:T(8,128)(2,1)S(1)}, u32[]{:S(2)}, u32[]{:S(2)}) collective-permute-start(bf16[64,1024]{1,0:T(8,128)(2,1)S(1)} %collective-permute-done.28.refs_1_), channel_id=1, source_target_pairs={{0,24},{2,26},{4,28},{6,30},{8,16},{10,18},{12,20},{14,22},{16,8},... | collective-permute-start | bytes 393224 | tf_op jit(solution)/shard_map/ppermute | solution.py:34
  91.2 2.6 %collective-permute-done.23.pair = bf16[128,768]{1,0:T(8,128)(2,1)S(1)} collective-permute-done((bf16[128,768]{1,0:T(8,128)(2,1)S(1)}, bf16[128,768]{1,0:T(8,128)(2,1)S(1)}, u32[]{:S(2)}, u32[]{:S(2)}) %collective-permute-start.23) | collective-permute-done | bytes 196640 | tf_op jit(solution)/shard_map/ppermute | solution.py:20
  95.7 1.3 %collective-permute-done.32.refs_5_ = bf16[64,1024]{1,0:T(8,128)(2,1)S(1)} collective-permute-done((bf16[64,1024]{1,0:T(8,128)(2,1)S(1)}, bf16[64,1024]{1,0:T(8,128)(2,1)S(1)}, u32[]{:S(2)}, u32[]{:S(2)}) %collective-permute-start.32) | collective-permute-done | bytes 131104 | tf_op jit(solution)/shard_map/ppermute | solution.py:34
  97.0 1.5 %shard_map.122 = (f32[256,512]{1,0:T(8,128)}, f32[256,512]{1,0:T(8,128)}, f32[256,512]{1,0:T(8,128)}, f32[256,512]{1,0:T(8,128)}) custom-call(bf16[64,1024]{1,0:T(8,128)(2,1)S(1)} %shard_map.121.refs_0_, bf16[64,1024]{1,0:T(8,128)(2,1)S(1)} %collective-permute-done.28.refs_1_, bf16[64,1024]{1,0:T(8,128)(2,1)S(1)} %collective-permute-done.29.refs_2_, ...), custom_call_target="tpu_custom_call" | custom-call | flops 1000000 | bytes 1000000 | tf_op jit(solution)/shard_map/pallas_call | solution.py:54
  (69 shorter events, 14.1 us)
Async XLA Ops:
  0.6 8.9 %collective-permute-start.2 = (bf16[256,512]{1,0:T(8,128)(2,1)}, bf16[256,512]{1,0:T(8,128)(2,1)S(1)}, u32[]{:S(2)}, u32[]{:S(2)}) collective-permute-start(bf16[256,512]{1,0:T(8,128)(2,1)} %wq0.1), channel_id=1, source_target_pairs={{0,1},{1,0},{2,3},{3,2},{4,5},{5,4},{6,7},{7,6},{8,9},{9,8},{10,11... | collective-permute-start | bytes 786440 | tf_op jit(solution)/shard_map/ppermute | solution.py:20
  1.1 8.4 %collective-permute-start.3 = (bf16[256,512]{1,0:T(8,128)(2,1)}, bf16[256,512]{1,0:T(8,128)(2,1)S(1)}, u32[]{:S(2)}, u32[]{:S(2)}) collective-permute-start(bf16[256,512]{1,0:T(8,128)(2,1)} %wk0.1), channel_id=1, source_target_pairs={{0,1},{1,0},{2,3},{3,2},{4,5},{5,4},{6,7},{7,6},{8,9},{9,8},{10,11... | collective-permute-start | bytes 786440 | tf_op jit(solution)/shard_map/ppermute | solution.py:20
  1.2 8.3 %collective-permute-start.4 = (bf16[256,512]{1,0:T(8,128)(2,1)}, bf16[256,512]{1,0:T(8,128)(2,1)S(1)}, u32[]{:S(2)}, u32[]{:S(2)}) collective-permute-start(bf16[256,512]{1,0:T(8,128)(2,1)} %wv0.1), channel_id=1, source_target_pairs={{0,1},{1,0},{2,3},{3,2},{4,5},{5,4},{6,7},{7,6},{8,9},{9,8},{10,11... | collective-permute-start | bytes 786440 | tf_op jit(solution)/shard_map/ppermute | solution.py:20
  2.7 6.8 %collective-permute-start = (bf16[128,512]{1,0:T(8,128)(2,1)S(1)}, bf16[128,512]{1,0:T(8,128)(2,1)S(1)}, u32[]{:S(2)}, u32[]{:S(2)}) collective-permute-start(bf16[128,512]{1,0:T(8,128)(2,1)S(1)} %reshape.22.own.f_own), channel_id=1, source_target_pairs={{0,2},{2,0},{4,6},{6,4},{1,3},{3,1},{5,7},{7,5},{8,10},{10,8},{12,... | collective-permute-start | bytes 393224 | tf_op jit(solution)/shard_map/ppermute | solution.py:20
  7.7 6.7 %collective-permute-start.7 = (bf16[128,768]{1,0:T(8,128)(2,1)S(1)}, bf16[128,768]{1,0:T(8,128)(2,1)S(1)}, u32[]{:S(2)}, u32[]{:S(2)}) collective-permute-start(bf16[128,768]{1,0:T(8,128)(2,1)S(1)} %get-tuple-element.55), channel_id=1, source_target_pairs={{0,2},{2,0},{4,6},{6,4},{1,3},{3,1},{5,7},{7,5},{8,10},{10,8},{12,... | collective-permute-start | bytes 589832 | tf_op jit(solution)/shard_map/ppermute | solution.py:20
  9.6 13.3 %collective-permute-start.6 = (bf16[128,768]{1,0:T(8,128)(2,1)S(1)}, bf16[128,768]{1,0:T(8,128)(2,1)S(1)}, u32[]{:S(2)}, u32[]{:S(2)}) collective-permute-start(bf16[128,768]{1,0:T(8,128)(2,1)S(1)} %get-tuple-element.54.own), channel_id=1, source_target_pairs={{0,1},{1,0},{2,3},{3,2},{4,5},{5,4},{6,7},{7,6},{8,9},{9,8},{10,11... | collective-permute-start | bytes 589832 | tf_op jit(solution)/shard_map/ppermute | solution.py:20
  14.4 8.8 %collective-permute-start.8 = (bf16[128,768]{1,0:T(8,128)(2,1)S(1)}, bf16[128,768]{1,0:T(8,128)(2,1)S(1)}, u32[]{:S(2)}, u32[]{:S(2)}) collective-permute-start(bf16[128,768]{1,0:T(8,128)(2,1)S(1)} %collective-permute-done.7.pair), channel_id=1, source_target_pairs={{0,1},{1,0},{2,3},{3,2},{4,5},{5,4},{6,7},{7,6},{8,9},{9,8},{10,11... | collective-permute-start | bytes 589832 | tf_op jit(solution)/shard_map/ppermute | solution.py:20
  17.8 12.9 %collective-permute-start.11 = (bf16[512,128]{1,0:T(8,128)(2,1)S(1)}, bf16[512,128]{1,0:T(8,128)(2,1)S(1)}, u32[]{:S(2)}, u32[]{:S(2)}) collective-permute-start(bf16[512,128]{1,0:T(8,128)(2,1)S(1)} %get-tuple-element.58.refs_0_), channel_id=1, source_target_pairs={{0,4},{2,6},{4,0},{6,2},{1,5},{3,7},{5,1},{7,3},{8,12},{10,14},{12... | collective-permute-start | bytes 393224 | tf_op jit(solution)/shard_map/ppermute | solution.py:25
  20.4 13.1 %collective-permute-start.10 = (bf16[512,128]{1,0:T(8,128)(2,1)S(1)}, bf16[512,128]{1,0:T(8,128)(2,1)S(1)}, u32[]{:S(2)}, u32[]{:S(2)}) collective-permute-start(bf16[512,128]{1,0:T(8,128)(2,1)S(1)} %get-tuple-element.58.refs_0_), channel_id=1, source_target_pairs={{0,24},{8,0},{16,8},{24,16},{1,25},{9,1},{17,9},{25,17},{2,26},{10... | collective-permute-start | bytes 393224 | tf_op jit(solution)/shard_map/ppermute | solution.py:25
  22.9 10.7 %collective-permute-start.9 = (bf16[512,128]{1,0:T(8,128)(2,1)S(1)}, bf16[512,128]{1,0:T(8,128)(2,1)S(1)}, u32[]{:S(2)}, u32[]{:S(2)}) collective-permute-start(bf16[512,128]{1,0:T(8,128)(2,1)S(1)} %get-tuple-element.58.refs_0_), channel_id=1, source_target_pairs={{0,8},{8,16},{16,24},{24,0},{1,9},{9,17},{17,25},{25,1},{2,10},{10... | collective-permute-start | bytes 393224 | tf_op jit(solution)/shard_map/ppermute | solution.py:25
  22.9 18.8 %collective-permute-start.14 = (bf16[512,128]{1,0:T(8,128)(2,1)S(1)}, bf16[512,128]{1,0:T(8,128)(2,1)S(1)}, u32[]{:S(2)}, u32[]{:S(2)}) collective-permute-start(bf16[512,128]{1,0:T(8,128)(2,1)S(1)} %get-tuple-element.61.refs_4_), channel_id=1, source_target_pairs={{0,4},{2,6},{4,0},{6,2},{1,5},{3,7},{5,1},{7,3},{8,12},{10,14},{12... | collective-permute-start | bytes 393224 | tf_op jit(solution)/shard_map/ppermute | solution.py:25
  23.2 18.5 %collective-permute-start.13 = (bf16[512,128]{1,0:T(8,128)(2,1)S(1)}, bf16[512,128]{1,0:T(8,128)(2,1)S(1)}, u32[]{:S(2)}, u32[]{:S(2)}) collective-permute-start(bf16[512,128]{1,0:T(8,128)(2,1)S(1)} %get-tuple-element.61.refs_4_), channel_id=1, source_target_pairs={{0,24},{8,0},{16,8},{24,16},{1,25},{9,1},{17,9},{25,17},{2,26},{10... | collective-permute-start | bytes 393224 | tf_op jit(solution)/shard_map/ppermute | solution.py:25
  30.6 11.0 %collective-permute-start.12 = (bf16[512,128]{1,0:T(8,128)(2,1)S(1)}, bf16[512,128]{1,0:T(8,128)(2,1)S(1)}, u32[]{:S(2)}, u32[]{:S(2)}) collective-permute-start(bf16[512,128]{1,0:T(8,128)(2,1)S(1)} %get-tuple-element.61.refs_4_), channel_id=1, source_target_pairs={{0,8},{8,16},{16,24},{24,0},{1,9},{9,17},{17,25},{25,1},{2,10},{10... | collective-permute-start | bytes 393224 | tf_op jit(solution)/shard_map/ppermute | solution.py:25
  39.6 8.0 %collective-permute-start.19 = (bf16[512,128]{1,0:T(8,128)(2,1)S(1)}, bf16[512,128]{1,0:T(8,128)(2,1)S(1)}, u32[]{:S(2)}, u32[]{:S(2)}) collective-permute-start(bf16[512,128]{1,0:T(8,128)(2,1)S(1)} %get-tuple-element.69), channel_id=1, source_target_pairs={{0,24},{8,0},{16,8},{24,16},{1,25},{9,1},{17,9},{25,17},{2,26},{10... | collective-permute-start | bytes 393224 | tf_op jit(solution)/shard_map/ppermute | solution.py:25
  41.1 6.5 %collective-permute-start.20 = (bf16[512,128]{1,0:T(8,128)(2,1)S(1)}, bf16[512,128]{1,0:T(8,128)(2,1)S(1)}, u32[]{:S(2)}, u32[]{:S(2)}) collective-permute-start(bf16[512,128]{1,0:T(8,128)(2,1)S(1)} %get-tuple-element.70), channel_id=1, source_target_pairs={{0,8},{8,16},{16,24},{24,0},{1,9},{9,17},{17,25},{25,1},{2,10},{10... | collective-permute-start | bytes 393224 | tf_op jit(solution)/shard_map/ppermute | solution.py:25
  41.7 7.4 %collective-permute-start.21 = (bf16[512,128]{1,0:T(8,128)(2,1)S(1)}, bf16[512,128]{1,0:T(8,128)(2,1)S(1)}, u32[]{:S(2)}, u32[]{:S(2)}) collective-permute-start(bf16[512,128]{1,0:T(8,128)(2,1)S(1)} %get-tuple-element.71), channel_id=1, source_target_pairs={{0,4},{2,6},{4,0},{6,2},{1,5},{3,7},{5,1},{7,3},{8,12},{10,14},{12... | collective-permute-start | bytes 393224 | tf_op jit(solution)/shard_map/ppermute | solution.py:25
  49.2 12.2 %collective-permute-start.22 = (bf16[512,256]{1,0:T(8,128)(2,1)S(1)}, bf16[512,256]{1,0:T(8,128)(2,1)S(1)}, u32[]{:S(2)}, u32[]{:S(2)}) collective-permute-start(bf16[512,256]{1,0:T(8,128)(2,1)S(1)} %shard_map.116.own), channel_id=1, source_target_pairs={{0,1},{1,0},{2,3},{3,2},{4,5},{5,4},{6,7},{7,6},{8,9},{9,8},{10,11... | collective-permute-start | bytes 786440 | tf_op jit(solution)/shard_map/ppermute | solution.py:20
  49.3 7.0 %collective-permute-start.15 = (bf16[512,128]{1,0:T(8,128)(2,1)S(1)}, bf16[512,128]{1,0:T(8,128)(2,1)S(1)}, u32[]{:S(2)}, u32[]{:S(2)}) collective-permute-start(bf16[512,128]{1,0:T(8,128)(2,1)S(1)} %get-tuple-element.63), channel_id=1, source_target_pairs={{0,24},{8,0},{16,8},{24,16},{1,25},{9,1},{17,9},{25,17},{2,26},{10... | collective-permute-start | bytes 393224 | tf_op jit(solution)/shard_map/ppermute | solution.py:25
  51.9 7.0 %collective-permute-start.16 = (bf16[512,128]{1,0:T(8,128)(2,1)S(1)}, bf16[512,128]{1,0:T(8,128)(2,1)S(1)}, u32[]{:S(2)}, u32[]{:S(2)}) collective-permute-start(bf16[512,128]{1,0:T(8,128)(2,1)S(1)} %get-tuple-element.64), channel_id=1, source_target_pairs={{0,8},{8,16},{16,24},{24,0},{1,9},{9,17},{17,25},{25,1},{2,10},{10... | collective-permute-start | bytes 393224 | tf_op jit(solution)/shard_map/ppermute | solution.py:25
  52.0 9.2 %collective-permute-start.17 = (bf16[512,128]{1,0:T(8,128)(2,1)S(1)}, bf16[512,128]{1,0:T(8,128)(2,1)S(1)}, u32[]{:S(2)}, u32[]{:S(2)}) collective-permute-start(bf16[512,128]{1,0:T(8,128)(2,1)S(1)} %get-tuple-element.65), channel_id=1, source_target_pairs={{0,4},{2,6},{4,0},{6,2},{1,5},{3,7},{5,1},{7,3},{8,12},{10,14},{12... | collective-permute-start | bytes 393224 | tf_op jit(solution)/shard_map/ppermute | solution.py:25
  63.0 6.6 %collective-permute-start.24 = (bf16[64,1024]{1,0:T(8,128)(2,1)S(1)}, bf16[64,1024]{1,0:T(8,128)(2,1)S(1)}, u32[]{:S(2)}, u32[]{:S(2)}) collective-permute-start(bf16[64,1024]{1,0:T(8,128)(2,1)S(1)} %get-tuple-element.78), channel_id=1, source_target_pairs={{0,8},{2,10},{4,12},{6,14},{8,0},{10,2},{12,4},{14,6},{16,24},{18,... | collective-permute-start | bytes 393224 | tf_op jit(solution)/shard_map/ppermute | solution.py:34
  65.7 8.1 %collective-permute-start.25 = (bf16[64,1024]{1,0:T(8,128)(2,1)S(1)}, bf16[64,1024]{1,0:T(8,128)(2,1)S(1)}, u32[]{:S(2)}, u32[]{:S(2)}) collective-permute-start(bf16[64,1024]{1,0:T(8,128)(2,1)S(1)} %get-tuple-element.79), channel_id=1, source_target_pairs={{0,16},{2,18},{4,20},{6,22},{8,24},{10,26},{12,28},{14,30},{16,0},... | collective-permute-start | bytes 393224 | tf_op jit(solution)/shard_map/ppermute | solution.py:34
  66.3 7.6 %collective-permute-start.26 = (bf16[64,1024]{1,0:T(8,128)(2,1)S(1)}, bf16[64,1024]{1,0:T(8,128)(2,1)S(1)}, u32[]{:S(2)}, u32[]{:S(2)}) collective-permute-start(bf16[64,1024]{1,0:T(8,128)(2,1)S(1)} %get-tuple-element.80), channel_id=1, source_target_pairs={{0,24},{2,26},{4,28},{6,30},{8,16},{10,18},{12,20},{14,22},{16,8},... | collective-permute-start | bytes 393224 | tf_op jit(solution)/shard_map/ppermute | solution.py:34
  73.9 7.2 %collective-permute-start.27 = (bf16[64,1024]{1,0:T(8,128)(2,1)S(1)}, bf16[64,1024]{1,0:T(8,128)(2,1)S(1)}, u32[]{:S(2)}, u32[]{:S(2)}) collective-permute-start(bf16[64,1024]{1,0:T(8,128)(2,1)S(1)} %shard_map.120.refs_0_), channel_id=1, source_target_pairs={{0,4},{2,6},{4,0},{6,2},{8,12},{10,14},{12,8},{14,10},{16,20},{18,... | collective-permute-start | bytes 393224 | tf_op jit(solution)/shard_map/ppermute | solution.py:34
  81.2 5.3 %collective-permute-start.31 = (bf16[64,1024]{1,0:T(8,128)(2,1)S(1)}, bf16[64,1024]{1,0:T(8,128)(2,1)S(1)}, u32[]{:S(2)}, u32[]{:S(2)}) collective-permute-start(bf16[64,1024]{1,0:T(8,128)(2,1)S(1)} %shard_map.121.refs_0_), channel_id=1, source_target_pairs={{0,16},{2,18},{4,20},{6,22},{8,24},{10,26},{12,28},{14,30},{16,0},... | collective-permute-start | bytes 393224 | tf_op jit(solution)/shard_map/ppermute | solution.py:34
  81.3 5.9 %collective-permute-start.29 = (bf16[64,1024]{1,0:T(8,128)(2,1)S(1)}, bf16[64,1024]{1,0:T(8,128)(2,1)S(1)}, u32[]{:S(2)}, u32[]{:S(2)}) collective-permute-start(bf16[64,1024]{1,0:T(8,128)(2,1)S(1)} %shard_map.121.refs_0_), channel_id=1, source_target_pairs={{0,8},{2,10},{4,12},{6,14},{8,0},{10,2},{12,4},{14,6},{16,24},{18,... | collective-permute-start | bytes 393224 | tf_op jit(solution)/shard_map/ppermute | solution.py:34
  83.3 6.4 %collective-permute-start.28 = (bf16[64,1024]{1,0:T(8,128)(2,1)S(1)}, bf16[64,1024]{1,0:T(8,128)(2,1)S(1)}, u32[]{:S(2)}, u32[]{:S(2)}) collective-permute-start(bf16[64,1024]{1,0:T(8,128)(2,1)S(1)} %shard_map.121.refs_0_), channel_id=1, source_target_pairs={{0,2},{2,0},{4,6},{6,4},{8,10},{10,8},{12,14},{14,12},{16,18},{18,... | collective-permute-start | bytes 393224 | tf_op jit(solution)/shard_map/ppermute | solution.py:34
  83.3 10.5 %collective-permute-start.23 = (bf16[128,768]{1,0:T(8,128)(2,1)S(1)}, bf16[128,768]{1,0:T(8,128)(2,1)S(1)}, u32[]{:S(2)}, u32[]{:S(2)}) collective-permute-start(bf16[128,768]{1,0:T(8,128)(2,1)S(1)} %get-tuple-element.76), channel_id=1, source_target_pairs={{0,2},{2,0},{4,6},{6,4},{1,3},{3,1},{5,7},{7,5},{8,10},{10,8},{12,... | collective-permute-start | bytes 589832 | tf_op jit(solution)/shard_map/ppermute | solution.py:20
  86.5 8.7 %collective-permute-start.33 = (bf16[64,1024]{1,0:T(8,128)(2,1)S(1)}, bf16[64,1024]{1,0:T(8,128)(2,1)S(1)}, u32[]{:S(2)}, u32[]{:S(2)}) collective-permute-start(bf16[64,1024]{1,0:T(8,128)(2,1)S(1)} %collective-permute-done.31.refs_4_), channel_id=1, source_target_pairs={{0,8},{2,10},{4,12},{6,14},{8,0},{10,2},{12,4},{14,6},{16,24},{18,... | collective-permute-start | bytes 393224 | tf_op jit(solution)/shard_map/ppermute | solution.py:34
  87.2 8.0 %collective-permute-start.30 = (bf16[64,1024]{1,0:T(8,128)(2,1)S(1)}, bf16[64,1024]{1,0:T(8,128)(2,1)S(1)}, u32[]{:S(2)}, u32[]{:S(2)}) collective-permute-start(bf16[64,1024]{1,0:T(8,128)(2,1)S(1)} %collective-permute-done.29.refs_2_), channel_id=1, source_target_pairs={{0,2},{2,0},{4,6},{6,4},{8,10},{10,8},{12,14},{14,12},{16,18},{18,... | collective-permute-start | bytes 393224 | tf_op jit(solution)/shard_map/ppermute | solution.py:34
  89.7 6.0 %collective-permute-start.34 = (bf16[64,1024]{1,0:T(8,128)(2,1)S(1)}, bf16[64,1024]{1,0:T(8,128)(2,1)S(1)}, u32[]{:S(2)}, u32[]{:S(2)}) collective-permute-start(bf16[64,1024]{1,0:T(8,128)(2,1)S(1)} %collective-permute-done.28.refs_1_), channel_id=1, source_target_pairs={{0,24},{2,26},{4,28},{6,30},{8,16},{10,18},{12,20},{14,22},{16,8},... | collective-permute-start | bytes 393224 | tf_op jit(solution)/shard_map/ppermute | solution.py:34
  91.2 5.8 %collective-permute-start.32 = (bf16[64,1024]{1,0:T(8,128)(2,1)S(1)}, bf16[64,1024]{1,0:T(8,128)(2,1)S(1)}, u32[]{:S(2)}, u32[]{:S(2)}) collective-permute-start(bf16[64,1024]{1,0:T(8,128)(2,1)S(1)} %collective-permute-done.28.refs_1_), channel_id=1, source_target_pairs={{0,16},{2,18},{4,20},{6,22},{8,24},{10,26},{12,28},{14,30},{16,0},... | collective-permute-start | bytes 393224 | tf_op jit(solution)/shard_map/ppermute | solution.py:34
  (10 other events, 171.4 us)

commit v3 on v2

--- a/solution.py
+++ b/solution.py
@@ -78,19 +78,20 @@
     own_ref[:, last:] = saved_ref[:, columns((z_bit * 2 + y_bit) * PART)]
 
 
-def project_kernel(
-    own_half, own, core, pair, far, wq0, wq1, wk0, wk1, wv0, wv1, q_ref, k_ref, v_ref, w_cols
-):
+def columns_kernel(own_half, wq0, wq1, wk0, wk1, wv0, wv1, w_cols):
     y_bit = lax.axis_index("gy") % 2
     z_bit = lax.axis_index("gz") % 2
     half = z_bit if own_half else z_bit * 0
     group = columns((z_bit * 2 + y_bit) * PART)
     half_rows = wq0.shape[0]
-    width = 2 * half_rows
     for at, (first, second) in enumerate(((wq0, wq1), (wk0, wk1), (wv0, wv1))):
         spot = slice(at * PART, (at + 1) * PART)
         w_cols[pl.ds(pl.multiple_of(half * half_rows, half_rows), half_rows), spot] = first[:, group]
         w_cols[pl.ds(pl.multiple_of((1 - half) * half_rows, half_rows), half_rows), spot] = second[:, group]
+
+
+def project_kernel(own, core, pair, far, w_cols, q_ref, k_ref, v_ref):
+    width = own.shape[1]
     for at, source in enumerate((own, core, pair, far)):
         rows = slice(at * PART, (at + 1) * PART)
         made = dot_nn(source[...], w_cols[...])
@@ -162,7 +163,7 @@
             total_s[pl.ds(2 * at + head, 1), :] = jnp.sum(grown, axis=0, keepdims=True)
         return carry
 
-    lax.fori_loop(0, count, first, 0)
+    lax.fori_loop(0, count, first, 0, unroll=True)
     for head in range(2):
         tops = [top_s[2 * at + head : 2 * at + head + 1, :] for at in range(count)]
         most = functools.reduce(jnp.maximum, tops)
@@ -188,7 +189,7 @@
         dv_s[at] = (dot_nn(e_ref[2 * at], g_heads[0]) + dot_nn(e_ref[2 * at + 1], g_heads[1])).astype(BF)
         return carry
 
-    lax.fori_loop(0, count, second, 0)
+    lax.fori_loop(0, count, second, 0, unroll=True)
     for at in range(count):
         dvs[at][...] = dv_s[at]
 
@@ -228,7 +229,7 @@
         dk_s[at] = dk.astype(BF)
         return carry
 
-    lax.fori_loop(0, count, step, 0)
+    lax.fori_loop(0, count, step, 0, unroll=True)
     for at in range(count):
         dks[at][...] = dk_s[at]
     dq_ref[...] = (dq_s[...].T * (1.0 / math.sqrt(head_dim))).astype(BF)
@@ -361,23 +362,28 @@
     feat = features.reshape(tokens, width)
     feat_pair = from_partner(feat, "gy")
     feat_core = from_partner(feat, "gz")
-    feat_pair, feat_core, *pairs = lax.optimization_barrier((feat_pair, feat_core, *pairs))
+    w_cols = call(
+        functools.partial(columns_kernel, own_half), shape_of((width, 3 * PART)), pairs
+    )
+    pair_message, own = call(
+        pack_kernel,
+        (message, message),
+        [value.reshape(tokens, width) for value in (grad_y, attn_out)],
+    )
+    feat_pair, feat_core, w_cols, own = lax.optimization_barrier(
+        (feat_pair, feat_core, w_cols, own)
+    )
+    pair = from_partner(pair_message, "gy")
     feat_far = from_partner(feat_pair, "gz")
     feats = [feat, feat_core, feat_pair, feat_far]
     column = shape_of((block_tokens, PART))
     query, own_keys, own_values = call(
-        functools.partial(project_kernel, own_half),
+        project_kernel,
         (column, column, column),
-        [*feats, *pairs],
-        scratch=[pltpu.VMEM((width, 3 * PART), BF)],
+        [*feats, w_cols],
         flops=2 * block_tokens * width * 3 * PART,
     )
-    pair_message, own = call(
-        pack_kernel,
-        (message, message),
-        [value.reshape(tokens, width) for value in (grad_y, attn_out)],
-    )
-    pair = from_partner(pair_message, "gy")
+    pair, query = lax.optimization_barrier((pair, query))
     core = from_partner(own, "gz")
     far = from_partner(pair, "gz")
 
@@ -395,7 +401,6 @@
     times = tuple(times)
     count = len(times)
     keys = [own_keys] + [shifted(own_keys, axis, step) for axis, step in routes]
-    values = [own_values] + [shifted(own_values, axis, step) for axis, step in routes]
     out_grad, delta, feat_t, out_term = call(
         early_kernel,
         (
@@ -408,6 +413,8 @@
         scratch=[pltpu.VMEM((block_tokens, PART), BF), pltpu.VMEM((block_tokens, width), BF)],
         flops=4 * block_tokens * width * PART,
     )
+    own_values, out_grad = lax.optimization_barrier((own_values, out_grad))
+    values = [own_values] + [shifted(own_values, axis, step) for axis, step in routes]
     rows = -(-2 * count // 8) * 8
     pixels = 2 * count * block_tokens * block_tokens
     grown, parts, *dvs = call(
@@ -447,6 +454,7 @@
         flops=6 * pixels * PART,
         moved=2 * pixels,
     )
+    dks, dv_back = lax.optimization_barrier((dks, dv_back))
     dk_back = [dks[0]]
     for partial, (axis, step) in zip(dks[1:], routes):
         dk_back.append(shifted(partial, axis, -step))
@@ -476,10 +484,24 @@
         flops=2 * block_tokens * half * 2 * PART,
     )
     pair_in = from_partner(pair_out, "gy")
+
+    def features_grad(pair_rows):
+        return call(
+            functools.partial(grad_x_kernel, own_half),
+            shape_of((tokens, width)),
+            [mine, pair_rows, *pairs],
+            scratch=[pltpu.VMEM((tokens, 3 * width), BF)],
+            flops=2 * tokens * 3 * width * width,
+        ).reshape(features.shape)
+
     if planned:
         terms = [pieces[0]] + [plane_swap(pieces[at], at, 0) for at in (1, 2, 3)]
         total = call(sum_kernel, piece, terms)
-        total = call(sum_kernel, piece, [total, plane_swap(total, 0, 2)])
+        total, pair_in = lax.optimization_barrier((total, pair_in))
+        other = plane_swap(total, 0, 2)
+        grad_x = features_grad(pair_in)
+        total, grad_x = lax.optimization_barrier((total, grad_x))
+        total = call(sum_kernel, piece, [total, other])
         by_x, by_y, by_z = plane_swap(total, 1, 0), plane_swap(total, 2, 0), plane_swap(total, 0, 1)
         by_xy, by_xz = plane_swap(by_y, 1, 0), plane_swap(by_x, 0, 1)
         by_yz, by_xyz = plane_swap(by_z, 2, 0), plane_swap(by_z, 3, 0)
@@ -489,6 +511,7 @@
             [total, by_z, by_x, by_xz, by_y, by_yz, by_xy, by_xyz],
         )
     else:
+        grad_x = features_grad(pair_in)
         terms = pieces[0].astype(F32)
         stacked = jnp.zeros((4, width, width), F32)
         for base, at in ((0, 0), (3, 1), (1, 2)):
@@ -506,13 +529,6 @@
         held_rows = w_query.shape[0]
         stacked = lax.dynamic_slice_in_dim(stacked, lax.axis_index("gz") * held_rows, held_rows, 1)
         weights = [stacked[at] for at in range(4)]
-    grad_x = call(
-        functools.partial(grad_x_kernel, own_half),
-        shape_of((tokens, width)),
-        [mine, pair_in, *pairs],
-        scratch=[pltpu.VMEM((tokens, 3 * width), BF)],
-        flops=2 * tokens * 3 * width * width,
-    ).reshape(features.shape)
     return (grad_x, *weights)
 
 

time: 98.8 us -> 92.4 us (0.935)
  Pallas kernels: 16.1 us -> 12.8 us
  waiting for transfers between devices: 42.8 us -> 41.1 us
  starting transfers between devices: 31.4 us -> 29.9 us
    ppermute x12, waiting for transfers between devices: 9.46 us -> 3.51 us  [from_partner(): return lax.ppermute(block, axis, route)]
    ppermute x11, waiting for transfers between devices: 19.3 us -> 23.2 us  [plane_swap(): return lax.ppermute(value, ('gx', 'gy'), route)]
    pallas_call x13 -> x14, Pallas kernels: 16.1 us -> 12.8 us  [call(): pl.pallas_call(kernel, out_shape=out_shape, scratch_shapes=list(scratch),...]
    ppermute x12, starting transfers between devices: 6.98 us -> 5.03 us  [from_partner(): return lax.ppermute(block, axis, route)]
    ppermute x11, starting transfers between devices: 8.6 us -> 9.82 us  [plane_swap(): return lax.ppermute(value, ('gx', 'gy'), route)]
  transfers between devices with their start and end apart: 35 -> 35, of which waited for: 16 -> 19; matrix products, arithmetic and copies ran while one was open for 4% -> 4% of each run, Pallas kernels for 14% -> 12%
where the time goes in v3:
time: 92.4 us; the launch traced here: 92.1 us
  waiting for transfers between devices  41.1 us (44%)
  starting transfers between devices  29.9 us (32%)
  Pallas kernels  12.8 us (14%)
  local copies, waits for them, and re-layouts  7.32 us (8%)
    ppermute x11, waiting for transfers between devices, plane_swap(): return lax.ppermute(value, ('gx', 'gy'), route)  23.2 us
    ppermute x12, starting transfers between devices, shifted(): lax.ppermute(value, axis, [(source, (source + steps) % count) for source...  15.1 us
    ppermute x12, waiting for transfers between devices, shifted(): lax.ppermute(value, axis, [(source, (source + steps) % count) for source...  14.4 us
    pallas_call x14, Pallas kernels, call(): pl.pallas_call(kernel, out_shape=out_shape, scratch_shapes=list(scratch),...  12.8 us
    ppermute x11, starting transfers between devices, plane_swap(): return lax.ppermute(value, ('gx', 'gy'), route)  9.82 us
    ppermute x12, starting transfers between devices, from_partner(): return lax.ppermute(block, axis, route)  5.03 us
    unnamed x14, local copies, waits for them, and re-layouts  3.81 us
    ppermute x12, waiting for transfers between devices, from_partner(): return lax.ppermute(block, axis, route)  3.51 us
  transfers between devices with their start and end apart: 35, of which 19 were waited for; matrix products, arithmetic and copies ran while one was open for 4% of the time, Pallas kernels for 12%

profile of v3, /device:TPU:0, one launch (start us, length us, event | category | flops | bytes accessed | tf_op | source)
XLA Modules:
  0.0 92.1 jit_solution(17582153500875592577)
XLA Ops:
  2.7 3.0 %collective-permute-start.1 = (bf16[128,512]{1,0:T(8,128)(2,1)S(1)}, bf16[128,512]{1,0:T(8,128)(2,1)S(1)}, u32[]{:S(2)}, u32[]{:S(2)}) collective-permute-start(bf16[128,512]{1,0:T(8,128)(2,1)S(1)} %reshape.24.own.f_own), channel_id=1, source_target_pairs={{0,2},{2,0},{4,6},{6,4},{1,3},{3,1},{5,7},{7,5},{8,10},{10,8},{12,... | collective-permute-start | bytes 393224 | tf_op jit(solution)/shard_map/ppermute | solution.py:20
  6.7 0.9 %reshape.23.saved_ref = bf16[128,512]{1,0:T(8,128)(2,1)S(1)} reshape(bf16[8,4,4,512]{3,2,1,0:T(4,128)(2,1)} %param.9) | data formatting | bytes 262144 | tf_op jit(solution)/shard_map/reshape | solution.py:371
  8.8 0.9 %copy-done.2 = bf16[256,512]{1,0:T(8,128)(2,1)S(1)} copy-done((bf16[256,512]{1,0:T(8,128)(2,1)S(1)}, bf16[256,512]{1,0:T(8,128)(2,1)}, u32[]{:S(2)}) %copy-start.2) | copy-done | bytes 262168
  9.7 0.9 %copy-done.4 = bf16[256,512]{1,0:T(8,128)(2,1)S(1)} copy-done((bf16[256,512]{1,0:T(8,128)(2,1)S(1)}, bf16[256,512]{1,0:T(8,128)(2,1)}, u32[]{:S(2)}) %copy-start.4) | copy-done | bytes 262168
  12.6 1.8 %collective-permute-done.pair = bf16[128,768]{1,0:T(8,128)(2,1)S(1)} collective-permute-done((bf16[128,768]{1,0:T(8,128)(2,1)S(1)}, bf16[128,768]{1,0:T(8,128)(2,1)S(1)}, u32[]{:S(2)}, u32[]{:S(2)}) %collective-permute-start) | collective-permute-done | bytes 196640 | tf_op jit(solution)/shard_map/ppermute | solution.py:20
  14.4 2.6 %collective-permute-start.11 = (bf16[512,128]{1,0:T(8,128)(2,1)S(1)}, bf16[512,128]{1,0:T(8,128)(2,1)S(1)}, u32[]{:S(2)}, u32[]{:S(2)}) collective-permute-start(bf16[512,128]{1,0:T(8,128)(2,1)S(1)} %get-tuple-element.70.refs_0_), channel_id=1, source_target_pairs={{0,4},{2,6},{4,0},{6,2},{1,5},{3,7},{5,1},{7,3},{8,12},{10,14},{12... | collective-permute-start | bytes 393224 | tf_op jit(solution)/shard_map/ppermute | solution.py:25
  17.0 2.4 %collective-permute-start.10 = (bf16[512,128]{1,0:T(8,128)(2,1)S(1)}, bf16[512,128]{1,0:T(8,128)(2,1)S(1)}, u32[]{:S(2)}, u32[]{:S(2)}) collective-permute-start(bf16[512,128]{1,0:T(8,128)(2,1)S(1)} %get-tuple-element.70.refs_0_), channel_id=1, source_target_pairs={{0,24},{8,0},{16,8},{24,16},{1,25},{9,1},{17,9},{25,17},{2,26},{10... | collective-permute-start | bytes 393224 | tf_op jit(solution)/shard_map/ppermute | solution.py:25
  21.3 2.9 %collective-permute-start.13 = (bf16[512,128]{1,0:T(8,128)(2,1)S(1)}, bf16[512,128]{1,0:T(8,128)(2,1)S(1)}, u32[]{:S(2)}, u32[]{:S(2)}) collective-permute-start(bf16[512,128]{1,0:T(8,128)(2,1)S(1)} %get-tuple-element.73.refs_4_), channel_id=1, source_target_pairs={{0,24},{8,0},{16,8},{24,16},{1,25},{9,1},{17,9},{25,17},{2,26},{10... | collective-permute-start | bytes 393224 | tf_op jit(solution)/shard_map/ppermute | solution.py:25
  24.2 1.3 %collective-permute-start.12 = (bf16[512,128]{1,0:T(8,128)(2,1)S(1)}, bf16[512,128]{1,0:T(8,128)(2,1)S(1)}, u32[]{:S(2)}, u32[]{:S(2)}) collective-permute-start(bf16[512,128]{1,0:T(8,128)(2,1)S(1)} %get-tuple-element.73.refs_4_), channel_id=1, source_target_pairs={{0,8},{8,16},{16,24},{24,0},{1,9},{9,17},{17,25},{25,1},{2,10},{10... | collective-permute-start | bytes 393224 | tf_op jit(solution)/shard_map/ppermute | solution.py:25
  25.5 1.5 %collective-permute-done.9.refs_1_ = bf16[512,128]{1,0:T(8,128)(2,1)S(1)} collective-permute-done((bf16[512,128]{1,0:T(8,128)(2,1)S(1)}, bf16[512,128]{1,0:T(8,128)(2,1)S(1)}, u32[]{:S(2)}, u32[]{:S(2)}) %collective-permute-start.9) | collective-permute-done | bytes 131104 | tf_op jit(solution)/shard_map/ppermute | solution.py:25
  27.0 4.8 %shard_map.114 = (bf16[8,512,512]{2,1,0:T(8,128)(2,1)S(1)}, f32[8,512]{1,0:T(8,128)S(1)}, bf16[512,128]{1,0:T(8,128)(2,1)S(1)}, bf16[512,128]{1,0:T(8,128)(2,1)S...) custom-call(bf16[512,128]{1,0:T(8,128)(2,1)S(1)} %get-tuple-element.63.q_ref, ...), custom_call_target="tpu_custom_call" | custom-call | flops 1073741824 | bytes 4194304 | tf_op jit(solution)/shard_map/pallas_call | solution.py:54
  31.8 1.5 %collective-permute-start.15 = (bf16[512,128]{1,0:T(8,128)(2,1)S(1)}, bf16[512,128]{1,0:T(8,128)(2,1)S(1)}, u32[]{:S(2)}, u32[]{:S(2)}) collective-permute-start(bf16[512,128]{1,0:T(8,128)(2,1)S(1)} %get-tuple-element.79), channel_id=1, source_target_pairs={{0,24},{8,0},{16,8},{24,16},{1,25},{9,1},{17,9},{25,17},{2,26},{10... | collective-permute-start | bytes 393224 | tf_op jit(solution)/shard_map/ppermute | solution.py:25
  34.6 3.8 %shard_map.115 = (bf16[512,128]{1,0:T(8,128)(2,1)S(1)}, bf16[512,128]{1,0:T(8,128)(2,1)S(1)}, bf16[512,128]{1,0:T(8,128)(2,1)S(1)}, bf16[512,128]{1,0:T(8,128)(2,1)S(1)}, bf16[512,128]{1,0:T(8,128)(2,1)S(1)}) custom-call(bf16[512,128]{1,0:T(8,128)(2,1)S(1)} %get-tuple-element.63.q_ref, bf16[512,128]{1,0:T(8,128)(2,1)S(1)} %get-tuple-element.68.do_ref, ...), custom_call_target="tpu_custom_call" | custom-call | flops 1610612736 | bytes 4194304 | tf_op jit(solution)/shard_map/pallas_call | solution.py:54
  38.4 1.0 %collective-permute-done.16.refs_2_ = bf16[512,128]{1,0:T(8,128)(2,1)S(1)} collective-permute-done((bf16[512,128]{1,0:T(8,128)(2,1)S(1)}, bf16[512,128]{1,0:T(8,128)(2,1)S(1)}, u32[]{:S(2)}, u32[]{:S(2)}) %collective-permute-start.16) | collective-permute-done | bytes 131104 | tf_op jit(solution)/shard_map/ppermute | solution.py:25
  39.4 2.8 %collective-permute-done.17.refs_3_ = bf16[512,128]{1,0:T(8,128)(2,1)S(1)} collective-permute-done((bf16[512,128]{1,0:T(8,128)(2,1)S(1)}, bf16[512,128]{1,0:T(8,128)(2,1)S(1)}, u32[]{:S(2)}, u32[]{:S(2)}) %collective-permute-start.17) | collective-permute-done | bytes 131104 | tf_op jit(solution)/shard_map/ppermute | solution.py:25
  42.4 2.4 %collective-permute-start.18 = (bf16[512,128]{1,0:T(8,128)(2,1)S(1)}, bf16[512,128]{1,0:T(8,128)(2,1)S(1)}, u32[]{:S(2)}, u32[]{:S(2)}) collective-permute-start(bf16[512,128]{1,0:T(8,128)(2,1)S(1)} %get-tuple-element.83), channel_id=1, source_target_pairs={{0,24},{8,0},{16,8},{24,16},{1,25},{9,1},{17,9},{25,17},{2,26},{10... | collective-permute-start | bytes 393224 | tf_op jit(solution)/shard_map/ppermute | solution.py:25
  45.1 4.1 %collective-permute-done.18.refs_1_ = bf16[512,128]{1,0:T(8,128)(2,1)S(1)} collective-permute-done((bf16[512,128]{1,0:T(8,128)(2,1)S(1)}, bf16[512,128]{1,0:T(8,128)(2,1)S(1)}, u32[]{:S(2)}, u32[]{:S(2)}) %collective-permute-start.18) | collective-permute-done | bytes 131104 | tf_op jit(solution)/shard_map/ppermute | solution.py:25
  49.2 2.7 %collective-permute-done.19.refs_2_ = bf16[512,128]{1,0:T(8,128)(2,1)S(1)} collective-permute-done((bf16[512,128]{1,0:T(8,128)(2,1)S(1)}, bf16[512,128]{1,0:T(8,128)(2,1)S(1)}, u32[]{:S(2)}, u32[]{:S(2)}) %collective-permute-start.19) | collective-permute-done | bytes 131104 | tf_op jit(solution)/shard_map/ppermute | solution.py:25
  51.9 2.3 %collective-permute-done.20.refs_3_ = bf16[512,128]{1,0:T(8,128)(2,1)S(1)} collective-permute-done((bf16[512,128]{1,0:T(8,128)(2,1)S(1)}, bf16[512,128]{1,0:T(8,128)(2,1)S(1)}, u32[]{:S(2)}, u32[]{:S(2)}) %collective-permute-start.20) | collective-permute-done | bytes 131104 | tf_op jit(solution)/shard_map/ppermute | solution.py:25
  56.1 2.7 %collective-permute-start.23 = (bf16[64,1024]{1,0:T(8,128)(2,1)S(1)}, bf16[64,1024]{1,0:T(8,128)(2,1)S(1)}, u32[]{:S(2)}, u32[]{:S(2)}) collective-permute-start(bf16[64,1024]{1,0:T(8,128)(2,1)S(1)} %get-tuple-element.96), channel_id=1, source_target_pairs={{0,8},{2,10},{4,12},{6,14},{8,0},{10,2},{12,4},{14,6},{16,24},{18,... | collective-permute-start | bytes 393224 | tf_op jit(solution)/shard_map/ppermute | solution.py:34
  59.3 1.0 %collective-permute-start.25 = (bf16[64,1024]{1,0:T(8,128)(2,1)S(1)}, bf16[64,1024]{1,0:T(8,128)(2,1)S(1)}, u32[]{:S(2)}, u32[]{:S(2)}) collective-permute-start(bf16[64,1024]{1,0:T(8,128)(2,1)S(1)} %get-tuple-element.98), channel_id=1, source_target_pairs={{0,24},{2,26},{4,28},{6,30},{8,16},{10,18},{12,20},{14,22},{16,8},... | collective-permute-start | bytes 393224 | tf_op jit(solution)/shard_map/ppermute | solution.py:34
  60.3 2.4 %collective-permute-done.23.refs_1_ = bf16[64,1024]{1,0:T(8,128)(2,1)S(1)} collective-permute-done((bf16[64,1024]{1,0:T(8,128)(2,1)S(1)}, bf16[64,1024]{1,0:T(8,128)(2,1)S(1)}, u32[]{:S(2)}, u32[]{:S(2)}) %collective-permute-start.23) | collective-permute-done | bytes 131104 | tf_op jit(solution)/shard_map/ppermute | solution.py:34
  62.7 4.2 %collective-permute-done.24.refs_2_ = bf16[64,1024]{1,0:T(8,128)(2,1)S(1)} collective-permute-done((bf16[64,1024]{1,0:T(8,128)(2,1)S(1)}, bf16[64,1024]{1,0:T(8,128)(2,1)S(1)}, u32[]{:S(2)}, u32[]{:S(2)}) %collective-permute-start.24) | collective-permute-done | bytes 131104 | tf_op jit(solution)/shard_map/ppermute | solution.py:34
  66.9 1.5 %collective-permute-start.27 = (bf16[64,1024]{1,0:T(8,128)(2,1)S(1)}, bf16[64,1024]{1,0:T(8,128)(2,1)S(1)}, u32[]{:S(2)}, u32[]{:S(2)}) collective-permute-start(bf16[64,1024]{1,0:T(8,128)(2,1)S(1)} %shard_map.120.refs_0_), channel_id=1, source_target_pairs={{0,4},{2,6},{4,0},{6,2},{8,12},{10,14},{12,8},{14,10},{16,20},{18,... | collective-permute-start | bytes 393224 | tf_op jit(solution)/shard_map/ppermute | solution.py:34
  69.7 5.4 %collective-permute-done.27.refs_1_ = bf16[64,1024]{1,0:T(8,128)(2,1)S(1)} collective-permute-done((bf16[64,1024]{1,0:T(8,128)(2,1)S(1)}, bf16[64,1024]{1,0:T(8,128)(2,1)S(1)}, u32[]{:S(2)}, u32[]{:S(2)}) %collective-permute-start.27) | collective-permute-done | bytes 131104 | tf_op jit(solution)/shard_map/ppermute | solution.py:34
  75.2 2.0 %collective-permute-start.29 = (bf16[64,1024]{1,0:T(8,128)(2,1)S(1)}, bf16[64,1024]{1,0:T(8,128)(2,1)S(1)}, u32[]{:S(2)}, u32[]{:S(2)}) collective-permute-start(bf16[64,1024]{1,0:T(8,128)(2,1)S(1)} %shard_map.122.refs_0_), channel_id=1, source_target_pairs={{0,8},{2,10},{4,12},{6,14},{8,0},{10,2},{12,4},{14,6},{16,24},{18,... | collective-permute-start | bytes 393224 | tf_op jit(solution)/shard_map/ppermute | solution.py:34
  77.3 2.9 %collective-permute-done.31.refs_4_ = bf16[64,1024]{1,0:T(8,128)(2,1)S(1)} collective-permute-done((bf16[64,1024]{1,0:T(8,128)(2,1)S(1)}, bf16[64,1024]{1,0:T(8,128)(2,1)S(1)}, u32[]{:S(2)}, u32[]{:S(2)}) %collective-permute-start.31) | collective-permute-done | bytes 131104 | tf_op jit(solution)/shard_map/ppermute | solution.py:34
  80.9 2.5 %collective-permute-done.28.refs_1_ = bf16[64,1024]{1,0:T(8,128)(2,1)S(1)} collective-permute-done((bf16[64,1024]{1,0:T(8,128)(2,1)S(1)}, bf16[64,1024]{1,0:T(8,128)(2,1)S(1)}, u32[]{:S(2)}, u32[]{:S(2)}) %collective-permute-start.28) | collective-permute-done | bytes 131104 | tf_op jit(solution)/shard_map/ppermute | solution.py:34
  83.3 1.4 %collective-permute-start.34 = (bf16[64,1024]{1,0:T(8,128)(2,1)S(1)}, bf16[64,1024]{1,0:T(8,128)(2,1)S(1)}, u32[]{:S(2)}, u32[]{:S(2)}) collective-permute-start(bf16[64,1024]{1,0:T(8,128)(2,1)S(1)} %collective-permute-done.28.refs_1_), channel_id=1, source_target_pairs={{0,24},{2,26},{4,28},{6,30},{8,16},{10,18},{12,20},{14,22},{16,8},... | collective-permute-start | bytes 393224 | tf_op jit(solution)/shard_map/ppermute | solution.py:34
  85.8 3.5 %collective-permute-done.34.refs_7_ = bf16[64,1024]{1,0:T(8,128)(2,1)S(1)} collective-permute-done((bf16[64,1024]{1,0:T(8,128)(2,1)S(1)}, bf16[64,1024]{1,0:T(8,128)(2,1)S(1)}, u32[]{:S(2)}, u32[]{:S(2)}) %collective-permute-start.34) | collective-permute-done | bytes 131104 | tf_op jit(solution)/shard_map/ppermute | solution.py:34
  89.3 1.3 %collective-permute-done.32.refs_5_ = bf16[64,1024]{1,0:T(8,128)(2,1)S(1)} collective-permute-done((bf16[64,1024]{1,0:T(8,128)(2,1)S(1)}, bf16[64,1024]{1,0:T(8,128)(2,1)S(1)}, u32[]{:S(2)}, u32[]{:S(2)}) %collective-permute-start.32) | collective-permute-done | bytes 131104 | tf_op jit(solution)/shard_map/ppermute | solution.py:34
  90.6 1.5 %shard_map.123 = (f32[256,512]{1,0:T(8,128)}, f32[256,512]{1,0:T(8,128)}, f32[256,512]{1,0:T(8,128)}, f32[256,512]{1,0:T(8,128)}) custom-call(bf16[64,1024]{1,0:T(8,128)(2,1)S(1)} %shard_map.122.refs_0_, bf16[64,1024]{1,0:T(8,128)(2,1)S(1)} %collective-permute-done.28.refs_1_, bf16[64,1024]{1,0:T(8,128)(2,1)S(1)} %collective-permute-done.29.refs_2_, ...), custom_call_target="tpu_custom_call" | custom-call | flops 1000000 | bytes 1000000 | tf_op jit(solution)/shard_map/pallas_call | solution.py:54
  (70 shorter events, 15.3 us)
Async XLA Ops:
  0.6 7.1 %collective-permute-start.3 = (bf16[256,512]{1,0:T(8,128)(2,1)}, bf16[256,512]{1,0:T(8,128)(2,1)S(1)}, u32[]{:S(2)}, u32[]{:S(2)}) collective-permute-start(bf16[256,512]{1,0:T(8,128)(2,1)} %wq0.3), channel_id=1, source_target_pairs={{0,1},{1,0},{2,3},{3,2},{4,5},{5,4},{6,7},{7,6},{8,9},{9,8},{10,11... | collective-permute-start | bytes 786440 | tf_op jit(solution)/shard_map/ppermute | solution.py:20
  1.1 6.6 %collective-permute-start.4 = (bf16[256,512]{1,0:T(8,128)(2,1)}, bf16[256,512]{1,0:T(8,128)(2,1)S(1)}, u32[]{:S(2)}, u32[]{:S(2)}) collective-permute-start(bf16[256,512]{1,0:T(8,128)(2,1)} %wk0.3), channel_id=1, source_target_pairs={{0,1},{1,0},{2,3},{3,2},{4,5},{5,4},{6,7},{7,6},{8,9},{9,8},{10,11... | collective-permute-start | bytes 786440 | tf_op jit(solution)/shard_map/ppermute | solution.py:20
  1.2 6.6 %collective-permute-start.5 = (bf16[256,512]{1,0:T(8,128)(2,1)}, bf16[256,512]{1,0:T(8,128)(2,1)S(1)}, u32[]{:S(2)}, u32[]{:S(2)}) collective-permute-start(bf16[256,512]{1,0:T(8,128)(2,1)} %wv0.3), channel_id=1, source_target_pairs={{0,1},{1,0},{2,3},{3,2},{4,5},{5,4},{6,7},{7,6},{8,9},{9,8},{10,11... | collective-permute-start | bytes 786440 | tf_op jit(solution)/shard_map/ppermute | solution.py:20
  2.6 8.1 %collective-permute-start.2 = (bf16[128,512]{1,0:T(8,128)(2,1)S(1)}, bf16[128,512]{1,0:T(8,128)(2,1)S(1)}, u32[]{:S(2)}, u32[]{:S(2)}) collective-permute-start(bf16[128,512]{1,0:T(8,128)(2,1)S(1)} %reshape.24.own.f_own), channel_id=1, source_target_pairs={{0,1},{1,0},{2,3},{3,2},{4,5},{5,4},{6,7},{7,6},{8,9},{9,8},{10,11... | collective-permute-start | bytes 393224 | tf_op jit(solution)/shard_map/ppermute | solution.py:20
  2.7 8.0 %collective-permute-start.1 = (bf16[128,512]{1,0:T(8,128)(2,1)S(1)}, bf16[128,512]{1,0:T(8,128)(2,1)S(1)}, u32[]{:S(2)}, u32[]{:S(2)}) collective-permute-start(bf16[128,512]{1,0:T(8,128)(2,1)S(1)} %reshape.24.own.f_own), channel_id=1, source_target_pairs={{0,2},{2,0},{4,6},{6,4},{1,3},{3,1},{5,7},{7,5},{8,10},{10,8},{12,... | collective-permute-start | bytes 393224 | tf_op jit(solution)/shard_map/ppermute | solution.py:20
  7.7 6.7 %collective-permute-start = (bf16[128,768]{1,0:T(8,128)(2,1)S(1)}, bf16[128,768]{1,0:T(8,128)(2,1)S(1)}, u32[]{:S(2)}, u32[]{:S(2)}) collective-permute-start(bf16[128,768]{1,0:T(8,128)(2,1)S(1)} %get-tuple-element.57), channel_id=1, source_target_pairs={{0,2},{2,0},{4,6},{6,4},{1,3},{3,1},{5,7},{7,5},{8,10},{10,8},{12,... | collective-permute-start | bytes 589832 | tf_op jit(solution)/shard_map/ppermute | solution.py:20
  10.8 8.6 %collective-permute-start.7 = (bf16[128,768]{1,0:T(8,128)(2,1)S(1)}, bf16[128,768]{1,0:T(8,128)(2,1)S(1)}, u32[]{:S(2)}, u32[]{:S(2)}) collective-permute-start(bf16[128,768]{1,0:T(8,128)(2,1)S(1)} %get-tuple-element.65.own), channel_id=1, source_target_pairs={{0,1},{1,0},{2,3},{3,2},{4,5},{5,4},{6,7},{7,6},{8,9},{9,8},{10,11... | collective-permute-start | bytes 589832 | tf_op jit(solution)/shard_map/ppermute | solution.py:20
  14.4 5.0 %collective-permute-start.8 = (bf16[128,768]{1,0:T(8,128)(2,1)S(1)}, bf16[128,768]{1,0:T(8,128)(2,1)S(1)}, u32[]{:S(2)}, u32[]{:S(2)}) collective-permute-start(bf16[128,768]{1,0:T(8,128)(2,1)S(1)} %collective-permute-done.pair), channel_id=1, source_target_pairs={{0,1},{1,0},{2,3},{3,2},{4,5},{5,4},{6,7},{7,6},{8,9},{9,8},{10,11... | collective-permute-start | bytes 589832 | tf_op jit(solution)/shard_map/ppermute | solution.py:20
  14.4 9.8 %collective-permute-start.11 = (bf16[512,128]{1,0:T(8,128)(2,1)S(1)}, bf16[512,128]{1,0:T(8,128)(2,1)S(1)}, u32[]{:S(2)}, u32[]{:S(2)}) collective-permute-start(bf16[512,128]{1,0:T(8,128)(2,1)S(1)} %get-tuple-element.70.refs_0_), channel_id=1, source_target_pairs={{0,4},{2,6},{4,0},{6,2},{1,5},{3,7},{5,1},{7,3},{8,12},{10,14},{12... | collective-permute-start | bytes 393224 | tf_op jit(solution)/shard_map/ppermute | solution.py:25
  17.0 8.5 %collective-permute-start.10 = (bf16[512,128]{1,0:T(8,128)(2,1)S(1)}, bf16[512,128]{1,0:T(8,128)(2,1)S(1)}, u32[]{:S(2)}, u32[]{:S(2)}) collective-permute-start(bf16[512,128]{1,0:T(8,128)(2,1)S(1)} %get-tuple-element.70.refs_0_), channel_id=1, source_target_pairs={{0,24},{8,0},{16,8},{24,16},{1,25},{9,1},{17,9},{25,17},{2,26},{10... | collective-permute-start | bytes 393224 | tf_op jit(solution)/shard_map/ppermute | solution.py:25
  19.4 7.6 %collective-permute-start.9 = (bf16[512,128]{1,0:T(8,128)(2,1)S(1)}, bf16[512,128]{1,0:T(8,128)(2,1)S(1)}, u32[]{:S(2)}, u32[]{:S(2)}) collective-permute-start(bf16[512,128]{1,0:T(8,128)(2,1)S(1)} %get-tuple-element.70.refs_0_), channel_id=1, source_target_pairs={{0,8},{8,16},{16,24},{24,0},{1,9},{9,17},{17,25},{25,1},{2,10},{10... | collective-permute-start | bytes 393224 | tf_op jit(solution)/shard_map/ppermute | solution.py:25
  20.9 13.0 %collective-permute-start.14 = (bf16[512,128]{1,0:T(8,128)(2,1)S(1)}, bf16[512,128]{1,0:T(8,128)(2,1)S(1)}, u32[]{:S(2)}, u32[]{:S(2)}) collective-permute-start(bf16[512,128]{1,0:T(8,128)(2,1)S(1)} %get-tuple-element.73.refs_4_), channel_id=1, source_target_pairs={{0,4},{2,6},{4,0},{6,2},{1,5},{3,7},{5,1},{7,3},{8,12},{10,14},{12... | collective-permute-start | bytes 393224 | tf_op jit(solution)/shard_map/ppermute | solution.py:25
  21.3 13.3 %collective-permute-start.13 = (bf16[512,128]{1,0:T(8,128)(2,1)S(1)}, bf16[512,128]{1,0:T(8,128)(2,1)S(1)}, u32[]{:S(2)}, u32[]{:S(2)}) collective-permute-start(bf16[512,128]{1,0:T(8,128)(2,1)S(1)} %get-tuple-element.73.refs_4_), channel_id=1, source_target_pairs={{0,24},{8,0},{16,8},{24,16},{1,25},{9,1},{17,9},{25,17},{2,26},{10... | collective-permute-start | bytes 393224 | tf_op jit(solution)/shard_map/ppermute | solution.py:25
  24.2 10.4 %collective-permute-start.12 = (bf16[512,128]{1,0:T(8,128)(2,1)S(1)}, bf16[512,128]{1,0:T(8,128)(2,1)S(1)}, u32[]{:S(2)}, u32[]{:S(2)}) collective-permute-start(bf16[512,128]{1,0:T(8,128)(2,1)S(1)} %get-tuple-element.73.refs_4_), channel_id=1, source_target_pairs={{0,8},{8,16},{16,24},{24,0},{1,9},{9,17},{17,25},{25,1},{2,10},{10... | collective-permute-start | bytes 393224 | tf_op jit(solution)/shard_map/ppermute | solution.py:25
  31.8 6.6 %collective-permute-start.15 = (bf16[512,128]{1,0:T(8,128)(2,1)S(1)}, bf16[512,128]{1,0:T(8,128)(2,1)S(1)}, u32[]{:S(2)}, u32[]{:S(2)}) collective-permute-start(bf16[512,128]{1,0:T(8,128)(2,1)S(1)} %get-tuple-element.79), channel_id=1, source_target_pairs={{0,24},{8,0},{16,8},{24,16},{1,25},{9,1},{17,9},{25,17},{2,26},{10... | collective-permute-start | bytes 393224 | tf_op jit(solution)/shard_map/ppermute | solution.py:25
  33.3 6.1 %collective-permute-start.16 = (bf16[512,128]{1,0:T(8,128)(2,1)S(1)}, bf16[512,128]{1,0:T(8,128)(2,1)S(1)}, u32[]{:S(2)}, u32[]{:S(2)}) collective-permute-start(bf16[512,128]{1,0:T(8,128)(2,1)S(1)} %get-tuple-element.80), channel_id=1, source_target_pairs={{0,8},{8,16},{16,24},{24,0},{1,9},{9,17},{17,25},{25,1},{2,10},{10... | collective-permute-start | bytes 393224 | tf_op jit(solution)/shard_map/ppermute | solution.py:25
  33.9 8.4 %collective-permute-start.17 = (bf16[512,128]{1,0:T(8,128)(2,1)S(1)}, bf16[512,128]{1,0:T(8,128)(2,1)S(1)}, u32[]{:S(2)}, u32[]{:S(2)}) collective-permute-start(bf16[512,128]{1,0:T(8,128)(2,1)S(1)} %get-tuple-element.81), channel_id=1, source_target_pairs={{0,4},{2,6},{4,0},{6,2},{1,5},{3,7},{5,1},{7,3},{8,12},{10,14},{12... | collective-permute-start | bytes 393224 | tf_op jit(solution)/shard_map/ppermute | solution.py:25
  42.3 12.0 %collective-permute-start.22 = (bf16[512,256]{1,0:T(8,128)(2,1)S(1)}, bf16[512,256]{1,0:T(8,128)(2,1)S(1)}, u32[]{:S(2)}, u32[]{:S(2)}) collective-permute-start(bf16[512,256]{1,0:T(8,128)(2,1)S(1)} %shard_map.117.own), channel_id=1, source_target_pairs={{0,1},{1,0},{2,3},{3,2},{4,5},{5,4},{6,7},{7,6},{8,9},{9,8},{10,11... | collective-permute-start | bytes 786440 | tf_op jit(solution)/shard_map/ppermute | solution.py:20
  42.4 6.8 %collective-permute-start.18 = (bf16[512,128]{1,0:T(8,128)(2,1)S(1)}, bf16[512,128]{1,0:T(8,128)(2,1)S(1)}, u32[]{:S(2)}, u32[]{:S(2)}) collective-permute-start(bf16[512,128]{1,0:T(8,128)(2,1)S(1)} %get-tuple-element.83), channel_id=1, source_target_pairs={{0,24},{8,0},{16,8},{24,16},{1,25},{9,1},{17,9},{25,17},{2,26},{10... | collective-permute-start | bytes 393224 | tf_op jit(solution)/shard_map/ppermute | solution.py:25
  44.8 7.1 %collective-permute-start.19 = (bf16[512,128]{1,0:T(8,128)(2,1)S(1)}, bf16[512,128]{1,0:T(8,128)(2,1)S(1)}, u32[]{:S(2)}, u32[]{:S(2)}) collective-permute-start(bf16[512,128]{1,0:T(8,128)(2,1)S(1)} %get-tuple-element.84), channel_id=1, source_target_pairs={{0,8},{8,16},{16,24},{24,0},{1,9},{9,17},{17,25},{25,1},{2,10},{10... | collective-permute-start | bytes 393224 | tf_op jit(solution)/shard_map/ppermute | solution.py:25
  45.1 9.0 %collective-permute-start.20 = (bf16[512,128]{1,0:T(8,128)(2,1)S(1)}, bf16[512,128]{1,0:T(8,128)(2,1)S(1)}, u32[]{:S(2)}, u32[]{:S(2)}) collective-permute-start(bf16[512,128]{1,0:T(8,128)(2,1)S(1)} %get-tuple-element.85), channel_id=1, source_target_pairs={{0,4},{2,6},{4,0},{6,2},{1,5},{3,7},{5,1},{7,3},{8,12},{10,14},{12... | collective-permute-start | bytes 393224 | tf_op jit(solution)/shard_map/ppermute | solution.py:25
  56.0 10.9 %collective-permute-start.26 = (bf16[128,768]{1,0:T(8,128)(2,1)S(1)}, bf16[128,768]{1,0:T(8,128)(2,1)S(1)}, u32[]{:S(2)}, u32[]{:S(2)}) collective-permute-start(bf16[128,768]{1,0:T(8,128)(2,1)S(1)} %get-tuple-element.99), channel_id=1, source_target_pairs={{0,2},{2,0},{4,6},{6,4},{1,3},{3,1},{5,7},{7,5},{8,10},{10,8},{12,... | collective-permute-start | bytes 589832 | tf_op jit(solution)/shard_map/ppermute | solution.py:20
  56.1 6.6 %collective-permute-start.23 = (bf16[64,1024]{1,0:T(8,128)(2,1)S(1)}, bf16[64,1024]{1,0:T(8,128)(2,1)S(1)}, u32[]{:S(2)}, u32[]{:S(2)}) collective-permute-start(bf16[64,1024]{1,0:T(8,128)(2,1)S(1)} %get-tuple-element.96), channel_id=1, source_target_pairs={{0,8},{2,10},{4,12},{6,14},{8,0},{10,2},{12,4},{14,6},{16,24},{18,... | collective-permute-start | bytes 393224 | tf_op jit(solution)/shard_map/ppermute | solution.py:34
  58.8 8.1 %collective-permute-start.24 = (bf16[64,1024]{1,0:T(8,128)(2,1)S(1)}, bf16[64,1024]{1,0:T(8,128)(2,1)S(1)}, u32[]{:S(2)}, u32[]{:S(2)}) collective-permute-start(bf16[64,1024]{1,0:T(8,128)(2,1)S(1)} %get-tuple-element.97), channel_id=1, source_target_pairs={{0,16},{2,18},{4,20},{6,22},{8,24},{10,26},{12,28},{14,30},{16,0},... | collective-permute-start | bytes 393224 | tf_op jit(solution)/shard_map/ppermute | solution.py:34
  59.3 7.6 %collective-permute-start.25 = (bf16[64,1024]{1,0:T(8,128)(2,1)S(1)}, bf16[64,1024]{1,0:T(8,128)(2,1)S(1)}, u32[]{:S(2)}, u32[]{:S(2)}) collective-permute-start(bf16[64,1024]{1,0:T(8,128)(2,1)S(1)} %get-tuple-element.98), channel_id=1, source_target_pairs={{0,24},{2,26},{4,28},{6,30},{8,16},{10,18},{12,20},{14,22},{16,8},... | collective-permute-start | bytes 393224 | tf_op jit(solution)/shard_map/ppermute | solution.py:34
  66.9 8.2 %collective-permute-start.27 = (bf16[64,1024]{1,0:T(8,128)(2,1)S(1)}, bf16[64,1024]{1,0:T(8,128)(2,1)S(1)}, u32[]{:S(2)}, u32[]{:S(2)}) collective-permute-start(bf16[64,1024]{1,0:T(8,128)(2,1)S(1)} %shard_map.120.refs_0_), channel_id=1, source_target_pairs={{0,4},{2,6},{4,0},{6,2},{8,12},{10,14},{12,8},{14,10},{16,20},{18,... | collective-permute-start | bytes 393224 | tf_op jit(solution)/shard_map/ppermute | solution.py:34
  75.1 5.0 %collective-permute-start.31 = (bf16[64,1024]{1,0:T(8,128)(2,1)S(1)}, bf16[64,1024]{1,0:T(8,128)(2,1)S(1)}, u32[]{:S(2)}, u32[]{:S(2)}) collective-permute-start(bf16[64,1024]{1,0:T(8,128)(2,1)S(1)} %shard_map.122.refs_0_), channel_id=1, source_target_pairs={{0,16},{2,18},{4,20},{6,22},{8,24},{10,26},{12,28},{14,30},{16,0},... | collective-permute-start | bytes 393224 | tf_op jit(solution)/shard_map/ppermute | solution.py:34
  75.2 5.6 %collective-permute-start.29 = (bf16[64,1024]{1,0:T(8,128)(2,1)S(1)}, bf16[64,1024]{1,0:T(8,128)(2,1)S(1)}, u32[]{:S(2)}, u32[]{:S(2)}) collective-permute-start(bf16[64,1024]{1,0:T(8,128)(2,1)S(1)} %shard_map.122.refs_0_), channel_id=1, source_target_pairs={{0,8},{2,10},{4,12},{6,14},{8,0},{10,2},{12,4},{14,6},{16,24},{18,... | collective-permute-start | bytes 393224 | tf_op jit(solution)/shard_map/ppermute | solution.py:34
  77.3 6.1 %collective-permute-start.28 = (bf16[64,1024]{1,0:T(8,128)(2,1)S(1)}, bf16[64,1024]{1,0:T(8,128)(2,1)S(1)}, u32[]{:S(2)}, u32[]{:S(2)}) collective-permute-start(bf16[64,1024]{1,0:T(8,128)(2,1)S(1)} %shard_map.122.refs_0_), channel_id=1, source_target_pairs={{0,2},{2,0},{4,6},{6,4},{8,10},{10,8},{12,14},{14,12},{16,18},{18,... | collective-permute-start | bytes 393224 | tf_op jit(solution)/shard_map/ppermute | solution.py:34
  80.2 5.0 %collective-permute-start.33 = (bf16[64,1024]{1,0:T(8,128)(2,1)S(1)}, bf16[64,1024]{1,0:T(8,128)(2,1)S(1)}, u32[]{:S(2)}, u32[]{:S(2)}) collective-permute-start(bf16[64,1024]{1,0:T(8,128)(2,1)S(1)} %collective-permute-done.31.refs_4_), channel_id=1, source_target_pairs={{0,8},{2,10},{4,12},{6,14},{8,0},{10,2},{12,4},{14,6},{16,24},{18,... | collective-permute-start | bytes 393224 | tf_op jit(solution)/shard_map/ppermute | solution.py:34
  83.3 6.0 %collective-permute-start.34 = (bf16[64,1024]{1,0:T(8,128)(2,1)S(1)}, bf16[64,1024]{1,0:T(8,128)(2,1)S(1)}, u32[]{:S(2)}, u32[]{:S(2)}) collective-permute-start(bf16[64,1024]{1,0:T(8,128)(2,1)S(1)} %collective-permute-done.28.refs_1_), channel_id=1, source_target_pairs={{0,24},{2,26},{4,28},{6,30},{8,16},{10,18},{12,20},{14,22},{16,8},... | collective-permute-start | bytes 393224 | tf_op jit(solution)/shard_map/ppermute | solution.py:34
  84.7 5.9 %collective-permute-start.32 = (bf16[64,1024]{1,0:T(8,128)(2,1)S(1)}, bf16[64,1024]{1,0:T(8,128)(2,1)S(1)}, u32[]{:S(2)}, u32[]{:S(2)}) collective-permute-start(bf16[64,1024]{1,0:T(8,128)(2,1)S(1)} %collective-permute-done.28.refs_1_), channel_id=1, source_target_pairs={{0,16},{2,18},{4,20},{6,22},{8,24},{10,26},{12,28},{14,30},{16,0},... | collective-permute-start | bytes 393224 | tf_op jit(solution)/shard_map/ppermute | solution.py:34
  (10 other events, 113.1 us)

commit v4 on v3

--- a/solution.py
+++ b/solution.py
@@ -50,10 +50,12 @@
     return pl.ds(pl.multiple_of(start, PART), PART)
 
 
-def call(kernel, out_shape, args, scratch=(), flops=1e6, moved=1e6, exps=0):
+def call(kernel, out_shape, args, scratch=(), flops=1e6, moved=1e6, exps=0, spaces=None):
+    specs = [pl.BlockSpec(memory_space=space or pltpu.VMEM) for space in spaces or [None] * len(args)]
     return pl.pallas_call(
         kernel,
         out_shape=out_shape,
+        in_specs=specs,
         scratch_shapes=list(scratch),
         compiler_params=pltpu.CompilerParams(vmem_limit_bytes=VMEM_BYTES),
         cost_estimate=pl.CostEstimate(
@@ -78,16 +80,28 @@
     own_ref[:, last:] = saved_ref[:, columns((z_bit * 2 + y_bit) * PART)]
 
 
-def columns_kernel(own_half, wq0, wq1, wk0, wk1, wv0, wv1, w_cols):
+def columns_kernel(own_half, wq0, wq1, wk0, wk1, wv0, wv1, w_cols, sems):
     y_bit = lax.axis_index("gy") % 2
     z_bit = lax.axis_index("gz") % 2
     half = z_bit if own_half else z_bit * 0
     group = columns((z_bit * 2 + y_bit) * PART)
     half_rows = wq0.shape[0]
-    for at, (first, second) in enumerate(((wq0, wq1), (wk0, wk1), (wv0, wv1))):
-        spot = slice(at * PART, (at + 1) * PART)
-        w_cols[pl.ds(pl.multiple_of(half * half_rows, half_rows), half_rows), spot] = first[:, group]
-        w_cols[pl.ds(pl.multiple_of((1 - half) * half_rows, half_rows), half_rows), spot] = second[:, group]
+    copies = []
+    for at, pair in enumerate(((wq0, wq1), (wk0, wk1), (wv0, wv1))):
+        for side, source in enumerate(pair):
+            place = half if side == 0 else 1 - half
+            rows = pl.ds(pl.multiple_of(place * half_rows, half_rows), half_rows)
+            copies.append(
+                pltpu.make_async_copy(
+                    source.at[:, group],
+                    w_cols.at[rows, at * PART : (at + 1) * PART],
+                    sems.at[2 * at + side],
+                )
+            )
+    for copy in copies:
+        copy.start()
+    for copy in copies:
+        copy.wait()
 
 
 def project_kernel(own, core, pair, far, w_cols, q_ref, k_ref, v_ref):
@@ -141,29 +155,20 @@
     return jnp.where(low, table[:, 2 * at : 2 * at + 1], table[:, 2 * at + 1 : 2 * at + 2])
 
 
-def score_kernel(times, q_ref, do_ref, *refs):
+def score_kernel(times, q_ref, *refs):
     count = len(times)
     keys_in = refs[:count]
-    e_ref, part_ref = refs[count : count + 2]
-    dvs = refs[count + 2 : 2 * count + 2]
-    keys_s, top_s, total_s, fcol_s, dv_s = refs[2 * count + 2 :]
-    tokens = q_ref.shape[0]
+    e_ref, part_ref, top_s, total_s = refs[count:]
+    q_heads = by_head(q_ref[...])
     for at in range(count):
-        keys_s[at] = keys_in[at][...]
-    q_heads = by_head(q_ref[...])
-
-    def first(at, carry):
-        keys = keys_s[at]
+        keys = keys_in[at][...]
         for head in range(2):
             scores = dot_nt(keys, q_heads[head])
             top = jnp.max(scores, axis=0, keepdims=True)
             grown = jnp.exp(scores - top)
             e_ref[2 * at + head] = grown.astype(BF)
-            top_s[pl.ds(2 * at + head, 1), :] = top
-            total_s[pl.ds(2 * at + head, 1), :] = jnp.sum(grown, axis=0, keepdims=True)
-        return carry
-
-    lax.fori_loop(0, count, first, 0, unroll=True)
+            top_s[2 * at + head : 2 * at + head + 1, :] = top
+            total_s[2 * at + head : 2 * at + head + 1, :] = jnp.sum(grown, axis=0, keepdims=True)
     for head in range(2):
         tops = [top_s[2 * at + head : 2 * at + head + 1, :] for at in range(count)]
         most = functools.reduce(jnp.maximum, tops)
@@ -178,77 +183,51 @@
         for at in range(count):
             part_ref[2 * at + head : 2 * at + head + 1, :] = lifts[at] / total
     if part_ref.shape[0] > 2 * count:
-        part_ref[2 * count :, :] = jnp.zeros((part_ref.shape[0] - 2 * count, tokens), F32)
-    turned = part_ref[...].T
-    for at in range(count):
-        fcol_s[at] = row_scale(turned, at, tokens)
-    grad = do_ref[...].astype(F32)
-
-    def second(at, carry):
-        g_heads = by_head((grad * fcol_s[at]).astype(BF))
-        dv_s[at] = (dot_nn(e_ref[2 * at], g_heads[0]) + dot_nn(e_ref[2 * at + 1], g_heads[1])).astype(BF)
-        return carry
-
-    lax.fori_loop(0, count, second, 0, unroll=True)
-    for at in range(count):
-        dvs[at][...] = dv_s[at]
+        part_ref[2 * count :, :] = jnp.zeros((part_ref.shape[0] - 2 * count, q_ref.shape[0]), F32)
 
 
 def gradient_kernel(times, q_ref, do_ref, delta_ref, e_ref, part_ref, *refs):
     count = len(times)
     keys_in, values_in = refs[:count], refs[count : 2 * count]
     dq_ref = refs[2 * count]
-    dks = refs[2 * count + 1 : 3 * count + 1]
-    keys_s, values_s, f_s, fcol_s, dq_s, dk_s = refs[3 * count + 1 :]
+    outs = refs[2 * count + 1 : 3 * count + 1]
+    dq_s = refs[3 * count + 1]
     tokens = q_ref.shape[0]
     head_dim = PART // 2
     turned = part_ref[...].T
-    for at in range(count):
-        keys_s[at] = keys_in[at][...]
-        values_s[at] = values_in[at][...]
-        fcol_s[at] = row_scale(turned, at, tokens)
-        f_s[2 * at : 2 * at + 2, :] = part_ref[2 * at : 2 * at + 2, :] * times[at]
-    g_heads = by_head(do_ref[...])
+    grad = do_ref[...]
+    g_heads = by_head(grad)
+    grad = grad.astype(F32)
     query = q_ref[...].astype(F32)
     delta = delta_ref[...]
-    dq_s[...] = jnp.zeros_like(dq_s)
-
-    def step(at, carry):
-        keys_t = keys_s[at].astype(F32).T.astype(BF)
-        values = values_s[at]
-        q_heads = by_head((query * fcol_s[at]).astype(BF))
-        dk = jnp.zeros((tokens, PART), F32)
+    for at in range(count):
+        keys_t = keys_in[at][...].astype(F32).T.astype(BF)
+        values = values_in[at][...]
+        scale = row_scale(turned, at, tokens)
+        q_scaled = by_head((query * scale).astype(BF))
+        g_scaled = by_head((grad * scale).astype(BF))
+        dks, dvs = [], []
         for head in range(2):
+            grown = e_ref[2 * at + head]
             dprob = dot_nt(values, g_heads[head])
-            dscore = (e_ref[2 * at + head].astype(F32) * (dprob - delta[head : head + 1, :])).astype(BF)
-            dk = dk + dot_nn(dscore, q_heads[head])
+            dscore = (grown.astype(F32) * (dprob - delta[head : head + 1, :])).astype(BF)
+            dvs.append(dot_nn(grown, g_scaled[head]))
+            dks.append(dot_nn(dscore, q_scaled[head]))
             spot = slice(head * head_dim, (head + 1) * head_dim)
-            dq_s[spot, :] = dq_s[spot, :] + dot_nn(keys_t[spot, :], dscore) * f_s[
-                pl.ds(2 * at + head, 1), :
-            ]
-        dk_s[at] = dk.astype(BF)
-        return carry
-
-    lax.fori_loop(0, count, step, 0, unroll=True)
-    for at in range(count):
-        dks[at][...] = dk_s[at]
+            part = part_ref[2 * at + head : 2 * at + head + 1, :] * times[at]
+            added = dot_nn(keys_t[spot, :], dscore) * part
+            dq_s[spot, :] = added if at == 0 else dq_s[spot, :] + added
+        outs[at][:, 0:PART] = (dks[0] + dks[1]).astype(BF)
+        outs[at][:, PART:] = (dvs[0] + dvs[1]).astype(BF)
     dq_ref[...] = (dq_s[...].T * (1.0 / math.sqrt(head_dim))).astype(BF)
 
 
-def combined(times, refs):
+def collect_kernel(times, dq_ref, *refs):
     total = times[0] * refs[0][...].astype(F32)
-    for time, ref in zip(times[1:], refs[1:]):
+    for time, ref in zip(times[1:], refs[1:-1]):
         total = total + time * ref[...].astype(F32)
-    return total.astype(BF)
-
-
-def collect_values_kernel(times, dq_ref, *refs):
     refs[-1][:, 0:PART] = dq_ref[...]
-    refs[-1][:, PART:] = combined(times, refs[:-1])
-
-
-def collect_keys_kernel(times, *refs):
-    refs[-1][...] = combined(times, refs[:-1])
+    refs[-1][:, PART:] = total.astype(BF)
 
 
 def place_grads(grads, own, core, count):
@@ -263,32 +242,20 @@
             ]
 
 
-def weight_early_kernel(own, core, feat_t, o_ref, held_ref, rows_ref, grads):
-    place_grads(grads, own, core, 2)
+def weight_kernel(chunks, own, core, feat_t, o_ref, pair_ref, mine_ref, *refs):
+    outs, (grads, made) = refs[:chunks], refs[chunks:]
+    place_grads(grads, own, core, 3)
+    mine_ref[...] = grads[0:PART, :]
+    pair_ref[...] = grads[2 * PART : 3 * PART, :]
     wide = grads.shape[1]
-    held_ref[:, 0:wide] = dot_nn(feat_t[...], grads[...]).astype(BF)
-    held_ref[:, wide:] = o_ref[...]
-    rows_ref[0] = grads[0:PART, :]
-    rows_ref[1] = grads[2 * PART : 3 * PART, :]
-
-
-def weight_late_kernel(chunks, own, core, feat_t, held_ref, rows_ref, pair_ref, mine_ref, *refs):
-    outs, (grads, made) = refs[:chunks], refs[chunks:]
-    place_grads(grads, own, core, 1)
-    early = rows_ref.shape[2]
-    mine_ref[:, 0:early] = rows_ref[0]
-    mine_ref[:, early:] = grads[0:PART, :]
-    pair_ref[:, 0:early] = rows_ref[1]
-    pair_ref[:, early:] = grads[2 * PART : 3 * PART, :]
-    made[...] = dot_nn(feat_t[...], grads[...]).astype(BF)
+    made[:, 0:wide] = dot_nn(feat_t[...], grads[...]).astype(BF)
+    made[:, wide:] = o_ref[...]
     rows = made.shape[0] // chunks
-    wide = held_ref.shape[1]
     for at in range(chunks):
         spot = pl.ds(0, rows)
         if chunks > 1:
             spot = pl.ds(pl.multiple_of((lax.axis_index("gx") ^ at) * rows, rows), rows)
-        outs[at][:, 0:wide] = held_ref[spot, :]
-        outs[at][:, wide:] = made[spot, :]
+        outs[at][...] = made[spot, :]
 
 
 def grad_x_kernel(own_half, mine, pair, wq0, wq1, wk0, wk1, wv0, wv1, out, full):
@@ -303,7 +270,7 @@
             base = at * width + side * 2 * PART
             full[:, columns(base + y_bit * PART)] = mine[:, spot]
             full[:, columns(base + (1 - y_bit) * PART)] = pair[:, spot]
-    for at, sources in ((half, (wq0, wv0, wk0)), (1 - half, (wq1, wv1, wk1))):
+    for at, sources in ((half, (wq0, wk0, wv0)), (1 - half, (wq1, wk1, wv1))):
         total = functools.reduce(
             jnp.add,
             [dot_nt(full[:, n * width : (n + 1) * width], sources[n][...]) for n in range(3)],
@@ -326,13 +293,13 @@
         place = lax.axis_index("gx") ^ (at // 2)
         bit = (lax.axis_index("gy") % 2) ^ (at % 2)
         spot = pl.ds(pl.multiple_of(place * rows, rows), rows)
-        for base, out in ((0, outs[0]), (3, outs[1]), (1, outs[2])):
+        for base, out in enumerate(outs[:3]):
             for side in range(2):
                 source = slice((base * 2 + side) * PART, (base * 2 + side + 1) * PART)
                 out[spot, columns(side * half + bit * PART)] = piece[:, source].astype(F32)
         spot = pl.ds(pl.multiple_of(bit * PART + place * (rows // 2), rows // 2), rows // 2)
-        outs[3][spot, 0:half] = piece[0 : rows // 2, 2 * half : 3 * half].astype(F32)
-        outs[3][spot, half:] = piece[rows // 2 :, 2 * half : 3 * half].astype(F32)
+        outs[3][spot, 0:half] = piece[0 : rows // 2, 3 * half :].astype(F32)
+        outs[3][spot, half:] = piece[rows // 2 :, 3 * half :].astype(F32)
 
 
 def on_device(features, grad_y, attn_out, w_query, w_key, w_value, w_out):
@@ -363,7 +330,11 @@
     feat_pair = from_partner(feat, "gy")
     feat_core = from_partner(feat, "gz")
     w_cols = call(
-        functools.partial(columns_kernel, own_half), shape_of((width, 3 * PART)), pairs
+        functools.partial(columns_kernel, own_half),
+        shape_of((width, 3 * PART)),
+        pairs,
+        scratch=[pltpu.SemaphoreType.DMA((6,))],
+        spaces=[pltpu.HBM if own_half else None, None] * 3,
     )
     pair_message, own = call(
         pack_kernel,
@@ -413,78 +384,46 @@
         scratch=[pltpu.VMEM((block_tokens, PART), BF), pltpu.VMEM((block_tokens, width), BF)],
         flops=4 * block_tokens * width * PART,
     )
-    own_values, out_grad = lax.optimization_barrier((own_values, out_grad))
     values = [own_values] + [shifted(own_values, axis, step) for axis, step in routes]
     rows = -(-2 * count // 8) * 8
     pixels = 2 * count * block_tokens * block_tokens
-    grown, parts, *dvs = call(
+    grown, parts = call(
         functools.partial(score_kernel, times),
         (
             shape_of((2 * count, block_tokens, block_tokens)),
             shape_of((rows, block_tokens), F32),
-            *[column] * count,
         ),
-        [query, out_grad, *keys],
-        scratch=[
-            pltpu.VMEM((count, block_tokens, PART), BF),
-            pltpu.VMEM((rows, block_tokens), F32),
-            pltpu.VMEM((rows, block_tokens), F32),
-            pltpu.VMEM((count, block_tokens, PART), F32),
-            pltpu.VMEM((count, block_tokens, PART), BF),
-        ],
-        flops=4 * pixels * PART,
+        [query, *keys],
+        scratch=[pltpu.VMEM((rows, block_tokens), F32), pltpu.VMEM((rows, block_tokens), F32)],
+        flops=2 * pixels * PART,
         moved=2 * pixels,
         exps=pixels,
     )
-    dv_back = [dvs[0]]
-    for partial, (axis, step) in zip(dvs[1:], routes):
-        dv_back.append(shifted(partial, axis, -step))
-    dq, *dks = call(
+    dq, *partials = call(
         functools.partial(gradient_kernel, times),
-        (column, *[column] * count),
+        (column, *[shape_of((block_tokens, 2 * PART))] * count),
         [query, out_grad, delta, grown, parts, *keys, *values],
-        scratch=[
-            pltpu.VMEM((count, block_tokens, PART), BF),
-            pltpu.VMEM((count, block_tokens, PART), BF),
-            pltpu.VMEM((rows, block_tokens), F32),
-            pltpu.VMEM((count, block_tokens, PART), F32),
-            pltpu.VMEM((PART, block_tokens), F32),
-            pltpu.VMEM((count, block_tokens, PART), BF),
-        ],
-        flops=6 * pixels * PART,
+        scratch=[pltpu.VMEM((PART, block_tokens), F32)],
+        flops=8 * pixels * PART,
         moved=2 * pixels,
     )
-    dks, dv_back = lax.optimization_barrier((dks, dv_back))
-    dk_back = [dks[0]]
-    for partial, (axis, step) in zip(dks[1:], routes):
-        dk_back.append(shifted(partial, axis, -step))
-    early = call(
-        functools.partial(collect_values_kernel, times),
-        shape_of((block_tokens, 2 * PART)),
-        [dq, *dv_back],
-    )
-    early_core = from_partner(early, "gz")
+    back = [partials[0]]
+    for partial, (axis, step) in zip(partials[1:], routes):
+        back.append(shifted(partial, axis, -step))
+    grads = call(
+        functools.partial(collect_kernel, times), shape_of((block_tokens, 3 * PART)), [dq, *back]
+    )
+    core_grads = from_partner(grads, "gz")
     planned = count_x == 4 and count_y == 4 and count_z == 2
     chunks = 4 if planned else 1
     piece = shape_of((half // chunks, 8 * PART))
-    held, early_rows = call(
-        weight_early_kernel,
-        (shape_of((half, 6 * PART)), shape_of((2, tokens, 4 * PART))),
-        [early, early_core, feat_t, out_term],
-        scratch=[pltpu.VMEM((block_tokens, 4 * PART), BF)],
-        flops=2 * block_tokens * half * 4 * PART,
-    )
-    late = call(functools.partial(collect_keys_kernel, times), column, dk_back)
-    late_core = from_partner(late, "gz")
     pair_out, mine, *pieces = call(
-        functools.partial(weight_late_kernel, chunks),
+        functools.partial(weight_kernel, chunks),
         (shape_of((tokens, 6 * PART)), shape_of((tokens, 6 * PART)), *[piece] * chunks),
-        [late, late_core, feat_t, held, early_rows],
-        scratch=[pltpu.VMEM((block_tokens, 2 * PART), BF), pltpu.VMEM((half, 2 * PART), BF)],
-        flops=2 * block_tokens * half * 2 * PART,
-    )
-    pair_in = from_partner(pair_out, "gy")
-
+        [grads, core_grads, feat_t, out_term],
+        scratch=[pltpu.VMEM((block_tokens, 6 * PART), BF), pltpu.VMEM((half, 8 * PART), BF)],
+        flops=2 * block_tokens * half * 6 * PART,
+    )
     def features_grad(pair_rows):
         return call(
             functools.partial(grad_x_kernel, own_half),
@@ -497,11 +436,12 @@
     if planned:
         terms = [pieces[0]] + [plane_swap(pieces[at], at, 0) for at in (1, 2, 3)]
         total = call(sum_kernel, piece, terms)
-        total, pair_in = lax.optimization_barrier((total, pair_in))
+        total, pair_out = lax.optimization_barrier((total, pair_out))
         other = plane_swap(total, 0, 2)
+        pair_in = from_partner(pair_out, "gy")
+        other, pair_in = lax.optimization_barrier((other, pair_in))
+        total = call(sum_kernel, piece, [total, other])
         grad_x = features_grad(pair_in)
-        total, grad_x = lax.optimization_barrier((total, grad_x))
-        total = call(sum_kernel, piece, [total, other])
         by_x, by_y, by_z = plane_swap(total, 1, 0), plane_swap(total, 2, 0), plane_swap(total, 0, 1)
         by_xy, by_xz = plane_swap(by_y, 1, 0), plane_swap(by_x, 0, 1)
         by_yz, by_xyz = plane_swap(by_z, 2, 0), plane_swap(by_z, 3, 0)
@@ -511,16 +451,16 @@
             [total, by_z, by_x, by_xz, by_y, by_yz, by_xy, by_xyz],
         )
     else:
-        grad_x = features_grad(pair_in)
+        grad_x = features_grad(from_partner(pair_out, "gy"))
         terms = pieces[0].astype(F32)
         stacked = jnp.zeros((4, width, width), F32)
-        for base, at in ((0, 0), (3, 1), (1, 2)):
+        for base, at in ((0, 0), (1, 1), (2, 2)):
             for side in range(2):
                 tile = terms[:, (base * 2 + side) * PART : (base * 2 + side + 1) * PART]
                 stacked = lax.dynamic_update_slice(
                     stacked, tile[None], (at, z_bit * half, side * half + y_bit * PART)
                 )
-        tile = terms[:, 4 * PART : 6 * PART].reshape(4, 2, 32, half)
+        tile = terms[:, 6 * PART :].reshape(4, 2, 32, half)
         tile = tile.transpose(0, 2, 1, 3).reshape(PART, width)
         stacked = lax.dynamic_update_slice(
             stacked, tile[None], (3, z_bit * half + y_bit * PART, 0)

time: 92.4 us -> 90.2 us (0.976)
  starting transfers between devices: 29.9 us -> 35.4 us
  waiting for transfers between devices: 41.1 us -> 35.6 us
  Pallas kernels: 12.8 us -> 11.6 us
  local copies, waits for them, and re-layouts: 7.32 us -> 6.37 us
    ppermute x11, waiting for transfers between devices: 23.2 us -> 15 us  [plane_swap(): return lax.ppermute(value, ('gx', 'gy'), route)]
    ppermute x11, starting transfers between devices: 9.82 us -> 16.5 us  [plane_swap(): return lax.ppermute(value, ('gx', 'gy'), route)]
    ppermute x12 -> x11, waiting for transfers between devices: 3.51 us -> 6.52 us  [from_partner(): return lax.ppermute(block, axis, route)]
    pallas_call x14 -> x12, Pallas kernels: 12.8 us -> 11.6 us  [call(): pl.pallas_call(kernel, out_shape=out_shape, in_specs=specs, scratch_shape...]
    ppermute x12 -> x9, starting transfers between devices: 15.1 us -> 14.1 us  [shifted(): lax.ppermute(value, axis, [(source, (source + steps) % count) for source...]
    unnamed x14, local copies, waits for them, and re-layouts: 3.81 us -> 2.86 us
    ppermute x12 -> x9, waiting for transfers between devices: 14.4 us -> 14.1 us  [shifted(): lax.ppermute(value, axis, [(source, (source + steps) % count) for source...]
    ppermute x12 -> x11, starting transfers between devices: 5.03 us -> 4.81 us  [from_partner(): return lax.ppermute(block, axis, route)]
  transfers between devices with their start and end apart: 35 -> 31, of which waited for: 19 -> 16; matrix products, arithmetic and copies ran while one was open for 4% -> 4% of each run, Pallas kernels for 12% -> 5%
where the time goes in v4:
time: 90.2 us; the launch traced here: 89.9 us
  waiting for transfers between devices  35.6 us (39%)
  starting transfers between devices  35.4 us (39%)
  Pallas kernels  11.6 us (13%)
  local copies, waits for them, and re-layouts  6.37 us (7%)
    ppermute x11, starting transfers between devices, plane_swap(): return lax.ppermute(value, ('gx', 'gy'), route)  16.5 us
    ppermute x11, waiting for transfers between devices, plane_swap(): return lax.ppermute(value, ('gx', 'gy'), route)  15 us
    ppermute x9, starting transfers between devices, shifted(): lax.ppermute(value, axis, [(source, (source + steps) % count) for source...  14.1 us
    ppermute x9, waiting for transfers between devices, shifted(): lax.ppermute(value, axis, [(source, (source + steps) % count) for source...  14.1 us
    pallas_call x12, Pallas kernels, call(): pl.pallas_call(kernel, out_shape=out_shape, in_specs=specs, scratch_shape...  11.6 us
    ppermute x11, waiting for transfers between devices, from_partner(): return lax.ppermute(block, axis, route)  6.52 us
    ppermute x11, starting transfers between devices, from_partner(): return lax.ppermute(block, axis, route)  4.81 us
    unnamed x14, local copies, waits for them, and re-layouts  2.86 us
  transfers between devices with their start and end apart: 31, of which 16 were waited for; matrix products, arithmetic and copies ran while one was open for 4% of the time, Pallas kernels for 5%

profile of v4, /device:TPU:0, one launch (start us, length us, event | category | flops | bytes accessed | tf_op | source)
XLA Modules:
  0.0 89.9 jit_solution(15270352983692210211)
XLA Ops:
  2.8 3.0 %collective-permute-start.1 = (bf16[128,512]{1,0:T(8,128)(2,1)S(1)}, bf16[128,512]{1,0:T(8,128)(2,1)S(1)}, u32[]{:S(2)}, u32[]{:S(2)}) collective-permute-start(bf16[128,512]{1,0:T(8,128)(2,1)S(1)} %reshape.24.own.f_own), channel_id=1, source_target_pairs={{0,2},{2,0},{4,6},{6,4},{1,3},{3,1},{5,7},{7,5},{8,10},{10,8},{12,... | collective-permute-start | bytes 393224 | tf_op jit(solution)/shard_map/ppermute | solution.py:20
  8.7 0.9 %copy-done.2 = bf16[256,512]{1,0:T(8,128)(2,1)S(1)} copy-done((bf16[256,512]{1,0:T(8,128)(2,1)S(1)}, bf16[256,512]{1,0:T(8,128)(2,1)}, u32[]{:S(2)}) %copy-start.2) | copy-done | bytes 262168
  9.6 0.9 %copy-done.4 = bf16[256,512]{1,0:T(8,128)(2,1)S(1)} copy-done((bf16[256,512]{1,0:T(8,128)(2,1)S(1)}, bf16[256,512]{1,0:T(8,128)(2,1)}, u32[]{:S(2)}) %copy-start.4) | copy-done | bytes 262168
  12.6 2.7 %collective-permute-start.11 = (bf16[512,128]{1,0:T(8,128)(2,1)S(1)}, bf16[512,128]{1,0:T(8,128)(2,1)S(1)}, u32[]{:S(2)}, u32[]{:S(2)}) collective-permute-start(bf16[512,128]{1,0:T(8,128)(2,1)S(1)} %get-tuple-element.52.refs_0_), channel_id=1, source_target_pairs={{0,4},{2,6},{4,0},{6,2},{1,5},{3,7},{5,1},{7,3},{8,12},{10,14},{12... | collective-permute-start | bytes 393224 | tf_op jit(solution)/shard_map/ppermute | solution.py:25
  15.2 2.4 %collective-permute-start.10 = (bf16[512,128]{1,0:T(8,128)(2,1)S(1)}, bf16[512,128]{1,0:T(8,128)(2,1)S(1)}, u32[]{:S(2)}, u32[]{:S(2)}) collective-permute-start(bf16[512,128]{1,0:T(8,128)(2,1)S(1)} %get-tuple-element.52.refs_0_), channel_id=1, source_target_pairs={{0,24},{8,0},{16,8},{24,16},{1,25},{9,1},{17,9},{25,17},{2,26},{10... | collective-permute-start | bytes 393224 | tf_op jit(solution)/shard_map/ppermute | solution.py:25
  17.7 3.3 %collective-permute-done.pair = bf16[128,768]{1,0:T(8,128)(2,1)S(1)} collective-permute-done((bf16[128,768]{1,0:T(8,128)(2,1)S(1)}, bf16[128,768]{1,0:T(8,128)(2,1)S(1)}, u32[]{:S(2)}, u32[]{:S(2)}) %collective-permute-start) | collective-permute-done | bytes 196640 | tf_op jit(solution)/shard_map/ppermute | solution.py:20
  21.0 1.4 %collective-permute-start.14 = (bf16[512,128]{1,0:T(8,128)(2,1)S(1)}, bf16[512,128]{1,0:T(8,128)(2,1)S(1)}, u32[]{:S(2)}, u32[]{:S(2)}) collective-permute-start(bf16[512,128]{1,0:T(8,128)(2,1)S(1)} %get-tuple-element.55.refs_4_), channel_id=1, source_target_pairs={{0,4},{2,6},{4,0},{6,2},{1,5},{3,7},{5,1},{7,3},{8,12},{10,14},{12... | collective-permute-start | bytes 393224 | tf_op jit(solution)/shard_map/ppermute | solution.py:25
  22.4 2.6 %collective-permute-start.13 = (bf16[512,128]{1,0:T(8,128)(2,1)S(1)}, bf16[512,128]{1,0:T(8,128)(2,1)S(1)}, u32[]{:S(2)}, u32[]{:S(2)}) collective-permute-start(bf16[512,128]{1,0:T(8,128)(2,1)S(1)} %get-tuple-element.55.refs_4_), channel_id=1, source_target_pairs={{0,24},{8,0},{16,8},{24,16},{1,25},{9,1},{17,9},{25,17},{2,26},{10... | collective-permute-start | bytes 393224 | tf_op jit(solution)/shard_map/ppermute | solution.py:25
  25.8 2.7 %shard_map.114 = (bf16[8,512,512]{2,1,0:T(8,128)(2,1)S(1)}, f32[8,512]{1,0:T(8,128)S(1)}) custom-call(bf16[512,128]{1,0:T(8,128)(2,1)S(1)} %get-tuple-element.47.q_ref, bf16[512,128]{1,0:T(8,128)(2,1)S(1)} %get-tuple-element.52.refs_0_, bf16[512,128]{1,0:T(8,128)(2,1)S(1)} %collective-permute-done.9.refs_1_, ...), custom_call_target="tpu_custom_call" | custom-call | flops 536870912 | bytes 4194304 | tf_op jit(solution)/shard_map/pallas_call | solution.py:55
  29.0 1.6 %collective-permute-done.14.refs_7_ = bf16[512,128]{1,0:T(8,128)(2,1)S(1)} collective-permute-done((bf16[512,128]{1,0:T(8,128)(2,1)S(1)}, bf16[512,128]{1,0:T(8,128)(2,1)S(1)}, u32[]{:S(2)}, u32[]{:S(2)}) %collective-permute-start.14) | collective-permute-done | bytes 131104 | tf_op jit(solution)/shard_map/ppermute | solution.py:25
  31.1 4.9 %shard_map.115 = (bf16[512,128]{1,0:T(8,128)(2,1)S(1)}, bf16[512,256]{1,0:T(8,128)(2,1)S(1)}, bf16[512,256]{1,0:T(8,128)(2,1)S(1)}, bf16[512,256]{1,0:T(8,128)(2,1)S(1)}, bf16[512,256]{1,0:T(8,128)(2,1)S(1)}) custom-call(bf16[512,128]{1,0:T(8,128)(2,1)S(1)} %get-tuple-element.47.q_ref, bf16[512,128]{1,0:T(8,128)(2,1)S(1)} %get-tuple-element.50.do_ref, ...), custom_call_target="tpu_custom_call" | custom-call | flops 2147483648 | bytes 4194304 | tf_op jit(solution)/shard_map/pallas_call | solution.py:55
  36.0 2.0 %collective-permute-start.15 = (bf16[512,256]{1,0:T(8,128)(2,1)S(1)}, bf16[512,256]{1,0:T(8,128)(2,1)S(1)}, u32[]{:S(2)}, u32[]{:S(2)}) collective-permute-start(bf16[512,256]{1,0:T(8,128)(2,1)S(1)} %get-tuple-element.58), channel_id=1, source_target_pairs={{0,24},{8,0},{16,8},{24,16},{1,25},{9,1},{17,9},{25,17},{2,26},{10... | collective-permute-start | bytes 786440 | tf_op jit(solution)/shard_map/ppermute | solution.py:25
  38.1 2.1 %collective-permute-start.17 = (bf16[512,256]{1,0:T(8,128)(2,1)S(1)}, bf16[512,256]{1,0:T(8,128)(2,1)S(1)}, u32[]{:S(2)}, u32[]{:S(2)}) collective-permute-start(bf16[512,256]{1,0:T(8,128)(2,1)S(1)} %get-tuple-element.60), channel_id=1, source_target_pairs={{0,4},{2,6},{4,0},{6,2},{1,5},{3,7},{5,1},{7,3},{8,12},{10,14},{12... | collective-permute-start | bytes 786440 | tf_op jit(solution)/shard_map/ppermute | solution.py:25
  40.2 5.1 %collective-permute-done.15.refs_1_ = bf16[512,256]{1,0:T(8,128)(2,1)S(1)} collective-permute-done((bf16[512,256]{1,0:T(8,128)(2,1)S(1)}, bf16[512,256]{1,0:T(8,128)(2,1)S(1)}, u32[]{:S(2)}, u32[]{:S(2)}) %collective-permute-start.15) | collective-permute-done | bytes 262176 | tf_op jit(solution)/shard_map/ppermute | solution.py:25
  45.3 4.7 %collective-permute-done.16.refs_2_ = bf16[512,256]{1,0:T(8,128)(2,1)S(1)} collective-permute-done((bf16[512,256]{1,0:T(8,128)(2,1)S(1)}, bf16[512,256]{1,0:T(8,128)(2,1)S(1)}, u32[]{:S(2)}, u32[]{:S(2)}) %collective-permute-start.16) | collective-permute-done | bytes 262176 | tf_op jit(solution)/shard_map/ppermute | solution.py:25
  50.1 2.1 %collective-permute-done.17.refs_3_ = bf16[512,256]{1,0:T(8,128)(2,1)S(1)} collective-permute-done((bf16[512,256]{1,0:T(8,128)(2,1)S(1)}, bf16[512,256]{1,0:T(8,128)(2,1)S(1)}, u32[]{:S(2)}, u32[]{:S(2)}) %collective-permute-start.17) | collective-permute-done | bytes 262176 | tf_op jit(solution)/shard_map/ppermute | solution.py:25
  52.4 1.7 %collective-permute-done.18.core = bf16[512,384]{1,0:T(8,128)(2,1)S(1)} collective-permute-done((bf16[512,384]{1,0:T(8,128)(2,1)S(1)}, bf16[512,384]{1,0:T(8,128)(2,1)S(1)}, u32[]{:S(2)}, u32[]{:S(2)}) %collective-permute-start.18) | collective-permute-done | bytes 393248 | tf_op jit(solution)/shard_map/ppermute | solution.py:20
  54.7 1.8 %collective-permute-start.19 = (bf16[64,1024]{1,0:T(8,128)(2,1)S(1)}, bf16[64,1024]{1,0:T(8,128)(2,1)S(1)}, u32[]{:S(2)}, u32[]{:S(2)}) collective-permute-start(bf16[64,1024]{1,0:T(8,128)(2,1)S(1)} %get-tuple-element.65), channel_id=1, source_target_pairs={{0,8},{2,10},{4,12},{6,14},{8,0},{10,2},{12,4},{14,6},{16,24},{18,... | collective-permute-start | bytes 393224 | tf_op jit(solution)/shard_map/ppermute | solution.py:34
  56.5 1.5 %collective-permute-start.20 = (bf16[64,1024]{1,0:T(8,128)(2,1)S(1)}, bf16[64,1024]{1,0:T(8,128)(2,1)S(1)}, u32[]{:S(2)}, u32[]{:S(2)}) collective-permute-start(bf16[64,1024]{1,0:T(8,128)(2,1)S(1)} %get-tuple-element.66), channel_id=1, source_target_pairs={{0,16},{2,18},{4,20},{6,22},{8,24},{10,26},{12,28},{14,30},{16,0},... | collective-permute-start | bytes 393224 | tf_op jit(solution)/shard_map/ppermute | solution.py:34
  58.3 2.2 %collective-permute-done.19.refs_1_ = bf16[64,1024]{1,0:T(8,128)(2,1)S(1)} collective-permute-done((bf16[64,1024]{1,0:T(8,128)(2,1)S(1)}, bf16[64,1024]{1,0:T(8,128)(2,1)S(1)}, u32[]{:S(2)}, u32[]{:S(2)}) %collective-permute-start.19) | collective-permute-done | bytes 131104 | tf_op jit(solution)/shard_map/ppermute | solution.py:34
  60.5 4.1 %collective-permute-done.20.refs_2_ = bf16[64,1024]{1,0:T(8,128)(2,1)S(1)} collective-permute-done((bf16[64,1024]{1,0:T(8,128)(2,1)S(1)}, bf16[64,1024]{1,0:T(8,128)(2,1)S(1)}, u32[]{:S(2)}, u32[]{:S(2)}) %collective-permute-start.20) | collective-permute-done | bytes 131104 | tf_op jit(solution)/shard_map/ppermute | solution.py:34
  64.7 3.1 %collective-permute-start.22 = (bf16[64,1024]{1,0:T(8,128)(2,1)S(1)}, bf16[64,1024]{1,0:T(8,128)(2,1)S(1)}, u32[]{:S(2)}, u32[]{:S(2)}) collective-permute-start(bf16[64,1024]{1,0:T(8,128)(2,1)S(1)} %shard_map.118.refs_0_), channel_id=1, source_target_pairs={{0,4},{2,6},{4,0},{6,2},{8,12},{10,14},{12,8},{14,10},{16,20},{18,... | collective-permute-start | bytes 393224 | tf_op jit(solution)/shard_map/ppermute | solution.py:34
  67.8 4.2 %collective-permute-done.22.refs_1_ = bf16[64,1024]{1,0:T(8,128)(2,1)S(1)} collective-permute-done((bf16[64,1024]{1,0:T(8,128)(2,1)S(1)}, bf16[64,1024]{1,0:T(8,128)(2,1)S(1)}, u32[]{:S(2)}, u32[]{:S(2)}) %collective-permute-start.22) | collective-permute-done | bytes 131104 | tf_op jit(solution)/shard_map/ppermute | solution.py:34
  72.7 2.2 %collective-permute-start.27 = (bf16[64,1024]{1,0:T(8,128)(2,1)S(1)}, bf16[64,1024]{1,0:T(8,128)(2,1)S(1)}, u32[]{:S(2)}, u32[]{:S(2)}) collective-permute-start(bf16[64,1024]{1,0:T(8,128)(2,1)S(1)} %shard_map.120.refs_0_), channel_id=1, source_target_pairs={{0,16},{2,18},{4,20},{6,22},{8,24},{10,26},{12,28},{14,30},{16,0},... | collective-permute-start | bytes 393224 | tf_op jit(solution)/shard_map/ppermute | solution.py:34
  75.5 1.4 %collective-permute-start.24 = (bf16[64,1024]{1,0:T(8,128)(2,1)S(1)}, bf16[64,1024]{1,0:T(8,128)(2,1)S(1)}, u32[]{:S(2)}, u32[]{:S(2)}) collective-permute-start(bf16[64,1024]{1,0:T(8,128)(2,1)S(1)} %shard_map.120.refs_0_), channel_id=1, source_target_pairs={{0,2},{2,0},{4,6},{6,4},{8,10},{10,8},{12,14},{14,12},{16,18},{18,... | collective-permute-start | bytes 393224 | tf_op jit(solution)/shard_map/ppermute | solution.py:34
  77.8 2.1 %collective-permute-start.29 = (bf16[64,1024]{1,0:T(8,128)(2,1)S(1)}, bf16[64,1024]{1,0:T(8,128)(2,1)S(1)}, u32[]{:S(2)}, u32[]{:S(2)}) collective-permute-start(bf16[64,1024]{1,0:T(8,128)(2,1)S(1)} %collective-permute-done.27.refs_4_), channel_id=1, source_target_pairs={{0,8},{2,10},{4,12},{6,14},{8,0},{10,2},{12,4},{14,6},{16,24},{18,... | collective-permute-start | bytes 393224 | tf_op jit(solution)/shard_map/ppermute | solution.py:34
  79.8 1.3 %collective-permute-done.25.refs_2_ = bf16[64,1024]{1,0:T(8,128)(2,1)S(1)} collective-permute-done((bf16[64,1024]{1,0:T(8,128)(2,1)S(1)}, bf16[64,1024]{1,0:T(8,128)(2,1)S(1)}, u32[]{:S(2)}, u32[]{:S(2)}) %collective-permute-start.25) | collective-permute-done | bytes 131104 | tf_op jit(solution)/shard_map/ppermute | solution.py:34
  81.1 1.8 %collective-permute-start.30 = (bf16[64,1024]{1,0:T(8,128)(2,1)S(1)}, bf16[64,1024]{1,0:T(8,128)(2,1)S(1)}, u32[]{:S(2)}, u32[]{:S(2)}) collective-permute-start(bf16[64,1024]{1,0:T(8,128)(2,1)S(1)} %collective-permute-done.24.refs_1_), channel_id=1, source_target_pairs={{0,24},{2,26},{4,28},{6,30},{8,16},{10,18},{12,20},{14,22},{16,8},... | collective-permute-start | bytes 393224 | tf_op jit(solution)/shard_map/ppermute | solution.py:34
  82.9 1.8 %collective-permute-start.28 = (bf16[64,1024]{1,0:T(8,128)(2,1)S(1)}, bf16[64,1024]{1,0:T(8,128)(2,1)S(1)}, u32[]{:S(2)}, u32[]{:S(2)}) collective-permute-start(bf16[64,1024]{1,0:T(8,128)(2,1)S(1)} %collective-permute-done.24.refs_1_), channel_id=1, source_target_pairs={{0,16},{2,18},{4,20},{6,22},{8,24},{10,26},{12,28},{14,30},{16,0},... | collective-permute-start | bytes 393224 | tf_op jit(solution)/shard_map/ppermute | solution.py:34
  86.1 1.0 %collective-permute-done.30.refs_7_ = bf16[64,1024]{1,0:T(8,128)(2,1)S(1)} collective-permute-done((bf16[64,1024]{1,0:T(8,128)(2,1)S(1)}, bf16[64,1024]{1,0:T(8,128)(2,1)S(1)}, u32[]{:S(2)}, u32[]{:S(2)}) %collective-permute-start.30) | collective-permute-done | bytes 131104 | tf_op jit(solution)/shard_map/ppermute | solution.py:34
  87.0 1.3 %collective-permute-done.28.refs_5_ = bf16[64,1024]{1,0:T(8,128)(2,1)S(1)} collective-permute-done((bf16[64,1024]{1,0:T(8,128)(2,1)S(1)}, bf16[64,1024]{1,0:T(8,128)(2,1)S(1)}, u32[]{:S(2)}, u32[]{:S(2)}) %collective-permute-start.28) | collective-permute-done | bytes 131104 | tf_op jit(solution)/shard_map/ppermute | solution.py:34
  88.4 1.5 %shard_map.121 = (f32[256,512]{1,0:T(8,128)}, f32[256,512]{1,0:T(8,128)}, f32[256,512]{1,0:T(8,128)}, f32[256,512]{1,0:T(8,128)}) custom-call(bf16[64,1024]{1,0:T(8,128)(2,1)S(1)} %shard_map.120.refs_0_, bf16[64,1024]{1,0:T(8,128)(2,1)S(1)} %collective-permute-done.24.refs_1_, bf16[64,1024]{1,0:T(8,128)(2,1)S(1)} %collective-permute-done.25.refs_2_, ...), custom_call_target="tpu_custom_call" | custom-call | flops 1000000 | bytes 1000000 | tf_op jit(solution)/shard_map/pallas_call | solution.py:55
  (60 shorter events, 13.9 us)
Async XLA Ops:
  0.6 7.1 %collective-permute-start.3 = (bf16[256,512]{1,0:T(8,128)(2,1)}, bf16[256,512]{1,0:T(8,128)(2,1)S(1)}, u32[]{:S(2)}, u32[]{:S(2)}) collective-permute-start(bf16[256,512]{1,0:T(8,128)(2,1)} %wq0.3), channel_id=1, source_target_pairs={{0,1},{1,0},{2,3},{3,2},{4,5},{5,4},{6,7},{7,6},{8,9},{9,8},{10,11... | collective-permute-start | bytes 786440 | tf_op jit(solution)/shard_map/ppermute | solution.py:20
  1.2 6.5 %collective-permute-start.4 = (bf16[256,512]{1,0:T(8,128)(2,1)}, bf16[256,512]{1,0:T(8,128)(2,1)S(1)}, u32[]{:S(2)}, u32[]{:S(2)}) collective-permute-start(bf16[256,512]{1,0:T(8,128)(2,1)} %wk0.3), channel_id=1, source_target_pairs={{0,1},{1,0},{2,3},{3,2},{4,5},{5,4},{6,7},{7,6},{8,9},{9,8},{10,11... | collective-permute-start | bytes 786440 | tf_op jit(solution)/shard_map/ppermute | solution.py:20
  1.2 6.5 %collective-permute-start.5 = (bf16[256,512]{1,0:T(8,128)(2,1)}, bf16[256,512]{1,0:T(8,128)(2,1)S(1)}, u32[]{:S(2)}, u32[]{:S(2)}) collective-permute-start(bf16[256,512]{1,0:T(8,128)(2,1)} %wv0.3), channel_id=1, source_target_pairs={{0,1},{1,0},{2,3},{3,2},{4,5},{5,4},{6,7},{7,6},{8,9},{9,8},{10,11... | collective-permute-start | bytes 786440 | tf_op jit(solution)/shard_map/ppermute | solution.py:20
  2.6 8.1 %collective-permute-start.2 = (bf16[128,512]{1,0:T(8,128)(2,1)S(1)}, bf16[128,512]{1,0:T(8,128)(2,1)S(1)}, u32[]{:S(2)}, u32[]{:S(2)}) collective-permute-start(bf16[128,512]{1,0:T(8,128)(2,1)S(1)} %reshape.24.own.f_own), channel_id=1, source_target_pairs={{0,1},{1,0},{2,3},{3,2},{4,5},{5,4},{6,7},{7,6},{8,9},{9,8},{10,11... | collective-permute-start | bytes 393224 | tf_op jit(solution)/shard_map/ppermute | solution.py:20
  2.8 8.0 %collective-permute-start.1 = (bf16[128,512]{1,0:T(8,128)(2,1)S(1)}, bf16[128,512]{1,0:T(8,128)(2,1)S(1)}, u32[]{:S(2)}, u32[]{:S(2)}) collective-permute-start(bf16[128,512]{1,0:T(8,128)(2,1)S(1)} %reshape.24.own.f_own), channel_id=1, source_target_pairs={{0,2},{2,0},{4,6},{6,4},{1,3},{3,1},{5,7},{7,5},{8,10},{10,8},{12,... | collective-permute-start | bytes 393224 | tf_op jit(solution)/shard_map/ppermute | solution.py:20
  10.7 1.4 %collective-permute-start.6 = (bf16[128,512]{1,0:T(8,128)(2,1)S(1)}, bf16[128,512]{1,0:T(8,128)(2,1)S(1)}, u32[]{:S(2)}, u32[]{:S(2)}) collective-permute-start(bf16[128,512]{1,0:T(8,128)(2,1)S(1)} %collective-permute-done.1.pair.f_pair), channel_id=1, source_target_pairs={{0,1},{1,0},{2,3},{3,2},{4,5},{5,4},{6,7},{7,6},{8,9},{9,8},{10,11... | collective-permute-start | bytes 393224 | tf_op jit(solution)/shard_map/ppermute | solution.py:20
  10.8 10.1 %collective-permute-start = (bf16[128,768]{1,0:T(8,128)(2,1)S(1)}, bf16[128,768]{1,0:T(8,128)(2,1)S(1)}, u32[]{:S(2)}, u32[]{:S(2)}) collective-permute-start(bf16[128,768]{1,0:T(8,128)(2,1)S(1)} %get-tuple-element.41), channel_id=1, source_target_pairs={{0,2},{2,0},{4,6},{6,4},{1,3},{3,1},{5,7},{7,5},{8,10},{10,8},{12,... | collective-permute-start | bytes 589832 | tf_op jit(solution)/shard_map/ppermute | solution.py:20
  12.6 8.4 %collective-permute-start.11 = (bf16[512,128]{1,0:T(8,128)(2,1)S(1)}, bf16[512,128]{1,0:T(8,128)(2,1)S(1)}, u32[]{:S(2)}, u32[]{:S(2)}) collective-permute-start(bf16[512,128]{1,0:T(8,128)(2,1)S(1)} %get-tuple-element.52.refs_0_), channel_id=1, source_target_pairs={{0,4},{2,6},{4,0},{6,2},{1,5},{3,7},{5,1},{7,3},{8,12},{10,14},{12... | collective-permute-start | bytes 393224 | tf_op jit(solution)/shard_map/ppermute | solution.py:25
  15.2 7.1 %collective-permute-start.10 = (bf16[512,128]{1,0:T(8,128)(2,1)S(1)}, bf16[512,128]{1,0:T(8,128)(2,1)S(1)}, u32[]{:S(2)}, u32[]{:S(2)}) collective-permute-start(bf16[512,128]{1,0:T(8,128)(2,1)S(1)} %get-tuple-element.52.refs_0_), channel_id=1, source_target_pairs={{0,24},{8,0},{16,8},{24,16},{1,25},{9,1},{17,9},{25,17},{2,26},{10... | collective-permute-start | bytes 393224 | tf_op jit(solution)/shard_map/ppermute | solution.py:25
  17.7 7.3 %collective-permute-start.9 = (bf16[512,128]{1,0:T(8,128)(2,1)S(1)}, bf16[512,128]{1,0:T(8,128)(2,1)S(1)}, u32[]{:S(2)}, u32[]{:S(2)}) collective-permute-start(bf16[512,128]{1,0:T(8,128)(2,1)S(1)} %get-tuple-element.52.refs_0_), channel_id=1, source_target_pairs={{0,8},{8,16},{16,24},{24,0},{1,9},{9,17},{17,25},{25,1},{2,10},{10... | collective-permute-start | bytes 393224 | tf_op jit(solution)/shard_map/ppermute | solution.py:25
  17.7 10.7 %collective-permute-start.7 = (bf16[128,768]{1,0:T(8,128)(2,1)S(1)}, bf16[128,768]{1,0:T(8,128)(2,1)S(1)}, u32[]{:S(2)}, u32[]{:S(2)}) collective-permute-start(bf16[128,768]{1,0:T(8,128)(2,1)S(1)} %get-tuple-element.48.own), channel_id=1, source_target_pairs={{0,1},{1,0},{2,3},{3,2},{4,5},{5,4},{6,7},{7,6},{8,9},{9,8},{10,11... | collective-permute-start | bytes 589832 | tf_op jit(solution)/shard_map/ppermute | solution.py:20
  21.0 7.5 %collective-permute-start.8 = (bf16[128,768]{1,0:T(8,128)(2,1)S(1)}, bf16[128,768]{1,0:T(8,128)(2,1)S(1)}, u32[]{:S(2)}, u32[]{:S(2)}) collective-permute-start(bf16[128,768]{1,0:T(8,128)(2,1)S(1)} %collective-permute-done.pair), channel_id=1, source_target_pairs={{0,1},{1,0},{2,3},{3,2},{4,5},{5,4},{6,7},{7,6},{8,9},{9,8},{10,11... | collective-permute-start | bytes 589832 | tf_op jit(solution)/shard_map/ppermute | solution.py:20
  21.0 9.6 %collective-permute-start.14 = (bf16[512,128]{1,0:T(8,128)(2,1)S(1)}, bf16[512,128]{1,0:T(8,128)(2,1)S(1)}, u32[]{:S(2)}, u32[]{:S(2)}) collective-permute-start(bf16[512,128]{1,0:T(8,128)(2,1)S(1)} %get-tuple-element.55.refs_4_), channel_id=1, source_target_pairs={{0,4},{2,6},{4,0},{6,2},{1,5},{3,7},{5,1},{7,3},{8,12},{10,14},{12... | collective-permute-start | bytes 393224 | tf_op jit(solution)/shard_map/ppermute | solution.py:25
  22.4 8.2 %collective-permute-start.13 = (bf16[512,128]{1,0:T(8,128)(2,1)S(1)}, bf16[512,128]{1,0:T(8,128)(2,1)S(1)}, u32[]{:S(2)}, u32[]{:S(2)}) collective-permute-start(bf16[512,128]{1,0:T(8,128)(2,1)S(1)} %get-tuple-element.55.refs_4_), channel_id=1, source_target_pairs={{0,24},{8,0},{16,8},{24,16},{1,25},{9,1},{17,9},{25,17},{2,26},{10... | collective-permute-start | bytes 393224 | tf_op jit(solution)/shard_map/ppermute | solution.py:25
  25.0 6.2 %collective-permute-start.12 = (bf16[512,128]{1,0:T(8,128)(2,1)S(1)}, bf16[512,128]{1,0:T(8,128)(2,1)S(1)}, u32[]{:S(2)}, u32[]{:S(2)}) collective-permute-start(bf16[512,128]{1,0:T(8,128)(2,1)S(1)} %get-tuple-element.55.refs_4_), channel_id=1, source_target_pairs={{0,8},{8,16},{16,24},{24,0},{1,9},{9,17},{17,25},{25,1},{2,10},{10... | collective-permute-start | bytes 393224 | tf_op jit(solution)/shard_map/ppermute | solution.py:25
  31.1 53.6 %copy-start.5 = (bf16[256,512]{1,0:T(8,128)(2,1)S(1)}, bf16[256,512]{1,0:T(8,128)(2,1)}, u32[]{:S(2)}) copy-start(bf16[256,512]{1,0:T(8,128)(2,1)} %wv0.3) | copy-start | bytes 786436
  36.0 9.3 %collective-permute-start.15 = (bf16[512,256]{1,0:T(8,128)(2,1)S(1)}, bf16[512,256]{1,0:T(8,128)(2,1)S(1)}, u32[]{:S(2)}, u32[]{:S(2)}) collective-permute-start(bf16[512,256]{1,0:T(8,128)(2,1)S(1)} %get-tuple-element.58), channel_id=1, source_target_pairs={{0,24},{8,0},{16,8},{24,16},{1,25},{9,1},{17,9},{25,17},{2,26},{10... | collective-permute-start | bytes 786440 | tf_op jit(solution)/shard_map/ppermute | solution.py:25
  38.0 12.1 %collective-permute-start.16 = (bf16[512,256]{1,0:T(8,128)(2,1)S(1)}, bf16[512,256]{1,0:T(8,128)(2,1)S(1)}, u32[]{:S(2)}, u32[]{:S(2)}) collective-permute-start(bf16[512,256]{1,0:T(8,128)(2,1)S(1)} %get-tuple-element.59), channel_id=1, source_target_pairs={{0,8},{8,16},{16,24},{24,0},{1,9},{9,17},{17,25},{25,1},{2,10},{10... | collective-permute-start | bytes 786440 | tf_op jit(solution)/shard_map/ppermute | solution.py:25
  38.1 14.1 %collective-permute-start.17 = (bf16[512,256]{1,0:T(8,128)(2,1)S(1)}, bf16[512,256]{1,0:T(8,128)(2,1)S(1)}, u32[]{:S(2)}, u32[]{:S(2)}) collective-permute-start(bf16[512,256]{1,0:T(8,128)(2,1)S(1)} %get-tuple-element.60), channel_id=1, source_target_pairs={{0,4},{2,6},{4,0},{6,2},{1,5},{3,7},{5,1},{7,3},{8,12},{10,14},{12... | collective-permute-start | bytes 786440 | tf_op jit(solution)/shard_map/ppermute | solution.py:25
  52.4 1.8 %collective-permute-start.18 = (bf16[512,384]{1,0:T(8,128)(2,1)S(1)}, bf16[512,384]{1,0:T(8,128)(2,1)S(1)}, u32[]{:S(2)}, u32[]{:S(2)}) collective-permute-start(bf16[512,384]{1,0:T(8,128)(2,1)S(1)} %shard_map.116.own), channel_id=1, source_target_pairs={{0,1},{1,0},{2,3},{3,2},{4,5},{5,4},{6,7},{7,6},{8,9},{9,8},{10,11... | collective-permute-start | bytes 1179656 | tf_op jit(solution)/shard_map/ppermute | solution.py:20
  54.7 5.8 %collective-permute-start.19 = (bf16[64,1024]{1,0:T(8,128)(2,1)S(1)}, bf16[64,1024]{1,0:T(8,128)(2,1)S(1)}, u32[]{:S(2)}, u32[]{:S(2)}) collective-permute-start(bf16[64,1024]{1,0:T(8,128)(2,1)S(1)} %get-tuple-element.65), channel_id=1, source_target_pairs={{0,8},{2,10},{4,12},{6,14},{8,0},{10,2},{12,4},{14,6},{16,24},{18,... | collective-permute-start | bytes 393224 | tf_op jit(solution)/shard_map/ppermute | solution.py:34
  56.5 8.1 %collective-permute-start.20 = (bf16[64,1024]{1,0:T(8,128)(2,1)S(1)}, bf16[64,1024]{1,0:T(8,128)(2,1)S(1)}, u32[]{:S(2)}, u32[]{:S(2)}) collective-permute-start(bf16[64,1024]{1,0:T(8,128)(2,1)S(1)} %get-tuple-element.66), channel_id=1, source_target_pairs={{0,16},{2,18},{4,20},{6,22},{8,24},{10,26},{12,28},{14,30},{16,0},... | collective-permute-start | bytes 393224 | tf_op jit(solution)/shard_map/ppermute | solution.py:34
  57.9 6.6 %collective-permute-start.21 = (bf16[64,1024]{1,0:T(8,128)(2,1)S(1)}, bf16[64,1024]{1,0:T(8,128)(2,1)S(1)}, u32[]{:S(2)}, u32[]{:S(2)}) collective-permute-start(bf16[64,1024]{1,0:T(8,128)(2,1)S(1)} %get-tuple-element.67), channel_id=1, source_target_pairs={{0,24},{2,26},{4,28},{6,30},{8,16},{10,18},{12,20},{14,22},{16,8},... | collective-permute-start | bytes 393224 | tf_op jit(solution)/shard_map/ppermute | solution.py:34
  64.6 8.0 %collective-permute-start.23 = (bf16[128,768]{1,0:T(8,128)(2,1)S(1)}, bf16[128,768]{1,0:T(8,128)(2,1)S(1)}, u32[]{:S(2)}, u32[]{:S(2)}) collective-permute-start(bf16[128,768]{1,0:T(8,128)(2,1)S(1)} %get-tuple-element.70), channel_id=1, source_target_pairs={{0,2},{2,0},{4,6},{6,4},{1,3},{3,1},{5,7},{7,5},{8,10},{10,8},{12,... | collective-permute-start | bytes 589832 | tf_op jit(solution)/shard_map/ppermute | solution.py:20
  64.7 7.3 %collective-permute-start.22 = (bf16[64,1024]{1,0:T(8,128)(2,1)S(1)}, bf16[64,1024]{1,0:T(8,128)(2,1)S(1)}, u32[]{:S(2)}, u32[]{:S(2)}) collective-permute-start(bf16[64,1024]{1,0:T(8,128)(2,1)S(1)} %shard_map.118.refs_0_), channel_id=1, source_target_pairs={{0,4},{2,6},{4,0},{6,2},{8,12},{10,14},{12,8},{14,10},{16,20},{18,... | collective-permute-start | bytes 393224 | tf_op jit(solution)/shard_map/ppermute | solution.py:34
  72.7 5.1 %collective-permute-start.27 = (bf16[64,1024]{1,0:T(8,128)(2,1)S(1)}, bf16[64,1024]{1,0:T(8,128)(2,1)S(1)}, u32[]{:S(2)}, u32[]{:S(2)}) collective-permute-start(bf16[64,1024]{1,0:T(8,128)(2,1)S(1)} %shard_map.120.refs_0_), channel_id=1, source_target_pairs={{0,16},{2,18},{4,20},{6,22},{8,24},{10,26},{12,28},{14,30},{16,0},... | collective-permute-start | bytes 393224 | tf_op jit(solution)/shard_map/ppermute | solution.py:34
  74.8 6.3 %collective-permute-start.25 = (bf16[64,1024]{1,0:T(8,128)(2,1)S(1)}, bf16[64,1024]{1,0:T(8,128)(2,1)S(1)}, u32[]{:S(2)}, u32[]{:S(2)}) collective-permute-start(bf16[64,1024]{1,0:T(8,128)(2,1)S(1)} %shard_map.120.refs_0_), channel_id=1, source_target_pairs={{0,8},{2,10},{4,12},{6,14},{8,0},{10,2},{12,4},{14,6},{16,24},{18,... | collective-permute-start | bytes 393224 | tf_op jit(solution)/shard_map/ppermute | solution.py:34
  75.5 5.7 %collective-permute-start.24 = (bf16[64,1024]{1,0:T(8,128)(2,1)S(1)}, bf16[64,1024]{1,0:T(8,128)(2,1)S(1)}, u32[]{:S(2)}, u32[]{:S(2)}) collective-permute-start(bf16[64,1024]{1,0:T(8,128)(2,1)S(1)} %shard_map.120.refs_0_), channel_id=1, source_target_pairs={{0,2},{2,0},{4,6},{6,4},{8,10},{10,8},{12,14},{14,12},{16,18},{18,... | collective-permute-start | bytes 393224 | tf_op jit(solution)/shard_map/ppermute | solution.py:34
  77.8 8.3 %collective-permute-start.29 = (bf16[64,1024]{1,0:T(8,128)(2,1)S(1)}, bf16[64,1024]{1,0:T(8,128)(2,1)S(1)}, u32[]{:S(2)}, u32[]{:S(2)}) collective-permute-start(bf16[64,1024]{1,0:T(8,128)(2,1)S(1)} %collective-permute-done.27.refs_4_), channel_id=1, source_target_pairs={{0,8},{2,10},{4,12},{6,14},{8,0},{10,2},{12,4},{14,6},{16,24},{18,... | collective-permute-start | bytes 393224 | tf_op jit(solution)/shard_map/ppermute | solution.py:34
  81.1 5.0 %collective-permute-start.26 = (bf16[64,1024]{1,0:T(8,128)(2,1)S(1)}, bf16[64,1024]{1,0:T(8,128)(2,1)S(1)}, u32[]{:S(2)}, u32[]{:S(2)}) collective-permute-start(bf16[64,1024]{1,0:T(8,128)(2,1)S(1)} %collective-permute-done.25.refs_2_), channel_id=1, source_target_pairs={{0,2},{2,0},{4,6},{6,4},{8,10},{10,8},{12,14},{14,12},{16,18},{18,... | collective-permute-start | bytes 393224 | tf_op jit(solution)/shard_map/ppermute | solution.py:34
  81.1 5.9 %collective-permute-start.30 = (bf16[64,1024]{1,0:T(8,128)(2,1)S(1)}, bf16[64,1024]{1,0:T(8,128)(2,1)S(1)}, u32[]{:S(2)}, u32[]{:S(2)}) collective-permute-start(bf16[64,1024]{1,0:T(8,128)(2,1)S(1)} %collective-permute-done.24.refs_1_), channel_id=1, source_target_pairs={{0,24},{2,26},{4,28},{6,30},{8,16},{10,18},{12,20},{14,22},{16,8},... | collective-permute-start | bytes 393224 | tf_op jit(solution)/shard_map/ppermute | solution.py:34
  82.9 5.5 %collective-permute-start.28 = (bf16[64,1024]{1,0:T(8,128)(2,1)S(1)}, bf16[64,1024]{1,0:T(8,128)(2,1)S(1)}, u32[]{:S(2)}, u32[]{:S(2)}) collective-permute-start(bf16[64,1024]{1,0:T(8,128)(2,1)S(1)} %collective-permute-done.24.refs_1_), channel_id=1, source_target_pairs={{0,16},{2,18},{4,20},{6,22},{8,24},{10,26},{12,28},{14,30},{16,0},... | collective-permute-start | bytes 393224 | tf_op jit(solution)/shard_map/ppermute | solution.py:34
  (6 other events, 137.8 us)

commit v5 on v4

--- a/solution.py
+++ b/solution.py
@@ -68,40 +68,32 @@
     return jax.ShapeDtypeStruct(dims, dtype)
 
 
-def pack_kernel(dy_ref, saved_ref, pair_ref, own_ref):
+def pack_kernel(dy_ref, saved_ref, pair_ref, own_ref, saved_s):
     y_bit = lax.axis_index("gy") % 2
     z_bit = lax.axis_index("gz") % 2
-    last = PART + dy_ref.shape[1]
+    tokens = pair_ref.shape[0]
+    width = dy_ref.shape[-1]
+    last = PART + width
+    dys = dy_ref[...].reshape(tokens, width)
+    saved_s[...] = saved_ref[...].reshape(tokens, width)
     for out in (pair_ref, own_ref):
-        out[:, PART:last] = dy_ref[...]
-    pair_ref[:, 0:PART] = saved_ref[:, columns((z_bit * 2 + 1 - y_bit) * PART)]
-    pair_ref[:, last:] = saved_ref[:, columns(((1 - z_bit) * 2 + 1 - y_bit) * PART)]
-    own_ref[:, 0:PART] = saved_ref[:, columns(((1 - z_bit) * 2 + y_bit) * PART)]
-    own_ref[:, last:] = saved_ref[:, columns((z_bit * 2 + y_bit) * PART)]
-
-
-def columns_kernel(own_half, wq0, wq1, wk0, wk1, wv0, wv1, w_cols, sems):
+        out[:, PART:last] = dys
+    pair_ref[:, 0:PART] = saved_s[:, columns((z_bit * 2 + 1 - y_bit) * PART)]
+    pair_ref[:, last:] = saved_s[:, columns(((1 - z_bit) * 2 + 1 - y_bit) * PART)]
+    own_ref[:, 0:PART] = saved_s[:, columns(((1 - z_bit) * 2 + y_bit) * PART)]
+    own_ref[:, last:] = saved_s[:, columns((z_bit * 2 + y_bit) * PART)]
+
+
+def columns_kernel(own_half, wq0, wq1, wk0, wk1, wv0, wv1, w_cols):
     y_bit = lax.axis_index("gy") % 2
     z_bit = lax.axis_index("gz") % 2
     half = z_bit if own_half else z_bit * 0
     group = columns((z_bit * 2 + y_bit) * PART)
     half_rows = wq0.shape[0]
-    copies = []
-    for at, pair in enumerate(((wq0, wq1), (wk0, wk1), (wv0, wv1))):
-        for side, source in enumerate(pair):
-            place = half if side == 0 else 1 - half
-            rows = pl.ds(pl.multiple_of(place * half_rows, half_rows), half_rows)
-            copies.append(
-                pltpu.make_async_copy(
-                    source.at[:, group],
-                    w_cols.at[rows, at * PART : (at + 1) * PART],
-                    sems.at[2 * at + side],
-                )
-            )
-    for copy in copies:
-        copy.start()
-    for copy in copies:
-        copy.wait()
+    for at, (first, second) in enumerate(((wq0, wq1), (wk0, wk1), (wv0, wv1))):
+        spot = slice(at * PART, (at + 1) * PART)
+        w_cols[pl.ds(pl.multiple_of(half * half_rows, half_rows), half_rows), spot] = first[:, group]
+        w_cols[pl.ds(pl.multiple_of((1 - half) * half_rows, half_rows), half_rows), spot] = second[:, group]
 
 
 def project_kernel(own, core, pair, far, w_cols, q_ref, k_ref, v_ref):
@@ -258,7 +250,7 @@
         outs[at][...] = made[spot, :]
 
 
-def grad_x_kernel(own_half, mine, pair, wq0, wq1, wk0, wk1, wv0, wv1, out, full):
+def grad_x_kernel(own_half, mine, pair, wq0, wq1, wk0, wk1, wv0, wv1, out, full, made):
     y_bit = lax.axis_index("gy") % 2
     z_bit = lax.axis_index("gz") % 2
     half = z_bit if own_half else z_bit * 0
@@ -275,7 +267,8 @@
             jnp.add,
             [dot_nt(full[:, n * width : (n + 1) * width], sources[n][...]) for n in range(3)],
         )
-        out[:, pl.ds(pl.multiple_of(at * half_rows, PART), half_rows)] = total.astype(BF)
+        made[:, pl.ds(pl.multiple_of(at * half_rows, PART), half_rows)] = total.astype(BF)
+    out[...] = made[...].reshape(out.shape)
 
 
 def sum_kernel(*refs):
@@ -333,13 +326,12 @@
         functools.partial(columns_kernel, own_half),
         shape_of((width, 3 * PART)),
         pairs,
-        scratch=[pltpu.SemaphoreType.DMA((6,))],
-        spaces=[pltpu.HBM if own_half else None, None] * 3,
     )
     pair_message, own = call(
         pack_kernel,
         (message, message),
-        [value.reshape(tokens, width) for value in (grad_y, attn_out)],
+        [grad_y, attn_out],
+        scratch=[pltpu.VMEM((tokens, width), BF)],
     )
     feat_pair, feat_core, w_cols, own = lax.optimization_barrier(
         (feat_pair, feat_core, w_cols, own)
@@ -384,6 +376,7 @@
         scratch=[pltpu.VMEM((block_tokens, PART), BF), pltpu.VMEM((block_tokens, width), BF)],
         flops=4 * block_tokens * width * PART,
     )
+    own_values, out_grad = lax.optimization_barrier((own_values, out_grad))
     values = [own_values] + [shifted(own_values, axis, step) for axis, step in routes]
     rows = -(-2 * count // 8) * 8
     pixels = 2 * count * block_tokens * block_tokens
@@ -427,21 +420,21 @@
     def features_grad(pair_rows):
         return call(
             functools.partial(grad_x_kernel, own_half),
-            shape_of((tokens, width)),
+            shape_of(features.shape),
             [mine, pair_rows, *pairs],
-            scratch=[pltpu.VMEM((tokens, 3 * width), BF)],
+            scratch=[pltpu.VMEM((tokens, 3 * width), BF), pltpu.VMEM((tokens, width), BF)],
             flops=2 * tokens * 3 * width * width,
-        ).reshape(features.shape)
+        )
 
     if planned:
         terms = [pieces[0]] + [plane_swap(pieces[at], at, 0) for at in (1, 2, 3)]
         total = call(sum_kernel, piece, terms)
-        total, pair_out = lax.optimization_barrier((total, pair_out))
+        pair_in = from_partner(pair_out, "gy")
+        total, pair_in = lax.optimization_barrier((total, pair_in))
         other = plane_swap(total, 0, 2)
-        pair_in = from_partner(pair_out, "gy")
-        other, pair_in = lax.optimization_barrier((other, pair_in))
+        grad_x = features_grad(pair_in)
+        total, grad_x = lax.optimization_barrier((total, grad_x))
         total = call(sum_kernel, piece, [total, other])
-        grad_x = features_grad(pair_in)
         by_x, by_y, by_z = plane_swap(total, 1, 0), plane_swap(total, 2, 0), plane_swap(total, 0, 1)
         by_xy, by_xz = plane_swap(by_y, 1, 0), plane_swap(by_x, 0, 1)
         by_yz, by_xyz = plane_swap(by_z, 2, 0), plane_swap(by_z, 3, 0)

time: 90.2 us -> 90.5 us (level)
  starting transfers between devices: 35.4 us -> 27.8 us
  waiting for transfers between devices: 35.6 us -> 42.9 us
    ppermute x11, waiting for transfers between devices: 15 us -> 21.8 us  [plane_swap(): return lax.ppermute(value, ('gx', 'gy'), route)]
    ppermute x11, starting transfers between devices: 16.5 us -> 10.4 us  [plane_swap(): return lax.ppermute(value, ('gx', 'gy'), route)]
    unnamed x14 -> x18, local copies, waits for them, and re-layouts: 2.86 us -> 5.61 us
    ppermute x9, waiting for transfers between devices: 14.1 us -> 16.8 us  [shifted(): lax.ppermute(value, axis, [(source, (source + steps) % count) for source...]
    reshape x3 -> x0, local copies, waits for them, and re-layouts: 2.57 us -> none  [the longest x2 1.88 us: on_device(): value.reshape(tokens, width)]
    ppermute x11, waiting for transfers between devices: 6.52 us -> 4.34 us  [from_partner(): return lax.ppermute(block, axis, route)]
    ppermute x9, starting transfers between devices: 14.1 us -> 12.4 us  [shifted(): lax.ppermute(value, axis, [(source, (source + steps) % count) for source...]
  transfers between devices with their start and end apart: 31 -> 31, of which waited for: 16 -> 18; matrix products, arithmetic and copies ran while one was open for 4% -> 1% of each run, Pallas kernels for 5% -> 6%
where the time goes in v5:
time: 90.5 us; the launch traced here: 90.2 us
  waiting for transfers between devices  42.9 us (47%)
  starting transfers between devices  27.8 us (31%)
  Pallas kernels  12.2 us (13%)
  local copies, waits for them, and re-layouts  6.55 us (7%)
    ppermute x11, waiting for transfers between devices, plane_swap(): return lax.ppermute(value, ('gx', 'gy'), route)  21.8 us
    ppermute x9, waiting for transfers between devices, shifted(): lax.ppermute(value, axis, [(source, (source + steps) % count) for source...  16.8 us
    ppermute x9, starting transfers between devices, shifted(): lax.ppermute(value, axis, [(source, (source + steps) % count) for source...  12.4 us
    pallas_call x12, Pallas kernels, call(): pl.pallas_call(kernel, out_shape=out_shape, in_specs=specs, scratch_shape...  12.2 us
    ppermute x11, starting transfers between devices, plane_swap(): return lax.ppermute(value, ('gx', 'gy'), route)  10.4 us
    unnamed x18, local copies, waits for them, and re-layouts  5.61 us
    ppermute x11, starting transfers between devices, from_partner(): return lax.ppermute(block, axis, route)  4.96 us
    ppermute x11, waiting for transfers between devices, from_partner(): return lax.ppermute(block, axis, route)  4.34 us
  transfers between devices with their start and end apart: 31, of which 18 were waited for; matrix products, arithmetic and copies ran while one was open for 1% of the time, Pallas kernels for 6%

profile of v5, /device:TPU:0, one launch (start us, length us, event | category | flops | bytes accessed | tf_op | source)
XLA Modules:
  0.0 90.2 jit_solution(4646328766613474264)
XLA Ops:
  2.7 3.0 %collective-permute-start.1 = (bf16[128,512]{1,0:T(8,128)(2,1)S(1)}, bf16[128,512]{1,0:T(8,128)(2,1)S(1)}, u32[]{:S(2)}, u32[]{:S(2)}) collective-permute-start(bf16[128,512]{1,0:T(8,128)(2,1)S(1)} %reshape.13.own.f_own), channel_id=1, source_target_pairs={{0,2},{2,0},{4,6},{6,4},{1,3},{3,1},{5,7},{7,5},{8,10},{10,8},{12,... | collective-permute-start | bytes 393224 | tf_op jit(solution)/shard_map/ppermute | solution.py:20
  7.7 0.9 %copy-done = bf16[256,512]{1,0:T(8,128)(2,1)S(1)} copy-done((bf16[256,512]{1,0:T(8,128)(2,1)S(1)}, bf16[256,512]{1,0:T(8,128)(2,1)}, u32[]{:S(2)}) %copy-start) | copy-done | bytes 262168
  8.7 0.9 %copy-done.2 = bf16[256,512]{1,0:T(8,128)(2,1)S(1)} copy-done((bf16[256,512]{1,0:T(8,128)(2,1)S(1)}, bf16[256,512]{1,0:T(8,128)(2,1)}, u32[]{:S(2)}) %copy-start.2) | copy-done | bytes 262168
  9.6 0.9 %copy-done.4 = bf16[256,512]{1,0:T(8,128)(2,1)S(1)} copy-done((bf16[256,512]{1,0:T(8,128)(2,1)S(1)}, bf16[256,512]{1,0:T(8,128)(2,1)}, u32[]{:S(2)}) %copy-start.4) | copy-done | bytes 262168
  12.5 1.8 %collective-permute-done.pair = bf16[128,768]{1,0:T(8,128)(2,1)S(1)} collective-permute-done((bf16[128,768]{1,0:T(8,128)(2,1)S(1)}, bf16[128,768]{1,0:T(8,128)(2,1)S(1)}, u32[]{:S(2)}, u32[]{:S(2)}) %collective-permute-start) | collective-permute-done | bytes 196640 | tf_op jit(solution)/shard_map/ppermute | solution.py:20
  14.3 2.6 %collective-permute-start.11 = (bf16[512,128]{1,0:T(8,128)(2,1)S(1)}, bf16[512,128]{1,0:T(8,128)(2,1)S(1)}, u32[]{:S(2)}, u32[]{:S(2)}) collective-permute-start(bf16[512,128]{1,0:T(8,128)(2,1)S(1)} %get-tuple-element.56.refs_0_), channel_id=1, source_target_pairs={{0,4},{2,6},{4,0},{6,2},{1,5},{3,7},{5,1},{7,3},{8,12},{10,14},{12... | collective-permute-start | bytes 393224 | tf_op jit(solution)/shard_map/ppermute | solution.py:25
  16.9 2.4 %collective-permute-start.10 = (bf16[512,128]{1,0:T(8,128)(2,1)S(1)}, bf16[512,128]{1,0:T(8,128)(2,1)S(1)}, u32[]{:S(2)}, u32[]{:S(2)}) collective-permute-start(bf16[512,128]{1,0:T(8,128)(2,1)S(1)} %get-tuple-element.56.refs_0_), channel_id=1, source_target_pairs={{0,24},{8,0},{16,8},{24,16},{1,25},{9,1},{17,9},{25,17},{2,26},{10... | collective-permute-start | bytes 393224 | tf_op jit(solution)/shard_map/ppermute | solution.py:25
  19.4 0.9 %copy-done.6 = bf16[256,512]{1,0:T(8,128)(2,1)S(1)} copy-done((bf16[256,512]{1,0:T(8,128)(2,1)S(1)}, bf16[256,512]{1,0:T(8,128)(2,1)}, u32[]{:S(2)}) %copy-start.6) | copy-done | bytes 262168
  21.2 2.9 %collective-permute-start.13 = (bf16[512,128]{1,0:T(8,128)(2,1)S(1)}, bf16[512,128]{1,0:T(8,128)(2,1)S(1)}, u32[]{:S(2)}, u32[]{:S(2)}) collective-permute-start(bf16[512,128]{1,0:T(8,128)(2,1)S(1)} %get-tuple-element.59.refs_4_), channel_id=1, source_target_pairs={{0,24},{8,0},{16,8},{24,16},{1,25},{9,1},{17,9},{25,17},{2,26},{10... | collective-permute-start | bytes 393224 | tf_op jit(solution)/shard_map/ppermute | solution.py:25
  24.1 1.3 %collective-permute-start.12 = (bf16[512,128]{1,0:T(8,128)(2,1)S(1)}, bf16[512,128]{1,0:T(8,128)(2,1)S(1)}, u32[]{:S(2)}, u32[]{:S(2)}) collective-permute-start(bf16[512,128]{1,0:T(8,128)(2,1)S(1)} %get-tuple-element.59.refs_4_), channel_id=1, source_target_pairs={{0,8},{8,16},{16,24},{24,0},{1,9},{9,17},{17,25},{25,1},{2,10},{10... | collective-permute-start | bytes 393224 | tf_op jit(solution)/shard_map/ppermute | solution.py:25
  25.4 1.5 %collective-permute-done.9.refs_1_ = bf16[512,128]{1,0:T(8,128)(2,1)S(1)} collective-permute-done((bf16[512,128]{1,0:T(8,128)(2,1)S(1)}, bf16[512,128]{1,0:T(8,128)(2,1)S(1)}, u32[]{:S(2)}, u32[]{:S(2)}) %collective-permute-start.9) | collective-permute-done | bytes 131104 | tf_op jit(solution)/shard_map/ppermute | solution.py:25
  26.9 2.7 %shard_map.114 = (bf16[8,512,512]{2,1,0:T(8,128)(2,1)S(1)}, f32[8,512]{1,0:T(8,128)S(1)}) custom-call(bf16[512,128]{1,0:T(8,128)(2,1)S(1)} %get-tuple-element.49.q_ref, bf16[512,128]{1,0:T(8,128)(2,1)S(1)} %get-tuple-element.56.refs_0_, bf16[512,128]{1,0:T(8,128)(2,1)S(1)} %collective-permute-done.9.refs_1_, ...), custom_call_target="tpu_custom_call" | custom-call | flops 536870912 | bytes 4194304 | tf_op jit(solution)/shard_map/pallas_call | solution.py:55
  29.9 2.0 %collective-permute-done.12.refs_5_ = bf16[512,128]{1,0:T(8,128)(2,1)S(1)} collective-permute-done((bf16[512,128]{1,0:T(8,128)(2,1)S(1)}, bf16[512,128]{1,0:T(8,128)(2,1)S(1)}, u32[]{:S(2)}, u32[]{:S(2)}) %collective-permute-start.12) | collective-permute-done | bytes 131104 | tf_op jit(solution)/shard_map/ppermute | solution.py:25
  31.9 4.8 %shard_map.115 = (bf16[512,128]{1,0:T(8,128)(2,1)S(1)}, bf16[512,256]{1,0:T(8,128)(2,1)S(1)}, bf16[512,256]{1,0:T(8,128)(2,1)S(1)}, bf16[512,256]{1,0:T(8,128)(2,1)S(1)}, bf16[512,256]{1,0:T(8,128)(2,1)S(1)}) custom-call(bf16[512,128]{1,0:T(8,128)(2,1)S(1)} %get-tuple-element.49.q_ref, bf16[512,128]{1,0:T(8,128)(2,1)S(1)} %get-tuple-element.54.do_ref, ...), custom_call_target="tpu_custom_call" | custom-call | flops 2147483648 | bytes 4194304 | tf_op jit(solution)/shard_map/pallas_call | solution.py:55
  36.7 1.5 %collective-permute-start.15 = (bf16[512,256]{1,0:T(8,128)(2,1)S(1)}, bf16[512,256]{1,0:T(8,128)(2,1)S(1)}, u32[]{:S(2)}, u32[]{:S(2)}) collective-permute-start(bf16[512,256]{1,0:T(8,128)(2,1)S(1)} %get-tuple-element.62), channel_id=1, source_target_pairs={{0,24},{8,0},{16,8},{24,16},{1,25},{9,1},{17,9},{25,17},{2,26},{10... | collective-permute-start | bytes 786440 | tf_op jit(solution)/shard_map/ppermute | solution.py:25
  39.5 6.5 %collective-permute-done.15.refs_1_ = bf16[512,256]{1,0:T(8,128)(2,1)S(1)} collective-permute-done((bf16[512,256]{1,0:T(8,128)(2,1)S(1)}, bf16[512,256]{1,0:T(8,128)(2,1)S(1)}, u32[]{:S(2)}, u32[]{:S(2)}) %collective-permute-start.15) | collective-permute-done | bytes 262176 | tf_op jit(solution)/shard_map/ppermute | solution.py:25
  46.0 4.0 %collective-permute-done.16.refs_2_ = bf16[512,256]{1,0:T(8,128)(2,1)S(1)} collective-permute-done((bf16[512,256]{1,0:T(8,128)(2,1)S(1)}, bf16[512,256]{1,0:T(8,128)(2,1)S(1)}, u32[]{:S(2)}, u32[]{:S(2)}) %collective-permute-start.16) | collective-permute-done | bytes 262176 | tf_op jit(solution)/shard_map/ppermute | solution.py:25
  50.0 2.4 %collective-permute-done.17.refs_3_ = bf16[512,256]{1,0:T(8,128)(2,1)S(1)} collective-permute-done((bf16[512,256]{1,0:T(8,128)(2,1)S(1)}, bf16[512,256]{1,0:T(8,128)(2,1)S(1)}, u32[]{:S(2)}, u32[]{:S(2)}) %collective-permute-start.17) | collective-permute-done | bytes 262176 | tf_op jit(solution)/shard_map/ppermute | solution.py:25
  52.7 1.7 %collective-permute-done.18.core = bf16[512,384]{1,0:T(8,128)(2,1)S(1)} collective-permute-done((bf16[512,384]{1,0:T(8,128)(2,1)S(1)}, bf16[512,384]{1,0:T(8,128)(2,1)S(1)}, u32[]{:S(2)}, u32[]{:S(2)}) %collective-permute-start.18) | collective-permute-done | bytes 393248 | tf_op jit(solution)/shard_map/ppermute | solution.py:20
  55.0 2.4 %collective-permute-start.19 = (bf16[64,1024]{1,0:T(8,128)(2,1)S(1)}, bf16[64,1024]{1,0:T(8,128)(2,1)S(1)}, u32[]{:S(2)}, u32[]{:S(2)}) collective-permute-start(bf16[64,1024]{1,0:T(8,128)(2,1)S(1)} %get-tuple-element.68), channel_id=1, source_target_pairs={{0,8},{2,10},{4,12},{6,14},{8,0},{10,2},{12,4},{14,6},{16,24},{18,... | collective-permute-start | bytes 393224 | tf_op jit(solution)/shard_map/ppermute | solution.py:34
  58.0 1.0 %collective-permute-start.21 = (bf16[64,1024]{1,0:T(8,128)(2,1)S(1)}, bf16[64,1024]{1,0:T(8,128)(2,1)S(1)}, u32[]{:S(2)}, u32[]{:S(2)}) collective-permute-start(bf16[64,1024]{1,0:T(8,128)(2,1)S(1)} %get-tuple-element.70), channel_id=1, source_target_pairs={{0,24},{2,26},{4,28},{6,30},{8,16},{10,18},{12,20},{14,22},{16,8},... | collective-permute-start | bytes 393224 | tf_op jit(solution)/shard_map/ppermute | solution.py:34
  59.0 2.4 %collective-permute-done.19.refs_1_ = bf16[64,1024]{1,0:T(8,128)(2,1)S(1)} collective-permute-done((bf16[64,1024]{1,0:T(8,128)(2,1)S(1)}, bf16[64,1024]{1,0:T(8,128)(2,1)S(1)}, u32[]{:S(2)}, u32[]{:S(2)}) %collective-permute-start.19) | collective-permute-done | bytes 131104 | tf_op jit(solution)/shard_map/ppermute | solution.py:34
  61.4 4.2 %collective-permute-done.20.refs_2_ = bf16[64,1024]{1,0:T(8,128)(2,1)S(1)} collective-permute-done((bf16[64,1024]{1,0:T(8,128)(2,1)S(1)}, bf16[64,1024]{1,0:T(8,128)(2,1)S(1)}, u32[]{:S(2)}, u32[]{:S(2)}) %collective-permute-start.20) | collective-permute-done | bytes 131104 | tf_op jit(solution)/shard_map/ppermute | solution.py:34
  65.6 1.5 %collective-permute-start.23 = (bf16[64,1024]{1,0:T(8,128)(2,1)S(1)}, bf16[64,1024]{1,0:T(8,128)(2,1)S(1)}, u32[]{:S(2)}, u32[]{:S(2)}) collective-permute-start(bf16[64,1024]{1,0:T(8,128)(2,1)S(1)} %shard_map.118.refs_0_), channel_id=1, source_target_pairs={{0,4},{2,6},{4,0},{6,2},{8,12},{10,14},{12,8},{14,10},{16,20},{18,... | collective-permute-start | bytes 393224 | tf_op jit(solution)/shard_map/ppermute | solution.py:34
  67.1 1.3 %shard_map.119 = bf16[8,4,4,512]{3,2,1,0:T(4,128)(2,1)} custom-call(bf16[128,768]{1,0:T(8,128)(2,1)S(1)} %get-tuple-element.73.mine, bf16[128,768]{1,0:T(8,128)(2,1)S(1)} %collective-permute-done.22.pair, bf16[256,512]{1,0:T(8,128)(2,1)S(1)} %copy-done.1, bf16[256,512]{1,0:T(8,128)(2,1)S(1)} %collective-permute-done.3.wq1, bf16[256,512]{1,0:T(8,128)(2,1)S(1)} %copy-done.3, ...), custom_call_target="tpu_custom_call" | custom-call | flops 201326592 | bytes 1000000 | tf_op jit(solution)/shard_map/pallas_call | solution.py:55
  68.4 4.8 %collective-permute-done.23.refs_1_ = bf16[64,1024]{1,0:T(8,128)(2,1)S(1)} collective-permute-done((bf16[64,1024]{1,0:T(8,128)(2,1)S(1)}, bf16[64,1024]{1,0:T(8,128)(2,1)S(1)}, u32[]{:S(2)}, u32[]{:S(2)}) %collective-permute-start.23) | collective-permute-done | bytes 131104 | tf_op jit(solution)/shard_map/ppermute | solution.py:34
  73.8 2.1 %collective-permute-start.25 = (bf16[64,1024]{1,0:T(8,128)(2,1)S(1)}, bf16[64,1024]{1,0:T(8,128)(2,1)S(1)}, u32[]{:S(2)}, u32[]{:S(2)}) collective-permute-start(bf16[64,1024]{1,0:T(8,128)(2,1)S(1)} %shard_map.120.refs_0_), channel_id=1, source_target_pairs={{0,8},{2,10},{4,12},{6,14},{8,0},{10,2},{12,4},{14,6},{16,24},{18,... | collective-permute-start | bytes 393224 | tf_op jit(solution)/shard_map/ppermute | solution.py:34
  75.9 2.4 %collective-permute-done.27.refs_4_ = bf16[64,1024]{1,0:T(8,128)(2,1)S(1)} collective-permute-done((bf16[64,1024]{1,0:T(8,128)(2,1)S(1)}, bf16[64,1024]{1,0:T(8,128)(2,1)S(1)}, u32[]{:S(2)}, u32[]{:S(2)}) %collective-permute-start.27) | collective-permute-done | bytes 131104 | tf_op jit(solution)/shard_map/ppermute | solution.py:34
  78.3 1.1 %collective-permute-start.29 = (bf16[64,1024]{1,0:T(8,128)(2,1)S(1)}, bf16[64,1024]{1,0:T(8,128)(2,1)S(1)}, u32[]{:S(2)}, u32[]{:S(2)}) collective-permute-start(bf16[64,1024]{1,0:T(8,128)(2,1)S(1)} %collective-permute-done.27.refs_4_), channel_id=1, source_target_pairs={{0,8},{2,10},{4,12},{6,14},{8,0},{10,2},{12,4},{14,6},{16,24},{18,... | collective-permute-start | bytes 393224 | tf_op jit(solution)/shard_map/ppermute | solution.py:34
  79.4 2.5 %collective-permute-done.24.refs_1_ = bf16[64,1024]{1,0:T(8,128)(2,1)S(1)} collective-permute-done((bf16[64,1024]{1,0:T(8,128)(2,1)S(1)}, bf16[64,1024]{1,0:T(8,128)(2,1)S(1)}, u32[]{:S(2)}, u32[]{:S(2)}) %collective-permute-start.24) | collective-permute-done | bytes 131104 | tf_op jit(solution)/shard_map/ppermute | solution.py:34
  84.4 3.6 %collective-permute-done.30.refs_7_ = bf16[64,1024]{1,0:T(8,128)(2,1)S(1)} collective-permute-done((bf16[64,1024]{1,0:T(8,128)(2,1)S(1)}, bf16[64,1024]{1,0:T(8,128)(2,1)S(1)}, u32[]{:S(2)}, u32[]{:S(2)}) %collective-permute-start.30) | collective-permute-done | bytes 131104 | tf_op jit(solution)/shard_map/ppermute | solution.py:34
  88.7 1.5 %shard_map.121 = (f32[256,512]{1,0:T(8,128)}, f32[256,512]{1,0:T(8,128)}, f32[256,512]{1,0:T(8,128)}, f32[256,512]{1,0:T(8,128)}) custom-call(bf16[64,1024]{1,0:T(8,128)(2,1)S(1)} %shard_map.120.refs_0_, bf16[64,1024]{1,0:T(8,128)(2,1)S(1)} %collective-permute-done.24.refs_1_, bf16[64,1024]{1,0:T(8,128)(2,1)S(1)} %collective-permute-done.25.refs_2_, ...), custom_call_target="tpu_custom_call" | custom-call | flops 1000000 | bytes 1000000 | tf_op jit(solution)/shard_map/pallas_call | solution.py:55
  (61 shorter events, 13.7 us)
Async XLA Ops:
  0.6 7.0 %collective-permute-start.3 = (bf16[256,512]{1,0:T(8,128)(2,1)}, bf16[256,512]{1,0:T(8,128)(2,1)S(1)}, u32[]{:S(2)}, u32[]{:S(2)}) collective-permute-start(bf16[256,512]{1,0:T(8,128)(2,1)} %wq0.3), channel_id=1, source_target_pairs={{0,1},{1,0},{2,3},{3,2},{4,5},{5,4},{6,7},{7,6},{8,9},{9,8},{10,11... | collective-permute-start | bytes 786440 | tf_op jit(solution)/shard_map/ppermute | solution.py:20
  1.1 6.6 %collective-permute-start.4 = (bf16[256,512]{1,0:T(8,128)(2,1)}, bf16[256,512]{1,0:T(8,128)(2,1)S(1)}, u32[]{:S(2)}, u32[]{:S(2)}) collective-permute-start(bf16[256,512]{1,0:T(8,128)(2,1)} %wk0.3), channel_id=1, source_target_pairs={{0,1},{1,0},{2,3},{3,2},{4,5},{5,4},{6,7},{7,6},{8,9},{9,8},{10,11... | collective-permute-start | bytes 786440 | tf_op jit(solution)/shard_map/ppermute | solution.py:20
  1.2 6.5 %collective-permute-start.5 = (bf16[256,512]{1,0:T(8,128)(2,1)}, bf16[256,512]{1,0:T(8,128)(2,1)S(1)}, u32[]{:S(2)}, u32[]{:S(2)}) collective-permute-start(bf16[256,512]{1,0:T(8,128)(2,1)} %wv0.3), channel_id=1, source_target_pairs={{0,1},{1,0},{2,3},{3,2},{4,5},{5,4},{6,7},{7,6},{8,9},{9,8},{10,11... | collective-permute-start | bytes 786440 | tf_op jit(solution)/shard_map/ppermute | solution.py:20
  2.6 8.1 %collective-permute-start.2 = (bf16[128,512]{1,0:T(8,128)(2,1)S(1)}, bf16[128,512]{1,0:T(8,128)(2,1)S(1)}, u32[]{:S(2)}, u32[]{:S(2)}) collective-permute-start(bf16[128,512]{1,0:T(8,128)(2,1)S(1)} %reshape.13.own.f_own), channel_id=1, source_target_pairs={{0,1},{1,0},{2,3},{3,2},{4,5},{5,4},{6,7},{7,6},{8,9},{9,8},{10,11... | collective-permute-start | bytes 393224 | tf_op jit(solution)/shard_map/ppermute | solution.py:20
  2.7 7.9 %collective-permute-start.1 = (bf16[128,512]{1,0:T(8,128)(2,1)S(1)}, bf16[128,512]{1,0:T(8,128)(2,1)S(1)}, u32[]{:S(2)}, u32[]{:S(2)}) collective-permute-start(bf16[128,512]{1,0:T(8,128)(2,1)S(1)} %reshape.13.own.f_own), channel_id=1, source_target_pairs={{0,2},{2,0},{4,6},{6,4},{1,3},{3,1},{5,7},{7,5},{8,10},{10,8},{12,... | collective-permute-start | bytes 393224 | tf_op jit(solution)/shard_map/ppermute | solution.py:20
  7.6 6.7 %collective-permute-start = (bf16[128,768]{1,0:T(8,128)(2,1)S(1)}, bf16[128,768]{1,0:T(8,128)(2,1)S(1)}, u32[]{:S(2)}, u32[]{:S(2)}) collective-permute-start(bf16[128,768]{1,0:T(8,128)(2,1)S(1)} %get-tuple-element.43), channel_id=1, source_target_pairs={{0,2},{2,0},{4,6},{6,4},{1,3},{3,1},{5,7},{7,5},{8,10},{10,8},{12,... | collective-permute-start | bytes 589832 | tf_op jit(solution)/shard_map/ppermute | solution.py:20
  10.7 1.4 %collective-permute-start.6 = (bf16[128,512]{1,0:T(8,128)(2,1)S(1)}, bf16[128,512]{1,0:T(8,128)(2,1)S(1)}, u32[]{:S(2)}, u32[]{:S(2)}) collective-permute-start(bf16[128,512]{1,0:T(8,128)(2,1)S(1)} %collective-permute-done.1.pair.f_pair), channel_id=1, source_target_pairs={{0,1},{1,0},{2,3},{3,2},{4,5},{5,4},{6,7},{7,6},{8,9},{9,8},{10,11... | collective-permute-start | bytes 393224 | tf_op jit(solution)/shard_map/ppermute | solution.py:20
  10.8 8.6 %collective-permute-start.7 = (bf16[128,768]{1,0:T(8,128)(2,1)S(1)}, bf16[128,768]{1,0:T(8,128)(2,1)S(1)}, u32[]{:S(2)}, u32[]{:S(2)}) collective-permute-start(bf16[128,768]{1,0:T(8,128)(2,1)S(1)} %get-tuple-element.51.own), channel_id=1, source_target_pairs={{0,1},{1,0},{2,3},{3,2},{4,5},{5,4},{6,7},{7,6},{8,9},{9,8},{10,11... | collective-permute-start | bytes 589832 | tf_op jit(solution)/shard_map/ppermute | solution.py:20
  14.3 5.0 %collective-permute-start.8 = (bf16[128,768]{1,0:T(8,128)(2,1)S(1)}, bf16[128,768]{1,0:T(8,128)(2,1)S(1)}, u32[]{:S(2)}, u32[]{:S(2)}) collective-permute-start(bf16[128,768]{1,0:T(8,128)(2,1)S(1)} %collective-permute-done.pair), channel_id=1, source_target_pairs={{0,1},{1,0},{2,3},{3,2},{4,5},{5,4},{6,7},{7,6},{8,9},{9,8},{10,11... | collective-permute-start | bytes 589832 | tf_op jit(solution)/shard_map/ppermute | solution.py:20
  14.3 9.8 %collective-permute-start.11 = (bf16[512,128]{1,0:T(8,128)(2,1)S(1)}, bf16[512,128]{1,0:T(8,128)(2,1)S(1)}, u32[]{:S(2)}, u32[]{:S(2)}) collective-permute-start(bf16[512,128]{1,0:T(8,128)(2,1)S(1)} %get-tuple-element.56.refs_0_), channel_id=1, source_target_pairs={{0,4},{2,6},{4,0},{6,2},{1,5},{3,7},{5,1},{7,3},{8,12},{10,14},{12... | collective-permute-start | bytes 393224 | tf_op jit(solution)/shard_map/ppermute | solution.py:25
  16.9 8.5 %collective-permute-start.10 = (bf16[512,128]{1,0:T(8,128)(2,1)S(1)}, bf16[512,128]{1,0:T(8,128)(2,1)S(1)}, u32[]{:S(2)}, u32[]{:S(2)}) collective-permute-start(bf16[512,128]{1,0:T(8,128)(2,1)S(1)} %get-tuple-element.56.refs_0_), channel_id=1, source_target_pairs={{0,24},{8,0},{16,8},{24,16},{1,25},{9,1},{17,9},{25,17},{2,26},{10... | collective-permute-start | bytes 393224 | tf_op jit(solution)/shard_map/ppermute | solution.py:25
  19.4 7.6 %collective-permute-start.9 = (bf16[512,128]{1,0:T(8,128)(2,1)S(1)}, bf16[512,128]{1,0:T(8,128)(2,1)S(1)}, u32[]{:S(2)}, u32[]{:S(2)}) collective-permute-start(bf16[512,128]{1,0:T(8,128)(2,1)S(1)} %get-tuple-element.56.refs_0_), channel_id=1, source_target_pairs={{0,8},{8,16},{16,24},{24,0},{1,9},{9,17},{17,25},{25,1},{2,10},{10... | collective-permute-start | bytes 393224 | tf_op jit(solution)/shard_map/ppermute | solution.py:25
  20.8 9.1 %collective-permute-start.14 = (bf16[512,128]{1,0:T(8,128)(2,1)S(1)}, bf16[512,128]{1,0:T(8,128)(2,1)S(1)}, u32[]{:S(2)}, u32[]{:S(2)}) collective-permute-start(bf16[512,128]{1,0:T(8,128)(2,1)S(1)} %get-tuple-element.59.refs_4_), channel_id=1, source_target_pairs={{0,4},{2,6},{4,0},{6,2},{1,5},{3,7},{5,1},{7,3},{8,12},{10,14},{12... | collective-permute-start | bytes 393224 | tf_op jit(solution)/shard_map/ppermute | solution.py:25
  21.2 8.7 %collective-permute-start.13 = (bf16[512,128]{1,0:T(8,128)(2,1)S(1)}, bf16[512,128]{1,0:T(8,128)(2,1)S(1)}, u32[]{:S(2)}, u32[]{:S(2)}) collective-permute-start(bf16[512,128]{1,0:T(8,128)(2,1)S(1)} %get-tuple-element.59.refs_4_), channel_id=1, source_target_pairs={{0,24},{8,0},{16,8},{24,16},{1,25},{9,1},{17,9},{25,17},{2,26},{10... | collective-permute-start | bytes 393224 | tf_op jit(solution)/shard_map/ppermute | solution.py:25
  24.1 7.8 %collective-permute-start.12 = (bf16[512,128]{1,0:T(8,128)(2,1)S(1)}, bf16[512,128]{1,0:T(8,128)(2,1)S(1)}, u32[]{:S(2)}, u32[]{:S(2)}) collective-permute-start(bf16[512,128]{1,0:T(8,128)(2,1)S(1)} %get-tuple-element.59.refs_4_), channel_id=1, source_target_pairs={{0,8},{8,16},{16,24},{24,0},{1,9},{9,17},{17,25},{25,1},{2,10},{10... | collective-permute-start | bytes 393224 | tf_op jit(solution)/shard_map/ppermute | solution.py:25
  31.9 35.2 %copy-start.5 = (bf16[256,512]{1,0:T(8,128)(2,1)S(1)}, bf16[256,512]{1,0:T(8,128)(2,1)}, u32[]{:S(2)}) copy-start(bf16[256,512]{1,0:T(8,128)(2,1)} %wv0.3) | copy-start | bytes 786436
  36.7 9.3 %collective-permute-start.15 = (bf16[512,256]{1,0:T(8,128)(2,1)S(1)}, bf16[512,256]{1,0:T(8,128)(2,1)S(1)}, u32[]{:S(2)}, u32[]{:S(2)}) collective-permute-start(bf16[512,256]{1,0:T(8,128)(2,1)S(1)} %get-tuple-element.62), channel_id=1, source_target_pairs={{0,24},{8,0},{16,8},{24,16},{1,25},{9,1},{17,9},{25,17},{2,26},{10... | collective-permute-start | bytes 786440 | tf_op jit(solution)/shard_map/ppermute | solution.py:25
  38.2 11.8 %collective-permute-start.16 = (bf16[512,256]{1,0:T(8,128)(2,1)S(1)}, bf16[512,256]{1,0:T(8,128)(2,1)S(1)}, u32[]{:S(2)}, u32[]{:S(2)}) collective-permute-start(bf16[512,256]{1,0:T(8,128)(2,1)S(1)} %get-tuple-element.63), channel_id=1, source_target_pairs={{0,8},{8,16},{16,24},{24,0},{1,9},{9,17},{17,25},{25,1},{2,10},{10... | collective-permute-start | bytes 786440 | tf_op jit(solution)/shard_map/ppermute | solution.py:25
  38.8 13.6 %collective-permute-start.17 = (bf16[512,256]{1,0:T(8,128)(2,1)S(1)}, bf16[512,256]{1,0:T(8,128)(2,1)S(1)}, u32[]{:S(2)}, u32[]{:S(2)}) collective-permute-start(bf16[512,256]{1,0:T(8,128)(2,1)S(1)} %get-tuple-element.64), channel_id=1, source_target_pairs={{0,4},{2,6},{4,0},{6,2},{1,5},{3,7},{5,1},{7,3},{8,12},{10,14},{12... | collective-permute-start | bytes 786440 | tf_op jit(solution)/shard_map/ppermute | solution.py:25
  52.6 1.8 %collective-permute-start.18 = (bf16[512,384]{1,0:T(8,128)(2,1)S(1)}, bf16[512,384]{1,0:T(8,128)(2,1)S(1)}, u32[]{:S(2)}, u32[]{:S(2)}) collective-permute-start(bf16[512,384]{1,0:T(8,128)(2,1)S(1)} %shard_map.116.own), channel_id=1, source_target_pairs={{0,1},{1,0},{2,3},{3,2},{4,5},{5,4},{6,7},{7,6},{8,9},{9,8},{10,11... | collective-permute-start | bytes 1179656 | tf_op jit(solution)/shard_map/ppermute | solution.py:20
  55.0 10.6 %collective-permute-start.22 = (bf16[128,768]{1,0:T(8,128)(2,1)S(1)}, bf16[128,768]{1,0:T(8,128)(2,1)S(1)}, u32[]{:S(2)}, u32[]{:S(2)}) collective-permute-start(bf16[128,768]{1,0:T(8,128)(2,1)S(1)} %get-tuple-element.71), channel_id=1, source_target_pairs={{0,2},{2,0},{4,6},{6,4},{1,3},{3,1},{5,7},{7,5},{8,10},{10,8},{12,... | collective-permute-start | bytes 589832 | tf_op jit(solution)/shard_map/ppermute | solution.py:20
  55.0 6.3 %collective-permute-start.19 = (bf16[64,1024]{1,0:T(8,128)(2,1)S(1)}, bf16[64,1024]{1,0:T(8,128)(2,1)S(1)}, u32[]{:S(2)}, u32[]{:S(2)}) collective-permute-start(bf16[64,1024]{1,0:T(8,128)(2,1)S(1)} %get-tuple-element.68), channel_id=1, source_target_pairs={{0,8},{2,10},{4,12},{6,14},{8,0},{10,2},{12,4},{14,6},{16,24},{18,... | collective-permute-start | bytes 393224 | tf_op jit(solution)/shard_map/ppermute | solution.py:34
  57.5 8.1 %collective-permute-start.20 = (bf16[64,1024]{1,0:T(8,128)(2,1)S(1)}, bf16[64,1024]{1,0:T(8,128)(2,1)S(1)}, u32[]{:S(2)}, u32[]{:S(2)}) collective-permute-start(bf16[64,1024]{1,0:T(8,128)(2,1)S(1)} %get-tuple-element.69), channel_id=1, source_target_pairs={{0,16},{2,18},{4,20},{6,22},{8,24},{10,26},{12,28},{14,30},{16,0},... | collective-permute-start | bytes 393224 | tf_op jit(solution)/shard_map/ppermute | solution.py:34
  58.0 7.6 %collective-permute-start.21 = (bf16[64,1024]{1,0:T(8,128)(2,1)S(1)}, bf16[64,1024]{1,0:T(8,128)(2,1)S(1)}, u32[]{:S(2)}, u32[]{:S(2)}) collective-permute-start(bf16[64,1024]{1,0:T(8,128)(2,1)S(1)} %get-tuple-element.70), channel_id=1, source_target_pairs={{0,24},{2,26},{4,28},{6,30},{8,16},{10,18},{12,20},{14,22},{16,8},... | collective-permute-start | bytes 393224 | tf_op jit(solution)/shard_map/ppermute | solution.py:34
  65.6 7.6 %collective-permute-start.23 = (bf16[64,1024]{1,0:T(8,128)(2,1)S(1)}, bf16[64,1024]{1,0:T(8,128)(2,1)S(1)}, u32[]{:S(2)}, u32[]{:S(2)}) collective-permute-start(bf16[64,1024]{1,0:T(8,128)(2,1)S(1)} %shard_map.118.refs_0_), channel_id=1, source_target_pairs={{0,4},{2,6},{4,0},{6,2},{8,12},{10,14},{12,8},{14,10},{16,20},{18,... | collective-permute-start | bytes 393224 | tf_op jit(solution)/shard_map/ppermute | solution.py:34
  73.3 5.0 %collective-permute-start.27 = (bf16[64,1024]{1,0:T(8,128)(2,1)S(1)}, bf16[64,1024]{1,0:T(8,128)(2,1)S(1)}, u32[]{:S(2)}, u32[]{:S(2)}) collective-permute-start(bf16[64,1024]{1,0:T(8,128)(2,1)S(1)} %shard_map.120.refs_0_), channel_id=1, source_target_pairs={{0,16},{2,18},{4,20},{6,22},{8,24},{10,26},{12,28},{14,30},{16,0},... | collective-permute-start | bytes 393224 | tf_op jit(solution)/shard_map/ppermute | solution.py:34
  73.8 5.6 %collective-permute-start.25 = (bf16[64,1024]{1,0:T(8,128)(2,1)S(1)}, bf16[64,1024]{1,0:T(8,128)(2,1)S(1)}, u32[]{:S(2)}, u32[]{:S(2)}) collective-permute-start(bf16[64,1024]{1,0:T(8,128)(2,1)S(1)} %shard_map.120.refs_0_), channel_id=1, source_target_pairs={{0,8},{2,10},{4,12},{6,14},{8,0},{10,2},{12,4},{14,6},{16,24},{18,... | collective-permute-start | bytes 393224 | tf_op jit(solution)/shard_map/ppermute | solution.py:34
  75.9 6.1 %collective-permute-start.24 = (bf16[64,1024]{1,0:T(8,128)(2,1)S(1)}, bf16[64,1024]{1,0:T(8,128)(2,1)S(1)}, u32[]{:S(2)}, u32[]{:S(2)}) collective-permute-start(bf16[64,1024]{1,0:T(8,128)(2,1)S(1)} %shard_map.120.refs_0_), channel_id=1, source_target_pairs={{0,2},{2,0},{4,6},{6,4},{8,10},{10,8},{12,14},{14,12},{16,18},{18,... | collective-permute-start | bytes 393224 | tf_op jit(solution)/shard_map/ppermute | solution.py:34
  78.3 5.8 %collective-permute-start.29 = (bf16[64,1024]{1,0:T(8,128)(2,1)S(1)}, bf16[64,1024]{1,0:T(8,128)(2,1)S(1)}, u32[]{:S(2)}, u32[]{:S(2)}) collective-permute-start(bf16[64,1024]{1,0:T(8,128)(2,1)S(1)} %collective-permute-done.27.refs_4_), channel_id=1, source_target_pairs={{0,8},{2,10},{4,12},{6,14},{8,0},{10,2},{12,4},{14,6},{16,24},{18,... | collective-permute-start | bytes 393224 | tf_op jit(solution)/shard_map/ppermute | solution.py:34
  79.4 5.0 %collective-permute-start.26 = (bf16[64,1024]{1,0:T(8,128)(2,1)S(1)}, bf16[64,1024]{1,0:T(8,128)(2,1)S(1)}, u32[]{:S(2)}, u32[]{:S(2)}) collective-permute-start(bf16[64,1024]{1,0:T(8,128)(2,1)S(1)} %collective-permute-done.25.refs_2_), channel_id=1, source_target_pairs={{0,2},{2,0},{4,6},{6,4},{8,10},{10,8},{12,14},{14,12},{16,18},{18,... | collective-permute-start | bytes 393224 | tf_op jit(solution)/shard_map/ppermute | solution.py:34
  82.0 6.0 %collective-permute-start.30 = (bf16[64,1024]{1,0:T(8,128)(2,1)S(1)}, bf16[64,1024]{1,0:T(8,128)(2,1)S(1)}, u32[]{:S(2)}, u32[]{:S(2)}) collective-permute-start(bf16[64,1024]{1,0:T(8,128)(2,1)S(1)} %collective-permute-done.24.refs_1_), channel_id=1, source_target_pairs={{0,24},{2,26},{4,28},{6,30},{8,16},{10,18},{12,20},{14,22},{16,8},... | collective-permute-start | bytes 393224 | tf_op jit(solution)/shard_map/ppermute | solution.py:34
  82.3 6.4 %collective-permute-start.28 = (bf16[64,1024]{1,0:T(8,128)(2,1)S(1)}, bf16[64,1024]{1,0:T(8,128)(2,1)S(1)}, u32[]{:S(2)}, u32[]{:S(2)}) collective-permute-start(bf16[64,1024]{1,0:T(8,128)(2,1)S(1)} %collective-permute-done.24.refs_1_), channel_id=1, source_target_pairs={{0,16},{2,18},{4,20},{6,22},{8,24},{10,26},{12,28},{14,30},{16,0},... | collective-permute-start | bytes 393224 | tf_op jit(solution)/shard_map/ppermute | solution.py:34
  (8 other events, 75.9 us)

commit v6 on v5

--- a/solution.py
+++ b/solution.py
@@ -129,11 +129,10 @@
     products = (out_grad.astype(F32) * saved[...].astype(F32)).T
     delta_ref[0:1, :] = jnp.sum(products[0:head_dim], axis=0, keepdims=True)
     delta_ref[1:2, :] = jnp.sum(products[head_dim:PART], axis=0, keepdims=True)
+    y_bit = lax.axis_index("gy") % 2
     out = dot_nn(saved[...].astype(F32).T.astype(BF), dys[...]).astype(BF)
-    for at in range(4):
-        low = out[at * 32 : (at + 1) * 32, :]
-        o_ref[at * 64 : at * 64 + 32, :] = low[:, 0:half]
-        o_ref[at * 64 + 32 : at * 64 + 64, :] = low[:, half:]
+    o_ref[pl.ds(pl.multiple_of(y_bit * PART, PART), PART), :] = out
+    o_ref[pl.ds(pl.multiple_of((1 - y_bit) * PART, PART), PART), :] = jnp.zeros_like(out)
 
 
 def by_head(value):
@@ -234,14 +233,12 @@
             ]
 
 
-def weight_kernel(chunks, own, core, feat_t, o_ref, pair_ref, mine_ref, *refs):
+def weight_kernel(chunks, own, core, feat_t, pair_ref, mine_ref, *refs):
     outs, (grads, made) = refs[:chunks], refs[chunks:]
     place_grads(grads, own, core, 3)
     mine_ref[...] = grads[0:PART, :]
     pair_ref[...] = grads[2 * PART : 3 * PART, :]
-    wide = grads.shape[1]
-    made[:, 0:wide] = dot_nn(feat_t[...], grads[...]).astype(BF)
-    made[:, wide:] = o_ref[...]
+    made[...] = dot_nn(feat_t[...], grads[...]).astype(BF)
     rows = made.shape[0] // chunks
     for at in range(chunks):
         spot = pl.ds(0, rows)
@@ -279,7 +276,7 @@
 
 
 def spread_kernel(*refs):
-    pieces, outs = refs[:8], refs[8:]
+    pieces, out_sum, outs = refs[:8], refs[8], refs[9:]
     half = 2 * PART
     rows = pieces[0].shape[0]
     for at, piece in enumerate(pieces):
@@ -290,9 +287,7 @@
             for side in range(2):
                 source = slice((base * 2 + side) * PART, (base * 2 + side + 1) * PART)
                 out[spot, columns(side * half + bit * PART)] = piece[:, source].astype(F32)
-        spot = pl.ds(pl.multiple_of(bit * PART + place * (rows // 2), rows // 2), rows // 2)
-        outs[3][spot, 0:half] = piece[0 : rows // 2, 3 * half :].astype(F32)
-        outs[3][spot, half:] = piece[rows // 2 :, 3 * half :].astype(F32)
+    outs[3][...] = out_sum[...].astype(F32)
 
 
 def on_device(features, grad_y, attn_out, w_query, w_key, w_value, w_out):
@@ -370,7 +365,7 @@
             column,
             shape_of((2, block_tokens), F32),
             shape_of((half, block_tokens)),
-            shape_of((half, half)),
+            shape_of((half, width)),
         ),
         [*feats, own, core, pair, far, out_rows],
         scratch=[pltpu.VMEM((block_tokens, PART), BF), pltpu.VMEM((block_tokens, width), BF)],
@@ -400,6 +395,11 @@
         flops=8 * pixels * PART,
         moved=2 * pixels,
     )
+    planned = count_x == 4 and count_y == 4 and count_z == 2
+    plane = ("gx", "gy")
+    if planned:
+        out_sum = lax.psum_scatter(out_term, plane, scatter_dimension=0, tiled=True)
+        partials, out_sum = lax.optimization_barrier((partials, out_sum))
     back = [partials[0]]
     for partial, (axis, step) in zip(partials[1:], routes):
         back.append(shifted(partial, axis, -step))
@@ -407,14 +407,13 @@
         functools.partial(collect_kernel, times), shape_of((block_tokens, 3 * PART)), [dq, *back]
     )
     core_grads = from_partner(grads, "gz")
-    planned = count_x == 4 and count_y == 4 and count_z == 2
     chunks = 4 if planned else 1
-    piece = shape_of((half // chunks, 8 * PART))
+    piece = shape_of((half // chunks, 6 * PART))
     pair_out, mine, *pieces = call(
         functools.partial(weight_kernel, chunks),
         (shape_of((tokens, 6 * PART)), shape_of((tokens, 6 * PART)), *[piece] * chunks),
-        [grads, core_grads, feat_t, out_term],
-        scratch=[pltpu.VMEM((block_tokens, 6 * PART), BF), pltpu.VMEM((half, 8 * PART), BF)],
+        [grads, core_grads, feat_t],
+        scratch=[pltpu.VMEM((block_tokens, 6 * PART), BF), pltpu.VMEM((half, 6 * PART), BF)],
         flops=2 * block_tokens * half * 6 * PART,
     )
     def features_grad(pair_rows):
@@ -427,10 +426,11 @@
         )
 
     if planned:
+        out_sum = lax.all_gather(out_sum, plane, axis=0, tiled=True)
         terms = [pieces[0]] + [plane_swap(pieces[at], at, 0) for at in (1, 2, 3)]
         total = call(sum_kernel, piece, terms)
         pair_in = from_partner(pair_out, "gy")
-        total, pair_in = lax.optimization_barrier((total, pair_in))
+        total, pair_in, out_sum = lax.optimization_barrier((total, pair_in, out_sum))
         other = plane_swap(total, 0, 2)
         grad_x = features_grad(pair_in)
         total, grad_x = lax.optimization_barrier((total, grad_x))
@@ -441,7 +441,7 @@
         weights = call(
             spread_kernel,
             tuple([shape_of((half, width), F32)] * 4),
-            [total, by_z, by_x, by_xz, by_y, by_yz, by_xy, by_xyz],
+            [total, by_z, by_x, by_xz, by_y, by_yz, by_xy, by_xyz, out_sum],
         )
     else:
         grad_x = features_grad(from_partner(pair_out, "gy"))
@@ -453,10 +453,8 @@
                 stacked = lax.dynamic_update_slice(
                     stacked, tile[None], (at, z_bit * half, side * half + y_bit * PART)
                 )
-        tile = terms[:, 6 * PART :].reshape(4, 2, 32, half)
-        tile = tile.transpose(0, 2, 1, 3).reshape(PART, width)
         stacked = lax.dynamic_update_slice(
-            stacked, tile[None], (3, z_bit * half + y_bit * PART, 0)
+            stacked, out_term.astype(F32)[None], (3, z_bit * half, 0)
         )
         stacked = lax.psum(stacked, ("gx", "gy", "gz"))
         held_rows = w_query.shape[0]

time: 90.5 us -> 187 us (2.07)
  waiting for transfers between devices: 42.9 us -> 85.2 us
  blocking collectives: 0 us -> 42.3 us
  between operations: 0.81 us -> 14.2 us
  starting transfers between devices: 27.8 us -> 25.6 us
    reduce_scatter x0 -> x1, waiting for transfers between devices: none -> 53.6 us  [on_device(): out_sum = lax.psum_scatter(out_term, plane, scatter_dimension=0, tiled=True)]
    all_gather x0 -> x1, blocking collectives: none -> 42.3 us  [on_device(): out_sum = lax.all_gather(out_sum, plane, axis=0, tiled=True)]
    ppermute x11, waiting for transfers between devices: 21.8 us -> 11.9 us  [plane_swap(): return lax.ppermute(value, ('gx', 'gy'), route)]
    ppermute x9, waiting for transfers between devices: 16.8 us -> 13.8 us  [shifted(): lax.ppermute(value, axis, [(source, (source + steps) % count) for source...]
  transfers between devices with their start and end apart: 31 -> 32, of which waited for: 18 -> 15; matrix products, arithmetic and copies ran while one was open for 1% -> 1% of each run, Pallas kernels for 6% -> 5%
where the time goes in v6:
time: 187 us
  waiting for transfers between devices  85.2 us (46%)
  blocking collectives  42.3 us (23%)
  starting transfers between devices  25.6 us (14%)
  between operations  14.2 us (8%)
  Pallas kernels  12.7 us (7%)
  local copies, waits for them, and re-layouts  6.55 us (4%)
    reduce_scatter x1, waiting for transfers between devices, on_device(): out_sum = lax.psum_scatter(out_term, plane, scatter_dimension=0, tiled=True)  53.6 us
    all_gather x1, blocking collectives, on_device(): out_sum = lax.all_gather(out_sum, plane, axis=0, tiled=True)  42.3 us
    ppermute x9, waiting for transfers between devices, shifted(): lax.ppermute(value, axis, [(source, (source + steps) % count) for source...  13.8 us
    pallas_call x12, Pallas kernels, call(): pl.pallas_call(kernel, out_shape=out_shape, in_specs=specs, scratch_shape...  12.7 us
    ppermute x11, waiting for transfers between devices, plane_swap(): return lax.ppermute(value, ('gx', 'gy'), route)  11.9 us
    ppermute x9, starting transfers between devices, shifted(): lax.ppermute(value, axis, [(source, (source + steps) % count) for source...  11.9 us
    ppermute x11, starting transfers between devices, plane_swap(): return lax.ppermute(value, ('gx', 'gy'), route)  8.73 us
    ppermute x11, waiting for transfers between devices, from_partner(): return lax.ppermute(block, axis, route)  5.78 us
  transfers between devices with their start and end apart: 32, of which 15 were waited for; matrix products, arithmetic and copies ran while one was open for 1% of the time, Pallas kernels for 5%

profile of v6, /device:TPU:0, one launch (start us, length us, event | category | flops | bytes accessed | tf_op | source)
XLA Modules:
  0.0 186.6 jit_solution(802116667414531898)
XLA Ops:
  9.3 3.0 %collective-permute-start.1 = (bf16[128,512]{1,0:T(8,128)(2,1)S(1)}, bf16[128,512]{1,0:T(8,128)(2,1)S(1)}, u32[]{:S(2)}, u32[]{:S(2)}) collective-permute-start(bf16[128,512]{1,0:T(8,128)(2,1)S(1)} %reshape.13.own.f_own), channel_id=1, source_target_pairs={{0,2},{2,0},{4,6},{6,4},{1,3},{3,1},{5,7},{7,5},{8,10},{10,8},{12,... | collective-permute-start | bytes 393224 | tf_op jit(solution)/shard_map/ppermute | solution.py:20
  15.3 0.9 copy-done.2
  19.1 1.8 collective-permute-done.pair
  20.9 1.4 collective-permute-done.8.far
  22.3 0.9 copy-done.6
  23.3 1.1 shard_map.113
  24.4 2.7 %collective-permute-start.11 = (bf16[512,128]{1,0:T(8,128)(2,1)S(1)}, bf16[512,128]{1,0:T(8,128)(2,1)S(1)}, u32[]{:S(2)}, u32[]{:S(2)}) collective-permute-start(bf16[512,128]{1,0:T(8,128)(2,1)S(1)} %get-tuple-element.62.refs_0_), channel_id=1, source_target_pairs={{0,4},{2,6},{4,0},{6,2},{1,5},{3,7},{5,1},{7,3},{8,12},{10,14},{12... | collective-permute-start | bytes 393224 | tf_op jit(solution)/shard_map/ppermute | solution.py:25
  27.1 2.4 %collective-permute-start.10 = (bf16[512,128]{1,0:T(8,128)(2,1)S(1)}, bf16[512,128]{1,0:T(8,128)(2,1)S(1)}, u32[]{:S(2)}, u32[]{:S(2)}) collective-permute-start(bf16[512,128]{1,0:T(8,128)(2,1)S(1)} %get-tuple-element.62.refs_0_), channel_id=1, source_target_pairs={{0,24},{8,0},{16,8},{24,16},{1,25},{9,1},{17,9},{25,17},{2,26},{10... | collective-permute-start | bytes 393224 | tf_op jit(solution)/shard_map/ppermute | solution.py:25
  29.8 2.9 %collective-permute-start.13 = (bf16[512,128]{1,0:T(8,128)(2,1)S(1)}, bf16[512,128]{1,0:T(8,128)(2,1)S(1)}, u32[]{:S(2)}, u32[]{:S(2)}) collective-permute-start(bf16[512,128]{1,0:T(8,128)(2,1)S(1)} %get-tuple-element.65.refs_4_), channel_id=1, source_target_pairs={{0,24},{8,0},{16,8},{24,16},{1,25},{9,1},{17,9},{25,17},{2,26},{10... | collective-permute-start | bytes 393224 | tf_op jit(solution)/shard_map/ppermute | solution.py:25
  32.8 4.8 %collective-permute-done.11.refs_3_ = bf16[512,128]{1,0:T(8,128)(2,1)S(1)} collective-permute-done((bf16[512,128]{1,0:T(8,128)(2,1)S(1)}, bf16[512,128]{1,0:T(8,128)(2,1)S(1)}, u32[]{:S(2)}, u32[]{:S(2)}) %collective-permute-start.11) | collective-permute-done | bytes 131104 | tf_op jit(solution)/shard_map/ppermute | solution.py:25
  37.6 1.5 collective-permute-start.12
  39.1 2.6 %shard_map.114 = (bf16[8,512,512]{2,1,0:T(8,128)(2,1)S(1)}, f32[8,512]{1,0:T(8,128)S(1)}) custom-call(bf16[512,128]{1,0:T(8,128)(2,1)S(1)} %get-tuple-element.55.q_ref, bf16[512,128]{1,0:T(8,128)(2,1)S(1)} %get-tuple-element.62.refs_0_, bf16[512,128]{1,0:T(8,128)(2,1)S(1)} %collective-permute-done.9.refs_1_, ...), custom_call_target="tpu_custom_call" | custom-call | flops 536870912 | bytes 4194304 | tf_op jit(solution)/shard_map/pallas_call | solution.py:55
  41.7 1.7 collective-permute-done.12.refs_5_
  43.4 4.8 %shard_map.115 = (bf16[512,128]{1,0:T(8,128)(2,1)S(1)}, bf16[512,256]{1,0:T(8,128)(2,1)S(1)}, bf16[512,256]{1,0:T(8,128)(2,1)S(1)}, bf16[512,256]{1,0:T(8,128)(2,1)S(1)}, bf16[512,256]{1,0:T(8,128)(2,1)S(1)}) custom-call(bf16[512,128]{1,0:T(8,128)(2,1)S(1)} %get-tuple-element.55.q_ref, bf16[512,128]{1,0:T(8,128)(2,1)S(1)} %get-tuple-element.60.do_ref, ...), custom_call_target="tpu_custom_call" | custom-call | flops 2147483648 | bytes 4194304 | tf_op jit(solution)/shard_map/pallas_call | solution.py:55
  48.2 53.6 %reduce-scatter.2.cloned.1.call-done = bf16[16,512]{1,0:T(8,128)(2,1)} async-done(((bf16[256,512]{1,0:T(8,128)(2,1)}), bf16[16,512]{1,0:T(8,128)(2,1)}) %reduce-scatter.2.cloned.1.call-update) | async-done | bytes 16400 | tf_op jit(solution)/shard_map/reduce_scatter | solution.py:401
  101.8 2.0 %collective-permute-start.16 = (bf16[512,256]{1,0:T(8,128)(2,1)S(1)}, bf16[512,256]{1,0:T(8,128)(2,1)S(1)}, u32[]{:S(2)}, u32[]{:S(2)}) collective-permute-start(bf16[512,256]{1,0:T(8,128)(2,1)S(1)} %get-tuple-element.74), channel_id=1, source_target_pairs={{0,8},{8,16},{16,24},{24,0},{1,9},{9,17},{17,25},{25,1},{2,10},{10... | collective-permute-start | bytes 786440 | tf_op jit(solution)/shard_map/ppermute | solution.py:25
  103.9 4.3 %collective-permute-done.15.refs_1_ = bf16[512,256]{1,0:T(8,128)(2,1)S(1)} collective-permute-done((bf16[512,256]{1,0:T(8,128)(2,1)S(1)}, bf16[512,256]{1,0:T(8,128)(2,1)S(1)}, u32[]{:S(2)}, u32[]{:S(2)}) %collective-permute-start.15) | collective-permute-done | bytes 262176 | tf_op jit(solution)/shard_map/ppermute | solution.py:25
  108.2 3.0 %collective-permute-done.16.refs_2_ = bf16[512,256]{1,0:T(8,128)(2,1)S(1)} collective-permute-done((bf16[512,256]{1,0:T(8,128)(2,1)S(1)}, bf16[512,256]{1,0:T(8,128)(2,1)S(1)}, u32[]{:S(2)}, u32[]{:S(2)}) %collective-permute-start.16) | collective-permute-done | bytes 262176 | tf_op jit(solution)/shard_map/ppermute | solution.py:25
  111.4 1.7 collective-permute-done.18.core
  113.8 2.0 %collective-permute-start.19 = (bf16[64,768]{1,0:T(8,128)(2,1)S(1)}, bf16[64,768]{1,0:T(8,128)(2,1)S(1)}, u32[]{:S(2)}, u32[]{:S(2)}) collective-permute-start(bf16[64,768]{1,0:T(8,128)(2,1)S(1)} %get-tuple-element.78), channel_id=1, source_target_pairs={{0,8},{2,10},{4,12},{6,14},{8,0},{10,2},{12,4},{14,6},{16,24},{18,... | collective-permute-start | bytes 294920 | tf_op jit(solution)/shard_map/ppermute | solution.py:34
  116.4 1.0 collective-permute-start.21
  117.4 42.3 %all_gather.3.refs_8_ = bf16[256,512]{1,0:T(8,128)(2,1)S(1)} all-gather(bf16[16,512]{1,0:T(8,128)(2,1)} %reduce-scatter.2.cloned.1.call-done), channel_id=1, replica_groups=mesh['gx'=4,'gy'=4,'gz'=2] {'gx','gy'}, dimensions={0}, use_global_device_ids=true | all-gather | bytes 278528 | tf_op jit(solution)/shard_map/all_gather | solution.py:429
  159.9 1.3 shard_map.119
  161.2 4.2 %collective-permute-done.23.refs_1_ = bf16[64,768]{1,0:T(8,128)(2,1)S(1)} collective-permute-done((bf16[64,768]{1,0:T(8,128)(2,1)S(1)}, bf16[64,768]{1,0:T(8,128)(2,1)S(1)}, u32[]{:S(2)}, u32[]{:S(2)}) %collective-permute-start.23) | collective-permute-done | bytes 98336 | tf_op jit(solution)/shard_map/ppermute | solution.py:34
  165.5 1.6 collective-permute-start.27
  167.1 3.1 %collective-permute-done.27.refs_4_ = bf16[64,768]{1,0:T(8,128)(2,1)S(1)} collective-permute-done((bf16[64,768]{1,0:T(8,128)(2,1)S(1)}, bf16[64,768]{1,0:T(8,128)(2,1)S(1)}, u32[]{:S(2)}, u32[]{:S(2)}) %collective-permute-start.27) | collective-permute-done | bytes 98336 | tf_op jit(solution)/shard_map/ppermute | solution.py:34
  170.2 1.5 collective-permute-done.25.refs_2_
  171.7 2.0 %collective-permute-start.30 = (bf16[64,768]{1,0:T(8,128)(2,1)S(1)}, bf16[64,768]{1,0:T(8,128)(2,1)S(1)}, u32[]{:S(2)}, u32[]{:S(2)}) collective-permute-start(bf16[64,768]{1,0:T(8,128)(2,1)S(1)} %collective-permute-done.24.refs_1_), channel_id=1, source_target_pairs={{0,24},{2,26},{4,28},{6,30},{8,16},{10,18},{12,20},{14,22},{16,8},... | collective-permute-start | bytes 294920 | tf_op jit(solution)/shard_map/ppermute | solution.py:34
  173.6 1.5 collective-permute-start.28
  175.2 1.1 collective-permute-done.26.refs_3_
  177.2 1.1 collective-permute-done.28.refs_5_
  178.3 1.5 shard_map.121
  (65 shorter events, 10.8 us)
Async XLA Ops:
  7.2 94.7 %reduce-scatter.2.cloned.1.call-start = ((), (), s32[]{:S(2)}) async-start(), calls=%async_computation.1 | async-start | bytes 278528 | tf_op jit(solution)/shard_map/reduce_scatter | solution.py:401
  7.2 7.0 %collective-permute-start.3 = (bf16[256,512]{1,0:T(8,128)(2,1)}, bf16[256,512]{1,0:T(8,128)(2,1)S(1)}, u32[]{:S(2)}, u32[]{:S(2)}) collective-permute-start(bf16[256,512]{1,0:T(8,128)(2,1)} %wq0.3), channel_id=1, source_target_pairs={{0,1},{1,0},{2,3},{3,2},{4,5},{5,4},{6,7},{7,6},{8,9},{9,8},{10,11... | collective-permute-start | bytes 786440 | tf_op jit(solution)/shard_map/ppermute | solution.py:20
  7.7 6.6 %collective-permute-start.4 = (bf16[256,512]{1,0:T(8,128)(2,1)}, bf16[256,512]{1,0:T(8,128)(2,1)S(1)}, u32[]{:S(2)}, u32[]{:S(2)}) collective-permute-start(bf16[256,512]{1,0:T(8,128)(2,1)} %wk0.3), channel_id=1, source_target_pairs={{0,1},{1,0},{2,3},{3,2},{4,5},{5,4},{6,7},{7,6},{8,9},{9,8},{10,11... | collective-permute-start | bytes 786440 | tf_op jit(solution)/shard_map/ppermute | solution.py:20
  7.8 6.5 %collective-permute-start.5 = (bf16[256,512]{1,0:T(8,128)(2,1)}, bf16[256,512]{1,0:T(8,128)(2,1)S(1)}, u32[]{:S(2)}, u32[]{:S(2)}) collective-permute-start(bf16[256,512]{1,0:T(8,128)(2,1)} %wv0.3), channel_id=1, source_target_pairs={{0,1},{1,0},{2,3},{3,2},{4,5},{5,4},{6,7},{7,6},{8,9},{9,8},{10,11... | collective-permute-start | bytes 786440 | tf_op jit(solution)/shard_map/ppermute | solution.py:20
  9.2 8.1 %collective-permute-start.2 = (bf16[128,512]{1,0:T(8,128)(2,1)S(1)}, bf16[128,512]{1,0:T(8,128)(2,1)S(1)}, u32[]{:S(2)}, u32[]{:S(2)}) collective-permute-start(bf16[128,512]{1,0:T(8,128)(2,1)S(1)} %reshape.13.own.f_own), channel_id=1, source_target_pairs={{0,1},{1,0},{2,3},{3,2},{4,5},{5,4},{6,7},{7,6},{8,9},{9,8},{10,11... | collective-permute-start | bytes 393224 | tf_op jit(solution)/shard_map/ppermute | solution.py:20
  9.3 7.9 %collective-permute-start.1 = (bf16[128,512]{1,0:T(8,128)(2,1)S(1)}, bf16[128,512]{1,0:T(8,128)(2,1)S(1)}, u32[]{:S(2)}, u32[]{:S(2)}) collective-permute-start(bf16[128,512]{1,0:T(8,128)(2,1)S(1)} %reshape.13.own.f_own), channel_id=1, source_target_pairs={{0,2},{2,0},{4,6},{6,4},{1,3},{3,1},{5,7},{7,5},{8,10},{10,8},{12,... | collective-permute-start | bytes 393224 | tf_op jit(solution)/shard_map/ppermute | solution.py:20
  14.2 6.7 %collective-permute-start = (bf16[128,768]{1,0:T(8,128)(2,1)S(1)}, bf16[128,768]{1,0:T(8,128)(2,1)S(1)}, u32[]{:S(2)}, u32[]{:S(2)}) collective-permute-start(bf16[128,768]{1,0:T(8,128)(2,1)S(1)} %get-tuple-element.49), channel_id=1, source_target_pairs={{0,2},{2,0},{4,6},{6,4},{1,3},{3,1},{5,7},{7,5},{8,10},{10,8},{12,... | collective-permute-start | bytes 589832 | tf_op jit(solution)/shard_map/ppermute | solution.py:20
  17.3 1.4 collective-permute-start.6
  17.3 3.6 %collective-permute-start.7 = (bf16[128,768]{1,0:T(8,128)(2,1)S(1)}, bf16[128,768]{1,0:T(8,128)(2,1)S(1)}, u32[]{:S(2)}, u32[]{:S(2)}) collective-permute-start(bf16[128,768]{1,0:T(8,128)(2,1)S(1)} %get-tuple-element.57.own), channel_id=1, source_target_pairs={{0,1},{1,0},{2,3},{3,2},{4,5},{5,4},{6,7},{7,6},{8,9},{9,8},{10,11... | collective-permute-start | bytes 589832 | tf_op jit(solution)/shard_map/ppermute | solution.py:20
  20.9 1.4 collective-permute-start.8
  24.4 13.2 %collective-permute-start.11 = (bf16[512,128]{1,0:T(8,128)(2,1)S(1)}, bf16[512,128]{1,0:T(8,128)(2,1)S(1)}, u32[]{:S(2)}, u32[]{:S(2)}) collective-permute-start(bf16[512,128]{1,0:T(8,128)(2,1)S(1)} %get-tuple-element.62.refs_0_), channel_id=1, source_target_pairs={{0,4},{2,6},{4,0},{6,2},{1,5},{3,7},{5,1},{7,3},{8,12},{10,14},{12... | collective-permute-start | bytes 393224 | tf_op jit(solution)/shard_map/ppermute | solution.py:25
  27.1 12.0 %collective-permute-start.10 = (bf16[512,128]{1,0:T(8,128)(2,1)S(1)}, bf16[512,128]{1,0:T(8,128)(2,1)S(1)}, u32[]{:S(2)}, u32[]{:S(2)}) collective-permute-start(bf16[512,128]{1,0:T(8,128)(2,1)S(1)} %get-tuple-element.62.refs_0_), channel_id=1, source_target_pairs={{0,24},{8,0},{16,8},{24,16},{1,25},{9,1},{17,9},{25,17},{2,26},{10... | collective-permute-start | bytes 393224 | tf_op jit(solution)/shard_map/ppermute | solution.py:25
  29.5 9.5 %collective-permute-start.9 = (bf16[512,128]{1,0:T(8,128)(2,1)S(1)}, bf16[512,128]{1,0:T(8,128)(2,1)S(1)}, u32[]{:S(2)}, u32[]{:S(2)}) collective-permute-start(bf16[512,128]{1,0:T(8,128)(2,1)S(1)} %get-tuple-element.62.refs_0_), channel_id=1, source_target_pairs={{0,8},{8,16},{16,24},{24,0},{1,9},{9,17},{17,25},{25,1},{2,10},{10... | collective-permute-start | bytes 393224 | tf_op jit(solution)/shard_map/ppermute | solution.py:25
  29.5 12.2 %collective-permute-start.14 = (bf16[512,128]{1,0:T(8,128)(2,1)S(1)}, bf16[512,128]{1,0:T(8,128)(2,1)S(1)}, u32[]{:S(2)}, u32[]{:S(2)}) collective-permute-start(bf16[512,128]{1,0:T(8,128)(2,1)S(1)} %get-tuple-element.65.refs_4_), channel_id=1, source_target_pairs={{0,4},{2,6},{4,0},{6,2},{1,5},{3,7},{5,1},{7,3},{8,12},{10,14},{12... | collective-permute-start | bytes 393224 | tf_op jit(solution)/shard_map/ppermute | solution.py:25
  29.8 11.9 %collective-permute-start.13 = (bf16[512,128]{1,0:T(8,128)(2,1)S(1)}, bf16[512,128]{1,0:T(8,128)(2,1)S(1)}, u32[]{:S(2)}, u32[]{:S(2)}) collective-permute-start(bf16[512,128]{1,0:T(8,128)(2,1)S(1)} %get-tuple-element.65.refs_4_), channel_id=1, source_target_pairs={{0,24},{8,0},{16,8},{24,16},{1,25},{9,1},{17,9},{25,17},{2,26},{10... | collective-permute-start | bytes 393224 | tf_op jit(solution)/shard_map/ppermute | solution.py:25
  37.6 5.9 %collective-permute-start.12 = (bf16[512,128]{1,0:T(8,128)(2,1)S(1)}, bf16[512,128]{1,0:T(8,128)(2,1)S(1)}, u32[]{:S(2)}, u32[]{:S(2)}) collective-permute-start(bf16[512,128]{1,0:T(8,128)(2,1)S(1)} %get-tuple-element.65.refs_4_), channel_id=1, source_target_pairs={{0,8},{8,16},{16,24},{24,0},{1,9},{9,17},{17,25},{25,1},{2,10},{10... | collective-permute-start | bytes 393224 | tf_op jit(solution)/shard_map/ppermute | solution.py:25
  101.8 6.4 %collective-permute-start.15 = (bf16[512,256]{1,0:T(8,128)(2,1)S(1)}, bf16[512,256]{1,0:T(8,128)(2,1)S(1)}, u32[]{:S(2)}, u32[]{:S(2)}) collective-permute-start(bf16[512,256]{1,0:T(8,128)(2,1)S(1)} %get-tuple-element.73), channel_id=1, source_target_pairs={{0,24},{8,0},{16,8},{24,16},{1,25},{9,1},{17,9},{25,17},{2,26},{10... | collective-permute-start | bytes 786440 | tf_op jit(solution)/shard_map/ppermute | solution.py:25
  101.8 9.3 %collective-permute-start.16 = (bf16[512,256]{1,0:T(8,128)(2,1)S(1)}, bf16[512,256]{1,0:T(8,128)(2,1)S(1)}, u32[]{:S(2)}, u32[]{:S(2)}) collective-permute-start(bf16[512,256]{1,0:T(8,128)(2,1)S(1)} %get-tuple-element.74), channel_id=1, source_target_pairs={{0,8},{8,16},{16,24},{24,0},{1,9},{9,17},{17,25},{25,1},{2,10},{10... | collective-permute-start | bytes 786440 | tf_op jit(solution)/shard_map/ppermute | solution.py:25
  103.9 7.3 %collective-permute-start.17 = (bf16[512,256]{1,0:T(8,128)(2,1)S(1)}, bf16[512,256]{1,0:T(8,128)(2,1)S(1)}, u32[]{:S(2)}, u32[]{:S(2)}) collective-permute-start(bf16[512,256]{1,0:T(8,128)(2,1)S(1)} %get-tuple-element.75), channel_id=1, source_target_pairs={{0,4},{2,6},{4,0},{6,2},{1,5},{3,7},{5,1},{7,3},{8,12},{10,14},{12... | collective-permute-start | bytes 786440 | tf_op jit(solution)/shard_map/ppermute | solution.py:25
  111.4 1.8 collective-permute-start.18
  113.7 46.0 %collective-permute-start.22 = (bf16[128,768]{1,0:T(8,128)(2,1)S(1)}, bf16[128,768]{1,0:T(8,128)(2,1)S(1)}, u32[]{:S(2)}, u32[]{:S(2)}) collective-permute-start(bf16[128,768]{1,0:T(8,128)(2,1)S(1)} %get-tuple-element.81), channel_id=1, source_target_pairs={{0,2},{2,0},{4,6},{6,4},{1,3},{3,1},{5,7},{7,5},{8,10},{10,8},{12,... | collective-permute-start | bytes 589832 | tf_op jit(solution)/shard_map/ppermute | solution.py:20
  113.8 45.9 %collective-permute-start.19 = (bf16[64,768]{1,0:T(8,128)(2,1)S(1)}, bf16[64,768]{1,0:T(8,128)(2,1)S(1)}, u32[]{:S(2)}, u32[]{:S(2)}) collective-permute-start(bf16[64,768]{1,0:T(8,128)(2,1)S(1)} %get-tuple-element.78), channel_id=1, source_target_pairs={{0,8},{2,10},{4,12},{6,14},{8,0},{10,2},{12,4},{14,6},{16,24},{18,... | collective-permute-start | bytes 294920 | tf_op jit(solution)/shard_map/ppermute | solution.py:34
  115.8 43.8 %collective-permute-start.20 = (bf16[64,768]{1,0:T(8,128)(2,1)S(1)}, bf16[64,768]{1,0:T(8,128)(2,1)S(1)}, u32[]{:S(2)}, u32[]{:S(2)}) collective-permute-start(bf16[64,768]{1,0:T(8,128)(2,1)S(1)} %get-tuple-element.79), channel_id=1, source_target_pairs={{0,16},{2,18},{4,20},{6,22},{8,24},{10,26},{12,28},{14,30},{16,0},... | collective-permute-start | bytes 294920 | tf_op jit(solution)/shard_map/ppermute | solution.py:34
  116.4 43.3 %collective-permute-start.21 = (bf16[64,768]{1,0:T(8,128)(2,1)S(1)}, bf16[64,768]{1,0:T(8,128)(2,1)S(1)}, u32[]{:S(2)}, u32[]{:S(2)}) collective-permute-start(bf16[64,768]{1,0:T(8,128)(2,1)S(1)} %get-tuple-element.80), channel_id=1, source_target_pairs={{0,24},{2,26},{4,28},{6,30},{8,16},{10,18},{12,20},{14,22},{16,8},... | collective-permute-start | bytes 294920 | tf_op jit(solution)/shard_map/ppermute | solution.py:34
  159.8 5.7 %collective-permute-start.23 = (bf16[64,768]{1,0:T(8,128)(2,1)S(1)}, bf16[64,768]{1,0:T(8,128)(2,1)S(1)}, u32[]{:S(2)}, u32[]{:S(2)}) collective-permute-start(bf16[64,768]{1,0:T(8,128)(2,1)S(1)} %shard_map.118.refs_0_), channel_id=1, source_target_pairs={{0,4},{2,6},{4,0},{6,2},{8,12},{10,14},{12,8},{14,10},{16,20},{18,... | collective-permute-start | bytes 294920 | tf_op jit(solution)/shard_map/ppermute | solution.py:34
  165.5 4.7 %collective-permute-start.27 = (bf16[64,768]{1,0:T(8,128)(2,1)S(1)}, bf16[64,768]{1,0:T(8,128)(2,1)S(1)}, u32[]{:S(2)}, u32[]{:S(2)}) collective-permute-start(bf16[64,768]{1,0:T(8,128)(2,1)S(1)} %shard_map.120.refs_0_), channel_id=1, source_target_pairs={{0,16},{2,18},{4,20},{6,22},{8,24},{10,26},{12,28},{14,30},{16,0},... | collective-permute-start | bytes 294920 | tf_op jit(solution)/shard_map/ppermute | solution.py:34
  167.1 4.6 %collective-permute-start.25 = (bf16[64,768]{1,0:T(8,128)(2,1)S(1)}, bf16[64,768]{1,0:T(8,128)(2,1)S(1)}, u32[]{:S(2)}, u32[]{:S(2)}) collective-permute-start(bf16[64,768]{1,0:T(8,128)(2,1)S(1)} %shard_map.120.refs_0_), channel_id=1, source_target_pairs={{0,8},{2,10},{4,12},{6,14},{8,0},{10,2},{12,4},{14,6},{16,24},{18,... | collective-permute-start | bytes 294920 | tf_op jit(solution)/shard_map/ppermute | solution.py:34
  167.1 4.6 %collective-permute-start.24 = (bf16[64,768]{1,0:T(8,128)(2,1)S(1)}, bf16[64,768]{1,0:T(8,128)(2,1)S(1)}, u32[]{:S(2)}, u32[]{:S(2)}) collective-permute-start(bf16[64,768]{1,0:T(8,128)(2,1)S(1)} %shard_map.120.refs_0_), channel_id=1, source_target_pairs={{0,2},{2,0},{4,6},{6,4},{8,10},{10,8},{12,14},{14,12},{16,18},{18,... | collective-permute-start | bytes 294920 | tf_op jit(solution)/shard_map/ppermute | solution.py:34
  170.2 5.0 %collective-permute-start.29 = (bf16[64,768]{1,0:T(8,128)(2,1)S(1)}, bf16[64,768]{1,0:T(8,128)(2,1)S(1)}, u32[]{:S(2)}, u32[]{:S(2)}) collective-permute-start(bf16[64,768]{1,0:T(8,128)(2,1)S(1)} %collective-permute-done.27.refs_4_), channel_id=1, source_target_pairs={{0,8},{2,10},{4,12},{6,14},{8,0},{10,2},{12,4},{14,6},{16,24},{18,... | collective-permute-start | bytes 294920 | tf_op jit(solution)/shard_map/ppermute | solution.py:34
  171.7 4.6 %collective-permute-start.26 = (bf16[64,768]{1,0:T(8,128)(2,1)S(1)}, bf16[64,768]{1,0:T(8,128)(2,1)S(1)}, u32[]{:S(2)}, u32[]{:S(2)}) collective-permute-start(bf16[64,768]{1,0:T(8,128)(2,1)S(1)} %collective-permute-done.25.refs_2_), channel_id=1, source_target_pairs={{0,2},{2,0},{4,6},{6,4},{8,10},{10,8},{12,14},{14,12},{16,18},{18,... | collective-permute-start | bytes 294920 | tf_op jit(solution)/shard_map/ppermute | solution.py:34
  171.7 5.5 %collective-permute-start.30 = (bf16[64,768]{1,0:T(8,128)(2,1)S(1)}, bf16[64,768]{1,0:T(8,128)(2,1)S(1)}, u32[]{:S(2)}, u32[]{:S(2)}) collective-permute-start(bf16[64,768]{1,0:T(8,128)(2,1)S(1)} %collective-permute-done.24.refs_1_), channel_id=1, source_target_pairs={{0,24},{2,26},{4,28},{6,30},{8,16},{10,18},{12,20},{14,22},{16,8},... | collective-permute-start | bytes 294920 | tf_op jit(solution)/shard_map/ppermute | solution.py:34
  173.6 4.6 %collective-permute-start.28 = (bf16[64,768]{1,0:T(8,128)(2,1)S(1)}, bf16[64,768]{1,0:T(8,128)(2,1)S(1)}, u32[]{:S(2)}, u32[]{:S(2)}) collective-permute-start(bf16[64,768]{1,0:T(8,128)(2,1)S(1)} %collective-permute-done.24.refs_1_), channel_id=1, source_target_pairs={{0,16},{2,18},{4,20},{6,22},{8,24},{10,26},{12,28},{14,30},{16,0},... | collective-permute-start | bytes 294920 | tf_op jit(solution)/shard_map/ppermute | solution.py:34
  (9 other events, 354.8 us)
Sparse Core Ops, SparseCore 0:
  24.5 77.2 reduce-scatter.1

commit v7 on v5

--- a/solution.py
+++ b/solution.py
@@ -96,14 +96,13 @@
         w_cols[pl.ds(pl.multiple_of((1 - half) * half_rows, half_rows), half_rows), spot] = second[:, group]
 
 
-def project_kernel(own, core, pair, far, w_cols, q_ref, k_ref, v_ref):
+def project_kernel(own, core, pair, far, w_cols, q_ref, kv_ref):
     width = own.shape[1]
     for at, source in enumerate((own, core, pair, far)):
         rows = slice(at * PART, (at + 1) * PART)
         made = dot_nn(source[...], w_cols[...])
         q_ref[rows, :] = made[:, 0:PART].astype(BF) * jnp.asarray(1.0 / math.sqrt(width // HEADS), BF)
-        k_ref[rows, :] = made[:, PART : 2 * PART].astype(BF)
-        v_ref[rows, :] = made[:, 2 * PART :].astype(BF)
+        kv_ref[rows, :] = made[:, PART:].astype(BF)
 
 
 def early_kernel(
@@ -147,66 +146,73 @@
     return jnp.where(low, table[:, 2 * at : 2 * at + 1], table[:, 2 * at + 1 : 2 * at + 2])
 
 
-def score_kernel(times, q_ref, *refs):
-    count = len(times)
-    keys_in = refs[:count]
-    e_ref, part_ref, top_s, total_s = refs[count:]
+def score_kernel(q_ref, *refs):
+    count = len(refs) - 2
+    e_ref, table_ref = refs[count:]
+    half = table_ref.shape[0] // 2
     q_heads = by_head(q_ref[...])
+    if half > 2 * count:
+        table_ref[...] = jnp.zeros_like(table_ref)
     for at in range(count):
-        keys = keys_in[at][...]
+        keys = refs[at][:, 0:PART]
         for head in range(2):
             scores = dot_nt(keys, q_heads[head])
             top = jnp.max(scores, axis=0, keepdims=True)
             grown = jnp.exp(scores - top)
-            e_ref[2 * at + head] = grown.astype(BF)
-            top_s[2 * at + head : 2 * at + head + 1, :] = top
-            total_s[2 * at + head : 2 * at + head + 1, :] = jnp.sum(grown, axis=0, keepdims=True)
+            row = 2 * at + head
+            e_ref[row] = grown.astype(BF)
+            table_ref[row : row + 1, :] = top
+            table_ref[half + row : half + row + 1, :] = jnp.sum(grown, axis=0, keepdims=True)
+
+
+def gradient_kernel(times, groups, q_ref, do_ref, delta_ref, *refs):
+    count = len(times)
+    e_refs, tables = refs[: 2 * len(groups) : 2], refs[1 : 2 * len(groups) : 2]
+    refs = refs[2 * len(groups) :]
+    kvs, dq_ref, outs, dq_s, part_s = (
+        refs[:count], refs[count], refs[count + 1 : 2 * count + 1], refs[-2], refs[-1]
+    )
+    where = [(group, at) for group, blocks in enumerate(groups) for at in range(blocks)]
+    if part_s.shape[0] > 2 * count:
+        part_s[...] = jnp.zeros_like(part_s)
     for head in range(2):
-        tops = [top_s[2 * at + head : 2 * at + head + 1, :] for at in range(count)]
+        tops, totals = [], []
+        for group, at in where:
+            half = tables[group].shape[0] // 2
+            row = 2 * at + head
+            tops.append(tables[group][row : row + 1, :])
+            totals.append(tables[group][half + row : half + row + 1, :])
         most = functools.reduce(jnp.maximum, tops)
         lifts = [jnp.exp(top - most) for top in tops]
         total = functools.reduce(
-            jnp.add,
-            [
-                times[at] * lifts[at] * total_s[2 * at + head : 2 * at + head + 1, :]
-                for at in range(count)
-            ],
+            jnp.add, [time * lift * part for time, lift, part in zip(times, lifts, totals)]
         )
         for at in range(count):
-            part_ref[2 * at + head : 2 * at + head + 1, :] = lifts[at] / total
-    if part_ref.shape[0] > 2 * count:
-        part_ref[2 * count :, :] = jnp.zeros((part_ref.shape[0] - 2 * count, q_ref.shape[0]), F32)
-
-
-def gradient_kernel(times, q_ref, do_ref, delta_ref, e_ref, part_ref, *refs):
-    count = len(times)
-    keys_in, values_in = refs[:count], refs[count : 2 * count]
-    dq_ref = refs[2 * count]
-    outs = refs[2 * count + 1 : 3 * count + 1]
-    dq_s = refs[3 * count + 1]
+            part_s[2 * at + head : 2 * at + head + 1, :] = lifts[at] / total
     tokens = q_ref.shape[0]
     head_dim = PART // 2
-    turned = part_ref[...].T
+    turned = part_s[...].T
     grad = do_ref[...]
     g_heads = by_head(grad)
     grad = grad.astype(F32)
     query = q_ref[...].astype(F32)
     delta = delta_ref[...]
     for at in range(count):
-        keys_t = keys_in[at][...].astype(F32).T.astype(BF)
-        values = values_in[at][...]
+        keys_t = kvs[at][:, 0:PART].astype(F32).T.astype(BF)
+        values = kvs[at][:, PART:]
+        group, place = where[at]
         scale = row_scale(turned, at, tokens)
         q_scaled = by_head((query * scale).astype(BF))
         g_scaled = by_head((grad * scale).astype(BF))
         dks, dvs = [], []
         for head in range(2):
-            grown = e_ref[2 * at + head]
+            grown = e_refs[group][2 * place + head]
             dprob = dot_nt(values, g_heads[head])
             dscore = (grown.astype(F32) * (dprob - delta[head : head + 1, :])).astype(BF)
             dvs.append(dot_nn(grown, g_scaled[head]))
             dks.append(dot_nn(dscore, q_scaled[head]))
             spot = slice(head * head_dim, (head + 1) * head_dim)
-            part = part_ref[2 * at + head : 2 * at + head + 1, :] * times[at]
+            part = part_s[2 * at + head : 2 * at + head + 1, :] * times[at]
             added = dot_nn(keys_t[spot, :], dscore) * part
             dq_s[spot, :] = added if at == 0 else dq_s[spot, :] + added
         outs[at][:, 0:PART] = (dks[0] + dks[1]).astype(BF)
@@ -327,28 +333,17 @@
         shape_of((width, 3 * PART)),
         pairs,
     )
-    pair_message, own = call(
-        pack_kernel,
-        (message, message),
-        [grad_y, attn_out],
-        scratch=[pltpu.VMEM((tokens, width), BF)],
-    )
-    feat_pair, feat_core, w_cols, own = lax.optimization_barrier(
-        (feat_pair, feat_core, w_cols, own)
-    )
-    pair = from_partner(pair_message, "gy")
+    feat_pair, feat_core, w_cols = lax.optimization_barrier((feat_pair, feat_core, w_cols))
     feat_far = from_partner(feat_pair, "gz")
     feats = [feat, feat_core, feat_pair, feat_far]
     column = shape_of((block_tokens, PART))
-    query, own_keys, own_values = call(
+    both = shape_of((block_tokens, 2 * PART))
+    query, own_kv = call(
         project_kernel,
-        (column, column, column),
+        (column, both),
         [*feats, w_cols],
         flops=2 * block_tokens * width * 3 * PART,
     )
-    pair, query = lax.optimization_barrier((pair, query))
-    core = from_partner(own, "gz")
-    far = from_partner(pair, "gz")
 
     times = [1.0]
     routes = []
@@ -363,7 +358,17 @@
             times += [1.0, 1.0]
     times = tuple(times)
     count = len(times)
-    keys = [own_keys] + [shifted(own_keys, axis, step) for axis, step in routes]
+    near = [own_kv] + [shifted(own_kv, axis, step) for axis, step in routes]
+    late_dy, late_saved, query = lax.optimization_barrier((grad_y, attn_out, query))
+    pair_message, own = call(
+        pack_kernel,
+        (message, message),
+        [late_dy, late_saved],
+        scratch=[pltpu.VMEM((tokens, width), BF)],
+    )
+    pair = from_partner(pair_message, "gy")
+    core = from_partner(own, "gz")
+    far = from_partner(pair, "gz")
     out_grad, delta, feat_t, out_term = call(
         early_kernel,
         (
@@ -376,29 +381,34 @@
         scratch=[pltpu.VMEM((block_tokens, PART), BF), pltpu.VMEM((block_tokens, width), BF)],
         flops=4 * block_tokens * width * PART,
     )
-    own_values, out_grad = lax.optimization_barrier((own_values, out_grad))
-    values = [own_values] + [shifted(own_values, axis, step) for axis, step in routes]
-    rows = -(-2 * count // 8) * 8
-    pixels = 2 * count * block_tokens * block_tokens
-    grown, parts = call(
-        functools.partial(score_kernel, times),
-        (
-            shape_of((2 * count, block_tokens, block_tokens)),
-            shape_of((rows, block_tokens), F32),
-        ),
-        [query, *keys],
-        scratch=[pltpu.VMEM((rows, block_tokens), F32), pltpu.VMEM((rows, block_tokens), F32)],
-        flops=2 * pixels * PART,
-        moved=2 * pixels,
-        exps=pixels,
-    )
+    pixels = 2 * block_tokens * block_tokens
+    groups = (2, count - 2)
+    scored = []
+    place = 0
+    for blocks in groups:
+        rows = -(-2 * blocks // 8) * 8
+        scored += call(
+            score_kernel,
+            (
+                shape_of((2 * blocks, block_tokens, block_tokens)),
+                shape_of((2 * rows, block_tokens), F32),
+            ),
+            [query, *near[place : place + blocks]],
+            flops=2 * pixels * blocks * PART,
+            moved=2 * pixels * blocks,
+            exps=pixels * blocks,
+        )
+        place += blocks
     dq, *partials = call(
-        functools.partial(gradient_kernel, times),
-        (column, *[shape_of((block_tokens, 2 * PART))] * count),
-        [query, out_grad, delta, grown, parts, *keys, *values],
-        scratch=[pltpu.VMEM((PART, block_tokens), F32)],
-        flops=8 * pixels * PART,
-        moved=2 * pixels,
+        functools.partial(gradient_kernel, times, groups),
+        (column, *[both] * count),
+        [query, out_grad, delta, *scored, *near],
+        scratch=[
+            pltpu.VMEM((PART, block_tokens), F32),
+            pltpu.VMEM((-(-2 * count // 8) * 8, block_tokens), F32),
+        ],
+        flops=8 * pixels * count * PART,
+        moved=2 * pixels * count,
     )
     back = [partials[0]]
     for partial, (axis, step) in zip(partials[1:], routes):

time: 90.5 us -> 89.6 us (0.990)
  waiting for transfers between devices: 42.9 us -> 46.2 us
  local copies, waits for them, and re-layouts: 6.55 us -> 3.82 us
  starting transfers between devices: 27.8 us -> 26 us
    ppermute x9 -> x6, starting transfers between devices: 12.4 us -> 8.97 us  [shifted(): lax.ppermute(value, axis, [(source, (source + steps) % count) for source...]
    unnamed x18, local copies, waits for them, and re-layouts: 5.61 us -> 2.88 us
    ppermute x11, waiting for transfers between devices: 4.34 us -> 6.14 us  [from_partner(): return lax.ppermute(block, axis, route)]
    ppermute x9 -> x6, waiting for transfers between devices: 16.8 us -> 18.1 us  [shifted(): lax.ppermute(value, axis, [(source, (source + steps) % count) for source...]
    ppermute x11, starting transfers between devices: 4.96 us -> 6.14 us  [from_partner(): return lax.ppermute(block, axis, route)]
    pallas_call x12 -> x13, Pallas kernels: 12.2 us -> 12.5 us  [call(): pl.pallas_call(kernel, out_shape=out_shape, in_specs=specs, scratch_shape...]
  transfers between devices with their start and end apart: 31 -> 28, of which waited for: 18 -> 19; matrix products, arithmetic and copies ran while one was open for 1% -> 1% of each run, Pallas kernels for 6% -> 5%
where the time goes in v7:
time: 89.6 us; the launch traced here: 89.4 us
  waiting for transfers between devices  46.2 us (52%)
  starting transfers between devices  26 us (29%)
  Pallas kernels  12.5 us (14%)
  local copies, waits for them, and re-layouts  3.82 us (4%)
    ppermute x11, waiting for transfers between devices, plane_swap(): return lax.ppermute(value, ('gx', 'gy'), route)  22 us
    ppermute x6, waiting for transfers between devices, shifted(): lax.ppermute(value, axis, [(source, (source + steps) % count) for source...  18.1 us
    pallas_call x13, Pallas kernels, call(): pl.pallas_call(kernel, out_shape=out_shape, in_specs=specs, scratch_shape...  12.5 us
    ppermute x11, starting transfers between devices, plane_swap(): return lax.ppermute(value, ('gx', 'gy'), route)  10.8 us
    ppermute x6, starting transfers between devices, shifted(): lax.ppermute(value, axis, [(source, (source + steps) % count) for source...  8.97 us
    ppermute x11, starting transfers between devices, from_partner(): return lax.ppermute(block, axis, route)  6.14 us
    ppermute x11, waiting for transfers between devices, from_partner(): return lax.ppermute(block, axis, route)  6.14 us
    unnamed x18, local copies, waits for them, and re-layouts  2.88 us
  transfers between devices with their start and end apart: 28, of which 19 were waited for; matrix products, arithmetic and copies ran while one was open for 1% of the time, Pallas kernels for 5%

profile of v7, /device:TPU:0, one launch (start us, length us, event | category | flops | bytes accessed | tf_op | source)
XLA Modules:
  0.0 89.4 jit_solution(4628310461014489224)
XLA Ops:
  2.8 3.0 %collective-permute-start = (bf16[128,512]{1,0:T(8,128)(2,1)S(1)}, bf16[128,512]{1,0:T(8,128)(2,1)S(1)}, u32[]{:S(2)}, u32[]{:S(2)}) collective-permute-start(bf16[128,512]{1,0:T(8,128)(2,1)S(1)} %reshape.13.own.f_own), channel_id=1, source_target_pairs={{0,2},{2,0},{4,6},{6,4},{1,3},{3,1},{5,7},{7,5},{8,10},{10,8},{12,... | collective-permute-start | bytes 393224 | tf_op jit(solution)/shard_map/ppermute | solution.py:20
  9.5 1.3 %collective-permute-done.5.far.f_far = bf16[128,512]{1,0:T(8,128)(2,1)S(1)} collective-permute-done((bf16[128,512]{1,0:T(8,128)(2,1)S(1)}, bf16[128,512]{1,0:T(8,128)(2,1)S(1)}, u32[]{:S(2)}, u32[]{:S(2)}) %collective-permute-start.5) | collective-permute-done | bytes 131104 | tf_op jit(solution)/shard_map/ppermute | solution.py:20
  11.4 1.8 %collective-permute-start.7 = (bf16[128,768]{1,0:T(8,128)(2,1)S(1)}, bf16[128,768]{1,0:T(8,128)(2,1)S(1)}, u32[]{:S(2)}, u32[]{:S(2)}) collective-permute-start(bf16[128,768]{1,0:T(8,128)(2,1)S(1)} %get-tuple-element.50), channel_id=1, source_target_pairs={{0,2},{2,0},{4,6},{6,4},{1,3},{3,1},{5,7},{7,5},{8,10},{10,8},{12,... | collective-permute-start | bytes 589832 | tf_op jit(solution)/shard_map/ppermute | solution.py:20
  13.2 1.5 %collective-permute-start.9 = (bf16[512,256]{1,0:T(8,128)(2,1)S(1)}, bf16[512,256]{1,0:T(8,128)(2,1)S(1)}, u32[]{:S(2)}, u32[]{:S(2)}) collective-permute-start(bf16[512,256]{1,0:T(8,128)(2,1)S(1)} %get-tuple-element.53.refs_0_.refs_4_), channel_id=1, source_target_pairs={{0,8},{8,16},{16,24},{24,0},{1,9},{9,17},{17,25},{25,1},{2,10},{10... | collective-permute-start | bytes 786440 | tf_op jit(solution)/shard_map/ppermute | solution.py:25
  14.7 2.6 %collective-permute-start.11 = (bf16[512,256]{1,0:T(8,128)(2,1)S(1)}, bf16[512,256]{1,0:T(8,128)(2,1)S(1)}, u32[]{:S(2)}, u32[]{:S(2)}) collective-permute-start(bf16[512,256]{1,0:T(8,128)(2,1)S(1)} %get-tuple-element.53.refs_0_.refs_4_), channel_id=1, source_target_pairs={{0,4},{2,6},{4,0},{6,2},{1,5},{3,7},{5,1},{7,3},{8,12},{10,14},{12... | collective-permute-start | bytes 786440 | tf_op jit(solution)/shard_map/ppermute | solution.py:25
  17.3 1.4 %collective-permute-start.10 = (bf16[512,256]{1,0:T(8,128)(2,1)S(1)}, bf16[512,256]{1,0:T(8,128)(2,1)S(1)}, u32[]{:S(2)}, u32[]{:S(2)}) collective-permute-start(bf16[512,256]{1,0:T(8,128)(2,1)S(1)} %get-tuple-element.53.refs_0_.refs_4_), channel_id=1, source_target_pairs={{0,24},{8,0},{16,8},{24,16},{1,25},{9,1},{17,9},{25,17},{2,26},{10... | collective-permute-start | bytes 786440 | tf_op jit(solution)/shard_map/ppermute | solution.py:25
  18.7 2.3 %collective-permute-done.7.pair = bf16[128,768]{1,0:T(8,128)(2,1)S(1)} collective-permute-done((bf16[128,768]{1,0:T(8,128)(2,1)S(1)}, bf16[128,768]{1,0:T(8,128)(2,1)S(1)}, u32[]{:S(2)}, u32[]{:S(2)}) %collective-permute-start.7) | collective-permute-done | bytes 196640 | tf_op jit(solution)/shard_map/ppermute | solution.py:20
  21.0 2.3 %collective-permute-done.9.refs_1_.refs_5_ = bf16[512,256]{1,0:T(8,128)(2,1)S(1)} collective-permute-done((bf16[512,256]{1,0:T(8,128)(2,1)S(1)}, bf16[512,256]{1,0:T(8,128)(2,1)S(1)}, u32[]{:S(2)}, u32[]{:S(2)}) %collective-permute-start.9) | collective-permute-done | bytes 262176 | tf_op jit(solution)/shard_map/ppermute | solution.py:25
  23.3 1.5 %shard_map.114 = (bf16[4,512,512]{2,1,0:T(8,128)(2,1)S(1)}, f32[16,512]{1,0:T(8,128)S(1)}) custom-call(bf16[512,128]{1,0:T(8,128)(2,1)S(1)} %get-tuple-element.46.q_ref, bf16[512,256]{1,0:T(8,128)(2,1)S(1)} %get-tuple-element.53.refs_0_.refs_4_, bf16[512,256]{1,0:T(8,128)(2,1)S(1)} %collective-permute-done.9.refs_1_.refs_5_), custom_call_target="tpu_custom_call" | custom-call | flops 268435456 | bytes 2097152 | tf_op jit(solution)/shard_map/pallas_call | solution.py:55
  24.8 4.3 %collective-permute-done.11.refs_1_.refs_7_ = bf16[512,256]{1,0:T(8,128)(2,1)S(1)} collective-permute-done((bf16[512,256]{1,0:T(8,128)(2,1)S(1)}, bf16[512,256]{1,0:T(8,128)(2,1)S(1)}, u32[]{:S(2)}, u32[]{:S(2)}) %collective-permute-start.11) | collective-permute-done | bytes 262176 | tf_op jit(solution)/shard_map/ppermute | solution.py:25
  29.1 1.5 %shard_map.115 = (bf16[4,512,512]{2,1,0:T(8,128)(2,1)S(1)}, f32[16,512]{1,0:T(8,128)S(1)}) custom-call(bf16[512,128]{1,0:T(8,128)(2,1)S(1)} %get-tuple-element.46.q_ref, bf16[512,256]{1,0:T(8,128)(2,1)S(1)} %collective-permute-done.10.refs_0_.refs_6_, bf16[512,256]{1,0:T(8,128)(2,1)S(1)} %collective-permute-done.11.refs_1_.refs_7_), custom_call_target="tpu_custom_call" | custom-call | flops 268435456 | bytes 2097152 | tf_op jit(solution)/shard_map/pallas_call | solution.py:55
  31.0 4.8 %shard_map.116 = (bf16[512,128]{1,0:T(8,128)(2,1)S(1)}, bf16[512,256]{1,0:T(8,128)(2,1)S(1)}, bf16[512,256]{1,0:T(8,128)(2,1)S(1)}, bf16[512,256]{1,0:T(8,128)(2,1)S(1)}, bf16[512,256]{1,0:T(8,128)(2,1)S(1)}) custom-call(bf16[512,128]{1,0:T(8,128)(2,1)S(1)} %get-tuple-element.46.q_ref, bf16[512,128]{1,0:T(8,128)(2,1)S(1)} %get-tuple-element.51.do_ref, ...), custom_call_target="tpu_custom_call" | custom-call | flops 2147483648 | bytes 4194304 | tf_op jit(solution)/shard_map/pallas_call | solution.py:55
  35.9 1.5 %collective-permute-start.12 = (bf16[512,256]{1,0:T(8,128)(2,1)S(1)}, bf16[512,256]{1,0:T(8,128)(2,1)S(1)}, u32[]{:S(2)}, u32[]{:S(2)}) collective-permute-start(bf16[512,256]{1,0:T(8,128)(2,1)S(1)} %get-tuple-element.60), channel_id=1, source_target_pairs={{0,24},{8,0},{16,8},{24,16},{1,25},{9,1},{17,9},{25,17},{2,26},{10... | collective-permute-start | bytes 786440 | tf_op jit(solution)/shard_map/ppermute | solution.py:25
  38.0 1.4 %collective-permute-start.14 = (bf16[512,256]{1,0:T(8,128)(2,1)S(1)}, bf16[512,256]{1,0:T(8,128)(2,1)S(1)}, u32[]{:S(2)}, u32[]{:S(2)}) collective-permute-start(bf16[512,256]{1,0:T(8,128)(2,1)S(1)} %get-tuple-element.62), channel_id=1, source_target_pairs={{0,4},{2,6},{4,0},{6,2},{1,5},{3,7},{5,1},{7,3},{8,12},{10,14},{12... | collective-permute-start | bytes 786440 | tf_op jit(solution)/shard_map/ppermute | solution.py:25
  39.4 5.8 %collective-permute-done.12.refs_1_ = bf16[512,256]{1,0:T(8,128)(2,1)S(1)} collective-permute-done((bf16[512,256]{1,0:T(8,128)(2,1)S(1)}, bf16[512,256]{1,0:T(8,128)(2,1)S(1)}, u32[]{:S(2)}, u32[]{:S(2)}) %collective-permute-start.12) | collective-permute-done | bytes 262176 | tf_op jit(solution)/shard_map/ppermute | solution.py:25
  45.2 4.3 %collective-permute-done.13.refs_2_ = bf16[512,256]{1,0:T(8,128)(2,1)S(1)} collective-permute-done((bf16[512,256]{1,0:T(8,128)(2,1)S(1)}, bf16[512,256]{1,0:T(8,128)(2,1)S(1)}, u32[]{:S(2)}, u32[]{:S(2)}) %collective-permute-start.13) | collective-permute-done | bytes 262176 | tf_op jit(solution)/shard_map/ppermute | solution.py:25
  49.5 1.4 %collective-permute-done.14.refs_3_ = bf16[512,256]{1,0:T(8,128)(2,1)S(1)} collective-permute-done((bf16[512,256]{1,0:T(8,128)(2,1)S(1)}, bf16[512,256]{1,0:T(8,128)(2,1)S(1)}, u32[]{:S(2)}, u32[]{:S(2)}) %collective-permute-start.14) | collective-permute-done | bytes 262176 | tf_op jit(solution)/shard_map/ppermute | solution.py:25
  51.2 1.7 %collective-permute-done.15.core = bf16[512,384]{1,0:T(8,128)(2,1)S(1)} collective-permute-done((bf16[512,384]{1,0:T(8,128)(2,1)S(1)}, bf16[512,384]{1,0:T(8,128)(2,1)S(1)}, u32[]{:S(2)}, u32[]{:S(2)}) %collective-permute-start.15) | collective-permute-done | bytes 393248 | tf_op jit(solution)/shard_map/ppermute | solution.py:20
  53.5 2.5 %collective-permute-start.16 = (bf16[64,1024]{1,0:T(8,128)(2,1)S(1)}, bf16[64,1024]{1,0:T(8,128)(2,1)S(1)}, u32[]{:S(2)}, u32[]{:S(2)}) collective-permute-start(bf16[64,1024]{1,0:T(8,128)(2,1)S(1)} %get-tuple-element.66), channel_id=1, source_target_pairs={{0,8},{2,10},{4,12},{6,14},{8,0},{10,2},{12,4},{14,6},{16,24},{18,... | collective-permute-start | bytes 393224 | tf_op jit(solution)/shard_map/ppermute | solution.py:34
  56.4 1.2 %collective-permute-start.18 = (bf16[64,1024]{1,0:T(8,128)(2,1)S(1)}, bf16[64,1024]{1,0:T(8,128)(2,1)S(1)}, u32[]{:S(2)}, u32[]{:S(2)}) collective-permute-start(bf16[64,1024]{1,0:T(8,128)(2,1)S(1)} %get-tuple-element.68), channel_id=1, source_target_pairs={{0,24},{2,26},{4,28},{6,30},{8,16},{10,18},{12,20},{14,22},{16,8},... | collective-permute-start | bytes 393224 | tf_op jit(solution)/shard_map/ppermute | solution.py:34
  57.5 2.4 %collective-permute-done.16.refs_1_ = bf16[64,1024]{1,0:T(8,128)(2,1)S(1)} collective-permute-done((bf16[64,1024]{1,0:T(8,128)(2,1)S(1)}, bf16[64,1024]{1,0:T(8,128)(2,1)S(1)}, u32[]{:S(2)}, u32[]{:S(2)}) %collective-permute-start.16) | collective-permute-done | bytes 131104 | tf_op jit(solution)/shard_map/ppermute | solution.py:34
  59.9 4.2 %collective-permute-done.17.refs_2_ = bf16[64,1024]{1,0:T(8,128)(2,1)S(1)} collective-permute-done((bf16[64,1024]{1,0:T(8,128)(2,1)S(1)}, bf16[64,1024]{1,0:T(8,128)(2,1)S(1)}, u32[]{:S(2)}, u32[]{:S(2)}) %collective-permute-start.17) | collective-permute-done | bytes 131104 | tf_op jit(solution)/shard_map/ppermute | solution.py:34
  64.1 2.8 %collective-permute-start.20 = (bf16[64,1024]{1,0:T(8,128)(2,1)S(1)}, bf16[64,1024]{1,0:T(8,128)(2,1)S(1)}, u32[]{:S(2)}, u32[]{:S(2)}) collective-permute-start(bf16[64,1024]{1,0:T(8,128)(2,1)S(1)} %shard_map.119.refs_0_), channel_id=1, source_target_pairs={{0,4},{2,6},{4,0},{6,2},{8,12},{10,14},{12,8},{14,10},{16,20},{18,... | collective-permute-start | bytes 393224 | tf_op jit(solution)/shard_map/ppermute | solution.py:34
  67.0 1.3 %shard_map.120 = bf16[8,4,4,512]{3,2,1,0:T(4,128)(2,1)} custom-call(bf16[128,768]{1,0:T(8,128)(2,1)S(1)} %get-tuple-element.71.mine, bf16[128,768]{1,0:T(8,128)(2,1)S(1)} %collective-permute-done.19.pair, bf16[256,512]{1,0:T(8,128)(2,1)S(1)} %copy-done.1, bf16[256,512]{1,0:T(8,128)(2,1)S(1)} %collective-permute-done.2.wq1, bf16[256,512]{1,0:T(8,128)(2,1)S(1)} %copy-done.3, ...), custom_call_target="tpu_custom_call" | custom-call | flops 201326592 | bytes 1000000 | tf_op jit(solution)/shard_map/pallas_call | solution.py:55
  68.3 4.0 %collective-permute-done.20.refs_1_ = bf16[64,1024]{1,0:T(8,128)(2,1)S(1)} collective-permute-done((bf16[64,1024]{1,0:T(8,128)(2,1)S(1)}, bf16[64,1024]{1,0:T(8,128)(2,1)S(1)}, u32[]{:S(2)}, u32[]{:S(2)}) %collective-permute-start.20) | collective-permute-done | bytes 131104 | tf_op jit(solution)/shard_map/ppermute | solution.py:34
  72.4 2.1 %collective-permute-start.22 = (bf16[64,1024]{1,0:T(8,128)(2,1)S(1)}, bf16[64,1024]{1,0:T(8,128)(2,1)S(1)}, u32[]{:S(2)}, u32[]{:S(2)}) collective-permute-start(bf16[64,1024]{1,0:T(8,128)(2,1)S(1)} %shard_map.121.refs_0_), channel_id=1, source_target_pairs={{0,8},{2,10},{4,12},{6,14},{8,0},{10,2},{12,4},{14,6},{16,24},{18,... | collective-permute-start | bytes 393224 | tf_op jit(solution)/shard_map/ppermute | solution.py:34
  74.5 2.9 %collective-permute-done.24.refs_4_ = bf16[64,1024]{1,0:T(8,128)(2,1)S(1)} collective-permute-done((bf16[64,1024]{1,0:T(8,128)(2,1)S(1)}, bf16[64,1024]{1,0:T(8,128)(2,1)S(1)}, u32[]{:S(2)}, u32[]{:S(2)}) %collective-permute-start.24) | collective-permute-done | bytes 131104 | tf_op jit(solution)/shard_map/ppermute | solution.py:34
  78.0 2.6 %collective-permute-done.21.refs_1_ = bf16[64,1024]{1,0:T(8,128)(2,1)S(1)} collective-permute-done((bf16[64,1024]{1,0:T(8,128)(2,1)S(1)}, bf16[64,1024]{1,0:T(8,128)(2,1)S(1)}, u32[]{:S(2)}, u32[]{:S(2)}) %collective-permute-start.21) | collective-permute-done | bytes 131104 | tf_op jit(solution)/shard_map/ppermute | solution.py:34
  80.6 1.0 %collective-permute-start.27 = (bf16[64,1024]{1,0:T(8,128)(2,1)S(1)}, bf16[64,1024]{1,0:T(8,128)(2,1)S(1)}, u32[]{:S(2)}, u32[]{:S(2)}) collective-permute-start(bf16[64,1024]{1,0:T(8,128)(2,1)S(1)} %collective-permute-done.21.refs_1_), channel_id=1, source_target_pairs={{0,24},{2,26},{4,28},{6,30},{8,16},{10,18},{12,20},{14,22},{16,8},... | collective-permute-start | bytes 393224 | tf_op jit(solution)/shard_map/ppermute | solution.py:34
  82.9 3.6 %collective-permute-done.27.refs_7_ = bf16[64,1024]{1,0:T(8,128)(2,1)S(1)} collective-permute-done((bf16[64,1024]{1,0:T(8,128)(2,1)S(1)}, bf16[64,1024]{1,0:T(8,128)(2,1)S(1)}, u32[]{:S(2)}, u32[]{:S(2)}) %collective-permute-start.27) | collective-permute-done | bytes 131104 | tf_op jit(solution)/shard_map/ppermute | solution.py:34
  86.6 1.3 %collective-permute-done.25.refs_5_ = bf16[64,1024]{1,0:T(8,128)(2,1)S(1)} collective-permute-done((bf16[64,1024]{1,0:T(8,128)(2,1)S(1)}, bf16[64,1024]{1,0:T(8,128)(2,1)S(1)}, u32[]{:S(2)}, u32[]{:S(2)}) %collective-permute-start.25) | collective-permute-done | bytes 131104 | tf_op jit(solution)/shard_map/ppermute | solution.py:34
  87.9 1.5 %shard_map.122 = (f32[256,512]{1,0:T(8,128)}, f32[256,512]{1,0:T(8,128)}, f32[256,512]{1,0:T(8,128)}, f32[256,512]{1,0:T(8,128)}) custom-call(bf16[64,1024]{1,0:T(8,128)(2,1)S(1)} %shard_map.121.refs_0_, bf16[64,1024]{1,0:T(8,128)(2,1)S(1)} %collective-permute-done.21.refs_1_, bf16[64,1024]{1,0:T(8,128)(2,1)S(1)} %collective-permute-done.22.refs_2_, ...), custom_call_target="tpu_custom_call" | custom-call | flops 1000000 | bytes 1000000 | tf_op jit(solution)/shard_map/pallas_call | solution.py:55
  (56 shorter events, 10.9 us)
Async XLA Ops:
  0.7 5.1 %collective-permute-start.2 = (bf16[256,512]{1,0:T(8,128)(2,1)}, bf16[256,512]{1,0:T(8,128)(2,1)S(1)}, u32[]{:S(2)}, u32[]{:S(2)}) collective-permute-start(bf16[256,512]{1,0:T(8,128)(2,1)} %wq0.3), channel_id=1, source_target_pairs={{0,1},{1,0},{2,3},{3,2},{4,5},{5,4},{6,7},{7,6},{8,9},{9,8},{10,11... | collective-permute-start | bytes 786440 | tf_op jit(solution)/shard_map/ppermute | solution.py:20
  1.2 4.6 %collective-permute-start.3 = (bf16[256,512]{1,0:T(8,128)(2,1)}, bf16[256,512]{1,0:T(8,128)(2,1)S(1)}, u32[]{:S(2)}, u32[]{:S(2)}) collective-permute-start(bf16[256,512]{1,0:T(8,128)(2,1)} %wk0.3), channel_id=1, source_target_pairs={{0,1},{1,0},{2,3},{3,2},{4,5},{5,4},{6,7},{7,6},{8,9},{9,8},{10,11... | collective-permute-start | bytes 786440 | tf_op jit(solution)/shard_map/ppermute | solution.py:20
  1.3 4.5 %collective-permute-start.4 = (bf16[256,512]{1,0:T(8,128)(2,1)}, bf16[256,512]{1,0:T(8,128)(2,1)S(1)}, u32[]{:S(2)}, u32[]{:S(2)}) collective-permute-start(bf16[256,512]{1,0:T(8,128)(2,1)} %wv0.3), channel_id=1, source_target_pairs={{0,1},{1,0},{2,3},{3,2},{4,5},{5,4},{6,7},{7,6},{8,9},{9,8},{10,11... | collective-permute-start | bytes 786440 | tf_op jit(solution)/shard_map/ppermute | solution.py:20
  2.6 6.1 %collective-permute-start.1 = (bf16[128,512]{1,0:T(8,128)(2,1)S(1)}, bf16[128,512]{1,0:T(8,128)(2,1)S(1)}, u32[]{:S(2)}, u32[]{:S(2)}) collective-permute-start(bf16[128,512]{1,0:T(8,128)(2,1)S(1)} %reshape.13.own.f_own), channel_id=1, source_target_pairs={{0,1},{1,0},{2,3},{3,2},{4,5},{5,4},{6,7},{7,6},{8,9},{9,8},{10,11... | collective-permute-start | bytes 393224 | tf_op jit(solution)/shard_map/ppermute | solution.py:20
  2.8 6.7 %collective-permute-start = (bf16[128,512]{1,0:T(8,128)(2,1)S(1)}, bf16[128,512]{1,0:T(8,128)(2,1)S(1)}, u32[]{:S(2)}, u32[]{:S(2)}) collective-permute-start(bf16[128,512]{1,0:T(8,128)(2,1)S(1)} %reshape.13.own.f_own), channel_id=1, source_target_pairs={{0,2},{2,0},{4,6},{6,4},{1,3},{3,1},{5,7},{7,5},{8,10},{10,8},{12,... | collective-permute-start | bytes 393224 | tf_op jit(solution)/shard_map/ppermute | solution.py:20
  9.5 1.3 %collective-permute-start.5 = (bf16[128,512]{1,0:T(8,128)(2,1)S(1)}, bf16[128,512]{1,0:T(8,128)(2,1)S(1)}, u32[]{:S(2)}, u32[]{:S(2)}) collective-permute-start(bf16[128,512]{1,0:T(8,128)(2,1)S(1)} %collective-permute-done.pair.f_pair), channel_id=1, source_target_pairs={{0,1},{1,0},{2,3},{3,2},{4,5},{5,4},{6,7},{7,6},{8,9},{9,8},{10,11... | collective-permute-start | bytes 393224 | tf_op jit(solution)/shard_map/ppermute | solution.py:20
  11.3 19.2 %copy-start.6 = (bf16[256,512]{1,0:T(8,128)(2,1)S(1)}, bf16[256,512]{1,0:T(8,128)(2,1)}, u32[]{:S(2)}) copy-start(bf16[256,512]{1,0:T(8,128)(2,1)} %wout.1) | copy-start | bytes 786436
  11.4 9.6 %collective-permute-start.7 = (bf16[128,768]{1,0:T(8,128)(2,1)S(1)}, bf16[128,768]{1,0:T(8,128)(2,1)S(1)}, u32[]{:S(2)}, u32[]{:S(2)}) collective-permute-start(bf16[128,768]{1,0:T(8,128)(2,1)S(1)} %get-tuple-element.50), channel_id=1, source_target_pairs={{0,2},{2,0},{4,6},{6,4},{1,3},{3,1},{5,7},{7,5},{8,10},{10,8},{12,... | collective-permute-start | bytes 589832 | tf_op jit(solution)/shard_map/ppermute | solution.py:20
  13.2 10.1 %collective-permute-start.9 = (bf16[512,256]{1,0:T(8,128)(2,1)S(1)}, bf16[512,256]{1,0:T(8,128)(2,1)S(1)}, u32[]{:S(2)}, u32[]{:S(2)}) collective-permute-start(bf16[512,256]{1,0:T(8,128)(2,1)S(1)} %get-tuple-element.53.refs_0_.refs_4_), channel_id=1, source_target_pairs={{0,8},{8,16},{16,24},{24,0},{1,9},{9,17},{17,25},{25,1},{2,10},{10... | collective-permute-start | bytes 786440 | tf_op jit(solution)/shard_map/ppermute | solution.py:25
  14.7 14.4 %collective-permute-start.11 = (bf16[512,256]{1,0:T(8,128)(2,1)S(1)}, bf16[512,256]{1,0:T(8,128)(2,1)S(1)}, u32[]{:S(2)}, u32[]{:S(2)}) collective-permute-start(bf16[512,256]{1,0:T(8,128)(2,1)S(1)} %get-tuple-element.53.refs_0_.refs_4_), channel_id=1, source_target_pairs={{0,4},{2,6},{4,0},{6,2},{1,5},{3,7},{5,1},{7,3},{8,12},{10,14},{12... | collective-permute-start | bytes 786440 | tf_op jit(solution)/shard_map/ppermute | solution.py:25
  17.3 11.8 %collective-permute-start.10 = (bf16[512,256]{1,0:T(8,128)(2,1)S(1)}, bf16[512,256]{1,0:T(8,128)(2,1)S(1)}, u32[]{:S(2)}, u32[]{:S(2)}) collective-permute-start(bf16[512,256]{1,0:T(8,128)(2,1)S(1)} %get-tuple-element.53.refs_0_.refs_4_), channel_id=1, source_target_pairs={{0,24},{8,0},{16,8},{24,16},{1,25},{9,1},{17,9},{25,17},{2,26},{10... | collective-permute-start | bytes 786440 | tf_op jit(solution)/shard_map/ppermute | solution.py:25
  18.7 11.8 %collective-permute-start.6 = (bf16[128,768]{1,0:T(8,128)(2,1)S(1)}, bf16[128,768]{1,0:T(8,128)(2,1)S(1)}, u32[]{:S(2)}, u32[]{:S(2)}) collective-permute-start(bf16[128,768]{1,0:T(8,128)(2,1)S(1)} %get-tuple-element.49.own), channel_id=1, source_target_pairs={{0,1},{1,0},{2,3},{3,2},{4,5},{5,4},{6,7},{7,6},{8,9},{9,8},{10,11... | collective-permute-start | bytes 589832 | tf_op jit(solution)/shard_map/ppermute | solution.py:20
  21.0 9.5 %collective-permute-start.8 = (bf16[128,768]{1,0:T(8,128)(2,1)S(1)}, bf16[128,768]{1,0:T(8,128)(2,1)S(1)}, u32[]{:S(2)}, u32[]{:S(2)}) collective-permute-start(bf16[128,768]{1,0:T(8,128)(2,1)S(1)} %collective-permute-done.7.pair), channel_id=1, source_target_pairs={{0,1},{1,0},{2,3},{3,2},{4,5},{5,4},{6,7},{7,6},{8,9},{9,8},{10,11... | collective-permute-start | bytes 589832 | tf_op jit(solution)/shard_map/ppermute | solution.py:20
  35.9 31.1 %copy-start.1 = (bf16[256,512]{1,0:T(8,128)(2,1)S(1)}, bf16[256,512]{1,0:T(8,128)(2,1)}, u32[]{:S(2)}) copy-start(bf16[256,512]{1,0:T(8,128)(2,1)} %wq0.3) | copy-start | bytes 786436
  35.9 31.1 %copy-start.3 = (bf16[256,512]{1,0:T(8,128)(2,1)S(1)}, bf16[256,512]{1,0:T(8,128)(2,1)}, u32[]{:S(2)}) copy-start(bf16[256,512]{1,0:T(8,128)(2,1)} %wk0.3) | copy-start | bytes 786436
  35.9 31.1 %copy-start.5 = (bf16[256,512]{1,0:T(8,128)(2,1)S(1)}, bf16[256,512]{1,0:T(8,128)(2,1)}, u32[]{:S(2)}) copy-start(bf16[256,512]{1,0:T(8,128)(2,1)} %wv0.3) | copy-start | bytes 786436
  35.9 9.3 %collective-permute-start.12 = (bf16[512,256]{1,0:T(8,128)(2,1)S(1)}, bf16[512,256]{1,0:T(8,128)(2,1)S(1)}, u32[]{:S(2)}, u32[]{:S(2)}) collective-permute-start(bf16[512,256]{1,0:T(8,128)(2,1)S(1)} %get-tuple-element.60), channel_id=1, source_target_pairs={{0,24},{8,0},{16,8},{24,16},{1,25},{9,1},{17,9},{25,17},{2,26},{10... | collective-permute-start | bytes 786440 | tf_op jit(solution)/shard_map/ppermute | solution.py:25
  37.4 12.1 %collective-permute-start.13 = (bf16[512,256]{1,0:T(8,128)(2,1)S(1)}, bf16[512,256]{1,0:T(8,128)(2,1)S(1)}, u32[]{:S(2)}, u32[]{:S(2)}) collective-permute-start(bf16[512,256]{1,0:T(8,128)(2,1)S(1)} %get-tuple-element.61), channel_id=1, source_target_pairs={{0,8},{8,16},{16,24},{24,0},{1,9},{9,17},{17,25},{25,1},{2,10},{10... | collective-permute-start | bytes 786440 | tf_op jit(solution)/shard_map/ppermute | solution.py:25
  38.0 12.9 %collective-permute-start.14 = (bf16[512,256]{1,0:T(8,128)(2,1)S(1)}, bf16[512,256]{1,0:T(8,128)(2,1)S(1)}, u32[]{:S(2)}, u32[]{:S(2)}) collective-permute-start(bf16[512,256]{1,0:T(8,128)(2,1)S(1)} %get-tuple-element.62), channel_id=1, source_target_pairs={{0,4},{2,6},{4,0},{6,2},{1,5},{3,7},{5,1},{7,3},{8,12},{10,14},{12... | collective-permute-start | bytes 786440 | tf_op jit(solution)/shard_map/ppermute | solution.py:25
  51.1 1.8 %collective-permute-start.15 = (bf16[512,384]{1,0:T(8,128)(2,1)S(1)}, bf16[512,384]{1,0:T(8,128)(2,1)S(1)}, u32[]{:S(2)}, u32[]{:S(2)}) collective-permute-start(bf16[512,384]{1,0:T(8,128)(2,1)S(1)} %shard_map.117.own), channel_id=1, source_target_pairs={{0,1},{1,0},{2,3},{3,2},{4,5},{5,4},{6,7},{7,6},{8,9},{9,8},{10,11... | collective-permute-start | bytes 1179656 | tf_op jit(solution)/shard_map/ppermute | solution.py:20
  53.4 10.7 %collective-permute-start.19 = (bf16[128,768]{1,0:T(8,128)(2,1)S(1)}, bf16[128,768]{1,0:T(8,128)(2,1)S(1)}, u32[]{:S(2)}, u32[]{:S(2)}) collective-permute-start(bf16[128,768]{1,0:T(8,128)(2,1)S(1)} %get-tuple-element.69), channel_id=1, source_target_pairs={{0,2},{2,0},{4,6},{6,4},{1,3},{3,1},{5,7},{7,5},{8,10},{10,8},{12,... | collective-permute-start | bytes 589832 | tf_op jit(solution)/shard_map/ppermute | solution.py:20
  53.5 6.4 %collective-permute-start.16 = (bf16[64,1024]{1,0:T(8,128)(2,1)S(1)}, bf16[64,1024]{1,0:T(8,128)(2,1)S(1)}, u32[]{:S(2)}, u32[]{:S(2)}) collective-permute-start(bf16[64,1024]{1,0:T(8,128)(2,1)S(1)} %get-tuple-element.66), channel_id=1, source_target_pairs={{0,8},{2,10},{4,12},{6,14},{8,0},{10,2},{12,4},{14,6},{16,24},{18,... | collective-permute-start | bytes 393224 | tf_op jit(solution)/shard_map/ppermute | solution.py:34
  56.0 8.1 %collective-permute-start.17 = (bf16[64,1024]{1,0:T(8,128)(2,1)S(1)}, bf16[64,1024]{1,0:T(8,128)(2,1)S(1)}, u32[]{:S(2)}, u32[]{:S(2)}) collective-permute-start(bf16[64,1024]{1,0:T(8,128)(2,1)S(1)} %get-tuple-element.67), channel_id=1, source_target_pairs={{0,16},{2,18},{4,20},{6,22},{8,24},{10,26},{12,28},{14,30},{16,0},... | collective-permute-start | bytes 393224 | tf_op jit(solution)/shard_map/ppermute | solution.py:34
  56.4 7.7 %collective-permute-start.18 = (bf16[64,1024]{1,0:T(8,128)(2,1)S(1)}, bf16[64,1024]{1,0:T(8,128)(2,1)S(1)}, u32[]{:S(2)}, u32[]{:S(2)}) collective-permute-start(bf16[64,1024]{1,0:T(8,128)(2,1)S(1)} %get-tuple-element.68), channel_id=1, source_target_pairs={{0,24},{2,26},{4,28},{6,30},{8,16},{10,18},{12,20},{14,22},{16,8},... | collective-permute-start | bytes 393224 | tf_op jit(solution)/shard_map/ppermute | solution.py:34
  64.1 8.1 %collective-permute-start.20 = (bf16[64,1024]{1,0:T(8,128)(2,1)S(1)}, bf16[64,1024]{1,0:T(8,128)(2,1)S(1)}, u32[]{:S(2)}, u32[]{:S(2)}) collective-permute-start(bf16[64,1024]{1,0:T(8,128)(2,1)S(1)} %shard_map.119.refs_0_), channel_id=1, source_target_pairs={{0,4},{2,6},{4,0},{6,2},{8,12},{10,14},{12,8},{14,10},{16,20},{18,... | collective-permute-start | bytes 393224 | tf_op jit(solution)/shard_map/ppermute | solution.py:34
  72.3 5.0 %collective-permute-start.24 = (bf16[64,1024]{1,0:T(8,128)(2,1)S(1)}, bf16[64,1024]{1,0:T(8,128)(2,1)S(1)}, u32[]{:S(2)}, u32[]{:S(2)}) collective-permute-start(bf16[64,1024]{1,0:T(8,128)(2,1)S(1)} %shard_map.121.refs_0_), channel_id=1, source_target_pairs={{0,16},{2,18},{4,20},{6,22},{8,24},{10,26},{12,28},{14,30},{16,0},... | collective-permute-start | bytes 393224 | tf_op jit(solution)/shard_map/ppermute | solution.py:34
  72.4 5.6 %collective-permute-start.22 = (bf16[64,1024]{1,0:T(8,128)(2,1)S(1)}, bf16[64,1024]{1,0:T(8,128)(2,1)S(1)}, u32[]{:S(2)}, u32[]{:S(2)}) collective-permute-start(bf16[64,1024]{1,0:T(8,128)(2,1)S(1)} %shard_map.121.refs_0_), channel_id=1, source_target_pairs={{0,8},{2,10},{4,12},{6,14},{8,0},{10,2},{12,4},{14,6},{16,24},{18,... | collective-permute-start | bytes 393224 | tf_op jit(solution)/shard_map/ppermute | solution.py:34
  74.5 6.1 %collective-permute-start.21 = (bf16[64,1024]{1,0:T(8,128)(2,1)S(1)}, bf16[64,1024]{1,0:T(8,128)(2,1)S(1)}, u32[]{:S(2)}, u32[]{:S(2)}) collective-permute-start(bf16[64,1024]{1,0:T(8,128)(2,1)S(1)} %shard_map.121.refs_0_), channel_id=1, source_target_pairs={{0,2},{2,0},{4,6},{6,4},{8,10},{10,8},{12,14},{14,12},{16,18},{18,... | collective-permute-start | bytes 393224 | tf_op jit(solution)/shard_map/ppermute | solution.py:34
  77.3 5.1 %collective-permute-start.26 = (bf16[64,1024]{1,0:T(8,128)(2,1)S(1)}, bf16[64,1024]{1,0:T(8,128)(2,1)S(1)}, u32[]{:S(2)}, u32[]{:S(2)}) collective-permute-start(bf16[64,1024]{1,0:T(8,128)(2,1)S(1)} %collective-permute-done.24.refs_4_), channel_id=1, source_target_pairs={{0,8},{2,10},{4,12},{6,14},{8,0},{10,2},{12,4},{14,6},{16,24},{18,... | collective-permute-start | bytes 393224 | tf_op jit(solution)/shard_map/ppermute | solution.py:34
  78.0 5.0 %collective-permute-start.23 = (bf16[64,1024]{1,0:T(8,128)(2,1)S(1)}, bf16[64,1024]{1,0:T(8,128)(2,1)S(1)}, u32[]{:S(2)}, u32[]{:S(2)}) collective-permute-start(bf16[64,1024]{1,0:T(8,128)(2,1)S(1)} %collective-permute-done.22.refs_2_), channel_id=1, source_target_pairs={{0,2},{2,0},{4,6},{6,4},{8,10},{10,8},{12,14},{14,12},{16,18},{18,... | collective-permute-start | bytes 393224 | tf_op jit(solution)/shard_map/ppermute | solution.py:34
  80.6 6.0 %collective-permute-start.27 = (bf16[64,1024]{1,0:T(8,128)(2,1)S(1)}, bf16[64,1024]{1,0:T(8,128)(2,1)S(1)}, u32[]{:S(2)}, u32[]{:S(2)}) collective-permute-start(bf16[64,1024]{1,0:T(8,128)(2,1)S(1)} %collective-permute-done.21.refs_1_), channel_id=1, source_target_pairs={{0,24},{2,26},{4,28},{6,30},{8,16},{10,18},{12,20},{14,22},{16,8},... | collective-permute-start | bytes 393224 | tf_op jit(solution)/shard_map/ppermute | solution.py:34
  81.6 6.2 %collective-permute-start.25 = (bf16[64,1024]{1,0:T(8,128)(2,1)S(1)}, bf16[64,1024]{1,0:T(8,128)(2,1)S(1)}, u32[]{:S(2)}, u32[]{:S(2)}) collective-permute-start(bf16[64,1024]{1,0:T(8,128)(2,1)S(1)} %collective-permute-done.21.refs_1_), channel_id=1, source_target_pairs={{0,16},{2,18},{4,20},{6,22},{8,24},{10,26},{12,28},{14,30},{16,0},... | collective-permute-start | bytes 393224 | tf_op jit(solution)/shard_map/ppermute | solution.py:34
  (5 other events, 24.2 us)

commit v8 on v7

--- a/solution.py
+++ b/solution.py
@@ -410,11 +410,12 @@
         flops=8 * pixels * count * PART,
         moved=2 * pixels * count,
     )
-    back = [partials[0]]
-    for partial, (axis, step) in zip(partials[1:], routes):
+    back = []
+    for partial, (axis, step) in reversed(list(zip(partials[1:], routes))):
         back.append(shifted(partial, axis, -step))
+    back.append(partials[0])
     grads = call(
-        functools.partial(collect_kernel, times), shape_of((block_tokens, 3 * PART)), [dq, *back]
+        functools.partial(collect_kernel, times[::-1]), shape_of((block_tokens, 3 * PART)), [dq, *back]
     )
     core_grads = from_partner(grads, "gz")
     planned = count_x == 4 and count_y == 4 and count_z == 2
@@ -447,7 +448,7 @@
         total = call(sum_kernel, piece, [total, other])
         by_x, by_y, by_z = plane_swap(total, 1, 0), plane_swap(total, 2, 0), plane_swap(total, 0, 1)
         by_xy, by_xz = plane_swap(by_y, 1, 0), plane_swap(by_x, 0, 1)
-        by_yz, by_xyz = plane_swap(by_z, 2, 0), plane_swap(by_z, 3, 0)
+        by_yz, by_xyz = plane_swap(by_z, 2, 0), plane_swap(by_xy, 0, 1)
         weights = call(
             spread_kernel,
             tuple([shape_of((half, width), F32)] * 4),

time: 89.6 us -> 87.8 us (0.980)
  waiting for transfers between devices: 46.2 us -> 41.4 us
  starting transfers between devices: 26 us -> 29.1 us
    ppermute x11, waiting for transfers between devices: 22 us -> 19 us  [plane_swap(): return lax.ppermute(value, ('gx', 'gy'), route)]
    ppermute x11, starting transfers between devices: 6.14 us -> 8.67 us  [from_partner(): return lax.ppermute(block, axis, route)]
    ppermute x6, waiting for transfers between devices: 18.1 us -> 16.2 us  [shifted(): lax.ppermute(value, axis, [(source, (source + steps) % count) for source...]
    ppermute x6, starting transfers between devices: 8.97 us -> 9.88 us  [shifted(): lax.ppermute(value, axis, [(source, (source + steps) % count) for source...]
  transfers between devices with their start and end apart: 28 -> 28, of which waited for: 19 -> 15; matrix products, arithmetic and copies ran while one was open for 1% -> 1% of each run, Pallas kernels for 5% -> 5%
where the time goes in v8:
time: 87.8 us; the launch traced here: 87.6 us
  waiting for transfers between devices  41.4 us (47%)
  starting transfers between devices  29.1 us (33%)
  Pallas kernels  12.5 us (14%)
  local copies, waits for them, and re-layouts  3.82 us (4%)
    ppermute x11, waiting for transfers between devices, plane_swap(): return lax.ppermute(value, ('gx', 'gy'), route)  19 us
    ppermute x6, waiting for transfers between devices, shifted(): lax.ppermute(value, axis, [(source, (source + steps) % count) for source...  16.2 us
    pallas_call x13, Pallas kernels, call(): pl.pallas_call(kernel, out_shape=out_shape, in_specs=specs, scratch_shape...  12.5 us
    ppermute x11, starting transfers between devices, plane_swap(): return lax.ppermute(value, ('gx', 'gy'), route)  10.5 us
    ppermute x6, starting transfers between devices, shifted(): lax.ppermute(value, axis, [(source, (source + steps) % count) for source...  9.88 us
    ppermute x11, starting transfers between devices, from_partner(): return lax.ppermute(block, axis, route)  8.67 us
    ppermute x11, waiting for transfers between devices, from_partner(): return lax.ppermute(block, axis, route)  6.14 us
    unnamed x18, local copies, waits for them, and re-layouts  2.88 us
  transfers between devices with their start and end apart: 28, of which 15 were waited for; matrix products, arithmetic and copies ran while one was open for 1% of the time, Pallas kernels for 5%

profile of v8, /device:TPU:0, one launch (start us, length us, event | category | flops | bytes accessed | tf_op | source)
XLA Modules:
  0.0 87.6 jit_solution(11865222328432071298)
XLA Ops:
  2.8 3.0 %collective-permute-start = (bf16[128,512]{1,0:T(8,128)(2,1)S(1)}, bf16[128,512]{1,0:T(8,128)(2,1)S(1)}, u32[]{:S(2)}, u32[]{:S(2)}) collective-permute-start(bf16[128,512]{1,0:T(8,128)(2,1)S(1)} %reshape.13.own.f_own), channel_id=1, source_target_pairs={{0,2},{2,0},{4,6},{6,4},{1,3},{3,1},{5,7},{7,5},{8,10},{10,8},{12,... | collective-permute-start | bytes 393224 | tf_op jit(solution)/shard_map/ppermute | solution.py:20
  9.5 1.3 %collective-permute-done.5.far.f_far = bf16[128,512]{1,0:T(8,128)(2,1)S(1)} collective-permute-done((bf16[128,512]{1,0:T(8,128)(2,1)S(1)}, bf16[128,512]{1,0:T(8,128)(2,1)S(1)}, u32[]{:S(2)}, u32[]{:S(2)}) %collective-permute-start.5) | collective-permute-done | bytes 131104 | tf_op jit(solution)/shard_map/ppermute | solution.py:20
  11.4 1.8 %collective-permute-start.7 = (bf16[128,768]{1,0:T(8,128)(2,1)S(1)}, bf16[128,768]{1,0:T(8,128)(2,1)S(1)}, u32[]{:S(2)}, u32[]{:S(2)}) collective-permute-start(bf16[128,768]{1,0:T(8,128)(2,1)S(1)} %get-tuple-element.50), channel_id=1, source_target_pairs={{0,2},{2,0},{4,6},{6,4},{1,3},{3,1},{5,7},{7,5},{8,10},{10,8},{12,... | collective-permute-start | bytes 589832 | tf_op jit(solution)/shard_map/ppermute | solution.py:20
  13.2 1.5 %collective-permute-start.9 = (bf16[512,256]{1,0:T(8,128)(2,1)S(1)}, bf16[512,256]{1,0:T(8,128)(2,1)S(1)}, u32[]{:S(2)}, u32[]{:S(2)}) collective-permute-start(bf16[512,256]{1,0:T(8,128)(2,1)S(1)} %get-tuple-element.53.refs_0_.refs_4_), channel_id=1, source_target_pairs={{0,8},{8,16},{16,24},{24,0},{1,9},{9,17},{17,25},{25,1},{2,10},{10... | collective-permute-start | bytes 786440 | tf_op jit(solution)/shard_map/ppermute | solution.py:25
  14.7 2.6 %collective-permute-start.11 = (bf16[512,256]{1,0:T(8,128)(2,1)S(1)}, bf16[512,256]{1,0:T(8,128)(2,1)S(1)}, u32[]{:S(2)}, u32[]{:S(2)}) collective-permute-start(bf16[512,256]{1,0:T(8,128)(2,1)S(1)} %get-tuple-element.53.refs_0_.refs_4_), channel_id=1, source_target_pairs={{0,4},{2,6},{4,0},{6,2},{1,5},{3,7},{5,1},{7,3},{8,12},{10,14},{12... | collective-permute-start | bytes 786440 | tf_op jit(solution)/shard_map/ppermute | solution.py:25
  17.3 1.4 %collective-permute-start.10 = (bf16[512,256]{1,0:T(8,128)(2,1)S(1)}, bf16[512,256]{1,0:T(8,128)(2,1)S(1)}, u32[]{:S(2)}, u32[]{:S(2)}) collective-permute-start(bf16[512,256]{1,0:T(8,128)(2,1)S(1)} %get-tuple-element.53.refs_0_.refs_4_), channel_id=1, source_target_pairs={{0,24},{8,0},{16,8},{24,16},{1,25},{9,1},{17,9},{25,17},{2,26},{10... | collective-permute-start | bytes 786440 | tf_op jit(solution)/shard_map/ppermute | solution.py:25
  18.7 2.3 %collective-permute-done.7.pair = bf16[128,768]{1,0:T(8,128)(2,1)S(1)} collective-permute-done((bf16[128,768]{1,0:T(8,128)(2,1)S(1)}, bf16[128,768]{1,0:T(8,128)(2,1)S(1)}, u32[]{:S(2)}, u32[]{:S(2)}) %collective-permute-start.7) | collective-permute-done | bytes 196640 | tf_op jit(solution)/shard_map/ppermute | solution.py:20
  21.0 2.3 %collective-permute-done.9.refs_1_.refs_5_ = bf16[512,256]{1,0:T(8,128)(2,1)S(1)} collective-permute-done((bf16[512,256]{1,0:T(8,128)(2,1)S(1)}, bf16[512,256]{1,0:T(8,128)(2,1)S(1)}, u32[]{:S(2)}, u32[]{:S(2)}) %collective-permute-start.9) | collective-permute-done | bytes 262176 | tf_op jit(solution)/shard_map/ppermute | solution.py:25
  23.3 1.5 %shard_map.114 = (bf16[4,512,512]{2,1,0:T(8,128)(2,1)S(1)}, f32[16,512]{1,0:T(8,128)S(1)}) custom-call(bf16[512,128]{1,0:T(8,128)(2,1)S(1)} %get-tuple-element.46.q_ref, bf16[512,256]{1,0:T(8,128)(2,1)S(1)} %get-tuple-element.53.refs_0_.refs_4_, bf16[512,256]{1,0:T(8,128)(2,1)S(1)} %collective-permute-done.9.refs_1_.refs_5_), custom_call_target="tpu_custom_call" | custom-call | flops 268435456 | bytes 2097152 | tf_op jit(solution)/shard_map/pallas_call | solution.py:55
  24.8 4.3 %collective-permute-done.11.refs_1_.refs_7_ = bf16[512,256]{1,0:T(8,128)(2,1)S(1)} collective-permute-done((bf16[512,256]{1,0:T(8,128)(2,1)S(1)}, bf16[512,256]{1,0:T(8,128)(2,1)S(1)}, u32[]{:S(2)}, u32[]{:S(2)}) %collective-permute-start.11) | collective-permute-done | bytes 262176 | tf_op jit(solution)/shard_map/ppermute | solution.py:25
  29.1 1.5 %shard_map.115 = (bf16[4,512,512]{2,1,0:T(8,128)(2,1)S(1)}, f32[16,512]{1,0:T(8,128)S(1)}) custom-call(bf16[512,128]{1,0:T(8,128)(2,1)S(1)} %get-tuple-element.46.q_ref, bf16[512,256]{1,0:T(8,128)(2,1)S(1)} %collective-permute-done.10.refs_0_.refs_6_, bf16[512,256]{1,0:T(8,128)(2,1)S(1)} %collective-permute-done.11.refs_1_.refs_7_), custom_call_target="tpu_custom_call" | custom-call | flops 268435456 | bytes 2097152 | tf_op jit(solution)/shard_map/pallas_call | solution.py:55
  31.0 4.8 %shard_map.116 = (bf16[512,128]{1,0:T(8,128)(2,1)S(1)}, bf16[512,256]{1,0:T(8,128)(2,1)S(1)}, bf16[512,256]{1,0:T(8,128)(2,1)S(1)}, bf16[512,256]{1,0:T(8,128)(2,1)S(1)}, bf16[512,256]{1,0:T(8,128)(2,1)S(1)}) custom-call(bf16[512,128]{1,0:T(8,128)(2,1)S(1)} %get-tuple-element.46.q_ref, bf16[512,128]{1,0:T(8,128)(2,1)S(1)} %get-tuple-element.51.do_ref, ...), custom_call_target="tpu_custom_call" | custom-call | flops 2147483648 | bytes 4194304 | tf_op jit(solution)/shard_map/pallas_call | solution.py:55
  35.9 1.4 %collective-permute-start.12 = (bf16[512,256]{1,0:T(8,128)(2,1)S(1)}, bf16[512,256]{1,0:T(8,128)(2,1)S(1)}, u32[]{:S(2)}, u32[]{:S(2)}) collective-permute-start(bf16[512,256]{1,0:T(8,128)(2,1)S(1)} %get-tuple-element.59), channel_id=1, source_target_pairs={{0,4},{2,6},{4,0},{6,2},{1,5},{3,7},{5,1},{7,3},{8,12},{10,14},{12... | collective-permute-start | bytes 786440 | tf_op jit(solution)/shard_map/ppermute | solution.py:25
  37.4 1.5 %collective-permute-start.13 = (bf16[512,256]{1,0:T(8,128)(2,1)S(1)}, bf16[512,256]{1,0:T(8,128)(2,1)S(1)}, u32[]{:S(2)}, u32[]{:S(2)}) collective-permute-start(bf16[512,256]{1,0:T(8,128)(2,1)S(1)} %get-tuple-element.60), channel_id=1, source_target_pairs={{0,8},{8,16},{16,24},{24,0},{1,9},{9,17},{17,25},{25,1},{2,10},{10... | collective-permute-start | bytes 786440 | tf_op jit(solution)/shard_map/ppermute | solution.py:25
  38.9 1.4 %collective-permute-start.14 = (bf16[512,256]{1,0:T(8,128)(2,1)S(1)}, bf16[512,256]{1,0:T(8,128)(2,1)S(1)}, u32[]{:S(2)}, u32[]{:S(2)}) collective-permute-start(bf16[512,256]{1,0:T(8,128)(2,1)S(1)} %get-tuple-element.61), channel_id=1, source_target_pairs={{0,24},{8,0},{16,8},{24,16},{1,25},{9,1},{17,9},{25,17},{2,26},{10... | collective-permute-start | bytes 786440 | tf_op jit(solution)/shard_map/ppermute | solution.py:25
  40.3 9.1 %collective-permute-done.12.refs_0_ = bf16[512,256]{1,0:T(8,128)(2,1)S(1)} collective-permute-done((bf16[512,256]{1,0:T(8,128)(2,1)S(1)}, bf16[512,256]{1,0:T(8,128)(2,1)S(1)}, u32[]{:S(2)}, u32[]{:S(2)}) %collective-permute-start.12) | collective-permute-done | bytes 262176 | tf_op jit(solution)/shard_map/ppermute | solution.py:25
  50.2 1.7 %collective-permute-done.15.core = bf16[512,384]{1,0:T(8,128)(2,1)S(1)} collective-permute-done((bf16[512,384]{1,0:T(8,128)(2,1)S(1)}, bf16[512,384]{1,0:T(8,128)(2,1)S(1)}, u32[]{:S(2)}, u32[]{:S(2)}) %collective-permute-start.15) | collective-permute-done | bytes 393248 | tf_op jit(solution)/shard_map/ppermute | solution.py:20
  52.4 2.6 %collective-permute-start.19 = (bf16[128,768]{1,0:T(8,128)(2,1)S(1)}, bf16[128,768]{1,0:T(8,128)(2,1)S(1)}, u32[]{:S(2)}, u32[]{:S(2)}) collective-permute-start(bf16[128,768]{1,0:T(8,128)(2,1)S(1)} %get-tuple-element.69), channel_id=1, source_target_pairs={{0,2},{2,0},{4,6},{6,4},{1,3},{3,1},{5,7},{7,5},{8,10},{10,8},{12,... | collective-permute-start | bytes 589832 | tf_op jit(solution)/shard_map/ppermute | solution.py:20
  55.4 1.7 %collective-permute-start.17 = (bf16[64,1024]{1,0:T(8,128)(2,1)S(1)}, bf16[64,1024]{1,0:T(8,128)(2,1)S(1)}, u32[]{:S(2)}, u32[]{:S(2)}) collective-permute-start(bf16[64,1024]{1,0:T(8,128)(2,1)S(1)} %get-tuple-element.67), channel_id=1, source_target_pairs={{0,16},{2,18},{4,20},{6,22},{8,24},{10,26},{12,28},{14,30},{16,0},... | collective-permute-start | bytes 393224 | tf_op jit(solution)/shard_map/ppermute | solution.py:34
  57.1 1.5 %collective-permute-start.18 = (bf16[64,1024]{1,0:T(8,128)(2,1)S(1)}, bf16[64,1024]{1,0:T(8,128)(2,1)S(1)}, u32[]{:S(2)}, u32[]{:S(2)}) collective-permute-start(bf16[64,1024]{1,0:T(8,128)(2,1)S(1)} %get-tuple-element.68), channel_id=1, source_target_pairs={{0,24},{2,26},{4,28},{6,30},{8,16},{10,18},{12,20},{14,22},{16,8},... | collective-permute-start | bytes 393224 | tf_op jit(solution)/shard_map/ppermute | solution.py:34
  58.5 2.9 %collective-permute-done.16.refs_1_ = bf16[64,1024]{1,0:T(8,128)(2,1)S(1)} collective-permute-done((bf16[64,1024]{1,0:T(8,128)(2,1)S(1)}, bf16[64,1024]{1,0:T(8,128)(2,1)S(1)}, u32[]{:S(2)}, u32[]{:S(2)}) %collective-permute-start.16) | collective-permute-done | bytes 131104 | tf_op jit(solution)/shard_map/ppermute | solution.py:34
  61.4 1.7 %collective-permute-done.17.refs_2_ = bf16[64,1024]{1,0:T(8,128)(2,1)S(1)} collective-permute-done((bf16[64,1024]{1,0:T(8,128)(2,1)S(1)}, bf16[64,1024]{1,0:T(8,128)(2,1)S(1)}, u32[]{:S(2)}, u32[]{:S(2)}) %collective-permute-start.17) | collective-permute-done | bytes 131104 | tf_op jit(solution)/shard_map/ppermute | solution.py:34
  63.3 1.4 %collective-permute-start.20 = (bf16[64,1024]{1,0:T(8,128)(2,1)S(1)}, bf16[64,1024]{1,0:T(8,128)(2,1)S(1)}, u32[]{:S(2)}, u32[]{:S(2)}) collective-permute-start(bf16[64,1024]{1,0:T(8,128)(2,1)S(1)} %shard_map.119.refs_0_), channel_id=1, source_target_pairs={{0,4},{2,6},{4,0},{6,2},{8,12},{10,14},{12,8},{14,10},{16,20},{18,... | collective-permute-start | bytes 393224 | tf_op jit(solution)/shard_map/ppermute | solution.py:34
  64.7 1.3 %shard_map.120 = bf16[8,4,4,512]{3,2,1,0:T(4,128)(2,1)} custom-call(bf16[128,768]{1,0:T(8,128)(2,1)S(1)} %get-tuple-element.71.mine, bf16[128,768]{1,0:T(8,128)(2,1)S(1)} %collective-permute-done.19.pair, bf16[256,512]{1,0:T(8,128)(2,1)S(1)} %copy-done.1, bf16[256,512]{1,0:T(8,128)(2,1)S(1)} %collective-permute-done.2.wq1, bf16[256,512]{1,0:T(8,128)(2,1)S(1)} %copy-done.3, ...), custom_call_target="tpu_custom_call" | custom-call | flops 201326592 | bytes 1000000 | tf_op jit(solution)/shard_map/pallas_call | solution.py:55
  66.0 5.1 %collective-permute-done.20.refs_1_ = bf16[64,1024]{1,0:T(8,128)(2,1)S(1)} collective-permute-done((bf16[64,1024]{1,0:T(8,128)(2,1)S(1)}, bf16[64,1024]{1,0:T(8,128)(2,1)S(1)}, u32[]{:S(2)}, u32[]{:S(2)}) %collective-permute-start.20) | collective-permute-done | bytes 131104 | tf_op jit(solution)/shard_map/ppermute | solution.py:34
  71.1 1.8 %collective-permute-start.24 = (bf16[64,1024]{1,0:T(8,128)(2,1)S(1)}, bf16[64,1024]{1,0:T(8,128)(2,1)S(1)}, u32[]{:S(2)}, u32[]{:S(2)}) collective-permute-start(bf16[64,1024]{1,0:T(8,128)(2,1)S(1)} %shard_map.121.refs_0_), channel_id=1, source_target_pairs={{0,16},{2,18},{4,20},{6,22},{8,24},{10,26},{12,28},{14,30},{16,0},... | collective-permute-start | bytes 393224 | tf_op jit(solution)/shard_map/ppermute | solution.py:34
  72.9 3.2 %collective-permute-done.24.refs_4_ = bf16[64,1024]{1,0:T(8,128)(2,1)S(1)} collective-permute-done((bf16[64,1024]{1,0:T(8,128)(2,1)S(1)}, bf16[64,1024]{1,0:T(8,128)(2,1)S(1)}, u32[]{:S(2)}, u32[]{:S(2)}) %collective-permute-start.24) | collective-permute-done | bytes 131104 | tf_op jit(solution)/shard_map/ppermute | solution.py:34
  76.1 1.7 %collective-permute-start.26 = (bf16[64,1024]{1,0:T(8,128)(2,1)S(1)}, bf16[64,1024]{1,0:T(8,128)(2,1)S(1)}, u32[]{:S(2)}, u32[]{:S(2)}) collective-permute-start(bf16[64,1024]{1,0:T(8,128)(2,1)S(1)} %collective-permute-done.24.refs_4_), channel_id=1, source_target_pairs={{0,8},{2,10},{4,12},{6,14},{8,0},{10,2},{12,4},{14,6},{16,24},{18,... | collective-permute-start | bytes 393224 | tf_op jit(solution)/shard_map/ppermute | solution.py:34
  79.0 2.1 %collective-permute-start.25 = (bf16[64,1024]{1,0:T(8,128)(2,1)S(1)}, bf16[64,1024]{1,0:T(8,128)(2,1)S(1)}, u32[]{:S(2)}, u32[]{:S(2)}) collective-permute-start(bf16[64,1024]{1,0:T(8,128)(2,1)S(1)} %collective-permute-done.21.refs_1_), channel_id=1, source_target_pairs={{0,16},{2,18},{4,20},{6,22},{8,24},{10,26},{12,28},{14,30},{16,0},... | collective-permute-start | bytes 393224 | tf_op jit(solution)/shard_map/ppermute | solution.py:34
  81.1 3.4 %collective-permute-done.23.refs_3_ = bf16[64,1024]{1,0:T(8,128)(2,1)S(1)} collective-permute-done((bf16[64,1024]{1,0:T(8,128)(2,1)S(1)}, bf16[64,1024]{1,0:T(8,128)(2,1)S(1)}, u32[]{:S(2)}, u32[]{:S(2)}) %collective-permute-start.23) | collective-permute-done | bytes 131104 | tf_op jit(solution)/shard_map/ppermute | solution.py:34
  84.5 1.5 %collective-permute-done.27.refs_7_ = bf16[64,1024]{1,0:T(8,128)(2,1)S(1)} collective-permute-done((bf16[64,1024]{1,0:T(8,128)(2,1)S(1)}, bf16[64,1024]{1,0:T(8,128)(2,1)S(1)}, u32[]{:S(2)}, u32[]{:S(2)}) %collective-permute-start.27) | collective-permute-done | bytes 131104 | tf_op jit(solution)/shard_map/ppermute | solution.py:34
  86.1 1.5 %shard_map.122 = (f32[256,512]{1,0:T(8,128)}, f32[256,512]{1,0:T(8,128)}, f32[256,512]{1,0:T(8,128)}, f32[256,512]{1,0:T(8,128)}) custom-call(bf16[64,1024]{1,0:T(8,128)(2,1)S(1)} %shard_map.121.refs_0_, bf16[64,1024]{1,0:T(8,128)(2,1)S(1)} %collective-permute-done.21.refs_1_, bf16[64,1024]{1,0:T(8,128)(2,1)S(1)} %collective-permute-done.22.refs_2_, ...), custom_call_target="tpu_custom_call" | custom-call | flops 1000000 | bytes 1000000 | tf_op jit(solution)/shard_map/pallas_call | solution.py:55
  (56 shorter events, 9.8 us)
Async XLA Ops:
  0.7 5.1 %collective-permute-start.2 = (bf16[256,512]{1,0:T(8,128)(2,1)}, bf16[256,512]{1,0:T(8,128)(2,1)S(1)}, u32[]{:S(2)}, u32[]{:S(2)}) collective-permute-start(bf16[256,512]{1,0:T(8,128)(2,1)} %wq0.3), channel_id=1, source_target_pairs={{0,1},{1,0},{2,3},{3,2},{4,5},{5,4},{6,7},{7,6},{8,9},{9,8},{10,11... | collective-permute-start | bytes 786440 | tf_op jit(solution)/shard_map/ppermute | solution.py:20
  1.2 4.6 %collective-permute-start.3 = (bf16[256,512]{1,0:T(8,128)(2,1)}, bf16[256,512]{1,0:T(8,128)(2,1)S(1)}, u32[]{:S(2)}, u32[]{:S(2)}) collective-permute-start(bf16[256,512]{1,0:T(8,128)(2,1)} %wk0.3), channel_id=1, source_target_pairs={{0,1},{1,0},{2,3},{3,2},{4,5},{5,4},{6,7},{7,6},{8,9},{9,8},{10,11... | collective-permute-start | bytes 786440 | tf_op jit(solution)/shard_map/ppermute | solution.py:20
  1.3 4.5 %collective-permute-start.4 = (bf16[256,512]{1,0:T(8,128)(2,1)}, bf16[256,512]{1,0:T(8,128)(2,1)S(1)}, u32[]{:S(2)}, u32[]{:S(2)}) collective-permute-start(bf16[256,512]{1,0:T(8,128)(2,1)} %wv0.3), channel_id=1, source_target_pairs={{0,1},{1,0},{2,3},{3,2},{4,5},{5,4},{6,7},{7,6},{8,9},{9,8},{10,11... | collective-permute-start | bytes 786440 | tf_op jit(solution)/shard_map/ppermute | solution.py:20
  2.6 6.1 %collective-permute-start.1 = (bf16[128,512]{1,0:T(8,128)(2,1)S(1)}, bf16[128,512]{1,0:T(8,128)(2,1)S(1)}, u32[]{:S(2)}, u32[]{:S(2)}) collective-permute-start(bf16[128,512]{1,0:T(8,128)(2,1)S(1)} %reshape.13.own.f_own), channel_id=1, source_target_pairs={{0,1},{1,0},{2,3},{3,2},{4,5},{5,4},{6,7},{7,6},{8,9},{9,8},{10,11... | collective-permute-start | bytes 393224 | tf_op jit(solution)/shard_map/ppermute | solution.py:20
  2.8 6.7 %collective-permute-start = (bf16[128,512]{1,0:T(8,128)(2,1)S(1)}, bf16[128,512]{1,0:T(8,128)(2,1)S(1)}, u32[]{:S(2)}, u32[]{:S(2)}) collective-permute-start(bf16[128,512]{1,0:T(8,128)(2,1)S(1)} %reshape.13.own.f_own), channel_id=1, source_target_pairs={{0,2},{2,0},{4,6},{6,4},{1,3},{3,1},{5,7},{7,5},{8,10},{10,8},{12,... | collective-permute-start | bytes 393224 | tf_op jit(solution)/shard_map/ppermute | solution.py:20
  9.5 1.3 %collective-permute-start.5 = (bf16[128,512]{1,0:T(8,128)(2,1)S(1)}, bf16[128,512]{1,0:T(8,128)(2,1)S(1)}, u32[]{:S(2)}, u32[]{:S(2)}) collective-permute-start(bf16[128,512]{1,0:T(8,128)(2,1)S(1)} %collective-permute-done.pair.f_pair), channel_id=1, source_target_pairs={{0,1},{1,0},{2,3},{3,2},{4,5},{5,4},{6,7},{7,6},{8,9},{9,8},{10,11... | collective-permute-start | bytes 393224 | tf_op jit(solution)/shard_map/ppermute | solution.py:20
  11.3 19.2 %copy-start.6 = (bf16[256,512]{1,0:T(8,128)(2,1)S(1)}, bf16[256,512]{1,0:T(8,128)(2,1)}, u32[]{:S(2)}) copy-start(bf16[256,512]{1,0:T(8,128)(2,1)} %wout.1) | copy-start | bytes 786436
  11.4 9.6 %collective-permute-start.7 = (bf16[128,768]{1,0:T(8,128)(2,1)S(1)}, bf16[128,768]{1,0:T(8,128)(2,1)S(1)}, u32[]{:S(2)}, u32[]{:S(2)}) collective-permute-start(bf16[128,768]{1,0:T(8,128)(2,1)S(1)} %get-tuple-element.50), channel_id=1, source_target_pairs={{0,2},{2,0},{4,6},{6,4},{1,3},{3,1},{5,7},{7,5},{8,10},{10,8},{12,... | collective-permute-start | bytes 589832 | tf_op jit(solution)/shard_map/ppermute | solution.py:20
  13.2 10.1 %collective-permute-start.9 = (bf16[512,256]{1,0:T(8,128)(2,1)S(1)}, bf16[512,256]{1,0:T(8,128)(2,1)S(1)}, u32[]{:S(2)}, u32[]{:S(2)}) collective-permute-start(bf16[512,256]{1,0:T(8,128)(2,1)S(1)} %get-tuple-element.53.refs_0_.refs_4_), channel_id=1, source_target_pairs={{0,8},{8,16},{16,24},{24,0},{1,9},{9,17},{17,25},{25,1},{2,10},{10... | collective-permute-start | bytes 786440 | tf_op jit(solution)/shard_map/ppermute | solution.py:25
  14.7 14.4 %collective-permute-start.11 = (bf16[512,256]{1,0:T(8,128)(2,1)S(1)}, bf16[512,256]{1,0:T(8,128)(2,1)S(1)}, u32[]{:S(2)}, u32[]{:S(2)}) collective-permute-start(bf16[512,256]{1,0:T(8,128)(2,1)S(1)} %get-tuple-element.53.refs_0_.refs_4_), channel_id=1, source_target_pairs={{0,4},{2,6},{4,0},{6,2},{1,5},{3,7},{5,1},{7,3},{8,12},{10,14},{12... | collective-permute-start | bytes 786440 | tf_op jit(solution)/shard_map/ppermute | solution.py:25
  17.3 11.8 %collective-permute-start.10 = (bf16[512,256]{1,0:T(8,128)(2,1)S(1)}, bf16[512,256]{1,0:T(8,128)(2,1)S(1)}, u32[]{:S(2)}, u32[]{:S(2)}) collective-permute-start(bf16[512,256]{1,0:T(8,128)(2,1)S(1)} %get-tuple-element.53.refs_0_.refs_4_), channel_id=1, source_target_pairs={{0,24},{8,0},{16,8},{24,16},{1,25},{9,1},{17,9},{25,17},{2,26},{10... | collective-permute-start | bytes 786440 | tf_op jit(solution)/shard_map/ppermute | solution.py:25
  18.7 11.8 %collective-permute-start.6 = (bf16[128,768]{1,0:T(8,128)(2,1)S(1)}, bf16[128,768]{1,0:T(8,128)(2,1)S(1)}, u32[]{:S(2)}, u32[]{:S(2)}) collective-permute-start(bf16[128,768]{1,0:T(8,128)(2,1)S(1)} %get-tuple-element.49.own), channel_id=1, source_target_pairs={{0,1},{1,0},{2,3},{3,2},{4,5},{5,4},{6,7},{7,6},{8,9},{9,8},{10,11... | collective-permute-start | bytes 589832 | tf_op jit(solution)/shard_map/ppermute | solution.py:20
  21.0 9.5 %collective-permute-start.8 = (bf16[128,768]{1,0:T(8,128)(2,1)S(1)}, bf16[128,768]{1,0:T(8,128)(2,1)S(1)}, u32[]{:S(2)}, u32[]{:S(2)}) collective-permute-start(bf16[128,768]{1,0:T(8,128)(2,1)S(1)} %collective-permute-done.7.pair), channel_id=1, source_target_pairs={{0,1},{1,0},{2,3},{3,2},{4,5},{5,4},{6,7},{7,6},{8,9},{9,8},{10,11... | collective-permute-start | bytes 589832 | tf_op jit(solution)/shard_map/ppermute | solution.py:20
  35.9 28.8 %copy-start.1 = (bf16[256,512]{1,0:T(8,128)(2,1)S(1)}, bf16[256,512]{1,0:T(8,128)(2,1)}, u32[]{:S(2)}) copy-start(bf16[256,512]{1,0:T(8,128)(2,1)} %wq0.3) | copy-start | bytes 786436
  35.9 28.7 %copy-start.3 = (bf16[256,512]{1,0:T(8,128)(2,1)S(1)}, bf16[256,512]{1,0:T(8,128)(2,1)}, u32[]{:S(2)}) copy-start(bf16[256,512]{1,0:T(8,128)(2,1)} %wk0.3) | copy-start | bytes 786436
  35.9 28.7 %copy-start.5 = (bf16[256,512]{1,0:T(8,128)(2,1)S(1)}, bf16[256,512]{1,0:T(8,128)(2,1)}, u32[]{:S(2)}) copy-start(bf16[256,512]{1,0:T(8,128)(2,1)} %wv0.3) | copy-start | bytes 786436
  35.9 13.5 %collective-permute-start.12 = (bf16[512,256]{1,0:T(8,128)(2,1)S(1)}, bf16[512,256]{1,0:T(8,128)(2,1)S(1)}, u32[]{:S(2)}, u32[]{:S(2)}) collective-permute-start(bf16[512,256]{1,0:T(8,128)(2,1)S(1)} %get-tuple-element.59), channel_id=1, source_target_pairs={{0,4},{2,6},{4,0},{6,2},{1,5},{3,7},{5,1},{7,3},{8,12},{10,14},{12... | collective-permute-start | bytes 786440 | tf_op jit(solution)/shard_map/ppermute | solution.py:25
  37.4 12.1 %collective-permute-start.13 = (bf16[512,256]{1,0:T(8,128)(2,1)S(1)}, bf16[512,256]{1,0:T(8,128)(2,1)S(1)}, u32[]{:S(2)}, u32[]{:S(2)}) collective-permute-start(bf16[512,256]{1,0:T(8,128)(2,1)S(1)} %get-tuple-element.60), channel_id=1, source_target_pairs={{0,8},{8,16},{16,24},{24,0},{1,9},{9,17},{17,25},{25,1},{2,10},{10... | collective-permute-start | bytes 786440 | tf_op jit(solution)/shard_map/ppermute | solution.py:25
  38.9 11.0 %collective-permute-start.14 = (bf16[512,256]{1,0:T(8,128)(2,1)S(1)}, bf16[512,256]{1,0:T(8,128)(2,1)S(1)}, u32[]{:S(2)}, u32[]{:S(2)}) collective-permute-start(bf16[512,256]{1,0:T(8,128)(2,1)S(1)} %get-tuple-element.61), channel_id=1, source_target_pairs={{0,24},{8,0},{16,8},{24,16},{1,25},{9,1},{17,9},{25,17},{2,26},{10... | collective-permute-start | bytes 786440 | tf_op jit(solution)/shard_map/ppermute | solution.py:25
  50.1 1.8 %collective-permute-start.15 = (bf16[512,384]{1,0:T(8,128)(2,1)S(1)}, bf16[512,384]{1,0:T(8,128)(2,1)S(1)}, u32[]{:S(2)}, u32[]{:S(2)}) collective-permute-start(bf16[512,384]{1,0:T(8,128)(2,1)S(1)} %shard_map.117.own), channel_id=1, source_target_pairs={{0,1},{1,0},{2,3},{3,2},{4,5},{5,4},{6,7},{7,6},{8,9},{9,8},{10,11... | collective-permute-start | bytes 1179656 | tf_op jit(solution)/shard_map/ppermute | solution.py:20
  52.4 10.8 %collective-permute-start.19 = (bf16[128,768]{1,0:T(8,128)(2,1)S(1)}, bf16[128,768]{1,0:T(8,128)(2,1)S(1)}, u32[]{:S(2)}, u32[]{:S(2)}) collective-permute-start(bf16[128,768]{1,0:T(8,128)(2,1)S(1)} %get-tuple-element.69), channel_id=1, source_target_pairs={{0,2},{2,0},{4,6},{6,4},{1,3},{3,1},{5,7},{7,5},{8,10},{10,8},{12,... | collective-permute-start | bytes 589832 | tf_op jit(solution)/shard_map/ppermute | solution.py:20
  55.1 6.4 %collective-permute-start.16 = (bf16[64,1024]{1,0:T(8,128)(2,1)S(1)}, bf16[64,1024]{1,0:T(8,128)(2,1)S(1)}, u32[]{:S(2)}, u32[]{:S(2)}) collective-permute-start(bf16[64,1024]{1,0:T(8,128)(2,1)S(1)} %get-tuple-element.66), channel_id=1, source_target_pairs={{0,8},{2,10},{4,12},{6,14},{8,0},{10,2},{12,4},{14,6},{16,24},{18,... | collective-permute-start | bytes 393224 | tf_op jit(solution)/shard_map/ppermute | solution.py:34
  55.4 7.8 %collective-permute-start.17 = (bf16[64,1024]{1,0:T(8,128)(2,1)S(1)}, bf16[64,1024]{1,0:T(8,128)(2,1)S(1)}, u32[]{:S(2)}, u32[]{:S(2)}) collective-permute-start(bf16[64,1024]{1,0:T(8,128)(2,1)S(1)} %get-tuple-element.67), channel_id=1, source_target_pairs={{0,16},{2,18},{4,20},{6,22},{8,24},{10,26},{12,28},{14,30},{16,0},... | collective-permute-start | bytes 393224 | tf_op jit(solution)/shard_map/ppermute | solution.py:34
  57.1 6.1 %collective-permute-start.18 = (bf16[64,1024]{1,0:T(8,128)(2,1)S(1)}, bf16[64,1024]{1,0:T(8,128)(2,1)S(1)}, u32[]{:S(2)}, u32[]{:S(2)}) collective-permute-start(bf16[64,1024]{1,0:T(8,128)(2,1)S(1)} %get-tuple-element.68), channel_id=1, source_target_pairs={{0,24},{2,26},{4,28},{6,30},{8,16},{10,18},{12,20},{14,22},{16,8},... | collective-permute-start | bytes 393224 | tf_op jit(solution)/shard_map/ppermute | solution.py:34
  63.3 7.8 %collective-permute-start.20 = (bf16[64,1024]{1,0:T(8,128)(2,1)S(1)}, bf16[64,1024]{1,0:T(8,128)(2,1)S(1)}, u32[]{:S(2)}, u32[]{:S(2)}) collective-permute-start(bf16[64,1024]{1,0:T(8,128)(2,1)S(1)} %shard_map.119.refs_0_), channel_id=1, source_target_pairs={{0,4},{2,6},{4,0},{6,2},{8,12},{10,14},{12,8},{14,10},{16,20},{18,... | collective-permute-start | bytes 393224 | tf_op jit(solution)/shard_map/ppermute | solution.py:34
  71.1 5.0 %collective-permute-start.24 = (bf16[64,1024]{1,0:T(8,128)(2,1)S(1)}, bf16[64,1024]{1,0:T(8,128)(2,1)S(1)}, u32[]{:S(2)}, u32[]{:S(2)}) collective-permute-start(bf16[64,1024]{1,0:T(8,128)(2,1)S(1)} %shard_map.121.refs_0_), channel_id=1, source_target_pairs={{0,16},{2,18},{4,20},{6,22},{8,24},{10,26},{12,28},{14,30},{16,0},... | collective-permute-start | bytes 393224 | tf_op jit(solution)/shard_map/ppermute | solution.py:34
  72.9 6.0 %collective-permute-start.22 = (bf16[64,1024]{1,0:T(8,128)(2,1)S(1)}, bf16[64,1024]{1,0:T(8,128)(2,1)S(1)}, u32[]{:S(2)}, u32[]{:S(2)}) collective-permute-start(bf16[64,1024]{1,0:T(8,128)(2,1)S(1)} %shard_map.121.refs_0_), channel_id=1, source_target_pairs={{0,8},{2,10},{4,12},{6,14},{8,0},{10,2},{12,4},{14,6},{16,24},{18,... | collective-permute-start | bytes 393224 | tf_op jit(solution)/shard_map/ppermute | solution.py:34
  72.9 6.1 %collective-permute-start.21 = (bf16[64,1024]{1,0:T(8,128)(2,1)S(1)}, bf16[64,1024]{1,0:T(8,128)(2,1)S(1)}, u32[]{:S(2)}, u32[]{:S(2)}) collective-permute-start(bf16[64,1024]{1,0:T(8,128)(2,1)S(1)} %shard_map.121.refs_0_), channel_id=1, source_target_pairs={{0,2},{2,0},{4,6},{6,4},{8,10},{10,8},{12,14},{14,12},{16,18},{18,... | collective-permute-start | bytes 393224 | tf_op jit(solution)/shard_map/ppermute | solution.py:34
  76.1 5.0 %collective-permute-start.26 = (bf16[64,1024]{1,0:T(8,128)(2,1)S(1)}, bf16[64,1024]{1,0:T(8,128)(2,1)S(1)}, u32[]{:S(2)}, u32[]{:S(2)}) collective-permute-start(bf16[64,1024]{1,0:T(8,128)(2,1)S(1)} %collective-permute-done.24.refs_4_), channel_id=1, source_target_pairs={{0,8},{2,10},{4,12},{6,14},{8,0},{10,2},{12,4},{14,6},{16,24},{18,... | collective-permute-start | bytes 393224 | tf_op jit(solution)/shard_map/ppermute | solution.py:34
  79.0 5.5 %collective-permute-start.23 = (bf16[64,1024]{1,0:T(8,128)(2,1)S(1)}, bf16[64,1024]{1,0:T(8,128)(2,1)S(1)}, u32[]{:S(2)}, u32[]{:S(2)}) collective-permute-start(bf16[64,1024]{1,0:T(8,128)(2,1)S(1)} %collective-permute-done.22.refs_2_), channel_id=1, source_target_pairs={{0,2},{2,0},{4,6},{6,4},{8,10},{10,8},{12,14},{14,12},{16,18},{18,... | collective-permute-start | bytes 393224 | tf_op jit(solution)/shard_map/ppermute | solution.py:34
  79.0 5.5 %collective-permute-start.25 = (bf16[64,1024]{1,0:T(8,128)(2,1)S(1)}, bf16[64,1024]{1,0:T(8,128)(2,1)S(1)}, u32[]{:S(2)}, u32[]{:S(2)}) collective-permute-start(bf16[64,1024]{1,0:T(8,128)(2,1)S(1)} %collective-permute-done.21.refs_1_), channel_id=1, source_target_pairs={{0,16},{2,18},{4,20},{6,22},{8,24},{10,26},{12,28},{14,30},{16,0},... | collective-permute-start | bytes 393224 | tf_op jit(solution)/shard_map/ppermute | solution.py:34
  81.1 5.0 %collective-permute-start.27 = (bf16[64,1024]{1,0:T(8,128)(2,1)S(1)}, bf16[64,1024]{1,0:T(8,128)(2,1)S(1)}, u32[]{:S(2)}, u32[]{:S(2)}) collective-permute-start(bf16[64,1024]{1,0:T(8,128)(2,1)S(1)} %collective-permute-done.26.refs_6_), channel_id=1, source_target_pairs={{0,2},{2,0},{4,6},{6,4},{8,10},{10,8},{12,14},{14,12},{16,18},{18,... | collective-permute-start | bytes 393224 | tf_op jit(solution)/shard_map/ppermute | solution.py:34
  (5 other events, 24.2 us)

commit v9 on v8

--- a/solution.py
+++ b/solution.py
@@ -146,29 +146,35 @@
     return jnp.where(low, table[:, 2 * at : 2 * at + 1], table[:, 2 * at + 1 : 2 * at + 2])
 
 
-def score_kernel(q_ref, *refs):
-    count = len(refs) - 2
-    e_ref, table_ref = refs[count:]
+def score_kernel(q_ref, do_ref, delta_ref, *refs):
+    count = len(refs) - 3
+    e_ref, ds_ref, table_ref = refs[count:]
     half = table_ref.shape[0] // 2
     q_heads = by_head(q_ref[...])
+    g_heads = by_head(do_ref[...])
+    delta = delta_ref[...]
     if half > 2 * count:
         table_ref[...] = jnp.zeros_like(table_ref)
     for at in range(count):
         keys = refs[at][:, 0:PART]
+        values = refs[at][:, PART:]
         for head in range(2):
             scores = dot_nt(keys, q_heads[head])
             top = jnp.max(scores, axis=0, keepdims=True)
             grown = jnp.exp(scores - top)
             row = 2 * at + head
-            e_ref[row] = grown.astype(BF)
+            rounded = grown.astype(BF)
+            e_ref[row] = rounded
+            dprob = dot_nt(values, g_heads[head])
+            ds_ref[row] = (rounded.astype(F32) * (dprob - delta[head : head + 1, :])).astype(BF)
             table_ref[row : row + 1, :] = top
             table_ref[half + row : half + row + 1, :] = jnp.sum(grown, axis=0, keepdims=True)
 
 
-def gradient_kernel(times, groups, q_ref, do_ref, delta_ref, *refs):
+def gradient_kernel(times, groups, q_ref, do_ref, *refs):
     count = len(times)
-    e_refs, tables = refs[: 2 * len(groups) : 2], refs[1 : 2 * len(groups) : 2]
-    refs = refs[2 * len(groups) :]
+    e_refs, ds_refs, tables = (refs[at : 3 * len(groups) : 3] for at in range(3))
+    refs = refs[3 * len(groups) :]
     kvs, dq_ref, outs, dq_s, part_s = (
         refs[:count], refs[count], refs[count + 1 : 2 * count + 1], refs[-2], refs[-1]
     )
@@ -192,14 +198,10 @@
     tokens = q_ref.shape[0]
     head_dim = PART // 2
     turned = part_s[...].T
-    grad = do_ref[...]
-    g_heads = by_head(grad)
-    grad = grad.astype(F32)
+    grad = do_ref[...].astype(F32)
     query = q_ref[...].astype(F32)
-    delta = delta_ref[...]
     for at in range(count):
         keys_t = kvs[at][:, 0:PART].astype(F32).T.astype(BF)
-        values = kvs[at][:, PART:]
         group, place = where[at]
         scale = row_scale(turned, at, tokens)
         q_scaled = by_head((query * scale).astype(BF))
@@ -207,8 +209,7 @@
         dks, dvs = [], []
         for head in range(2):
             grown = e_refs[group][2 * place + head]
-            dprob = dot_nt(values, g_heads[head])
-            dscore = (grown.astype(F32) * (dprob - delta[head : head + 1, :])).astype(BF)
+            dscore = ds_refs[group][2 * place + head]
             dvs.append(dot_nn(grown, g_scaled[head]))
             dks.append(dot_nn(dscore, q_scaled[head]))
             spot = slice(head * head_dim, (head + 1) * head_dim)
@@ -391,24 +392,25 @@
             score_kernel,
             (
                 shape_of((2 * blocks, block_tokens, block_tokens)),
+                shape_of((2 * blocks, block_tokens, block_tokens)),
                 shape_of((2 * rows, block_tokens), F32),
             ),
-            [query, *near[place : place + blocks]],
-            flops=2 * pixels * blocks * PART,
-            moved=2 * pixels * blocks,
+            [query, out_grad, delta, *near[place : place + blocks]],
+            flops=4 * pixels * blocks * PART,
+            moved=4 * pixels * blocks,
             exps=pixels * blocks,
         )
         place += blocks
     dq, *partials = call(
         functools.partial(gradient_kernel, times, groups),
         (column, *[both] * count),
-        [query, out_grad, delta, *scored, *near],
+        [query, out_grad, *scored, *near],
         scratch=[
             pltpu.VMEM((PART, block_tokens), F32),
             pltpu.VMEM((-(-2 * count // 8) * 8, block_tokens), F32),
         ],
-        flops=8 * pixels * count * PART,
-        moved=2 * pixels * count,
+        flops=6 * pixels * count * PART,
+        moved=4 * pixels * count,
     )
     back = []
     for partial, (axis, step) in reversed(list(zip(partials[1:], routes))):

time: 87.8 us -> 86.5 us (0.985)
  waiting for transfers between devices: 41.4 us -> 40.3 us
    ppermute x6, waiting for transfers between devices: 16.2 us -> 13.6 us  [shifted(): lax.ppermute(value, axis, [(source, (source + steps) % count) for source...]
    ppermute x11, waiting for transfers between devices: 6.14 us -> 7.58 us  [from_partner(): return lax.ppermute(block, axis, route)]
  transfers between devices with their start and end apart: 28 -> 28, of which waited for: 15 -> 17; matrix products, arithmetic and copies ran while one was open for 1% -> 1% of each run, Pallas kernels for 5% -> 5%
where the time goes in v9:
time: 86.5 us; the launch traced here: 86.3 us
  waiting for transfers between devices  40.3 us (47%)
  starting transfers between devices  29 us (34%)
  Pallas kernels  12.4 us (14%)
  local copies, waits for them, and re-layouts  3.81 us (4%)
    ppermute x11, waiting for transfers between devices, plane_swap(): return lax.ppermute(value, ('gx', 'gy'), route)  19.1 us
    ppermute x6, waiting for transfers between devices, shifted(): lax.ppermute(value, axis, [(source, (source + steps) % count) for source...  13.6 us
    pallas_call x13, Pallas kernels, call(): pl.pallas_call(kernel, out_shape=out_shape, in_specs=specs, scratch_shape...  12.4 us
    ppermute x11, starting transfers between devices, plane_swap(): return lax.ppermute(value, ('gx', 'gy'), route)  10.4 us
    ppermute x6, starting transfers between devices, shifted(): lax.ppermute(value, axis, [(source, (source + steps) % count) for source...  9.89 us
    ppermute x11, starting transfers between devices, from_partner(): return lax.ppermute(block, axis, route)  8.66 us
    ppermute x11, waiting for transfers between devices, from_partner(): return lax.ppermute(block, axis, route)  7.58 us
    unnamed x18, local copies, waits for them, and re-layouts  2.87 us
  transfers between devices with their start and end apart: 28, of which 17 were waited for; matrix products, arithmetic and copies ran while one was open for 1% of the time, Pallas kernels for 5%

profile of v9, /device:TPU:0, one launch (start us, length us, event | category | flops | bytes accessed | tf_op | source)
XLA Modules:
  0.0 86.3 jit_solution(1341804616704677487)
XLA Ops:
  2.8 3.0 %collective-permute-start = (bf16[128,512]{1,0:T(8,128)(2,1)S(1)}, bf16[128,512]{1,0:T(8,128)(2,1)S(1)}, u32[]{:S(2)}, u32[]{:S(2)}) collective-permute-start(bf16[128,512]{1,0:T(8,128)(2,1)S(1)} %reshape.13.own.f_own), channel_id=1, source_target_pairs={{0,2},{2,0},{4,6},{6,4},{1,3},{3,1},{5,7},{7,5},{8,10},{10,8},{12,... | collective-permute-start | bytes 393224 | tf_op jit(solution)/shard_map/ppermute | solution.py:20
  9.5 1.3 %collective-permute-done.5.far.f_far = bf16[128,512]{1,0:T(8,128)(2,1)S(1)} collective-permute-done((bf16[128,512]{1,0:T(8,128)(2,1)S(1)}, bf16[128,512]{1,0:T(8,128)(2,1)S(1)}, u32[]{:S(2)}, u32[]{:S(2)}) %collective-permute-start.5) | collective-permute-done | bytes 131104 | tf_op jit(solution)/shard_map/ppermute | solution.py:20
  11.4 1.8 %collective-permute-start.7 = (bf16[128,768]{1,0:T(8,128)(2,1)S(1)}, bf16[128,768]{1,0:T(8,128)(2,1)S(1)}, u32[]{:S(2)}, u32[]{:S(2)}) collective-permute-start(bf16[128,768]{1,0:T(8,128)(2,1)S(1)} %get-tuple-element.52), channel_id=1, source_target_pairs={{0,2},{2,0},{4,6},{6,4},{1,3},{3,1},{5,7},{7,5},{8,10},{10,8},{12,... | collective-permute-start | bytes 589832 | tf_op jit(solution)/shard_map/ppermute | solution.py:20
  13.2 1.5 %collective-permute-start.9 = (bf16[512,256]{1,0:T(8,128)(2,1)S(1)}, bf16[512,256]{1,0:T(8,128)(2,1)S(1)}, u32[]{:S(2)}, u32[]{:S(2)}) collective-permute-start(bf16[512,256]{1,0:T(8,128)(2,1)S(1)} %get-tuple-element.55.refs_0_.refs_6_), channel_id=1, source_target_pairs={{0,8},{8,16},{16,24},{24,0},{1,9},{9,17},{17,25},{25,1},{2,10},{10... | collective-permute-start | bytes 786440 | tf_op jit(solution)/shard_map/ppermute | solution.py:25
  14.7 2.6 %collective-permute-start.11 = (bf16[512,256]{1,0:T(8,128)(2,1)S(1)}, bf16[512,256]{1,0:T(8,128)(2,1)S(1)}, u32[]{:S(2)}, u32[]{:S(2)}) collective-permute-start(bf16[512,256]{1,0:T(8,128)(2,1)S(1)} %get-tuple-element.55.refs_0_.refs_6_), channel_id=1, source_target_pairs={{0,4},{2,6},{4,0},{6,2},{1,5},{3,7},{5,1},{7,3},{8,12},{10,14},{12... | collective-permute-start | bytes 786440 | tf_op jit(solution)/shard_map/ppermute | solution.py:25
  17.3 1.4 %collective-permute-start.10 = (bf16[512,256]{1,0:T(8,128)(2,1)S(1)}, bf16[512,256]{1,0:T(8,128)(2,1)S(1)}, u32[]{:S(2)}, u32[]{:S(2)}) collective-permute-start(bf16[512,256]{1,0:T(8,128)(2,1)S(1)} %get-tuple-element.55.refs_0_.refs_6_), channel_id=1, source_target_pairs={{0,24},{8,0},{16,8},{24,16},{1,25},{9,1},{17,9},{25,17},{2,26},{10... | collective-permute-start | bytes 786440 | tf_op jit(solution)/shard_map/ppermute | solution.py:25
  18.7 2.3 %collective-permute-done.7.pair = bf16[128,768]{1,0:T(8,128)(2,1)S(1)} collective-permute-done((bf16[128,768]{1,0:T(8,128)(2,1)S(1)}, bf16[128,768]{1,0:T(8,128)(2,1)S(1)}, u32[]{:S(2)}, u32[]{:S(2)}) %collective-permute-start.7) | collective-permute-done | bytes 196640 | tf_op jit(solution)/shard_map/ppermute | solution.py:20
  21.0 1.4 %collective-permute-done.8.far = bf16[128,768]{1,0:T(8,128)(2,1)S(1)} collective-permute-done((bf16[128,768]{1,0:T(8,128)(2,1)S(1)}, bf16[128,768]{1,0:T(8,128)(2,1)S(1)}, u32[]{:S(2)}, u32[]{:S(2)}) %collective-permute-start.8) | collective-permute-done | bytes 196640 | tf_op jit(solution)/shard_map/ppermute | solution.py:20
  23.3 2.1 %shard_map.114 = (bf16[4,512,512]{2,1,0:T(8,128)(2,1)S(1)}, bf16[4,512,512]{2,1,0:T(8,128)(2,1)S(1)}, f32[16,512]{1,0:T(8,128)S(1)}) custom-call(bf16[512,128]{1,0:T(8,128)(2,1)S(1)} %get-tuple-element.48.q_ref, bf16[512,128]{1,0:T(8,128)(2,1)S(1)} %get-tuple-element.53.do_ref, f32[2,512]{1,0:T(2,128)S(1)} %get-tuple-element.54.delta_ref, ...), custom_call_target="tpu_custom_call" | custom-call | flops 536870912 | bytes 4194304 | tf_op jit(solution)/shard_map/pallas_call | solution.py:55
  25.4 3.6 %collective-permute-done.11.refs_1_.refs_9_ = bf16[512,256]{1,0:T(8,128)(2,1)S(1)} collective-permute-done((bf16[512,256]{1,0:T(8,128)(2,1)S(1)}, bf16[512,256]{1,0:T(8,128)(2,1)S(1)}, u32[]{:S(2)}, u32[]{:S(2)}) %collective-permute-start.11) | collective-permute-done | bytes 262176 | tf_op jit(solution)/shard_map/ppermute | solution.py:25
  29.0 2.1 %shard_map.115 = (bf16[4,512,512]{2,1,0:T(8,128)(2,1)S(1)}, bf16[4,512,512]{2,1,0:T(8,128)(2,1)S(1)}, f32[16,512]{1,0:T(8,128)S(1)}) custom-call(bf16[512,128]{1,0:T(8,128)(2,1)S(1)} %get-tuple-element.48.q_ref, bf16[512,128]{1,0:T(8,128)(2,1)S(1)} %get-tuple-element.53.do_ref, f32[2,512]{1,0:T(2,128)S(1)} %get-tuple-element.54.delta_ref, ...), custom_call_target="tpu_custom_call" | custom-call | flops 536870912 | bytes 4194304 | tf_op jit(solution)/shard_map/pallas_call | solution.py:55
  31.2 3.4 %shard_map.116 = (bf16[512,128]{1,0:T(8,128)(2,1)S(1)}, bf16[512,256]{1,0:T(8,128)(2,1)S(1)}, bf16[512,256]{1,0:T(8,128)(2,1)S(1)}, bf16[512,256]{1,0:T(8,128)(2,1)S(1)}, bf16[512,256]{1,0:T(8,128)(2,1)S(1)}) custom-call(bf16[512,128]{1,0:T(8,128)(2,1)S(1)} %get-tuple-element.48.q_ref, bf16[512,128]{1,0:T(8,128)(2,1)S(1)} %get-tuple-element.53.do_ref, ...), custom_call_target="tpu_custom_call" | custom-call | flops 1610612736 | bytes 8388608 | tf_op jit(solution)/shard_map/pallas_call | solution.py:55
  34.6 1.5 %collective-permute-start.12 = (bf16[512,256]{1,0:T(8,128)(2,1)S(1)}, bf16[512,256]{1,0:T(8,128)(2,1)S(1)}, u32[]{:S(2)}, u32[]{:S(2)}) collective-permute-start(bf16[512,256]{1,0:T(8,128)(2,1)S(1)} %get-tuple-element.63), channel_id=1, source_target_pairs={{0,4},{2,6},{4,0},{6,2},{1,5},{3,7},{5,1},{7,3},{8,12},{10,14},{12... | collective-permute-start | bytes 786440 | tf_op jit(solution)/shard_map/ppermute | solution.py:25
  36.1 1.5 %collective-permute-start.13 = (bf16[512,256]{1,0:T(8,128)(2,1)S(1)}, bf16[512,256]{1,0:T(8,128)(2,1)S(1)}, u32[]{:S(2)}, u32[]{:S(2)}) collective-permute-start(bf16[512,256]{1,0:T(8,128)(2,1)S(1)} %get-tuple-element.64), channel_id=1, source_target_pairs={{0,8},{8,16},{16,24},{24,0},{1,9},{9,17},{17,25},{25,1},{2,10},{10... | collective-permute-start | bytes 786440 | tf_op jit(solution)/shard_map/ppermute | solution.py:25
  37.6 1.4 %collective-permute-start.14 = (bf16[512,256]{1,0:T(8,128)(2,1)S(1)}, bf16[512,256]{1,0:T(8,128)(2,1)S(1)}, u32[]{:S(2)}, u32[]{:S(2)}) collective-permute-start(bf16[512,256]{1,0:T(8,128)(2,1)S(1)} %get-tuple-element.65), channel_id=1, source_target_pairs={{0,24},{8,0},{16,8},{24,16},{1,25},{9,1},{17,9},{25,17},{2,26},{10... | collective-permute-start | bytes 786440 | tf_op jit(solution)/shard_map/ppermute | solution.py:25
  39.0 9.1 %collective-permute-done.12.refs_0_ = bf16[512,256]{1,0:T(8,128)(2,1)S(1)} collective-permute-done((bf16[512,256]{1,0:T(8,128)(2,1)S(1)}, bf16[512,256]{1,0:T(8,128)(2,1)S(1)}, u32[]{:S(2)}, u32[]{:S(2)}) %collective-permute-start.12) | collective-permute-done | bytes 262176 | tf_op jit(solution)/shard_map/ppermute | solution.py:25
  48.9 1.7 %collective-permute-done.15.core = bf16[512,384]{1,0:T(8,128)(2,1)S(1)} collective-permute-done((bf16[512,384]{1,0:T(8,128)(2,1)S(1)}, bf16[512,384]{1,0:T(8,128)(2,1)S(1)}, u32[]{:S(2)}, u32[]{:S(2)}) %collective-permute-start.15) | collective-permute-done | bytes 393248 | tf_op jit(solution)/shard_map/ppermute | solution.py:20
  51.2 2.6 %collective-permute-start.19 = (bf16[128,768]{1,0:T(8,128)(2,1)S(1)}, bf16[128,768]{1,0:T(8,128)(2,1)S(1)}, u32[]{:S(2)}, u32[]{:S(2)}) collective-permute-start(bf16[128,768]{1,0:T(8,128)(2,1)S(1)} %get-tuple-element.73), channel_id=1, source_target_pairs={{0,2},{2,0},{4,6},{6,4},{1,3},{3,1},{5,7},{7,5},{8,10},{10,8},{12,... | collective-permute-start | bytes 589832 | tf_op jit(solution)/shard_map/ppermute | solution.py:20
  54.1 1.7 %collective-permute-start.17 = (bf16[64,1024]{1,0:T(8,128)(2,1)S(1)}, bf16[64,1024]{1,0:T(8,128)(2,1)S(1)}, u32[]{:S(2)}, u32[]{:S(2)}) collective-permute-start(bf16[64,1024]{1,0:T(8,128)(2,1)S(1)} %get-tuple-element.71), channel_id=1, source_target_pairs={{0,16},{2,18},{4,20},{6,22},{8,24},{10,26},{12,28},{14,30},{16,0},... | collective-permute-start | bytes 393224 | tf_op jit(solution)/shard_map/ppermute | solution.py:34
  55.8 1.5 %collective-permute-start.18 = (bf16[64,1024]{1,0:T(8,128)(2,1)S(1)}, bf16[64,1024]{1,0:T(8,128)(2,1)S(1)}, u32[]{:S(2)}, u32[]{:S(2)}) collective-permute-start(bf16[64,1024]{1,0:T(8,128)(2,1)S(1)} %get-tuple-element.72), channel_id=1, source_target_pairs={{0,24},{2,26},{4,28},{6,30},{8,16},{10,18},{12,20},{14,22},{16,8},... | collective-permute-start | bytes 393224 | tf_op jit(solution)/shard_map/ppermute | solution.py:34
  57.2 2.9 %collective-permute-done.16.refs_1_ = bf16[64,1024]{1,0:T(8,128)(2,1)S(1)} collective-permute-done((bf16[64,1024]{1,0:T(8,128)(2,1)S(1)}, bf16[64,1024]{1,0:T(8,128)(2,1)S(1)}, u32[]{:S(2)}, u32[]{:S(2)}) %collective-permute-start.16) | collective-permute-done | bytes 131104 | tf_op jit(solution)/shard_map/ppermute | solution.py:34
  60.1 1.7 %collective-permute-done.18.refs_3_ = bf16[64,1024]{1,0:T(8,128)(2,1)S(1)} collective-permute-done((bf16[64,1024]{1,0:T(8,128)(2,1)S(1)}, bf16[64,1024]{1,0:T(8,128)(2,1)S(1)}, u32[]{:S(2)}, u32[]{:S(2)}) %collective-permute-start.18) | collective-permute-done | bytes 131104 | tf_op jit(solution)/shard_map/ppermute | solution.py:34
  62.0 1.4 %collective-permute-start.20 = (bf16[64,1024]{1,0:T(8,128)(2,1)S(1)}, bf16[64,1024]{1,0:T(8,128)(2,1)S(1)}, u32[]{:S(2)}, u32[]{:S(2)}) collective-permute-start(bf16[64,1024]{1,0:T(8,128)(2,1)S(1)} %shard_map.119.refs_0_), channel_id=1, source_target_pairs={{0,4},{2,6},{4,0},{6,2},{8,12},{10,14},{12,8},{14,10},{16,20},{18,... | collective-permute-start | bytes 393224 | tf_op jit(solution)/shard_map/ppermute | solution.py:34
  63.4 1.3 %shard_map.120 = bf16[8,4,4,512]{3,2,1,0:T(4,128)(2,1)} custom-call(bf16[128,768]{1,0:T(8,128)(2,1)S(1)} %get-tuple-element.75.mine, bf16[128,768]{1,0:T(8,128)(2,1)S(1)} %collective-permute-done.19.pair, bf16[256,512]{1,0:T(8,128)(2,1)S(1)} %copy-done.1, bf16[256,512]{1,0:T(8,128)(2,1)S(1)} %collective-permute-done.2.wq1, bf16[256,512]{1,0:T(8,128)(2,1)S(1)} %copy-done.3, ...), custom_call_target="tpu_custom_call" | custom-call | flops 201326592 | bytes 1000000 | tf_op jit(solution)/shard_map/pallas_call | solution.py:55
  64.7 5.1 %collective-permute-done.20.refs_1_ = bf16[64,1024]{1,0:T(8,128)(2,1)S(1)} collective-permute-done((bf16[64,1024]{1,0:T(8,128)(2,1)S(1)}, bf16[64,1024]{1,0:T(8,128)(2,1)S(1)}, u32[]{:S(2)}, u32[]{:S(2)}) %collective-permute-start.20) | collective-permute-done | bytes 131104 | tf_op jit(solution)/shard_map/ppermute | solution.py:34
  69.8 1.8 %collective-permute-start.24 = (bf16[64,1024]{1,0:T(8,128)(2,1)S(1)}, bf16[64,1024]{1,0:T(8,128)(2,1)S(1)}, u32[]{:S(2)}, u32[]{:S(2)}) collective-permute-start(bf16[64,1024]{1,0:T(8,128)(2,1)S(1)} %shard_map.121.refs_0_), channel_id=1, source_target_pairs={{0,16},{2,18},{4,20},{6,22},{8,24},{10,26},{12,28},{14,30},{16,0},... | collective-permute-start | bytes 393224 | tf_op jit(solution)/shard_map/ppermute | solution.py:34
  71.6 3.2 %collective-permute-done.24.refs_4_ = bf16[64,1024]{1,0:T(8,128)(2,1)S(1)} collective-permute-done((bf16[64,1024]{1,0:T(8,128)(2,1)S(1)}, bf16[64,1024]{1,0:T(8,128)(2,1)S(1)}, u32[]{:S(2)}, u32[]{:S(2)}) %collective-permute-start.24) | collective-permute-done | bytes 131104 | tf_op jit(solution)/shard_map/ppermute | solution.py:34
  74.9 1.7 %collective-permute-start.26 = (bf16[64,1024]{1,0:T(8,128)(2,1)S(1)}, bf16[64,1024]{1,0:T(8,128)(2,1)S(1)}, u32[]{:S(2)}, u32[]{:S(2)}) collective-permute-start(bf16[64,1024]{1,0:T(8,128)(2,1)S(1)} %collective-permute-done.24.refs_4_), channel_id=1, source_target_pairs={{0,8},{2,10},{4,12},{6,14},{8,0},{10,2},{12,4},{14,6},{16,24},{18,... | collective-permute-start | bytes 393224 | tf_op jit(solution)/shard_map/ppermute | solution.py:34
  77.7 2.1 %collective-permute-start.25 = (bf16[64,1024]{1,0:T(8,128)(2,1)S(1)}, bf16[64,1024]{1,0:T(8,128)(2,1)S(1)}, u32[]{:S(2)}, u32[]{:S(2)}) collective-permute-start(bf16[64,1024]{1,0:T(8,128)(2,1)S(1)} %collective-permute-done.21.refs_1_), channel_id=1, source_target_pairs={{0,16},{2,18},{4,20},{6,22},{8,24},{10,26},{12,28},{14,30},{16,0},... | collective-permute-start | bytes 393224 | tf_op jit(solution)/shard_map/ppermute | solution.py:34
  79.8 3.4 %collective-permute-done.23.refs_3_ = bf16[64,1024]{1,0:T(8,128)(2,1)S(1)} collective-permute-done((bf16[64,1024]{1,0:T(8,128)(2,1)S(1)}, bf16[64,1024]{1,0:T(8,128)(2,1)S(1)}, u32[]{:S(2)}, u32[]{:S(2)}) %collective-permute-start.23) | collective-permute-done | bytes 131104 | tf_op jit(solution)/shard_map/ppermute | solution.py:34
  83.2 1.6 %collective-permute-done.27.refs_7_ = bf16[64,1024]{1,0:T(8,128)(2,1)S(1)} collective-permute-done((bf16[64,1024]{1,0:T(8,128)(2,1)S(1)}, bf16[64,1024]{1,0:T(8,128)(2,1)S(1)}, u32[]{:S(2)}, u32[]{:S(2)}) %collective-permute-start.27) | collective-permute-done | bytes 131104 | tf_op jit(solution)/shard_map/ppermute | solution.py:34
  84.8 1.5 %shard_map.122 = (f32[256,512]{1,0:T(8,128)}, f32[256,512]{1,0:T(8,128)}, f32[256,512]{1,0:T(8,128)}, f32[256,512]{1,0:T(8,128)}) custom-call(bf16[64,1024]{1,0:T(8,128)(2,1)S(1)} %shard_map.121.refs_0_, bf16[64,1024]{1,0:T(8,128)(2,1)S(1)} %collective-permute-done.21.refs_1_, bf16[64,1024]{1,0:T(8,128)(2,1)S(1)} %collective-permute-done.22.refs_2_, ...), custom_call_target="tpu_custom_call" | custom-call | flops 1000000 | bytes 1000000 | tf_op jit(solution)/shard_map/pallas_call | solution.py:55
  (56 shorter events, 10.1 us)
Async XLA Ops:
  0.6 21.8 %copy-start.6 = (bf16[256,512]{1,0:T(8,128)(2,1)S(1)}, bf16[256,512]{1,0:T(8,128)(2,1)}, u32[]{:S(2)}) copy-start(bf16[256,512]{1,0:T(8,128)(2,1)} %wout.1) | copy-start | bytes 786436
  0.6 5.1 %collective-permute-start.2 = (bf16[256,512]{1,0:T(8,128)(2,1)}, bf16[256,512]{1,0:T(8,128)(2,1)S(1)}, u32[]{:S(2)}, u32[]{:S(2)}) collective-permute-start(bf16[256,512]{1,0:T(8,128)(2,1)} %wq0.3), channel_id=1, source_target_pairs={{0,1},{1,0},{2,3},{3,2},{4,5},{5,4},{6,7},{7,6},{8,9},{9,8},{10,11... | collective-permute-start | bytes 786440 | tf_op jit(solution)/shard_map/ppermute | solution.py:20
  1.2 4.6 %collective-permute-start.3 = (bf16[256,512]{1,0:T(8,128)(2,1)}, bf16[256,512]{1,0:T(8,128)(2,1)S(1)}, u32[]{:S(2)}, u32[]{:S(2)}) collective-permute-start(bf16[256,512]{1,0:T(8,128)(2,1)} %wk0.3), channel_id=1, source_target_pairs={{0,1},{1,0},{2,3},{3,2},{4,5},{5,4},{6,7},{7,6},{8,9},{9,8},{10,11... | collective-permute-start | bytes 786440 | tf_op jit(solution)/shard_map/ppermute | solution.py:20
  1.2 4.5 %collective-permute-start.4 = (bf16[256,512]{1,0:T(8,128)(2,1)}, bf16[256,512]{1,0:T(8,128)(2,1)S(1)}, u32[]{:S(2)}, u32[]{:S(2)}) collective-permute-start(bf16[256,512]{1,0:T(8,128)(2,1)} %wv0.3), channel_id=1, source_target_pairs={{0,1},{1,0},{2,3},{3,2},{4,5},{5,4},{6,7},{7,6},{8,9},{9,8},{10,11... | collective-permute-start | bytes 786440 | tf_op jit(solution)/shard_map/ppermute | solution.py:20
  2.6 6.1 %collective-permute-start.1 = (bf16[128,512]{1,0:T(8,128)(2,1)S(1)}, bf16[128,512]{1,0:T(8,128)(2,1)S(1)}, u32[]{:S(2)}, u32[]{:S(2)}) collective-permute-start(bf16[128,512]{1,0:T(8,128)(2,1)S(1)} %reshape.13.own.f_own), channel_id=1, source_target_pairs={{0,1},{1,0},{2,3},{3,2},{4,5},{5,4},{6,7},{7,6},{8,9},{9,8},{10,11... | collective-permute-start | bytes 393224 | tf_op jit(solution)/shard_map/ppermute | solution.py:20
  2.8 6.7 %collective-permute-start = (bf16[128,512]{1,0:T(8,128)(2,1)S(1)}, bf16[128,512]{1,0:T(8,128)(2,1)S(1)}, u32[]{:S(2)}, u32[]{:S(2)}) collective-permute-start(bf16[128,512]{1,0:T(8,128)(2,1)S(1)} %reshape.13.own.f_own), channel_id=1, source_target_pairs={{0,2},{2,0},{4,6},{6,4},{1,3},{3,1},{5,7},{7,5},{8,10},{10,8},{12,... | collective-permute-start | bytes 393224 | tf_op jit(solution)/shard_map/ppermute | solution.py:20
  9.5 1.3 %collective-permute-start.5 = (bf16[128,512]{1,0:T(8,128)(2,1)S(1)}, bf16[128,512]{1,0:T(8,128)(2,1)S(1)}, u32[]{:S(2)}, u32[]{:S(2)}) collective-permute-start(bf16[128,512]{1,0:T(8,128)(2,1)S(1)} %collective-permute-done.pair.f_pair), channel_id=1, source_target_pairs={{0,1},{1,0},{2,3},{3,2},{4,5},{5,4},{6,7},{7,6},{8,9},{9,8},{10,11... | collective-permute-start | bytes 393224 | tf_op jit(solution)/shard_map/ppermute | solution.py:20
  11.4 9.6 %collective-permute-start.7 = (bf16[128,768]{1,0:T(8,128)(2,1)S(1)}, bf16[128,768]{1,0:T(8,128)(2,1)S(1)}, u32[]{:S(2)}, u32[]{:S(2)}) collective-permute-start(bf16[128,768]{1,0:T(8,128)(2,1)S(1)} %get-tuple-element.52), channel_id=1, source_target_pairs={{0,2},{2,0},{4,6},{6,4},{1,3},{3,1},{5,7},{7,5},{8,10},{10,8},{12,... | collective-permute-start | bytes 589832 | tf_op jit(solution)/shard_map/ppermute | solution.py:20
  13.2 10.1 %collective-permute-start.9 = (bf16[512,256]{1,0:T(8,128)(2,1)S(1)}, bf16[512,256]{1,0:T(8,128)(2,1)S(1)}, u32[]{:S(2)}, u32[]{:S(2)}) collective-permute-start(bf16[512,256]{1,0:T(8,128)(2,1)S(1)} %get-tuple-element.55.refs_0_.refs_6_), channel_id=1, source_target_pairs={{0,8},{8,16},{16,24},{24,0},{1,9},{9,17},{17,25},{25,1},{2,10},{10... | collective-permute-start | bytes 786440 | tf_op jit(solution)/shard_map/ppermute | solution.py:25
  14.7 14.4 %collective-permute-start.11 = (bf16[512,256]{1,0:T(8,128)(2,1)S(1)}, bf16[512,256]{1,0:T(8,128)(2,1)S(1)}, u32[]{:S(2)}, u32[]{:S(2)}) collective-permute-start(bf16[512,256]{1,0:T(8,128)(2,1)S(1)} %get-tuple-element.55.refs_0_.refs_6_), channel_id=1, source_target_pairs={{0,4},{2,6},{4,0},{6,2},{1,5},{3,7},{5,1},{7,3},{8,12},{10,14},{12... | collective-permute-start | bytes 786440 | tf_op jit(solution)/shard_map/ppermute | solution.py:25
  17.3 11.8 %collective-permute-start.10 = (bf16[512,256]{1,0:T(8,128)(2,1)S(1)}, bf16[512,256]{1,0:T(8,128)(2,1)S(1)}, u32[]{:S(2)}, u32[]{:S(2)}) collective-permute-start(bf16[512,256]{1,0:T(8,128)(2,1)S(1)} %get-tuple-element.55.refs_0_.refs_6_), channel_id=1, source_target_pairs={{0,24},{8,0},{16,8},{24,16},{1,25},{9,1},{17,9},{25,17},{2,26},{10... | collective-permute-start | bytes 786440 | tf_op jit(solution)/shard_map/ppermute | solution.py:25
  18.7 2.3 %collective-permute-start.6 = (bf16[128,768]{1,0:T(8,128)(2,1)S(1)}, bf16[128,768]{1,0:T(8,128)(2,1)S(1)}, u32[]{:S(2)}, u32[]{:S(2)}) collective-permute-start(bf16[128,768]{1,0:T(8,128)(2,1)S(1)} %get-tuple-element.51.own), channel_id=1, source_target_pairs={{0,1},{1,0},{2,3},{3,2},{4,5},{5,4},{6,7},{7,6},{8,9},{9,8},{10,11... | collective-permute-start | bytes 589832 | tf_op jit(solution)/shard_map/ppermute | solution.py:20
  21.0 1.4 %collective-permute-start.8 = (bf16[128,768]{1,0:T(8,128)(2,1)S(1)}, bf16[128,768]{1,0:T(8,128)(2,1)S(1)}, u32[]{:S(2)}, u32[]{:S(2)}) collective-permute-start(bf16[128,768]{1,0:T(8,128)(2,1)S(1)} %collective-permute-done.7.pair), channel_id=1, source_target_pairs={{0,1},{1,0},{2,3},{3,2},{4,5},{5,4},{6,7},{7,6},{8,9},{9,8},{10,11... | collective-permute-start | bytes 589832 | tf_op jit(solution)/shard_map/ppermute | solution.py:20
  34.6 28.7 %copy-start.1 = (bf16[256,512]{1,0:T(8,128)(2,1)S(1)}, bf16[256,512]{1,0:T(8,128)(2,1)}, u32[]{:S(2)}) copy-start(bf16[256,512]{1,0:T(8,128)(2,1)} %wq0.3) | copy-start | bytes 786436
  34.6 28.7 %copy-start.3 = (bf16[256,512]{1,0:T(8,128)(2,1)S(1)}, bf16[256,512]{1,0:T(8,128)(2,1)}, u32[]{:S(2)}) copy-start(bf16[256,512]{1,0:T(8,128)(2,1)} %wk0.3) | copy-start | bytes 786436
  34.6 28.7 %copy-start.5 = (bf16[256,512]{1,0:T(8,128)(2,1)S(1)}, bf16[256,512]{1,0:T(8,128)(2,1)}, u32[]{:S(2)}) copy-start(bf16[256,512]{1,0:T(8,128)(2,1)} %wv0.3) | copy-start | bytes 786436
  34.6 13.5 %collective-permute-start.12 = (bf16[512,256]{1,0:T(8,128)(2,1)S(1)}, bf16[512,256]{1,0:T(8,128)(2,1)S(1)}, u32[]{:S(2)}, u32[]{:S(2)}) collective-permute-start(bf16[512,256]{1,0:T(8,128)(2,1)S(1)} %get-tuple-element.63), channel_id=1, source_target_pairs={{0,4},{2,6},{4,0},{6,2},{1,5},{3,7},{5,1},{7,3},{8,12},{10,14},{12... | collective-permute-start | bytes 786440 | tf_op jit(solution)/shard_map/ppermute | solution.py:25
  36.1 12.1 %collective-permute-start.13 = (bf16[512,256]{1,0:T(8,128)(2,1)S(1)}, bf16[512,256]{1,0:T(8,128)(2,1)S(1)}, u32[]{:S(2)}, u32[]{:S(2)}) collective-permute-start(bf16[512,256]{1,0:T(8,128)(2,1)S(1)} %get-tuple-element.64), channel_id=1, source_target_pairs={{0,8},{8,16},{16,24},{24,0},{1,9},{9,17},{17,25},{25,1},{2,10},{10... | collective-permute-start | bytes 786440 | tf_op jit(solution)/shard_map/ppermute | solution.py:25
  37.6 11.0 %collective-permute-start.14 = (bf16[512,256]{1,0:T(8,128)(2,1)S(1)}, bf16[512,256]{1,0:T(8,128)(2,1)S(1)}, u32[]{:S(2)}, u32[]{:S(2)}) collective-permute-start(bf16[512,256]{1,0:T(8,128)(2,1)S(1)} %get-tuple-element.65), channel_id=1, source_target_pairs={{0,24},{8,0},{16,8},{24,16},{1,25},{9,1},{17,9},{25,17},{2,26},{10... | collective-permute-start | bytes 786440 | tf_op jit(solution)/shard_map/ppermute | solution.py:25
  48.8 1.8 %collective-permute-start.15 = (bf16[512,384]{1,0:T(8,128)(2,1)S(1)}, bf16[512,384]{1,0:T(8,128)(2,1)S(1)}, u32[]{:S(2)}, u32[]{:S(2)}) collective-permute-start(bf16[512,384]{1,0:T(8,128)(2,1)S(1)} %shard_map.117.own), channel_id=1, source_target_pairs={{0,1},{1,0},{2,3},{3,2},{4,5},{5,4},{6,7},{7,6},{8,9},{9,8},{10,11... | collective-permute-start | bytes 1179656 | tf_op jit(solution)/shard_map/ppermute | solution.py:20
  51.2 10.8 %collective-permute-start.19 = (bf16[128,768]{1,0:T(8,128)(2,1)S(1)}, bf16[128,768]{1,0:T(8,128)(2,1)S(1)}, u32[]{:S(2)}, u32[]{:S(2)}) collective-permute-start(bf16[128,768]{1,0:T(8,128)(2,1)S(1)} %get-tuple-element.73), channel_id=1, source_target_pairs={{0,2},{2,0},{4,6},{6,4},{1,3},{3,1},{5,7},{7,5},{8,10},{10,8},{12,... | collective-permute-start | bytes 589832 | tf_op jit(solution)/shard_map/ppermute | solution.py:20
  53.8 6.4 %collective-permute-start.16 = (bf16[64,1024]{1,0:T(8,128)(2,1)S(1)}, bf16[64,1024]{1,0:T(8,128)(2,1)S(1)}, u32[]{:S(2)}, u32[]{:S(2)}) collective-permute-start(bf16[64,1024]{1,0:T(8,128)(2,1)S(1)} %get-tuple-element.70), channel_id=1, source_target_pairs={{0,8},{2,10},{4,12},{6,14},{8,0},{10,2},{12,4},{14,6},{16,24},{18,... | collective-permute-start | bytes 393224 | tf_op jit(solution)/shard_map/ppermute | solution.py:34
  54.1 6.1 %collective-permute-start.17 = (bf16[64,1024]{1,0:T(8,128)(2,1)S(1)}, bf16[64,1024]{1,0:T(8,128)(2,1)S(1)}, u32[]{:S(2)}, u32[]{:S(2)}) collective-permute-start(bf16[64,1024]{1,0:T(8,128)(2,1)S(1)} %get-tuple-element.71), channel_id=1, source_target_pairs={{0,16},{2,18},{4,20},{6,22},{8,24},{10,26},{12,28},{14,30},{16,0},... | collective-permute-start | bytes 393224 | tf_op jit(solution)/shard_map/ppermute | solution.py:34
  55.8 6.1 %collective-permute-start.18 = (bf16[64,1024]{1,0:T(8,128)(2,1)S(1)}, bf16[64,1024]{1,0:T(8,128)(2,1)S(1)}, u32[]{:S(2)}, u32[]{:S(2)}) collective-permute-start(bf16[64,1024]{1,0:T(8,128)(2,1)S(1)} %get-tuple-element.72), channel_id=1, source_target_pairs={{0,24},{2,26},{4,28},{6,30},{8,16},{10,18},{12,20},{14,22},{16,8},... | collective-permute-start | bytes 393224 | tf_op jit(solution)/shard_map/ppermute | solution.py:34
  62.0 7.8 %collective-permute-start.20 = (bf16[64,1024]{1,0:T(8,128)(2,1)S(1)}, bf16[64,1024]{1,0:T(8,128)(2,1)S(1)}, u32[]{:S(2)}, u32[]{:S(2)}) collective-permute-start(bf16[64,1024]{1,0:T(8,128)(2,1)S(1)} %shard_map.119.refs_0_), channel_id=1, source_target_pairs={{0,4},{2,6},{4,0},{6,2},{8,12},{10,14},{12,8},{14,10},{16,20},{18,... | collective-permute-start | bytes 393224 | tf_op jit(solution)/shard_map/ppermute | solution.py:34
  69.8 5.0 %collective-permute-start.24 = (bf16[64,1024]{1,0:T(8,128)(2,1)S(1)}, bf16[64,1024]{1,0:T(8,128)(2,1)S(1)}, u32[]{:S(2)}, u32[]{:S(2)}) collective-permute-start(bf16[64,1024]{1,0:T(8,128)(2,1)S(1)} %shard_map.121.refs_0_), channel_id=1, source_target_pairs={{0,16},{2,18},{4,20},{6,22},{8,24},{10,26},{12,28},{14,30},{16,0},... | collective-permute-start | bytes 393224 | tf_op jit(solution)/shard_map/ppermute | solution.py:34
  71.6 6.0 %collective-permute-start.22 = (bf16[64,1024]{1,0:T(8,128)(2,1)S(1)}, bf16[64,1024]{1,0:T(8,128)(2,1)S(1)}, u32[]{:S(2)}, u32[]{:S(2)}) collective-permute-start(bf16[64,1024]{1,0:T(8,128)(2,1)S(1)} %shard_map.121.refs_0_), channel_id=1, source_target_pairs={{0,8},{2,10},{4,12},{6,14},{8,0},{10,2},{12,4},{14,6},{16,24},{18,... | collective-permute-start | bytes 393224 | tf_op jit(solution)/shard_map/ppermute | solution.py:34
  71.6 6.1 %collective-permute-start.21 = (bf16[64,1024]{1,0:T(8,128)(2,1)S(1)}, bf16[64,1024]{1,0:T(8,128)(2,1)S(1)}, u32[]{:S(2)}, u32[]{:S(2)}) collective-permute-start(bf16[64,1024]{1,0:T(8,128)(2,1)S(1)} %shard_map.121.refs_0_), channel_id=1, source_target_pairs={{0,2},{2,0},{4,6},{6,4},{8,10},{10,8},{12,14},{14,12},{16,18},{18,... | collective-permute-start | bytes 393224 | tf_op jit(solution)/shard_map/ppermute | solution.py:34
  74.9 5.0 %collective-permute-start.26 = (bf16[64,1024]{1,0:T(8,128)(2,1)S(1)}, bf16[64,1024]{1,0:T(8,128)(2,1)S(1)}, u32[]{:S(2)}, u32[]{:S(2)}) collective-permute-start(bf16[64,1024]{1,0:T(8,128)(2,1)S(1)} %collective-permute-done.24.refs_4_), channel_id=1, source_target_pairs={{0,8},{2,10},{4,12},{6,14},{8,0},{10,2},{12,4},{14,6},{16,24},{18,... | collective-permute-start | bytes 393224 | tf_op jit(solution)/shard_map/ppermute | solution.py:34
  77.7 5.5 %collective-permute-start.23 = (bf16[64,1024]{1,0:T(8,128)(2,1)S(1)}, bf16[64,1024]{1,0:T(8,128)(2,1)S(1)}, u32[]{:S(2)}, u32[]{:S(2)}) collective-permute-start(bf16[64,1024]{1,0:T(8,128)(2,1)S(1)} %collective-permute-done.22.refs_2_), channel_id=1, source_target_pairs={{0,2},{2,0},{4,6},{6,4},{8,10},{10,8},{12,14},{14,12},{16,18},{18,... | collective-permute-start | bytes 393224 | tf_op jit(solution)/shard_map/ppermute | solution.py:34
  77.7 5.5 %collective-permute-start.25 = (bf16[64,1024]{1,0:T(8,128)(2,1)S(1)}, bf16[64,1024]{1,0:T(8,128)(2,1)S(1)}, u32[]{:S(2)}, u32[]{:S(2)}) collective-permute-start(bf16[64,1024]{1,0:T(8,128)(2,1)S(1)} %collective-permute-done.21.refs_1_), channel_id=1, source_target_pairs={{0,16},{2,18},{4,20},{6,22},{8,24},{10,26},{12,28},{14,30},{16,0},... | collective-permute-start | bytes 393224 | tf_op jit(solution)/shard_map/ppermute | solution.py:34
  79.8 5.0 %collective-permute-start.27 = (bf16[64,1024]{1,0:T(8,128)(2,1)S(1)}, bf16[64,1024]{1,0:T(8,128)(2,1)S(1)}, u32[]{:S(2)}, u32[]{:S(2)}) collective-permute-start(bf16[64,1024]{1,0:T(8,128)(2,1)S(1)} %collective-permute-done.26.refs_6_), channel_id=1, source_target_pairs={{0,2},{2,0},{4,6},{6,4},{8,10},{10,8},{12,14},{14,12},{16,18},{18,... | collective-permute-start | bytes 393224 | tf_op jit(solution)/shard_map/ppermute | solution.py:34
  (5 other events, 8.2 us)

commit v10 on v9

--- a/solution.py
+++ b/solution.py
@@ -175,9 +175,7 @@
     count = len(times)
     e_refs, ds_refs, tables = (refs[at : 3 * len(groups) : 3] for at in range(3))
     refs = refs[3 * len(groups) :]
-    kvs, dq_ref, outs, dq_s, part_s = (
-        refs[:count], refs[count], refs[count + 1 : 2 * count + 1], refs[-2], refs[-1]
-    )
+    part_s, outs = refs[0], refs[1:]
     where = [(group, at) for group, blocks in enumerate(groups) for at in range(blocks)]
     if part_s.shape[0] > 2 * count:
         part_s[...] = jnp.zeros_like(part_s)
@@ -195,29 +193,37 @@
         )
         for at in range(count):
             part_s[2 * at + head : 2 * at + head + 1, :] = lifts[at] / total
-    tokens = q_ref.shape[0]
+    turned = part_s[...].T
+    for at, (group, place) in enumerate(where):
+        if at > 0:
+            block_partials(turned, at, place, q_ref, do_ref, e_refs[group], ds_refs[group], outs[at - 1])
+
+
+def block_partials(turned, at, place, q_ref, do_ref, e_ref, ds_ref, out_ref):
+    scale = row_scale(turned, at, q_ref.shape[0])
+    q_scaled = by_head((q_ref[...].astype(F32) * scale).astype(BF))
+    g_scaled = by_head((do_ref[...].astype(F32) * scale).astype(BF))
+    dks, dvs = [], []
+    for head in range(2):
+        dvs.append(dot_nn(e_ref[2 * place + head], g_scaled[head]))
+        dks.append(dot_nn(ds_ref[2 * place + head], q_scaled[head]))
+    out_ref[:, 0:PART] = (dks[0] + dks[1]).astype(BF)
+    out_ref[:, PART:] = (dvs[0] + dvs[1]).astype(BF)
+
+
+def query_kernel(times, groups, part_ref, q_ref, do_ref, e_ref, *refs):
+    ds_refs, kvs = refs[: len(groups)], refs[len(groups) : -3]
+    dq_ref, own_ref, dq_s = refs[-3:]
+    block_partials(part_ref[...].T, 0, 0, q_ref, do_ref, e_ref, ds_refs[0], own_ref)
     head_dim = PART // 2
-    turned = part_s[...].T
-    grad = do_ref[...].astype(F32)
-    query = q_ref[...].astype(F32)
-    for at in range(count):
+    where = [(group, at) for group, blocks in enumerate(groups) for at in range(blocks)]
+    for at, (group, place) in enumerate(where):
         keys_t = kvs[at][:, 0:PART].astype(F32).T.astype(BF)
-        group, place = where[at]
-        scale = row_scale(turned, at, tokens)
-        q_scaled = by_head((query * scale).astype(BF))
-        g_scaled = by_head((grad * scale).astype(BF))
-        dks, dvs = [], []
         for head in range(2):
-            grown = e_refs[group][2 * place + head]
-            dscore = ds_refs[group][2 * place + head]
-            dvs.append(dot_nn(grown, g_scaled[head]))
-            dks.append(dot_nn(dscore, q_scaled[head]))
             spot = slice(head * head_dim, (head + 1) * head_dim)
-            part = part_s[2 * at + head : 2 * at + head + 1, :] * times[at]
-            added = dot_nn(keys_t[spot, :], dscore) * part
+            part = part_ref[2 * at + head : 2 * at + head + 1, :] * times[at]
+            added = dot_nn(keys_t[spot, :], ds_refs[group][2 * place + head]) * part
             dq_s[spot, :] = added if at == 0 else dq_s[spot, :] + added
-        outs[at][:, 0:PART] = (dks[0] + dks[1]).astype(BF)
-        outs[at][:, PART:] = (dvs[0] + dvs[1]).astype(BF)
     dq_ref[...] = (dq_s[...].T * (1.0 / math.sqrt(head_dim))).astype(BF)
 
 
@@ -401,21 +407,26 @@
             exps=pixels * blocks,
         )
         place += blocks
-    dq, *partials = call(
+    table = shape_of((-(-2 * count // 8) * 8, block_tokens), F32)
+    parts, *partials = call(
         functools.partial(gradient_kernel, times, groups),
-        (column, *[both] * count),
-        [query, out_grad, *scored, *near],
-        scratch=[
-            pltpu.VMEM((PART, block_tokens), F32),
-            pltpu.VMEM((-(-2 * count // 8) * 8, block_tokens), F32),
-        ],
-        flops=6 * pixels * count * PART,
+        (table, *[both] * (count - 1)),
+        [query, out_grad, *scored],
+        flops=4 * pixels * count * PART,
         moved=4 * pixels * count,
     )
+    dq, own_partial = call(
+        functools.partial(query_kernel, times, groups),
+        (column, both),
+        [parts, query, out_grad, scored[0], *scored[1::3], *near],
+        scratch=[pltpu.VMEM((PART, block_tokens), F32)],
+        flops=2 * pixels * count * PART,
+        moved=2 * pixels * count,
+    )
     back = []
-    for partial, (axis, step) in reversed(list(zip(partials[1:], routes))):
+    for partial, (axis, step) in reversed(list(zip(partials, routes))):
         back.append(shifted(partial, axis, -step))
-    back.append(partials[0])
+    back.append(own_partial)
     grads = call(
         functools.partial(collect_kernel, times[::-1]), shape_of((block_tokens, 3 * PART)), [dq, *back]
     )

time: 86.5 us -> 85.2 us (0.985)
  waiting for transfers between devices: 40.3 us -> 38.5 us
    ppermute x6, waiting for transfers between devices: 13.6 us -> 11.7 us  [shifted(): lax.ppermute(value, axis, [(source, (source + steps) % count) for source...]
    pallas_call x13 -> x14, Pallas kernels: 12.4 us -> 13 us  [call(): pl.pallas_call(kernel, out_shape=out_shape, in_specs=specs, scratch_shape...]
  transfers between devices with their start and end apart: 28 -> 28, of which waited for: 17 -> 17; matrix products, arithmetic and copies ran while one was open for 1% -> 1% of each run, Pallas kernels for 5% -> 7%
where the time goes in v10:
time: 85.2 us; the launch traced here: 85 us
  waiting for transfers between devices  38.5 us (45%)
  starting transfers between devices  29 us (34%)
  Pallas kernels  13 us (15%)
  local copies, waits for them, and re-layouts  3.81 us (4%)
    ppermute x11, waiting for transfers between devices, plane_swap(): return lax.ppermute(value, ('gx', 'gy'), route)  19.2 us
    pallas_call x14, Pallas kernels, call(): pl.pallas_call(kernel, out_shape=out_shape, in_specs=specs, scratch_shape...  13 us
    ppermute x6, waiting for transfers between devices, shifted(): lax.ppermute(value, axis, [(source, (source + steps) % count) for source...  11.7 us
    ppermute x11, starting transfers between devices, plane_swap(): return lax.ppermute(value, ('gx', 'gy'), route)  10.4 us
    ppermute x6, starting transfers between devices, shifted(): lax.ppermute(value, axis, [(source, (source + steps) % count) for source...  9.9 us
    ppermute x11, starting transfers between devices, from_partner(): return lax.ppermute(block, axis, route)  8.66 us
    ppermute x11, waiting for transfers between devices, from_partner(): return lax.ppermute(block, axis, route)  7.58 us
    unnamed x18, local copies, waits for them, and re-layouts  2.87 us
  transfers between devices with their start and end apart: 28, of which 17 were waited for; matrix products, arithmetic and copies ran while one was open for 1% of the time, Pallas kernels for 7%

profile of v10, /device:TPU:0, one launch (start us, length us, event | category | flops | bytes accessed | tf_op | source)
XLA Modules:
  0.0 85.0 jit_solution(18302841649280317696)
XLA Ops:
  2.8 3.0 %collective-permute-start = (bf16[128,512]{1,0:T(8,128)(2,1)S(1)}, bf16[128,512]{1,0:T(8,128)(2,1)S(1)}, u32[]{:S(2)}, u32[]{:S(2)}) collective-permute-start(bf16[128,512]{1,0:T(8,128)(2,1)S(1)} %reshape.13.own.f_own), channel_id=1, source_target_pairs={{0,2},{2,0},{4,6},{6,4},{1,3},{3,1},{5,7},{7,5},{8,10},{10,8},{12,... | collective-permute-start | bytes 393224 | tf_op jit(solution)/shard_map/ppermute | solution.py:20
  9.5 1.3 %collective-permute-done.5.far.f_far = bf16[128,512]{1,0:T(8,128)(2,1)S(1)} collective-permute-done((bf16[128,512]{1,0:T(8,128)(2,1)S(1)}, bf16[128,512]{1,0:T(8,128)(2,1)S(1)}, u32[]{:S(2)}, u32[]{:S(2)}) %collective-permute-start.5) | collective-permute-done | bytes 131104 | tf_op jit(solution)/shard_map/ppermute | solution.py:20
  11.4 1.8 %collective-permute-start.7 = (bf16[128,768]{1,0:T(8,128)(2,1)S(1)}, bf16[128,768]{1,0:T(8,128)(2,1)S(1)}, u32[]{:S(2)}, u32[]{:S(2)}) collective-permute-start(bf16[128,768]{1,0:T(8,128)(2,1)S(1)} %get-tuple-element.53), channel_id=1, source_target_pairs={{0,2},{2,0},{4,6},{6,4},{1,3},{3,1},{5,7},{7,5},{8,10},{10,8},{12,... | collective-permute-start | bytes 589832 | tf_op jit(solution)/shard_map/ppermute | solution.py:20
  13.2 1.5 %collective-permute-start.9 = (bf16[512,256]{1,0:T(8,128)(2,1)S(1)}, bf16[512,256]{1,0:T(8,128)(2,1)S(1)}, u32[]{:S(2)}, u32[]{:S(2)}) collective-permute-start(bf16[512,256]{1,0:T(8,128)(2,1)S(1)} %get-tuple-element.56.refs_0_.refs_2_), channel_id=1, source_target_pairs={{0,8},{8,16},{16,24},{24,0},{1,9},{9,17},{17,25},{25,1},{2,10},{10... | collective-permute-start | bytes 786440 | tf_op jit(solution)/shard_map/ppermute | solution.py:25
  14.7 2.6 %collective-permute-start.11 = (bf16[512,256]{1,0:T(8,128)(2,1)S(1)}, bf16[512,256]{1,0:T(8,128)(2,1)S(1)}, u32[]{:S(2)}, u32[]{:S(2)}) collective-permute-start(bf16[512,256]{1,0:T(8,128)(2,1)S(1)} %get-tuple-element.56.refs_0_.refs_2_), channel_id=1, source_target_pairs={{0,4},{2,6},{4,0},{6,2},{1,5},{3,7},{5,1},{7,3},{8,12},{10,14},{12... | collective-permute-start | bytes 786440 | tf_op jit(solution)/shard_map/ppermute | solution.py:25
  17.3 1.4 %collective-permute-start.10 = (bf16[512,256]{1,0:T(8,128)(2,1)S(1)}, bf16[512,256]{1,0:T(8,128)(2,1)S(1)}, u32[]{:S(2)}, u32[]{:S(2)}) collective-permute-start(bf16[512,256]{1,0:T(8,128)(2,1)S(1)} %get-tuple-element.56.refs_0_.refs_2_), channel_id=1, source_target_pairs={{0,24},{8,0},{16,8},{24,16},{1,25},{9,1},{17,9},{25,17},{2,26},{10... | collective-permute-start | bytes 786440 | tf_op jit(solution)/shard_map/ppermute | solution.py:25
  18.7 2.3 %collective-permute-done.7.pair = bf16[128,768]{1,0:T(8,128)(2,1)S(1)} collective-permute-done((bf16[128,768]{1,0:T(8,128)(2,1)S(1)}, bf16[128,768]{1,0:T(8,128)(2,1)S(1)}, u32[]{:S(2)}, u32[]{:S(2)}) %collective-permute-start.7) | collective-permute-done | bytes 196640 | tf_op jit(solution)/shard_map/ppermute | solution.py:20
  21.0 1.4 %collective-permute-done.8.far = bf16[128,768]{1,0:T(8,128)(2,1)S(1)} collective-permute-done((bf16[128,768]{1,0:T(8,128)(2,1)S(1)}, bf16[128,768]{1,0:T(8,128)(2,1)S(1)}, u32[]{:S(2)}, u32[]{:S(2)}) %collective-permute-start.8) | collective-permute-done | bytes 196640 | tf_op jit(solution)/shard_map/ppermute | solution.py:20
  23.3 2.1 %shard_map.114 = (bf16[4,512,512]{2,1,0:T(8,128)(2,1)S(1)}, bf16[4,512,512]{2,1,0:T(8,128)(2,1)S(1)}, f32[16,512]{1,0:T(8,128)S(1)}) custom-call(bf16[512,128]{1,0:T(8,128)(2,1)S(1)} %get-tuple-element.49.q_ref, bf16[512,128]{1,0:T(8,128)(2,1)S(1)} %get-tuple-element.54.do_ref, f32[2,512]{1,0:T(2,128)S(1)} %get-tuple-element.55.delta_ref, ...), custom_call_target="tpu_custom_call" | custom-call | flops 536870912 | bytes 4194304 | tf_op jit(solution)/shard_map/pallas_call | solution.py:55
  25.4 3.7 %collective-permute-done.11.refs_1_.refs_5_ = bf16[512,256]{1,0:T(8,128)(2,1)S(1)} collective-permute-done((bf16[512,256]{1,0:T(8,128)(2,1)S(1)}, bf16[512,256]{1,0:T(8,128)(2,1)S(1)}, u32[]{:S(2)}, u32[]{:S(2)}) %collective-permute-start.11) | collective-permute-done | bytes 262176 | tf_op jit(solution)/shard_map/ppermute | solution.py:25
  29.0 2.1 %shard_map.115 = (bf16[4,512,512]{2,1,0:T(8,128)(2,1)S(1)}, bf16[4,512,512]{2,1,0:T(8,128)(2,1)S(1)}, f32[16,512]{1,0:T(8,128)S(1)}) custom-call(bf16[512,128]{1,0:T(8,128)(2,1)S(1)} %get-tuple-element.49.q_ref, bf16[512,128]{1,0:T(8,128)(2,1)S(1)} %get-tuple-element.54.do_ref, f32[2,512]{1,0:T(2,128)S(1)} %get-tuple-element.55.delta_ref, ...), custom_call_target="tpu_custom_call" | custom-call | flops 536870912 | bytes 4194304 | tf_op jit(solution)/shard_map/pallas_call | solution.py:55
  31.1 2.2 %shard_map.116 = (f32[8,512]{1,0:T(8,128)S(1)}, bf16[512,256]{1,0:T(8,128)(2,1)S(1)}, bf16[512,256]{1,0:T(8,128)(2,1)S(1)}, bf16[512,256]{1,0:T(8,128)(2,1)S(1)}) custom-call(bf16[512,128]{1,0:T(8,128)(2,1)S(1)} %get-tuple-element.49.q_ref, bf16[512,128]{1,0:T(8,128)(2,1)S(1)} %get-tuple-element.54.do_ref, ...), custom_call_target="tpu_custom_call" | custom-call | flops 1073741824 | bytes 8388608 | tf_op jit(solution)/shard_map/pallas_call | solution.py:55
  33.3 1.5 %collective-permute-start.12 = (bf16[512,256]{1,0:T(8,128)(2,1)S(1)}, bf16[512,256]{1,0:T(8,128)(2,1)S(1)}, u32[]{:S(2)}, u32[]{:S(2)}) collective-permute-start(bf16[512,256]{1,0:T(8,128)(2,1)S(1)} %get-tuple-element.65), channel_id=1, source_target_pairs={{0,4},{2,6},{4,0},{6,2},{1,5},{3,7},{5,1},{7,3},{8,12},{10,14},{12... | collective-permute-start | bytes 786440 | tf_op jit(solution)/shard_map/ppermute | solution.py:25
  34.8 1.5 %collective-permute-start.13 = (bf16[512,256]{1,0:T(8,128)(2,1)S(1)}, bf16[512,256]{1,0:T(8,128)(2,1)S(1)}, u32[]{:S(2)}, u32[]{:S(2)}) collective-permute-start(bf16[512,256]{1,0:T(8,128)(2,1)S(1)} %get-tuple-element.66), channel_id=1, source_target_pairs={{0,8},{8,16},{16,24},{24,0},{1,9},{9,17},{17,25},{25,1},{2,10},{10... | collective-permute-start | bytes 786440 | tf_op jit(solution)/shard_map/ppermute | solution.py:25
  36.3 1.4 %collective-permute-start.14 = (bf16[512,256]{1,0:T(8,128)(2,1)S(1)}, bf16[512,256]{1,0:T(8,128)(2,1)S(1)}, u32[]{:S(2)}, u32[]{:S(2)}) collective-permute-start(bf16[512,256]{1,0:T(8,128)(2,1)S(1)} %get-tuple-element.67), channel_id=1, source_target_pairs={{0,24},{8,0},{16,8},{24,16},{1,25},{9,1},{17,9},{25,17},{2,26},{10... | collective-permute-start | bytes 786440 | tf_op jit(solution)/shard_map/ppermute | solution.py:25
  37.7 1.8 %shard_map.117 = (bf16[512,128]{1,0:T(8,128)(2,1)S(1)}, bf16[512,256]{1,0:T(8,128)(2,1)S(1)}) custom-call(f32[8,512]{1,0:T(8,128)S(1)} %get-tuple-element.63.part_ref, bf16[512,128]{1,0:T(8,128)(2,1)S(1)} %get-tuple-element.49.q_ref, bf16[512,128]{1,0:T(8,128)(2,1)S(1)} %get-tuple-element.54.do_ref, ...), custom_call_target="tpu_custom_call" | custom-call | flops 536870912 | bytes 4194304 | tf_op jit(solution)/shard_map/pallas_call | solution.py:55
  39.6 7.2 %collective-permute-done.12.refs_0_ = bf16[512,256]{1,0:T(8,128)(2,1)S(1)} collective-permute-done((bf16[512,256]{1,0:T(8,128)(2,1)S(1)}, bf16[512,256]{1,0:T(8,128)(2,1)S(1)}, u32[]{:S(2)}, u32[]{:S(2)}) %collective-permute-start.12) | collective-permute-done | bytes 262176 | tf_op jit(solution)/shard_map/ppermute | solution.py:25
  47.6 1.7 %collective-permute-done.15.core = bf16[512,384]{1,0:T(8,128)(2,1)S(1)} collective-permute-done((bf16[512,384]{1,0:T(8,128)(2,1)S(1)}, bf16[512,384]{1,0:T(8,128)(2,1)S(1)}, u32[]{:S(2)}, u32[]{:S(2)}) %collective-permute-start.15) | collective-permute-done | bytes 393248 | tf_op jit(solution)/shard_map/ppermute | solution.py:20
  49.9 2.6 %collective-permute-start.19 = (bf16[128,768]{1,0:T(8,128)(2,1)S(1)}, bf16[128,768]{1,0:T(8,128)(2,1)S(1)}, u32[]{:S(2)}, u32[]{:S(2)}) collective-permute-start(bf16[128,768]{1,0:T(8,128)(2,1)S(1)} %get-tuple-element.75), channel_id=1, source_target_pairs={{0,2},{2,0},{4,6},{6,4},{1,3},{3,1},{5,7},{7,5},{8,10},{10,8},{12,... | collective-permute-start | bytes 589832 | tf_op jit(solution)/shard_map/ppermute | solution.py:20
  52.8 1.7 %collective-permute-start.17 = (bf16[64,1024]{1,0:T(8,128)(2,1)S(1)}, bf16[64,1024]{1,0:T(8,128)(2,1)S(1)}, u32[]{:S(2)}, u32[]{:S(2)}) collective-permute-start(bf16[64,1024]{1,0:T(8,128)(2,1)S(1)} %get-tuple-element.73), channel_id=1, source_target_pairs={{0,16},{2,18},{4,20},{6,22},{8,24},{10,26},{12,28},{14,30},{16,0},... | collective-permute-start | bytes 393224 | tf_op jit(solution)/shard_map/ppermute | solution.py:34
  54.5 1.5 %collective-permute-start.18 = (bf16[64,1024]{1,0:T(8,128)(2,1)S(1)}, bf16[64,1024]{1,0:T(8,128)(2,1)S(1)}, u32[]{:S(2)}, u32[]{:S(2)}) collective-permute-start(bf16[64,1024]{1,0:T(8,128)(2,1)S(1)} %get-tuple-element.74), channel_id=1, source_target_pairs={{0,24},{2,26},{4,28},{6,30},{8,16},{10,18},{12,20},{14,22},{16,8},... | collective-permute-start | bytes 393224 | tf_op jit(solution)/shard_map/ppermute | solution.py:34
  56.0 2.9 %collective-permute-done.16.refs_1_ = bf16[64,1024]{1,0:T(8,128)(2,1)S(1)} collective-permute-done((bf16[64,1024]{1,0:T(8,128)(2,1)S(1)}, bf16[64,1024]{1,0:T(8,128)(2,1)S(1)}, u32[]{:S(2)}, u32[]{:S(2)}) %collective-permute-start.16) | collective-permute-done | bytes 131104 | tf_op jit(solution)/shard_map/ppermute | solution.py:34
  58.8 1.7 %collective-permute-done.18.refs_3_ = bf16[64,1024]{1,0:T(8,128)(2,1)S(1)} collective-permute-done((bf16[64,1024]{1,0:T(8,128)(2,1)S(1)}, bf16[64,1024]{1,0:T(8,128)(2,1)S(1)}, u32[]{:S(2)}, u32[]{:S(2)}) %collective-permute-start.18) | collective-permute-done | bytes 131104 | tf_op jit(solution)/shard_map/ppermute | solution.py:34
  60.7 1.4 %collective-permute-start.20 = (bf16[64,1024]{1,0:T(8,128)(2,1)S(1)}, bf16[64,1024]{1,0:T(8,128)(2,1)S(1)}, u32[]{:S(2)}, u32[]{:S(2)}) collective-permute-start(bf16[64,1024]{1,0:T(8,128)(2,1)S(1)} %shard_map.120.refs_0_), channel_id=1, source_target_pairs={{0,4},{2,6},{4,0},{6,2},{8,12},{10,14},{12,8},{14,10},{16,20},{18,... | collective-permute-start | bytes 393224 | tf_op jit(solution)/shard_map/ppermute | solution.py:34
  63.4 5.1 %collective-permute-done.20.refs_1_ = bf16[64,1024]{1,0:T(8,128)(2,1)S(1)} collective-permute-done((bf16[64,1024]{1,0:T(8,128)(2,1)S(1)}, bf16[64,1024]{1,0:T(8,128)(2,1)S(1)}, u32[]{:S(2)}, u32[]{:S(2)}) %collective-permute-start.20) | collective-permute-done | bytes 131104 | tf_op jit(solution)/shard_map/ppermute | solution.py:34
  68.5 1.8 %collective-permute-start.24 = (bf16[64,1024]{1,0:T(8,128)(2,1)S(1)}, bf16[64,1024]{1,0:T(8,128)(2,1)S(1)}, u32[]{:S(2)}, u32[]{:S(2)}) collective-permute-start(bf16[64,1024]{1,0:T(8,128)(2,1)S(1)} %shard_map.122.refs_0_), channel_id=1, source_target_pairs={{0,16},{2,18},{4,20},{6,22},{8,24},{10,26},{12,28},{14,30},{16,0},... | collective-permute-start | bytes 393224 | tf_op jit(solution)/shard_map/ppermute | solution.py:34
  70.3 3.2 %collective-permute-done.24.refs_4_ = bf16[64,1024]{1,0:T(8,128)(2,1)S(1)} collective-permute-done((bf16[64,1024]{1,0:T(8,128)(2,1)S(1)}, bf16[64,1024]{1,0:T(8,128)(2,1)S(1)}, u32[]{:S(2)}, u32[]{:S(2)}) %collective-permute-start.24) | collective-permute-done | bytes 131104 | tf_op jit(solution)/shard_map/ppermute | solution.py:34
  73.6 1.6 %collective-permute-start.26 = (bf16[64,1024]{1,0:T(8,128)(2,1)S(1)}, bf16[64,1024]{1,0:T(8,128)(2,1)S(1)}, u32[]{:S(2)}, u32[]{:S(2)}) collective-permute-start(bf16[64,1024]{1,0:T(8,128)(2,1)S(1)} %collective-permute-done.24.refs_4_), channel_id=1, source_target_pairs={{0,8},{2,10},{4,12},{6,14},{8,0},{10,2},{12,4},{14,6},{16,24},{18,... | collective-permute-start | bytes 393224 | tf_op jit(solution)/shard_map/ppermute | solution.py:34
  76.4 2.1 %collective-permute-start.25 = (bf16[64,1024]{1,0:T(8,128)(2,1)S(1)}, bf16[64,1024]{1,0:T(8,128)(2,1)S(1)}, u32[]{:S(2)}, u32[]{:S(2)}) collective-permute-start(bf16[64,1024]{1,0:T(8,128)(2,1)S(1)} %collective-permute-done.21.refs_1_), channel_id=1, source_target_pairs={{0,16},{2,18},{4,20},{6,22},{8,24},{10,26},{12,28},{14,30},{16,0},... | collective-permute-start | bytes 393224 | tf_op jit(solution)/shard_map/ppermute | solution.py:34
  78.5 3.4 %collective-permute-done.23.refs_3_ = bf16[64,1024]{1,0:T(8,128)(2,1)S(1)} collective-permute-done((bf16[64,1024]{1,0:T(8,128)(2,1)S(1)}, bf16[64,1024]{1,0:T(8,128)(2,1)S(1)}, u32[]{:S(2)}, u32[]{:S(2)}) %collective-permute-start.23) | collective-permute-done | bytes 131104 | tf_op jit(solution)/shard_map/ppermute | solution.py:34
  81.9 1.6 %collective-permute-done.27.refs_7_ = bf16[64,1024]{1,0:T(8,128)(2,1)S(1)} collective-permute-done((bf16[64,1024]{1,0:T(8,128)(2,1)S(1)}, bf16[64,1024]{1,0:T(8,128)(2,1)S(1)}, u32[]{:S(2)}, u32[]{:S(2)}) %collective-permute-start.27) | collective-permute-done | bytes 131104 | tf_op jit(solution)/shard_map/ppermute | solution.py:34
  83.5 1.5 %shard_map.123 = (f32[256,512]{1,0:T(8,128)}, f32[256,512]{1,0:T(8,128)}, f32[256,512]{1,0:T(8,128)}, f32[256,512]{1,0:T(8,128)}) custom-call(bf16[64,1024]{1,0:T(8,128)(2,1)S(1)} %shard_map.122.refs_0_, bf16[64,1024]{1,0:T(8,128)(2,1)S(1)} %collective-permute-done.21.refs_1_, bf16[64,1024]{1,0:T(8,128)(2,1)S(1)} %collective-permute-done.22.refs_2_, ...), custom_call_target="tpu_custom_call" | custom-call | flops 1000000 | bytes 1000000 | tf_op jit(solution)/shard_map/pallas_call | solution.py:55
  (57 shorter events, 11.5 us)
Async XLA Ops:
  0.6 21.8 %copy-start.6 = (bf16[256,512]{1,0:T(8,128)(2,1)S(1)}, bf16[256,512]{1,0:T(8,128)(2,1)}, u32[]{:S(2)}) copy-start(bf16[256,512]{1,0:T(8,128)(2,1)} %wout.1) | copy-start | bytes 786436
  0.6 5.1 %collective-permute-start.2 = (bf16[256,512]{1,0:T(8,128)(2,1)}, bf16[256,512]{1,0:T(8,128)(2,1)S(1)}, u32[]{:S(2)}, u32[]{:S(2)}) collective-permute-start(bf16[256,512]{1,0:T(8,128)(2,1)} %wq0.3), channel_id=1, source_target_pairs={{0,1},{1,0},{2,3},{3,2},{4,5},{5,4},{6,7},{7,6},{8,9},{9,8},{10,11... | collective-permute-start | bytes 786440 | tf_op jit(solution)/shard_map/ppermute | solution.py:20
  1.2 4.6 %collective-permute-start.3 = (bf16[256,512]{1,0:T(8,128)(2,1)}, bf16[256,512]{1,0:T(8,128)(2,1)S(1)}, u32[]{:S(2)}, u32[]{:S(2)}) collective-permute-start(bf16[256,512]{1,0:T(8,128)(2,1)} %wk0.3), channel_id=1, source_target_pairs={{0,1},{1,0},{2,3},{3,2},{4,5},{5,4},{6,7},{7,6},{8,9},{9,8},{10,11... | collective-permute-start | bytes 786440 | tf_op jit(solution)/shard_map/ppermute | solution.py:20
  1.2 4.5 %collective-permute-start.4 = (bf16[256,512]{1,0:T(8,128)(2,1)}, bf16[256,512]{1,0:T(8,128)(2,1)S(1)}, u32[]{:S(2)}, u32[]{:S(2)}) collective-permute-start(bf16[256,512]{1,0:T(8,128)(2,1)} %wv0.3), channel_id=1, source_target_pairs={{0,1},{1,0},{2,3},{3,2},{4,5},{5,4},{6,7},{7,6},{8,9},{9,8},{10,11... | collective-permute-start | bytes 786440 | tf_op jit(solution)/shard_map/ppermute | solution.py:20
  2.6 6.1 %collective-permute-start.1 = (bf16[128,512]{1,0:T(8,128)(2,1)S(1)}, bf16[128,512]{1,0:T(8,128)(2,1)S(1)}, u32[]{:S(2)}, u32[]{:S(2)}) collective-permute-start(bf16[128,512]{1,0:T(8,128)(2,1)S(1)} %reshape.13.own.f_own), channel_id=1, source_target_pairs={{0,1},{1,0},{2,3},{3,2},{4,5},{5,4},{6,7},{7,6},{8,9},{9,8},{10,11... | collective-permute-start | bytes 393224 | tf_op jit(solution)/shard_map/ppermute | solution.py:20
  2.8 6.7 %collective-permute-start = (bf16[128,512]{1,0:T(8,128)(2,1)S(1)}, bf16[128,512]{1,0:T(8,128)(2,1)S(1)}, u32[]{:S(2)}, u32[]{:S(2)}) collective-permute-start(bf16[128,512]{1,0:T(8,128)(2,1)S(1)} %reshape.13.own.f_own), channel_id=1, source_target_pairs={{0,2},{2,0},{4,6},{6,4},{1,3},{3,1},{5,7},{7,5},{8,10},{10,8},{12,... | collective-permute-start | bytes 393224 | tf_op jit(solution)/shard_map/ppermute | solution.py:20
  9.5 1.3 %collective-permute-start.5 = (bf16[128,512]{1,0:T(8,128)(2,1)S(1)}, bf16[128,512]{1,0:T(8,128)(2,1)S(1)}, u32[]{:S(2)}, u32[]{:S(2)}) collective-permute-start(bf16[128,512]{1,0:T(8,128)(2,1)S(1)} %collective-permute-done.pair.f_pair), channel_id=1, source_target_pairs={{0,1},{1,0},{2,3},{3,2},{4,5},{5,4},{6,7},{7,6},{8,9},{9,8},{10,11... | collective-permute-start | bytes 393224 | tf_op jit(solution)/shard_map/ppermute | solution.py:20
  11.4 9.6 %collective-permute-start.7 = (bf16[128,768]{1,0:T(8,128)(2,1)S(1)}, bf16[128,768]{1,0:T(8,128)(2,1)S(1)}, u32[]{:S(2)}, u32[]{:S(2)}) collective-permute-start(bf16[128,768]{1,0:T(8,128)(2,1)S(1)} %get-tuple-element.53), channel_id=1, source_target_pairs={{0,2},{2,0},{4,6},{6,4},{1,3},{3,1},{5,7},{7,5},{8,10},{10,8},{12,... | collective-permute-start | bytes 589832 | tf_op jit(solution)/shard_map/ppermute | solution.py:20
  13.2 10.1 %collective-permute-start.9 = (bf16[512,256]{1,0:T(8,128)(2,1)S(1)}, bf16[512,256]{1,0:T(8,128)(2,1)S(1)}, u32[]{:S(2)}, u32[]{:S(2)}) collective-permute-start(bf16[512,256]{1,0:T(8,128)(2,1)S(1)} %get-tuple-element.56.refs_0_.refs_2_), channel_id=1, source_target_pairs={{0,8},{8,16},{16,24},{24,0},{1,9},{9,17},{17,25},{25,1},{2,10},{10... | collective-permute-start | bytes 786440 | tf_op jit(solution)/shard_map/ppermute | solution.py:25
  14.7 14.4 %collective-permute-start.11 = (bf16[512,256]{1,0:T(8,128)(2,1)S(1)}, bf16[512,256]{1,0:T(8,128)(2,1)S(1)}, u32[]{:S(2)}, u32[]{:S(2)}) collective-permute-start(bf16[512,256]{1,0:T(8,128)(2,1)S(1)} %get-tuple-element.56.refs_0_.refs_2_), channel_id=1, source_target_pairs={{0,4},{2,6},{4,0},{6,2},{1,5},{3,7},{5,1},{7,3},{8,12},{10,14},{12... | collective-permute-start | bytes 786440 | tf_op jit(solution)/shard_map/ppermute | solution.py:25
  17.3 11.8 %collective-permute-start.10 = (bf16[512,256]{1,0:T(8,128)(2,1)S(1)}, bf16[512,256]{1,0:T(8,128)(2,1)S(1)}, u32[]{:S(2)}, u32[]{:S(2)}) collective-permute-start(bf16[512,256]{1,0:T(8,128)(2,1)S(1)} %get-tuple-element.56.refs_0_.refs_2_), channel_id=1, source_target_pairs={{0,24},{8,0},{16,8},{24,16},{1,25},{9,1},{17,9},{25,17},{2,26},{10... | collective-permute-start | bytes 786440 | tf_op jit(solution)/shard_map/ppermute | solution.py:25
  18.7 2.3 %collective-permute-start.6 = (bf16[128,768]{1,0:T(8,128)(2,1)S(1)}, bf16[128,768]{1,0:T(8,128)(2,1)S(1)}, u32[]{:S(2)}, u32[]{:S(2)}) collective-permute-start(bf16[128,768]{1,0:T(8,128)(2,1)S(1)} %get-tuple-element.52.own), channel_id=1, source_target_pairs={{0,1},{1,0},{2,3},{3,2},{4,5},{5,4},{6,7},{7,6},{8,9},{9,8},{10,11... | collective-permute-start | bytes 589832 | tf_op jit(solution)/shard_map/ppermute | solution.py:20
  21.0 1.4 %collective-permute-start.8 = (bf16[128,768]{1,0:T(8,128)(2,1)S(1)}, bf16[128,768]{1,0:T(8,128)(2,1)S(1)}, u32[]{:S(2)}, u32[]{:S(2)}) collective-permute-start(bf16[128,768]{1,0:T(8,128)(2,1)S(1)} %collective-permute-done.7.pair), channel_id=1, source_target_pairs={{0,1},{1,0},{2,3},{3,2},{4,5},{5,4},{6,7},{7,6},{8,9},{9,8},{10,11... | collective-permute-start | bytes 589832 | tf_op jit(solution)/shard_map/ppermute | solution.py:20
  33.3 13.5 %collective-permute-start.12 = (bf16[512,256]{1,0:T(8,128)(2,1)S(1)}, bf16[512,256]{1,0:T(8,128)(2,1)S(1)}, u32[]{:S(2)}, u32[]{:S(2)}) collective-permute-start(bf16[512,256]{1,0:T(8,128)(2,1)S(1)} %get-tuple-element.65), channel_id=1, source_target_pairs={{0,4},{2,6},{4,0},{6,2},{1,5},{3,7},{5,1},{7,3},{8,12},{10,14},{12... | collective-permute-start | bytes 786440 | tf_op jit(solution)/shard_map/ppermute | solution.py:25
  34.8 12.1 %collective-permute-start.13 = (bf16[512,256]{1,0:T(8,128)(2,1)S(1)}, bf16[512,256]{1,0:T(8,128)(2,1)S(1)}, u32[]{:S(2)}, u32[]{:S(2)}) collective-permute-start(bf16[512,256]{1,0:T(8,128)(2,1)S(1)} %get-tuple-element.66), channel_id=1, source_target_pairs={{0,8},{8,16},{16,24},{24,0},{1,9},{9,17},{17,25},{25,1},{2,10},{10... | collective-permute-start | bytes 786440 | tf_op jit(solution)/shard_map/ppermute | solution.py:25
  36.3 11.0 %collective-permute-start.14 = (bf16[512,256]{1,0:T(8,128)(2,1)S(1)}, bf16[512,256]{1,0:T(8,128)(2,1)S(1)}, u32[]{:S(2)}, u32[]{:S(2)}) collective-permute-start(bf16[512,256]{1,0:T(8,128)(2,1)S(1)} %get-tuple-element.67), channel_id=1, source_target_pairs={{0,24},{8,0},{16,8},{24,16},{1,25},{9,1},{17,9},{25,17},{2,26},{10... | collective-permute-start | bytes 786440 | tf_op jit(solution)/shard_map/ppermute | solution.py:25
  39.6 22.5 %copy-start.1 = (bf16[256,512]{1,0:T(8,128)(2,1)S(1)}, bf16[256,512]{1,0:T(8,128)(2,1)}, u32[]{:S(2)}) copy-start(bf16[256,512]{1,0:T(8,128)(2,1)} %wq0.3) | copy-start | bytes 786436
  39.6 22.5 %copy-start.3 = (bf16[256,512]{1,0:T(8,128)(2,1)S(1)}, bf16[256,512]{1,0:T(8,128)(2,1)}, u32[]{:S(2)}) copy-start(bf16[256,512]{1,0:T(8,128)(2,1)} %wk0.3) | copy-start | bytes 786436
  39.6 22.5 %copy-start.5 = (bf16[256,512]{1,0:T(8,128)(2,1)S(1)}, bf16[256,512]{1,0:T(8,128)(2,1)}, u32[]{:S(2)}) copy-start(bf16[256,512]{1,0:T(8,128)(2,1)} %wv0.3) | copy-start | bytes 786436
  47.5 1.8 %collective-permute-start.15 = (bf16[512,384]{1,0:T(8,128)(2,1)S(1)}, bf16[512,384]{1,0:T(8,128)(2,1)S(1)}, u32[]{:S(2)}, u32[]{:S(2)}) collective-permute-start(bf16[512,384]{1,0:T(8,128)(2,1)S(1)} %shard_map.118.own), channel_id=1, source_target_pairs={{0,1},{1,0},{2,3},{3,2},{4,5},{5,4},{6,7},{7,6},{8,9},{9,8},{10,11... | collective-permute-start | bytes 1179656 | tf_op jit(solution)/shard_map/ppermute | solution.py:20
  49.9 10.8 %collective-permute-start.19 = (bf16[128,768]{1,0:T(8,128)(2,1)S(1)}, bf16[128,768]{1,0:T(8,128)(2,1)S(1)}, u32[]{:S(2)}, u32[]{:S(2)}) collective-permute-start(bf16[128,768]{1,0:T(8,128)(2,1)S(1)} %get-tuple-element.75), channel_id=1, source_target_pairs={{0,2},{2,0},{4,6},{6,4},{1,3},{3,1},{5,7},{7,5},{8,10},{10,8},{12,... | collective-permute-start | bytes 589832 | tf_op jit(solution)/shard_map/ppermute | solution.py:20
  52.5 6.4 %collective-permute-start.16 = (bf16[64,1024]{1,0:T(8,128)(2,1)S(1)}, bf16[64,1024]{1,0:T(8,128)(2,1)S(1)}, u32[]{:S(2)}, u32[]{:S(2)}) collective-permute-start(bf16[64,1024]{1,0:T(8,128)(2,1)S(1)} %get-tuple-element.72), channel_id=1, source_target_pairs={{0,8},{2,10},{4,12},{6,14},{8,0},{10,2},{12,4},{14,6},{16,24},{18,... | collective-permute-start | bytes 393224 | tf_op jit(solution)/shard_map/ppermute | solution.py:34
  52.8 6.1 %collective-permute-start.17 = (bf16[64,1024]{1,0:T(8,128)(2,1)S(1)}, bf16[64,1024]{1,0:T(8,128)(2,1)S(1)}, u32[]{:S(2)}, u32[]{:S(2)}) collective-permute-start(bf16[64,1024]{1,0:T(8,128)(2,1)S(1)} %get-tuple-element.73), channel_id=1, source_target_pairs={{0,16},{2,18},{4,20},{6,22},{8,24},{10,26},{12,28},{14,30},{16,0},... | collective-permute-start | bytes 393224 | tf_op jit(solution)/shard_map/ppermute | solution.py:34
  54.5 6.1 %collective-permute-start.18 = (bf16[64,1024]{1,0:T(8,128)(2,1)S(1)}, bf16[64,1024]{1,0:T(8,128)(2,1)S(1)}, u32[]{:S(2)}, u32[]{:S(2)}) collective-permute-start(bf16[64,1024]{1,0:T(8,128)(2,1)S(1)} %get-tuple-element.74), channel_id=1, source_target_pairs={{0,24},{2,26},{4,28},{6,30},{8,16},{10,18},{12,20},{14,22},{16,8},... | collective-permute-start | bytes 393224 | tf_op jit(solution)/shard_map/ppermute | solution.py:34
  60.7 7.8 %collective-permute-start.20 = (bf16[64,1024]{1,0:T(8,128)(2,1)S(1)}, bf16[64,1024]{1,0:T(8,128)(2,1)S(1)}, u32[]{:S(2)}, u32[]{:S(2)}) collective-permute-start(bf16[64,1024]{1,0:T(8,128)(2,1)S(1)} %shard_map.120.refs_0_), channel_id=1, source_target_pairs={{0,4},{2,6},{4,0},{6,2},{8,12},{10,14},{12,8},{14,10},{16,20},{18,... | collective-permute-start | bytes 393224 | tf_op jit(solution)/shard_map/ppermute | solution.py:34
  68.5 5.0 %collective-permute-start.24 = (bf16[64,1024]{1,0:T(8,128)(2,1)S(1)}, bf16[64,1024]{1,0:T(8,128)(2,1)S(1)}, u32[]{:S(2)}, u32[]{:S(2)}) collective-permute-start(bf16[64,1024]{1,0:T(8,128)(2,1)S(1)} %shard_map.122.refs_0_), channel_id=1, source_target_pairs={{0,16},{2,18},{4,20},{6,22},{8,24},{10,26},{12,28},{14,30},{16,0},... | collective-permute-start | bytes 393224 | tf_op jit(solution)/shard_map/ppermute | solution.py:34
  70.3 6.0 %collective-permute-start.22 = (bf16[64,1024]{1,0:T(8,128)(2,1)S(1)}, bf16[64,1024]{1,0:T(8,128)(2,1)S(1)}, u32[]{:S(2)}, u32[]{:S(2)}) collective-permute-start(bf16[64,1024]{1,0:T(8,128)(2,1)S(1)} %shard_map.122.refs_0_), channel_id=1, source_target_pairs={{0,8},{2,10},{4,12},{6,14},{8,0},{10,2},{12,4},{14,6},{16,24},{18,... | collective-permute-start | bytes 393224 | tf_op jit(solution)/shard_map/ppermute | solution.py:34
  70.3 6.0 %collective-permute-start.21 = (bf16[64,1024]{1,0:T(8,128)(2,1)S(1)}, bf16[64,1024]{1,0:T(8,128)(2,1)S(1)}, u32[]{:S(2)}, u32[]{:S(2)}) collective-permute-start(bf16[64,1024]{1,0:T(8,128)(2,1)S(1)} %shard_map.122.refs_0_), channel_id=1, source_target_pairs={{0,2},{2,0},{4,6},{6,4},{8,10},{10,8},{12,14},{14,12},{16,18},{18,... | collective-permute-start | bytes 393224 | tf_op jit(solution)/shard_map/ppermute | solution.py:34
  73.6 5.0 %collective-permute-start.26 = (bf16[64,1024]{1,0:T(8,128)(2,1)S(1)}, bf16[64,1024]{1,0:T(8,128)(2,1)S(1)}, u32[]{:S(2)}, u32[]{:S(2)}) collective-permute-start(bf16[64,1024]{1,0:T(8,128)(2,1)S(1)} %collective-permute-done.24.refs_4_), channel_id=1, source_target_pairs={{0,8},{2,10},{4,12},{6,14},{8,0},{10,2},{12,4},{14,6},{16,24},{18,... | collective-permute-start | bytes 393224 | tf_op jit(solution)/shard_map/ppermute | solution.py:34
  76.4 5.6 %collective-permute-start.23 = (bf16[64,1024]{1,0:T(8,128)(2,1)S(1)}, bf16[64,1024]{1,0:T(8,128)(2,1)S(1)}, u32[]{:S(2)}, u32[]{:S(2)}) collective-permute-start(bf16[64,1024]{1,0:T(8,128)(2,1)S(1)} %collective-permute-done.22.refs_2_), channel_id=1, source_target_pairs={{0,2},{2,0},{4,6},{6,4},{8,10},{10,8},{12,14},{14,12},{16,18},{18,... | collective-permute-start | bytes 393224 | tf_op jit(solution)/shard_map/ppermute | solution.py:34
  76.4 5.6 %collective-permute-start.25 = (bf16[64,1024]{1,0:T(8,128)(2,1)S(1)}, bf16[64,1024]{1,0:T(8,128)(2,1)S(1)}, u32[]{:S(2)}, u32[]{:S(2)}) collective-permute-start(bf16[64,1024]{1,0:T(8,128)(2,1)S(1)} %collective-permute-done.21.refs_1_), channel_id=1, source_target_pairs={{0,16},{2,18},{4,20},{6,22},{8,24},{10,26},{12,28},{14,30},{16,0},... | collective-permute-start | bytes 393224 | tf_op jit(solution)/shard_map/ppermute | solution.py:34
  78.5 5.0 %collective-permute-start.27 = (bf16[64,1024]{1,0:T(8,128)(2,1)S(1)}, bf16[64,1024]{1,0:T(8,128)(2,1)S(1)}, u32[]{:S(2)}, u32[]{:S(2)}) collective-permute-start(bf16[64,1024]{1,0:T(8,128)(2,1)S(1)} %collective-permute-done.26.refs_6_), channel_id=1, source_target_pairs={{0,2},{2,0},{4,6},{6,4},{8,10},{10,8},{12,14},{14,12},{16,18},{18,... | collective-permute-start | bytes 393224 | tf_op jit(solution)/shard_map/ppermute | solution.py:34
  (5 other events, 8.2 us)

commit v11 on v10

--- a/solution.py
+++ b/solution.py
@@ -454,10 +454,8 @@
         terms = [pieces[0]] + [plane_swap(pieces[at], at, 0) for at in (1, 2, 3)]
         total = call(sum_kernel, piece, terms)
         pair_in = from_partner(pair_out, "gy")
-        total, pair_in = lax.optimization_barrier((total, pair_in))
         other = plane_swap(total, 0, 2)
         grad_x = features_grad(pair_in)
-        total, grad_x = lax.optimization_barrier((total, grad_x))
         total = call(sum_kernel, piece, [total, other])
         by_x, by_y, by_z = plane_swap(total, 1, 0), plane_swap(total, 2, 0), plane_swap(total, 0, 1)
         by_xy, by_xz = plane_swap(by_y, 1, 0), plane_swap(by_x, 0, 1)

time: 85.2 us -> 86.5 us (1.015)
  waiting for transfers between devices: 38.5 us -> 42.1 us
  starting transfers between devices: 29 us -> 26.5 us
    ppermute x11, waiting for transfers between devices: 7.58 us -> 11.8 us  [from_partner(): return lax.ppermute(block, axis, route)]
    ppermute x11, starting transfers between devices: 8.66 us -> 6.06 us  [from_partner(): return lax.ppermute(block, axis, route)]
  transfers between devices with their start and end apart: 28 -> 28, of which waited for: 17 -> 18; matrix products, arithmetic and copies ran while one was open for 1% -> 1% of each run, Pallas kernels for 7% -> 7%
where the time goes in v11:
time: 86.5 us; the launch traced here: 86.2 us
  waiting for transfers between devices  42.1 us (49%)
  starting transfers between devices  26.5 us (31%)
  Pallas kernels  13 us (15%)
  local copies, waits for them, and re-layouts  3.81 us (4%)
    ppermute x11, waiting for transfers between devices, plane_swap(): return lax.ppermute(value, ('gx', 'gy'), route)  18.6 us
    pallas_call x14, Pallas kernels, call(): pl.pallas_call(kernel, out_shape=out_shape, in_specs=specs, scratch_shape...  13 us
    ppermute x11, waiting for transfers between devices, from_partner(): return lax.ppermute(block, axis, route)  11.8 us
    ppermute x6, waiting for transfers between devices, shifted(): lax.ppermute(value, axis, [(source, (source + steps) % count) for source...  11.7 us
    ppermute x11, starting transfers between devices, plane_swap(): return lax.ppermute(value, ('gx', 'gy'), route)  10.6 us
    ppermute x6, starting transfers between devices, shifted(): lax.ppermute(value, axis, [(source, (source + steps) % count) for source...  9.9 us
    ppermute x11, starting transfers between devices, from_partner(): return lax.ppermute(block, axis, route)  6.06 us
    unnamed x18, local copies, waits for them, and re-layouts  2.87 us
  transfers between devices with their start and end apart: 28, of which 18 were waited for; matrix products, arithmetic and copies ran while one was open for 1% of the time, Pallas kernels for 7%

profile of v11, /device:TPU:0, one launch (start us, length us, event | category | flops | bytes accessed | tf_op | source)
XLA Modules:
  0.0 86.2 jit_solution(1220085390652514855)
XLA Ops:
  2.8 3.0 %collective-permute-start = (bf16[128,512]{1,0:T(8,128)(2,1)S(1)}, bf16[128,512]{1,0:T(8,128)(2,1)S(1)}, u32[]{:S(2)}, u32[]{:S(2)}) collective-permute-start(bf16[128,512]{1,0:T(8,128)(2,1)S(1)} %reshape.13.own.f_own), channel_id=1, source_target_pairs={{0,2},{2,0},{4,6},{6,4},{1,3},{3,1},{5,7},{7,5},{8,10},{10,8},{12,... | collective-permute-start | bytes 393224 | tf_op jit(solution)/shard_map/ppermute | solution.py:20
  9.5 1.3 %collective-permute-done.5.far.f_far = bf16[128,512]{1,0:T(8,128)(2,1)S(1)} collective-permute-done((bf16[128,512]{1,0:T(8,128)(2,1)S(1)}, bf16[128,512]{1,0:T(8,128)(2,1)S(1)}, u32[]{:S(2)}, u32[]{:S(2)}) %collective-permute-start.5) | collective-permute-done | bytes 131104 | tf_op jit(solution)/shard_map/ppermute | solution.py:20
  11.4 1.8 %collective-permute-start.7 = (bf16[128,768]{1,0:T(8,128)(2,1)S(1)}, bf16[128,768]{1,0:T(8,128)(2,1)S(1)}, u32[]{:S(2)}, u32[]{:S(2)}) collective-permute-start(bf16[128,768]{1,0:T(8,128)(2,1)S(1)} %get-tuple-element.49), channel_id=1, source_target_pairs={{0,2},{2,0},{4,6},{6,4},{1,3},{3,1},{5,7},{7,5},{8,10},{10,8},{12,... | collective-permute-start | bytes 589832 | tf_op jit(solution)/shard_map/ppermute | solution.py:20
  13.2 1.5 %collective-permute-start.9 = (bf16[512,256]{1,0:T(8,128)(2,1)S(1)}, bf16[512,256]{1,0:T(8,128)(2,1)S(1)}, u32[]{:S(2)}, u32[]{:S(2)}) collective-permute-start(bf16[512,256]{1,0:T(8,128)(2,1)S(1)} %get-tuple-element.52.refs_0_.refs_2_), channel_id=1, source_target_pairs={{0,8},{8,16},{16,24},{24,0},{1,9},{9,17},{17,25},{25,1},{2,10},{10... | collective-permute-start | bytes 786440 | tf_op jit(solution)/shard_map/ppermute | solution.py:25
  14.7 2.6 %collective-permute-start.11 = (bf16[512,256]{1,0:T(8,128)(2,1)S(1)}, bf16[512,256]{1,0:T(8,128)(2,1)S(1)}, u32[]{:S(2)}, u32[]{:S(2)}) collective-permute-start(bf16[512,256]{1,0:T(8,128)(2,1)S(1)} %get-tuple-element.52.refs_0_.refs_2_), channel_id=1, source_target_pairs={{0,4},{2,6},{4,0},{6,2},{1,5},{3,7},{5,1},{7,3},{8,12},{10,14},{12... | collective-permute-start | bytes 786440 | tf_op jit(solution)/shard_map/ppermute | solution.py:25
  17.3 1.4 %collective-permute-start.10 = (bf16[512,256]{1,0:T(8,128)(2,1)S(1)}, bf16[512,256]{1,0:T(8,128)(2,1)S(1)}, u32[]{:S(2)}, u32[]{:S(2)}) collective-permute-start(bf16[512,256]{1,0:T(8,128)(2,1)S(1)} %get-tuple-element.52.refs_0_.refs_2_), channel_id=1, source_target_pairs={{0,24},{8,0},{16,8},{24,16},{1,25},{9,1},{17,9},{25,17},{2,26},{10... | collective-permute-start | bytes 786440 | tf_op jit(solution)/shard_map/ppermute | solution.py:25
  18.7 2.3 %collective-permute-done.7.pair = bf16[128,768]{1,0:T(8,128)(2,1)S(1)} collective-permute-done((bf16[128,768]{1,0:T(8,128)(2,1)S(1)}, bf16[128,768]{1,0:T(8,128)(2,1)S(1)}, u32[]{:S(2)}, u32[]{:S(2)}) %collective-permute-start.7) | collective-permute-done | bytes 196640 | tf_op jit(solution)/shard_map/ppermute | solution.py:20
  21.0 1.4 %collective-permute-done.8.far = bf16[128,768]{1,0:T(8,128)(2,1)S(1)} collective-permute-done((bf16[128,768]{1,0:T(8,128)(2,1)S(1)}, bf16[128,768]{1,0:T(8,128)(2,1)S(1)}, u32[]{:S(2)}, u32[]{:S(2)}) %collective-permute-start.8) | collective-permute-done | bytes 196640 | tf_op jit(solution)/shard_map/ppermute | solution.py:20
  23.3 2.1 %shard_map.114 = (bf16[4,512,512]{2,1,0:T(8,128)(2,1)S(1)}, bf16[4,512,512]{2,1,0:T(8,128)(2,1)S(1)}, f32[16,512]{1,0:T(8,128)S(1)}) custom-call(bf16[512,128]{1,0:T(8,128)(2,1)S(1)} %get-tuple-element.45.q_ref, bf16[512,128]{1,0:T(8,128)(2,1)S(1)} %get-tuple-element.50.do_ref, f32[2,512]{1,0:T(2,128)S(1)} %get-tuple-element.51.delta_ref, ...), custom_call_target="tpu_custom_call" | custom-call | flops 536870912 | bytes 4194304 | tf_op jit(solution)/shard_map/pallas_call | solution.py:55
  25.4 3.7 %collective-permute-done.11.refs_1_.refs_5_ = bf16[512,256]{1,0:T(8,128)(2,1)S(1)} collective-permute-done((bf16[512,256]{1,0:T(8,128)(2,1)S(1)}, bf16[512,256]{1,0:T(8,128)(2,1)S(1)}, u32[]{:S(2)}, u32[]{:S(2)}) %collective-permute-start.11) | collective-permute-done | bytes 262176 | tf_op jit(solution)/shard_map/ppermute | solution.py:25
  29.0 2.1 %shard_map.115 = (bf16[4,512,512]{2,1,0:T(8,128)(2,1)S(1)}, bf16[4,512,512]{2,1,0:T(8,128)(2,1)S(1)}, f32[16,512]{1,0:T(8,128)S(1)}) custom-call(bf16[512,128]{1,0:T(8,128)(2,1)S(1)} %get-tuple-element.45.q_ref, bf16[512,128]{1,0:T(8,128)(2,1)S(1)} %get-tuple-element.50.do_ref, f32[2,512]{1,0:T(2,128)S(1)} %get-tuple-element.51.delta_ref, ...), custom_call_target="tpu_custom_call" | custom-call | flops 536870912 | bytes 4194304 | tf_op jit(solution)/shard_map/pallas_call | solution.py:55
  31.1 2.2 %shard_map.116 = (f32[8,512]{1,0:T(8,128)S(1)}, bf16[512,256]{1,0:T(8,128)(2,1)S(1)}, bf16[512,256]{1,0:T(8,128)(2,1)S(1)}, bf16[512,256]{1,0:T(8,128)(2,1)S(1)}) custom-call(bf16[512,128]{1,0:T(8,128)(2,1)S(1)} %get-tuple-element.45.q_ref, bf16[512,128]{1,0:T(8,128)(2,1)S(1)} %get-tuple-element.50.do_ref, ...), custom_call_target="tpu_custom_call" | custom-call | flops 1073741824 | bytes 8388608 | tf_op jit(solution)/shard_map/pallas_call | solution.py:55
  33.3 1.5 %collective-permute-start.12 = (bf16[512,256]{1,0:T(8,128)(2,1)S(1)}, bf16[512,256]{1,0:T(8,128)(2,1)S(1)}, u32[]{:S(2)}, u32[]{:S(2)}) collective-permute-start(bf16[512,256]{1,0:T(8,128)(2,1)S(1)} %get-tuple-element.61), channel_id=1, source_target_pairs={{0,4},{2,6},{4,0},{6,2},{1,5},{3,7},{5,1},{7,3},{8,12},{10,14},{12... | collective-permute-start | bytes 786440 | tf_op jit(solution)/shard_map/ppermute | solution.py:25
  34.8 1.5 %collective-permute-start.13 = (bf16[512,256]{1,0:T(8,128)(2,1)S(1)}, bf16[512,256]{1,0:T(8,128)(2,1)S(1)}, u32[]{:S(2)}, u32[]{:S(2)}) collective-permute-start(bf16[512,256]{1,0:T(8,128)(2,1)S(1)} %get-tuple-element.62), channel_id=1, source_target_pairs={{0,8},{8,16},{16,24},{24,0},{1,9},{9,17},{17,25},{25,1},{2,10},{10... | collective-permute-start | bytes 786440 | tf_op jit(solution)/shard_map/ppermute | solution.py:25
  36.3 1.4 %collective-permute-start.14 = (bf16[512,256]{1,0:T(8,128)(2,1)S(1)}, bf16[512,256]{1,0:T(8,128)(2,1)S(1)}, u32[]{:S(2)}, u32[]{:S(2)}) collective-permute-start(bf16[512,256]{1,0:T(8,128)(2,1)S(1)} %get-tuple-element.63), channel_id=1, source_target_pairs={{0,24},{8,0},{16,8},{24,16},{1,25},{9,1},{17,9},{25,17},{2,26},{10... | collective-permute-start | bytes 786440 | tf_op jit(solution)/shard_map/ppermute | solution.py:25
  37.7 1.8 %shard_map.117 = (bf16[512,128]{1,0:T(8,128)(2,1)S(1)}, bf16[512,256]{1,0:T(8,128)(2,1)S(1)}) custom-call(f32[8,512]{1,0:T(8,128)S(1)} %get-tuple-element.59.part_ref, bf16[512,128]{1,0:T(8,128)(2,1)S(1)} %get-tuple-element.45.q_ref, bf16[512,128]{1,0:T(8,128)(2,1)S(1)} %get-tuple-element.50.do_ref, ...), custom_call_target="tpu_custom_call" | custom-call | flops 536870912 | bytes 4194304 | tf_op jit(solution)/shard_map/pallas_call | solution.py:55
  39.6 7.2 %collective-permute-done.12.refs_0_ = bf16[512,256]{1,0:T(8,128)(2,1)S(1)} collective-permute-done((bf16[512,256]{1,0:T(8,128)(2,1)S(1)}, bf16[512,256]{1,0:T(8,128)(2,1)S(1)}, u32[]{:S(2)}, u32[]{:S(2)}) %collective-permute-start.12) | collective-permute-done | bytes 262176 | tf_op jit(solution)/shard_map/ppermute | solution.py:25
  47.6 1.7 %collective-permute-done.15.core = bf16[512,384]{1,0:T(8,128)(2,1)S(1)} collective-permute-done((bf16[512,384]{1,0:T(8,128)(2,1)S(1)}, bf16[512,384]{1,0:T(8,128)(2,1)S(1)}, u32[]{:S(2)}, u32[]{:S(2)}) %collective-permute-start.15) | collective-permute-done | bytes 393248 | tf_op jit(solution)/shard_map/ppermute | solution.py:20
  49.9 1.5 %collective-permute-start.17 = (bf16[64,1024]{1,0:T(8,128)(2,1)S(1)}, bf16[64,1024]{1,0:T(8,128)(2,1)S(1)}, u32[]{:S(2)}, u32[]{:S(2)}) collective-permute-start(bf16[64,1024]{1,0:T(8,128)(2,1)S(1)} %get-tuple-element.70), channel_id=1, source_target_pairs={{0,8},{2,10},{4,12},{6,14},{8,0},{10,2},{12,4},{14,6},{16,24},{18,... | collective-permute-start | bytes 393224 | tf_op jit(solution)/shard_map/ppermute | solution.py:34
  51.4 1.5 %collective-permute-start.18 = (bf16[64,1024]{1,0:T(8,128)(2,1)S(1)}, bf16[64,1024]{1,0:T(8,128)(2,1)S(1)}, u32[]{:S(2)}, u32[]{:S(2)}) collective-permute-start(bf16[64,1024]{1,0:T(8,128)(2,1)S(1)} %get-tuple-element.71), channel_id=1, source_target_pairs={{0,16},{2,18},{4,20},{6,22},{8,24},{10,26},{12,28},{14,30},{16,0},... | collective-permute-start | bytes 393224 | tf_op jit(solution)/shard_map/ppermute | solution.py:34
  53.4 2.4 %collective-permute-done.17.refs_1_ = bf16[64,1024]{1,0:T(8,128)(2,1)S(1)} collective-permute-done((bf16[64,1024]{1,0:T(8,128)(2,1)S(1)}, bf16[64,1024]{1,0:T(8,128)(2,1)S(1)}, u32[]{:S(2)}, u32[]{:S(2)}) %collective-permute-start.17) | collective-permute-done | bytes 131104 | tf_op jit(solution)/shard_map/ppermute | solution.py:34
  55.8 3.7 %collective-permute-done.18.refs_2_ = bf16[64,1024]{1,0:T(8,128)(2,1)S(1)} collective-permute-done((bf16[64,1024]{1,0:T(8,128)(2,1)S(1)}, bf16[64,1024]{1,0:T(8,128)(2,1)S(1)}, u32[]{:S(2)}, u32[]{:S(2)}) %collective-permute-start.18) | collective-permute-done | bytes 131104 | tf_op jit(solution)/shard_map/ppermute | solution.py:34
  59.5 1.3 %collective-permute-start.20 = (bf16[64,1024]{1,0:T(8,128)(2,1)S(1)}, bf16[64,1024]{1,0:T(8,128)(2,1)S(1)}, u32[]{:S(2)}, u32[]{:S(2)}) collective-permute-start(bf16[64,1024]{1,0:T(8,128)(2,1)S(1)} %shard_map.121.refs_0_), channel_id=1, source_target_pairs={{0,4},{2,6},{4,0},{6,2},{8,12},{10,14},{12,8},{14,10},{16,20},{18,... | collective-permute-start | bytes 393224 | tf_op jit(solution)/shard_map/ppermute | solution.py:34
  60.9 6.7 %collective-permute-done.20.refs_1_ = bf16[64,1024]{1,0:T(8,128)(2,1)S(1)} collective-permute-done((bf16[64,1024]{1,0:T(8,128)(2,1)S(1)}, bf16[64,1024]{1,0:T(8,128)(2,1)S(1)}, u32[]{:S(2)}, u32[]{:S(2)}) %collective-permute-start.20) | collective-permute-done | bytes 131104 | tf_op jit(solution)/shard_map/ppermute | solution.py:34
  67.6 1.7 %collective-permute-start.24 = (bf16[64,1024]{1,0:T(8,128)(2,1)S(1)}, bf16[64,1024]{1,0:T(8,128)(2,1)S(1)}, u32[]{:S(2)}, u32[]{:S(2)}) collective-permute-start(bf16[64,1024]{1,0:T(8,128)(2,1)S(1)} %shard_map.122.refs_0_), channel_id=1, source_target_pairs={{0,16},{2,18},{4,20},{6,22},{8,24},{10,26},{12,28},{14,30},{16,0},... | collective-permute-start | bytes 393224 | tf_op jit(solution)/shard_map/ppermute | solution.py:34
  69.9 2.7 %collective-permute-done.24.refs_4_ = bf16[64,1024]{1,0:T(8,128)(2,1)S(1)} collective-permute-done((bf16[64,1024]{1,0:T(8,128)(2,1)S(1)}, bf16[64,1024]{1,0:T(8,128)(2,1)S(1)}, u32[]{:S(2)}, u32[]{:S(2)}) %collective-permute-start.24) | collective-permute-done | bytes 131104 | tf_op jit(solution)/shard_map/ppermute | solution.py:34
  72.7 1.7 %collective-permute-start.26 = (bf16[64,1024]{1,0:T(8,128)(2,1)S(1)}, bf16[64,1024]{1,0:T(8,128)(2,1)S(1)}, u32[]{:S(2)}, u32[]{:S(2)}) collective-permute-start(bf16[64,1024]{1,0:T(8,128)(2,1)S(1)} %collective-permute-done.24.refs_4_), channel_id=1, source_target_pairs={{0,8},{2,10},{4,12},{6,14},{8,0},{10,2},{12,4},{14,6},{16,24},{18,... | collective-permute-start | bytes 393224 | tf_op jit(solution)/shard_map/ppermute | solution.py:34
  74.3 1.2 %collective-permute-done.22.refs_2_ = bf16[64,1024]{1,0:T(8,128)(2,1)S(1)} collective-permute-done((bf16[64,1024]{1,0:T(8,128)(2,1)S(1)}, bf16[64,1024]{1,0:T(8,128)(2,1)S(1)}, u32[]{:S(2)}, u32[]{:S(2)}) %collective-permute-start.22) | collective-permute-done | bytes 131104 | tf_op jit(solution)/shard_map/ppermute | solution.py:34
  77.6 4.3 %collective-permute-done.16.pair = bf16[128,768]{1,0:T(8,128)(2,1)S(1)} collective-permute-done((bf16[128,768]{1,0:T(8,128)(2,1)S(1)}, bf16[128,768]{1,0:T(8,128)(2,1)S(1)}, u32[]{:S(2)}, u32[]{:S(2)}) %collective-permute-start.16) | collective-permute-done | bytes 196640 | tf_op jit(solution)/shard_map/ppermute | solution.py:20
  81.9 1.3 %shard_map.120 = bf16[8,4,4,512]{3,2,1,0:T(4,128)(2,1)} custom-call(bf16[128,768]{1,0:T(8,128)(2,1)S(1)} %get-tuple-element.67.mine, bf16[128,768]{1,0:T(8,128)(2,1)S(1)} %collective-permute-done.16.pair, bf16[256,512]{1,0:T(8,128)(2,1)S(1)} %copy-done.1, bf16[256,512]{1,0:T(8,128)(2,1)S(1)} %collective-permute-done.2.wq1, bf16[256,512]{1,0:T(8,128)(2,1)S(1)} %copy-done.3, ...), custom_call_target="tpu_custom_call" | custom-call | flops 201326592 | bytes 1000000 | tf_op jit(solution)/shard_map/pallas_call | solution.py:55
  83.3 1.4 %collective-permute-done.27.refs_7_ = bf16[64,1024]{1,0:T(8,128)(2,1)S(1)} collective-permute-done((bf16[64,1024]{1,0:T(8,128)(2,1)S(1)}, bf16[64,1024]{1,0:T(8,128)(2,1)S(1)}, u32[]{:S(2)}, u32[]{:S(2)}) %collective-permute-start.27) | collective-permute-done | bytes 131104 | tf_op jit(solution)/shard_map/ppermute | solution.py:34
  84.7 1.5 %shard_map.123 = (f32[256,512]{1,0:T(8,128)}, f32[256,512]{1,0:T(8,128)}, f32[256,512]{1,0:T(8,128)}, f32[256,512]{1,0:T(8,128)}) custom-call(bf16[64,1024]{1,0:T(8,128)(2,1)S(1)} %shard_map.122.refs_0_, bf16[64,1024]{1,0:T(8,128)(2,1)S(1)} %collective-permute-done.21.refs_1_, bf16[64,1024]{1,0:T(8,128)(2,1)S(1)} %collective-permute-done.22.refs_2_, ...), custom_call_target="tpu_custom_call" | custom-call | flops 1000000 | bytes 1000000 | tf_op jit(solution)/shard_map/pallas_call | solution.py:55
  (57 shorter events, 11.8 us)
Async XLA Ops:
  0.6 21.8 %copy-start.6 = (bf16[256,512]{1,0:T(8,128)(2,1)S(1)}, bf16[256,512]{1,0:T(8,128)(2,1)}, u32[]{:S(2)}) copy-start(bf16[256,512]{1,0:T(8,128)(2,1)} %wout.1) | copy-start | bytes 786436
  0.6 5.1 %collective-permute-start.2 = (bf16[256,512]{1,0:T(8,128)(2,1)}, bf16[256,512]{1,0:T(8,128)(2,1)S(1)}, u32[]{:S(2)}, u32[]{:S(2)}) collective-permute-start(bf16[256,512]{1,0:T(8,128)(2,1)} %wq0.3), channel_id=1, source_target_pairs={{0,1},{1,0},{2,3},{3,2},{4,5},{5,4},{6,7},{7,6},{8,9},{9,8},{10,11... | collective-permute-start | bytes 786440 | tf_op jit(solution)/shard_map/ppermute | solution.py:20
  1.2 4.6 %collective-permute-start.3 = (bf16[256,512]{1,0:T(8,128)(2,1)}, bf16[256,512]{1,0:T(8,128)(2,1)S(1)}, u32[]{:S(2)}, u32[]{:S(2)}) collective-permute-start(bf16[256,512]{1,0:T(8,128)(2,1)} %wk0.3), channel_id=1, source_target_pairs={{0,1},{1,0},{2,3},{3,2},{4,5},{5,4},{6,7},{7,6},{8,9},{9,8},{10,11... | collective-permute-start | bytes 786440 | tf_op jit(solution)/shard_map/ppermute | solution.py:20
  1.2 4.5 %collective-permute-start.4 = (bf16[256,512]{1,0:T(8,128)(2,1)}, bf16[256,512]{1,0:T(8,128)(2,1)S(1)}, u32[]{:S(2)}, u32[]{:S(2)}) collective-permute-start(bf16[256,512]{1,0:T(8,128)(2,1)} %wv0.3), channel_id=1, source_target_pairs={{0,1},{1,0},{2,3},{3,2},{4,5},{5,4},{6,7},{7,6},{8,9},{9,8},{10,11... | collective-permute-start | bytes 786440 | tf_op jit(solution)/shard_map/ppermute | solution.py:20
  2.6 6.1 %collective-permute-start.1 = (bf16[128,512]{1,0:T(8,128)(2,1)S(1)}, bf16[128,512]{1,0:T(8,128)(2,1)S(1)}, u32[]{:S(2)}, u32[]{:S(2)}) collective-permute-start(bf16[128,512]{1,0:T(8,128)(2,1)S(1)} %reshape.13.own.f_own), channel_id=1, source_target_pairs={{0,1},{1,0},{2,3},{3,2},{4,5},{5,4},{6,7},{7,6},{8,9},{9,8},{10,11... | collective-permute-start | bytes 393224 | tf_op jit(solution)/shard_map/ppermute | solution.py:20
  2.8 6.7 %collective-permute-start = (bf16[128,512]{1,0:T(8,128)(2,1)S(1)}, bf16[128,512]{1,0:T(8,128)(2,1)S(1)}, u32[]{:S(2)}, u32[]{:S(2)}) collective-permute-start(bf16[128,512]{1,0:T(8,128)(2,1)S(1)} %reshape.13.own.f_own), channel_id=1, source_target_pairs={{0,2},{2,0},{4,6},{6,4},{1,3},{3,1},{5,7},{7,5},{8,10},{10,8},{12,... | collective-permute-start | bytes 393224 | tf_op jit(solution)/shard_map/ppermute | solution.py:20
  9.5 1.3 %collective-permute-start.5 = (bf16[128,512]{1,0:T(8,128)(2,1)S(1)}, bf16[128,512]{1,0:T(8,128)(2,1)S(1)}, u32[]{:S(2)}, u32[]{:S(2)}) collective-permute-start(bf16[128,512]{1,0:T(8,128)(2,1)S(1)} %collective-permute-done.pair.f_pair), channel_id=1, source_target_pairs={{0,1},{1,0},{2,3},{3,2},{4,5},{5,4},{6,7},{7,6},{8,9},{9,8},{10,11... | collective-permute-start | bytes 393224 | tf_op jit(solution)/shard_map/ppermute | solution.py:20
  11.4 9.6 %collective-permute-start.7 = (bf16[128,768]{1,0:T(8,128)(2,1)S(1)}, bf16[128,768]{1,0:T(8,128)(2,1)S(1)}, u32[]{:S(2)}, u32[]{:S(2)}) collective-permute-start(bf16[128,768]{1,0:T(8,128)(2,1)S(1)} %get-tuple-element.49), channel_id=1, source_target_pairs={{0,2},{2,0},{4,6},{6,4},{1,3},{3,1},{5,7},{7,5},{8,10},{10,8},{12,... | collective-permute-start | bytes 589832 | tf_op jit(solution)/shard_map/ppermute | solution.py:20
  13.2 10.1 %collective-permute-start.9 = (bf16[512,256]{1,0:T(8,128)(2,1)S(1)}, bf16[512,256]{1,0:T(8,128)(2,1)S(1)}, u32[]{:S(2)}, u32[]{:S(2)}) collective-permute-start(bf16[512,256]{1,0:T(8,128)(2,1)S(1)} %get-tuple-element.52.refs_0_.refs_2_), channel_id=1, source_target_pairs={{0,8},{8,16},{16,24},{24,0},{1,9},{9,17},{17,25},{25,1},{2,10},{10... | collective-permute-start | bytes 786440 | tf_op jit(solution)/shard_map/ppermute | solution.py:25
  14.7 14.4 %collective-permute-start.11 = (bf16[512,256]{1,0:T(8,128)(2,1)S(1)}, bf16[512,256]{1,0:T(8,128)(2,1)S(1)}, u32[]{:S(2)}, u32[]{:S(2)}) collective-permute-start(bf16[512,256]{1,0:T(8,128)(2,1)S(1)} %get-tuple-element.52.refs_0_.refs_2_), channel_id=1, source_target_pairs={{0,4},{2,6},{4,0},{6,2},{1,5},{3,7},{5,1},{7,3},{8,12},{10,14},{12... | collective-permute-start | bytes 786440 | tf_op jit(solution)/shard_map/ppermute | solution.py:25
  17.3 11.8 %collective-permute-start.10 = (bf16[512,256]{1,0:T(8,128)(2,1)S(1)}, bf16[512,256]{1,0:T(8,128)(2,1)S(1)}, u32[]{:S(2)}, u32[]{:S(2)}) collective-permute-start(bf16[512,256]{1,0:T(8,128)(2,1)S(1)} %get-tuple-element.52.refs_0_.refs_2_), channel_id=1, source_target_pairs={{0,24},{8,0},{16,8},{24,16},{1,25},{9,1},{17,9},{25,17},{2,26},{10... | collective-permute-start | bytes 786440 | tf_op jit(solution)/shard_map/ppermute | solution.py:25
  18.7 2.3 %collective-permute-start.6 = (bf16[128,768]{1,0:T(8,128)(2,1)S(1)}, bf16[128,768]{1,0:T(8,128)(2,1)S(1)}, u32[]{:S(2)}, u32[]{:S(2)}) collective-permute-start(bf16[128,768]{1,0:T(8,128)(2,1)S(1)} %get-tuple-element.48.own), channel_id=1, source_target_pairs={{0,1},{1,0},{2,3},{3,2},{4,5},{5,4},{6,7},{7,6},{8,9},{9,8},{10,11... | collective-permute-start | bytes 589832 | tf_op jit(solution)/shard_map/ppermute | solution.py:20
  21.0 1.4 %collective-permute-start.8 = (bf16[128,768]{1,0:T(8,128)(2,1)S(1)}, bf16[128,768]{1,0:T(8,128)(2,1)S(1)}, u32[]{:S(2)}, u32[]{:S(2)}) collective-permute-start(bf16[128,768]{1,0:T(8,128)(2,1)S(1)} %collective-permute-done.7.pair), channel_id=1, source_target_pairs={{0,1},{1,0},{2,3},{3,2},{4,5},{5,4},{6,7},{7,6},{8,9},{9,8},{10,11... | collective-permute-start | bytes 589832 | tf_op jit(solution)/shard_map/ppermute | solution.py:20
  33.3 13.5 %collective-permute-start.12 = (bf16[512,256]{1,0:T(8,128)(2,1)S(1)}, bf16[512,256]{1,0:T(8,128)(2,1)S(1)}, u32[]{:S(2)}, u32[]{:S(2)}) collective-permute-start(bf16[512,256]{1,0:T(8,128)(2,1)S(1)} %get-tuple-element.61), channel_id=1, source_target_pairs={{0,4},{2,6},{4,0},{6,2},{1,5},{3,7},{5,1},{7,3},{8,12},{10,14},{12... | collective-permute-start | bytes 786440 | tf_op jit(solution)/shard_map/ppermute | solution.py:25
  34.8 12.1 %collective-permute-start.13 = (bf16[512,256]{1,0:T(8,128)(2,1)S(1)}, bf16[512,256]{1,0:T(8,128)(2,1)S(1)}, u32[]{:S(2)}, u32[]{:S(2)}) collective-permute-start(bf16[512,256]{1,0:T(8,128)(2,1)S(1)} %get-tuple-element.62), channel_id=1, source_target_pairs={{0,8},{8,16},{16,24},{24,0},{1,9},{9,17},{17,25},{25,1},{2,10},{10... | collective-permute-start | bytes 786440 | tf_op jit(solution)/shard_map/ppermute | solution.py:25
  36.3 11.0 %collective-permute-start.14 = (bf16[512,256]{1,0:T(8,128)(2,1)S(1)}, bf16[512,256]{1,0:T(8,128)(2,1)S(1)}, u32[]{:S(2)}, u32[]{:S(2)}) collective-permute-start(bf16[512,256]{1,0:T(8,128)(2,1)S(1)} %get-tuple-element.63), channel_id=1, source_target_pairs={{0,24},{8,0},{16,8},{24,16},{1,25},{9,1},{17,9},{25,17},{2,26},{10... | collective-permute-start | bytes 786440 | tf_op jit(solution)/shard_map/ppermute | solution.py:25
  39.6 42.3 %copy-start.1 = (bf16[256,512]{1,0:T(8,128)(2,1)S(1)}, bf16[256,512]{1,0:T(8,128)(2,1)}, u32[]{:S(2)}) copy-start(bf16[256,512]{1,0:T(8,128)(2,1)} %wq0.3) | copy-start | bytes 786436
  39.6 42.3 %copy-start.3 = (bf16[256,512]{1,0:T(8,128)(2,1)S(1)}, bf16[256,512]{1,0:T(8,128)(2,1)}, u32[]{:S(2)}) copy-start(bf16[256,512]{1,0:T(8,128)(2,1)} %wk0.3) | copy-start | bytes 786436
  39.6 42.3 %copy-start.5 = (bf16[256,512]{1,0:T(8,128)(2,1)S(1)}, bf16[256,512]{1,0:T(8,128)(2,1)}, u32[]{:S(2)}) copy-start(bf16[256,512]{1,0:T(8,128)(2,1)} %wv0.3) | copy-start | bytes 786436
  47.5 1.8 %collective-permute-start.15 = (bf16[512,384]{1,0:T(8,128)(2,1)S(1)}, bf16[512,384]{1,0:T(8,128)(2,1)S(1)}, u32[]{:S(2)}, u32[]{:S(2)}) collective-permute-start(bf16[512,384]{1,0:T(8,128)(2,1)S(1)} %shard_map.118.own), channel_id=1, source_target_pairs={{0,1},{1,0},{2,3},{3,2},{4,5},{5,4},{6,7},{7,6},{8,9},{9,8},{10,11... | collective-permute-start | bytes 1179656 | tf_op jit(solution)/shard_map/ppermute | solution.py:20
  49.9 6.0 %collective-permute-start.17 = (bf16[64,1024]{1,0:T(8,128)(2,1)S(1)}, bf16[64,1024]{1,0:T(8,128)(2,1)S(1)}, u32[]{:S(2)}, u32[]{:S(2)}) collective-permute-start(bf16[64,1024]{1,0:T(8,128)(2,1)S(1)} %get-tuple-element.70), channel_id=1, source_target_pairs={{0,8},{2,10},{4,12},{6,14},{8,0},{10,2},{12,4},{14,6},{16,24},{18,... | collective-permute-start | bytes 393224 | tf_op jit(solution)/shard_map/ppermute | solution.py:34
  51.4 8.1 %collective-permute-start.18 = (bf16[64,1024]{1,0:T(8,128)(2,1)S(1)}, bf16[64,1024]{1,0:T(8,128)(2,1)S(1)}, u32[]{:S(2)}, u32[]{:S(2)}) collective-permute-start(bf16[64,1024]{1,0:T(8,128)(2,1)S(1)} %get-tuple-element.71), channel_id=1, source_target_pairs={{0,16},{2,18},{4,20},{6,22},{8,24},{10,26},{12,28},{14,30},{16,0},... | collective-permute-start | bytes 393224 | tf_op jit(solution)/shard_map/ppermute | solution.py:34
  52.9 6.5 %collective-permute-start.19 = (bf16[64,1024]{1,0:T(8,128)(2,1)S(1)}, bf16[64,1024]{1,0:T(8,128)(2,1)S(1)}, u32[]{:S(2)}, u32[]{:S(2)}) collective-permute-start(bf16[64,1024]{1,0:T(8,128)(2,1)S(1)} %get-tuple-element.72), channel_id=1, source_target_pairs={{0,24},{2,26},{4,28},{6,30},{8,16},{10,18},{12,20},{14,22},{16,8},... | collective-permute-start | bytes 393224 | tf_op jit(solution)/shard_map/ppermute | solution.py:34
  59.5 8.1 %collective-permute-start.20 = (bf16[64,1024]{1,0:T(8,128)(2,1)S(1)}, bf16[64,1024]{1,0:T(8,128)(2,1)S(1)}, u32[]{:S(2)}, u32[]{:S(2)}) collective-permute-start(bf16[64,1024]{1,0:T(8,128)(2,1)S(1)} %shard_map.121.refs_0_), channel_id=1, source_target_pairs={{0,4},{2,6},{4,0},{6,2},{8,12},{10,14},{12,8},{14,10},{16,20},{18,... | collective-permute-start | bytes 393224 | tf_op jit(solution)/shard_map/ppermute | solution.py:34
  67.6 5.0 %collective-permute-start.24 = (bf16[64,1024]{1,0:T(8,128)(2,1)S(1)}, bf16[64,1024]{1,0:T(8,128)(2,1)S(1)}, u32[]{:S(2)}, u32[]{:S(2)}) collective-permute-start(bf16[64,1024]{1,0:T(8,128)(2,1)S(1)} %shard_map.122.refs_0_), channel_id=1, source_target_pairs={{0,16},{2,18},{4,20},{6,22},{8,24},{10,26},{12,28},{14,30},{16,0},... | collective-permute-start | bytes 393224 | tf_op jit(solution)/shard_map/ppermute | solution.py:34
  69.3 6.2 %collective-permute-start.22 = (bf16[64,1024]{1,0:T(8,128)(2,1)S(1)}, bf16[64,1024]{1,0:T(8,128)(2,1)S(1)}, u32[]{:S(2)}, u32[]{:S(2)}) collective-permute-start(bf16[64,1024]{1,0:T(8,128)(2,1)S(1)} %shard_map.122.refs_0_), channel_id=1, source_target_pairs={{0,8},{2,10},{4,12},{6,14},{8,0},{10,2},{12,4},{14,6},{16,24},{18,... | collective-permute-start | bytes 393224 | tf_op jit(solution)/shard_map/ppermute | solution.py:34
  69.9 6.5 %collective-permute-start.21 = (bf16[64,1024]{1,0:T(8,128)(2,1)S(1)}, bf16[64,1024]{1,0:T(8,128)(2,1)S(1)}, u32[]{:S(2)}, u32[]{:S(2)}) collective-permute-start(bf16[64,1024]{1,0:T(8,128)(2,1)S(1)} %shard_map.122.refs_0_), channel_id=1, source_target_pairs={{0,2},{2,0},{4,6},{6,4},{8,10},{10,8},{12,14},{14,12},{16,18},{18,... | collective-permute-start | bytes 393224 | tf_op jit(solution)/shard_map/ppermute | solution.py:34
  72.7 5.0 %collective-permute-start.26 = (bf16[64,1024]{1,0:T(8,128)(2,1)S(1)}, bf16[64,1024]{1,0:T(8,128)(2,1)S(1)}, u32[]{:S(2)}, u32[]{:S(2)}) collective-permute-start(bf16[64,1024]{1,0:T(8,128)(2,1)S(1)} %collective-permute-done.24.refs_4_), channel_id=1, source_target_pairs={{0,8},{2,10},{4,12},{6,14},{8,0},{10,2},{12,4},{14,6},{16,24},{18,... | collective-permute-start | bytes 393224 | tf_op jit(solution)/shard_map/ppermute | solution.py:34
  74.3 7.6 %collective-permute-start.16 = (bf16[128,768]{1,0:T(8,128)(2,1)S(1)}, bf16[128,768]{1,0:T(8,128)(2,1)S(1)}, u32[]{:S(2)}, u32[]{:S(2)}) collective-permute-start(bf16[128,768]{1,0:T(8,128)(2,1)S(1)} %get-tuple-element.68), channel_id=1, source_target_pairs={{0,2},{2,0},{4,6},{6,4},{1,3},{3,1},{5,7},{7,5},{8,10},{10,8},{12,... | collective-permute-start | bytes 589832 | tf_op jit(solution)/shard_map/ppermute | solution.py:20
  75.5 7.8 %collective-permute-start.23 = (bf16[64,1024]{1,0:T(8,128)(2,1)S(1)}, bf16[64,1024]{1,0:T(8,128)(2,1)S(1)}, u32[]{:S(2)}, u32[]{:S(2)}) collective-permute-start(bf16[64,1024]{1,0:T(8,128)(2,1)S(1)} %collective-permute-done.22.refs_2_), channel_id=1, source_target_pairs={{0,2},{2,0},{4,6},{6,4},{8,10},{10,8},{12,14},{14,12},{16,18},{18,... | collective-permute-start | bytes 393224 | tf_op jit(solution)/shard_map/ppermute | solution.py:34
  76.4 6.9 %collective-permute-start.25 = (bf16[64,1024]{1,0:T(8,128)(2,1)S(1)}, bf16[64,1024]{1,0:T(8,128)(2,1)S(1)}, u32[]{:S(2)}, u32[]{:S(2)}) collective-permute-start(bf16[64,1024]{1,0:T(8,128)(2,1)S(1)} %collective-permute-done.21.refs_1_), channel_id=1, source_target_pairs={{0,16},{2,18},{4,20},{6,22},{8,24},{10,26},{12,28},{14,30},{16,0},... | collective-permute-start | bytes 393224 | tf_op jit(solution)/shard_map/ppermute | solution.py:34
  77.6 7.1 %collective-permute-start.27 = (bf16[64,1024]{1,0:T(8,128)(2,1)S(1)}, bf16[64,1024]{1,0:T(8,128)(2,1)S(1)}, u32[]{:S(2)}, u32[]{:S(2)}) collective-permute-start(bf16[64,1024]{1,0:T(8,128)(2,1)S(1)} %collective-permute-done.26.refs_6_), channel_id=1, source_target_pairs={{0,2},{2,0},{4,6},{6,4},{8,10},{10,8},{12,14},{14,12},{16,18},{18,... | collective-permute-start | bytes 393224 | tf_op jit(solution)/shard_map/ppermute | solution.py:34
  (5 other events, 8.2 us)

commit v12 on v10

--- a/solution.py
+++ b/solution.py
@@ -228,11 +228,13 @@
 
 
 def collect_kernel(times, dq_ref, *refs):
+    out_ref, pair_ref = refs[-2:]
     total = times[0] * refs[0][...].astype(F32)
-    for time, ref in zip(times[1:], refs[1:-1]):
+    for time, ref in zip(times[1:], refs[1:-2]):
         total = total + time * ref[...].astype(F32)
-    refs[-1][:, 0:PART] = dq_ref[...]
-    refs[-1][:, PART:] = total.astype(BF)
+    out_ref[:, 0:PART] = dq_ref[...]
+    out_ref[:, PART:] = total.astype(BF)
+    pair_ref[...] = out_ref[2 * PART :, :]
 
 
 def place_grads(grads, own, core, count):
@@ -247,11 +249,9 @@
             ]
 
 
-def weight_kernel(chunks, own, core, feat_t, o_ref, pair_ref, mine_ref, *refs):
+def weight_kernel(chunks, own, core, feat_t, o_ref, *refs):
     outs, (grads, made) = refs[:chunks], refs[chunks:]
     place_grads(grads, own, core, 3)
-    mine_ref[...] = grads[0:PART, :]
-    pair_ref[...] = grads[2 * PART : 3 * PART, :]
     wide = grads.shape[1]
     made[:, 0:wide] = dot_nn(feat_t[...], grads[...]).astype(BF)
     made[:, wide:] = o_ref[...]
@@ -263,18 +263,22 @@
         outs[at][...] = made[spot, :]
 
 
-def grad_x_kernel(own_half, mine, pair, wq0, wq1, wk0, wk1, wv0, wv1, out, full, made):
+def grad_x_kernel(own_half, own, core, pair, far, wq0, wq1, wk0, wk1, wv0, wv1, out, full, made):
     y_bit = lax.axis_index("gy") % 2
     z_bit = lax.axis_index("gz") % 2
     half = z_bit if own_half else z_bit * 0
     width = wq0.shape[1]
     half_rows = wq0.shape[0]
+    sources = (
+        (own, 0, z_bit, y_bit), (core, 1, 1 - z_bit, y_bit),
+        (pair, 0, z_bit, 1 - y_bit), (far, 1, 1 - z_bit, 1 - y_bit),
+    )
     for at in range(3):
-        for side in range(2):
-            spot = slice((at * 2 + side) * PART, (at * 2 + side + 1) * PART)
-            base = at * width + side * 2 * PART
-            full[:, columns(base + y_bit * PART)] = mine[:, spot]
-            full[:, columns(base + (1 - y_bit) * PART)] = pair[:, spot]
+        spot = slice(at * PART, (at + 1) * PART)
+        for source, part, z_at, y_at in sources:
+            full[:, columns(at * width + z_at * 2 * PART + y_at * PART)] = source[
+                part * PART : (part + 1) * PART, spot
+            ]
     for at, sources in ((half, (wq0, wk0, wv0)), (1 - half, (wq1, wk1, wv1))):
         total = functools.reduce(
             jnp.add,
@@ -427,25 +431,28 @@
     for partial, (axis, step) in reversed(list(zip(partials, routes))):
         back.append(shifted(partial, axis, -step))
     back.append(own_partial)
-    grads = call(
-        functools.partial(collect_kernel, times[::-1]), shape_of((block_tokens, 3 * PART)), [dq, *back]
-    )
+    grads, pair_out = call(
+        functools.partial(collect_kernel, times[::-1]),
+        (shape_of((block_tokens, 3 * PART)), shape_of((2 * tokens, 3 * PART))),
+        [dq, *back],
+    )
+    pair_in = from_partner(pair_out, "gy")
     core_grads = from_partner(grads, "gz")
     planned = count_x == 4 and count_y == 4 and count_z == 2
     chunks = 4 if planned else 1
     piece = shape_of((half // chunks, 8 * PART))
-    pair_out, mine, *pieces = call(
+    pieces = call(
         functools.partial(weight_kernel, chunks),
-        (shape_of((tokens, 6 * PART)), shape_of((tokens, 6 * PART)), *[piece] * chunks),
+        tuple([piece] * chunks),
         [grads, core_grads, feat_t, out_term],
         scratch=[pltpu.VMEM((block_tokens, 6 * PART), BF), pltpu.VMEM((half, 8 * PART), BF)],
         flops=2 * block_tokens * half * 6 * PART,
     )
-    def features_grad(pair_rows):
+    def features_grad(far_in):
         return call(
             functools.partial(grad_x_kernel, own_half),
             shape_of(features.shape),
-            [mine, pair_rows, *pairs],
+            [grads, core_grads, pair_in, far_in, *pairs],
             scratch=[pltpu.VMEM((tokens, 3 * width), BF), pltpu.VMEM((tokens, width), BF)],
             flops=2 * tokens * 3 * width * width,
         )
@@ -453,10 +460,10 @@
     if planned:
         terms = [pieces[0]] + [plane_swap(pieces[at], at, 0) for at in (1, 2, 3)]
         total = call(sum_kernel, piece, terms)
-        pair_in = from_partner(pair_out, "gy")
         total, pair_in = lax.optimization_barrier((total, pair_in))
         other = plane_swap(total, 0, 2)
-        grad_x = features_grad(pair_in)
+        far_in = from_partner(pair_in, "gz")
+        grad_x = features_grad(far_in)
         total, grad_x = lax.optimization_barrier((total, grad_x))
         total = call(sum_kernel, piece, [total, other])
         by_x, by_y, by_z = plane_swap(total, 1, 0), plane_swap(total, 2, 0), plane_swap(total, 0, 1)
@@ -468,7 +475,7 @@
             [total, by_z, by_x, by_xz, by_y, by_yz, by_xy, by_xyz],
         )
     else:
-        grad_x = features_grad(from_partner(pair_out, "gy"))
+        grad_x = features_grad(from_partner(pair_in, "gz"))
         terms = pieces[0].astype(F32)
         stacked = jnp.zeros((4, width, width), F32)
         for base, at in ((0, 0), (1, 1), (2, 2)):

time: 85.2 us -> 86.2 us (1.012)
  waiting for transfers between devices: 38.5 us -> 39.5 us
    ppermute x11, waiting for transfers between devices: 19.2 us -> 21.8 us  [plane_swap(): return lax.ppermute(value, ('gx', 'gy'), route)]
    ppermute x11 -> x12, waiting for transfers between devices: 7.58 us -> 5.97 us  [from_partner(): return lax.ppermute(block, axis, route)]
    ppermute x11 -> x12, starting transfers between devices: 8.66 us -> 8.72 us  [from_partner(): return lax.ppermute(block, axis, route)]
  transfers between devices with their start and end apart: 28 -> 29, of which waited for: 17 -> 17; matrix products, arithmetic and copies ran while one was open for 1% -> 1% of each run, Pallas kernels for 7% -> 7%
where the time goes in v12:
time: 86.2 us; the launch traced here: 85.9 us
  waiting for transfers between devices  39.5 us (46%)
  starting transfers between devices  28.7 us (33%)
  Pallas kernels  13 us (15%)
  local copies, waits for them, and re-layouts  3.81 us (4%)
    ppermute x11, waiting for transfers between devices, plane_swap(): return lax.ppermute(value, ('gx', 'gy'), route)  21.8 us
    pallas_call x14, Pallas kernels, call(): pl.pallas_call(kernel, out_shape=out_shape, in_specs=specs, scratch_shape...  13 us
    ppermute x6, waiting for transfers between devices, shifted(): lax.ppermute(value, axis, [(source, (source + steps) % count) for source...  11.7 us
    ppermute x11, starting transfers between devices, plane_swap(): return lax.ppermute(value, ('gx', 'gy'), route)  10.1 us
    ppermute x6, starting transfers between devices, shifted(): lax.ppermute(value, axis, [(source, (source + steps) % count) for source...  9.89 us
    ppermute x12, starting transfers between devices, from_partner(): return lax.ppermute(block, axis, route)  8.72 us
    ppermute x12, waiting for transfers between devices, from_partner(): return lax.ppermute(block, axis, route)  5.97 us
    unnamed x18, local copies, waits for them, and re-layouts  2.87 us
  transfers between devices with their start and end apart: 29, of which 17 were waited for; matrix products, arithmetic and copies ran while one was open for 1% of the time, Pallas kernels for 7%

profile of v12, /device:TPU:0, one launch (start us, length us, event | category | flops | bytes accessed | tf_op | source)
XLA Modules:
  0.0 85.9 jit_solution(17528626998316102722)
XLA Ops:
  2.8 3.0 %collective-permute-start = (bf16[128,512]{1,0:T(8,128)(2,1)S(1)}, bf16[128,512]{1,0:T(8,128)(2,1)S(1)}, u32[]{:S(2)}, u32[]{:S(2)}) collective-permute-start(bf16[128,512]{1,0:T(8,128)(2,1)S(1)} %reshape.13.own.f_own), channel_id=1, source_target_pairs={{0,2},{2,0},{4,6},{6,4},{1,3},{3,1},{5,7},{7,5},{8,10},{10,8},{12,... | collective-permute-start | bytes 393224 | tf_op jit(solution)/shard_map/ppermute | solution.py:20
  9.5 1.3 %collective-permute-done.5.far.f_far = bf16[128,512]{1,0:T(8,128)(2,1)S(1)} collective-permute-done((bf16[128,512]{1,0:T(8,128)(2,1)S(1)}, bf16[128,512]{1,0:T(8,128)(2,1)S(1)}, u32[]{:S(2)}, u32[]{:S(2)}) %collective-permute-start.5) | collective-permute-done | bytes 131104 | tf_op jit(solution)/shard_map/ppermute | solution.py:20
  11.4 1.8 %collective-permute-start.7 = (bf16[128,768]{1,0:T(8,128)(2,1)S(1)}, bf16[128,768]{1,0:T(8,128)(2,1)S(1)}, u32[]{:S(2)}, u32[]{:S(2)}) collective-permute-start(bf16[128,768]{1,0:T(8,128)(2,1)S(1)} %get-tuple-element.53), channel_id=1, source_target_pairs={{0,2},{2,0},{4,6},{6,4},{1,3},{3,1},{5,7},{7,5},{8,10},{10,8},{12,... | collective-permute-start | bytes 589832 | tf_op jit(solution)/shard_map/ppermute | solution.py:20
  13.2 1.5 %collective-permute-start.9 = (bf16[512,256]{1,0:T(8,128)(2,1)S(1)}, bf16[512,256]{1,0:T(8,128)(2,1)S(1)}, u32[]{:S(2)}, u32[]{:S(2)}) collective-permute-start(bf16[512,256]{1,0:T(8,128)(2,1)S(1)} %get-tuple-element.56.refs_0_.refs_2_), channel_id=1, source_target_pairs={{0,8},{8,16},{16,24},{24,0},{1,9},{9,17},{17,25},{25,1},{2,10},{10... | collective-permute-start | bytes 786440 | tf_op jit(solution)/shard_map/ppermute | solution.py:25
  14.7 2.6 %collective-permute-start.11 = (bf16[512,256]{1,0:T(8,128)(2,1)S(1)}, bf16[512,256]{1,0:T(8,128)(2,1)S(1)}, u32[]{:S(2)}, u32[]{:S(2)}) collective-permute-start(bf16[512,256]{1,0:T(8,128)(2,1)S(1)} %get-tuple-element.56.refs_0_.refs_2_), channel_id=1, source_target_pairs={{0,4},{2,6},{4,0},{6,2},{1,5},{3,7},{5,1},{7,3},{8,12},{10,14},{12... | collective-permute-start | bytes 786440 | tf_op jit(solution)/shard_map/ppermute | solution.py:25
  17.3 1.4 %collective-permute-start.10 = (bf16[512,256]{1,0:T(8,128)(2,1)S(1)}, bf16[512,256]{1,0:T(8,128)(2,1)S(1)}, u32[]{:S(2)}, u32[]{:S(2)}) collective-permute-start(bf16[512,256]{1,0:T(8,128)(2,1)S(1)} %get-tuple-element.56.refs_0_.refs_2_), channel_id=1, source_target_pairs={{0,24},{8,0},{16,8},{24,16},{1,25},{9,1},{17,9},{25,17},{2,26},{10... | collective-permute-start | bytes 786440 | tf_op jit(solution)/shard_map/ppermute | solution.py:25
  18.7 2.3 %collective-permute-done.7.pair = bf16[128,768]{1,0:T(8,128)(2,1)S(1)} collective-permute-done((bf16[128,768]{1,0:T(8,128)(2,1)S(1)}, bf16[128,768]{1,0:T(8,128)(2,1)S(1)}, u32[]{:S(2)}, u32[]{:S(2)}) %collective-permute-start.7) | collective-permute-done | bytes 196640 | tf_op jit(solution)/shard_map/ppermute | solution.py:20
  21.0 1.4 %collective-permute-done.8.far = bf16[128,768]{1,0:T(8,128)(2,1)S(1)} collective-permute-done((bf16[128,768]{1,0:T(8,128)(2,1)S(1)}, bf16[128,768]{1,0:T(8,128)(2,1)S(1)}, u32[]{:S(2)}, u32[]{:S(2)}) %collective-permute-start.8) | collective-permute-done | bytes 196640 | tf_op jit(solution)/shard_map/ppermute | solution.py:20
  23.3 2.1 %shard_map.114 = (bf16[4,512,512]{2,1,0:T(8,128)(2,1)S(1)}, bf16[4,512,512]{2,1,0:T(8,128)(2,1)S(1)}, f32[16,512]{1,0:T(8,128)S(1)}) custom-call(bf16[512,128]{1,0:T(8,128)(2,1)S(1)} %get-tuple-element.49.q_ref, bf16[512,128]{1,0:T(8,128)(2,1)S(1)} %get-tuple-element.54.do_ref, f32[2,512]{1,0:T(2,128)S(1)} %get-tuple-element.55.delta_ref, ...), custom_call_target="tpu_custom_call" | custom-call | flops 536870912 | bytes 4194304 | tf_op jit(solution)/shard_map/pallas_call | solution.py:55
  25.4 3.7 %collective-permute-done.11.refs_1_.refs_5_ = bf16[512,256]{1,0:T(8,128)(2,1)S(1)} collective-permute-done((bf16[512,256]{1,0:T(8,128)(2,1)S(1)}, bf16[512,256]{1,0:T(8,128)(2,1)S(1)}, u32[]{:S(2)}, u32[]{:S(2)}) %collective-permute-start.11) | collective-permute-done | bytes 262176 | tf_op jit(solution)/shard_map/ppermute | solution.py:25
  29.0 2.1 %shard_map.115 = (bf16[4,512,512]{2,1,0:T(8,128)(2,1)S(1)}, bf16[4,512,512]{2,1,0:T(8,128)(2,1)S(1)}, f32[16,512]{1,0:T(8,128)S(1)}) custom-call(bf16[512,128]{1,0:T(8,128)(2,1)S(1)} %get-tuple-element.49.q_ref, bf16[512,128]{1,0:T(8,128)(2,1)S(1)} %get-tuple-element.54.do_ref, f32[2,512]{1,0:T(2,128)S(1)} %get-tuple-element.55.delta_ref, ...), custom_call_target="tpu_custom_call" | custom-call | flops 536870912 | bytes 4194304 | tf_op jit(solution)/shard_map/pallas_call | solution.py:55
  31.1 2.2 %shard_map.116 = (f32[8,512]{1,0:T(8,128)S(1)}, bf16[512,256]{1,0:T(8,128)(2,1)S(1)}, bf16[512,256]{1,0:T(8,128)(2,1)S(1)}, bf16[512,256]{1,0:T(8,128)(2,1)S(1)}) custom-call(bf16[512,128]{1,0:T(8,128)(2,1)S(1)} %get-tuple-element.49.q_ref, bf16[512,128]{1,0:T(8,128)(2,1)S(1)} %get-tuple-element.54.do_ref, ...), custom_call_target="tpu_custom_call" | custom-call | flops 1073741824 | bytes 8388608 | tf_op jit(solution)/shard_map/pallas_call | solution.py:55
  33.3 1.5 %collective-permute-start.12 = (bf16[512,256]{1,0:T(8,128)(2,1)S(1)}, bf16[512,256]{1,0:T(8,128)(2,1)S(1)}, u32[]{:S(2)}, u32[]{:S(2)}) collective-permute-start(bf16[512,256]{1,0:T(8,128)(2,1)S(1)} %get-tuple-element.65), channel_id=1, source_target_pairs={{0,4},{2,6},{4,0},{6,2},{1,5},{3,7},{5,1},{7,3},{8,12},{10,14},{12... | collective-permute-start | bytes 786440 | tf_op jit(solution)/shard_map/ppermute | solution.py:25
  34.8 1.5 %collective-permute-start.13 = (bf16[512,256]{1,0:T(8,128)(2,1)S(1)}, bf16[512,256]{1,0:T(8,128)(2,1)S(1)}, u32[]{:S(2)}, u32[]{:S(2)}) collective-permute-start(bf16[512,256]{1,0:T(8,128)(2,1)S(1)} %get-tuple-element.66), channel_id=1, source_target_pairs={{0,8},{8,16},{16,24},{24,0},{1,9},{9,17},{17,25},{25,1},{2,10},{10... | collective-permute-start | bytes 786440 | tf_op jit(solution)/shard_map/ppermute | solution.py:25
  36.3 1.4 %collective-permute-start.14 = (bf16[512,256]{1,0:T(8,128)(2,1)S(1)}, bf16[512,256]{1,0:T(8,128)(2,1)S(1)}, u32[]{:S(2)}, u32[]{:S(2)}) collective-permute-start(bf16[512,256]{1,0:T(8,128)(2,1)S(1)} %get-tuple-element.67), channel_id=1, source_target_pairs={{0,24},{8,0},{16,8},{24,16},{1,25},{9,1},{17,9},{25,17},{2,26},{10... | collective-permute-start | bytes 786440 | tf_op jit(solution)/shard_map/ppermute | solution.py:25
  37.7 1.8 %shard_map.117 = (bf16[512,128]{1,0:T(8,128)(2,1)S(1)}, bf16[512,256]{1,0:T(8,128)(2,1)S(1)}) custom-call(f32[8,512]{1,0:T(8,128)S(1)} %get-tuple-element.63.part_ref, bf16[512,128]{1,0:T(8,128)(2,1)S(1)} %get-tuple-element.49.q_ref, bf16[512,128]{1,0:T(8,128)(2,1)S(1)} %get-tuple-element.54.do_ref, ...), custom_call_target="tpu_custom_call" | custom-call | flops 536870912 | bytes 4194304 | tf_op jit(solution)/shard_map/pallas_call | solution.py:55
  39.6 7.2 %collective-permute-done.12.refs_0_ = bf16[512,256]{1,0:T(8,128)(2,1)S(1)} collective-permute-done((bf16[512,256]{1,0:T(8,128)(2,1)S(1)}, bf16[512,256]{1,0:T(8,128)(2,1)S(1)}, u32[]{:S(2)}, u32[]{:S(2)}) %collective-permute-start.12) | collective-permute-done | bytes 262176 | tf_op jit(solution)/shard_map/ppermute | solution.py:25
  47.7 2.6 %collective-permute-start.19 = (bf16[256,384]{1,0:T(8,128)(2,1)S(1)}, bf16[256,384]{1,0:T(8,128)(2,1)S(1)}, u32[]{:S(2)}, u32[]{:S(2)}) collective-permute-start(bf16[256,384]{1,0:T(8,128)(2,1)S(1)} %get-tuple-element.76), channel_id=1, source_target_pairs={{0,2},{2,0},{4,6},{6,4},{1,3},{3,1},{5,7},{7,5},{8,10},{10,8},{12,... | collective-permute-start | bytes 589832 | tf_op jit(solution)/shard_map/ppermute | solution.py:20
  51.5 1.5 %collective-permute-start.17 = (bf16[64,1024]{1,0:T(8,128)(2,1)S(1)}, bf16[64,1024]{1,0:T(8,128)(2,1)S(1)}, u32[]{:S(2)}, u32[]{:S(2)}) collective-permute-start(bf16[64,1024]{1,0:T(8,128)(2,1)S(1)} %get-tuple-element.74), channel_id=1, source_target_pairs={{0,16},{2,18},{4,20},{6,22},{8,24},{10,26},{12,28},{14,30},{16,0},... | collective-permute-start | bytes 393224 | tf_op jit(solution)/shard_map/ppermute | solution.py:34
  53.0 1.4 %collective-permute-start.18 = (bf16[64,1024]{1,0:T(8,128)(2,1)S(1)}, bf16[64,1024]{1,0:T(8,128)(2,1)S(1)}, u32[]{:S(2)}, u32[]{:S(2)}) collective-permute-start(bf16[64,1024]{1,0:T(8,128)(2,1)S(1)} %get-tuple-element.75), channel_id=1, source_target_pairs={{0,24},{2,26},{4,28},{6,30},{8,16},{10,18},{12,20},{14,22},{16,8},... | collective-permute-start | bytes 393224 | tf_op jit(solution)/shard_map/ppermute | solution.py:34
  54.4 2.9 %collective-permute-done.16.refs_1_ = bf16[64,1024]{1,0:T(8,128)(2,1)S(1)} collective-permute-done((bf16[64,1024]{1,0:T(8,128)(2,1)S(1)}, bf16[64,1024]{1,0:T(8,128)(2,1)S(1)}, u32[]{:S(2)}, u32[]{:S(2)}) %collective-permute-start.16) | collective-permute-done | bytes 131104 | tf_op jit(solution)/shard_map/ppermute | solution.py:34
  57.2 2.3 %collective-permute-done.17.refs_2_ = bf16[64,1024]{1,0:T(8,128)(2,1)S(1)} collective-permute-done((bf16[64,1024]{1,0:T(8,128)(2,1)S(1)}, bf16[64,1024]{1,0:T(8,128)(2,1)S(1)}, u32[]{:S(2)}, u32[]{:S(2)}) %collective-permute-start.17) | collective-permute-done | bytes 131104 | tf_op jit(solution)/shard_map/ppermute | solution.py:34
  61.2 1.3 %shard_map.121 = bf16[8,4,4,512]{3,2,1,0:T(4,128)(2,1)} custom-call(bf16[512,384]{1,0:T(8,128)(2,1)S(1)} %get-tuple-element.69.own, bf16[512,384]{1,0:T(8,128)(2,1)S(1)} %collective-permute-done.15.core, bf16[256,384]{1,0:T(8,128)(2,1)S(1)} %collective-permute-done.19.pair, bf16[256,384]{1,0:T(8,128)(2,1)S(1)} %collective-permute-done.20.far, ...), custom_call_target="tpu_custom_call" | custom-call | flops 201326592 | bytes 1000000 | tf_op jit(solution)/shard_map/pallas_call | solution.py:55
  62.5 6.8 %collective-permute-done.21.refs_1_ = bf16[64,1024]{1,0:T(8,128)(2,1)S(1)} collective-permute-done((bf16[64,1024]{1,0:T(8,128)(2,1)S(1)}, bf16[64,1024]{1,0:T(8,128)(2,1)S(1)}, u32[]{:S(2)}, u32[]{:S(2)}) %collective-permute-start.21) | collective-permute-done | bytes 131104 | tf_op jit(solution)/shard_map/ppermute | solution.py:34
  69.4 1.6 %collective-permute-start.25 = (bf16[64,1024]{1,0:T(8,128)(2,1)S(1)}, bf16[64,1024]{1,0:T(8,128)(2,1)S(1)}, u32[]{:S(2)}, u32[]{:S(2)}) collective-permute-start(bf16[64,1024]{1,0:T(8,128)(2,1)S(1)} %shard_map.122.refs_0_), channel_id=1, source_target_pairs={{0,16},{2,18},{4,20},{6,22},{8,24},{10,26},{12,28},{14,30},{16,0},... | collective-permute-start | bytes 393224 | tf_op jit(solution)/shard_map/ppermute | solution.py:34
  71.5 3.0 %collective-permute-done.25.refs_4_ = bf16[64,1024]{1,0:T(8,128)(2,1)S(1)} collective-permute-done((bf16[64,1024]{1,0:T(8,128)(2,1)S(1)}, bf16[64,1024]{1,0:T(8,128)(2,1)S(1)}, u32[]{:S(2)}, u32[]{:S(2)}) %collective-permute-start.25) | collective-permute-done | bytes 131104 | tf_op jit(solution)/shard_map/ppermute | solution.py:34
  74.5 1.5 %collective-permute-start.27 = (bf16[64,1024]{1,0:T(8,128)(2,1)S(1)}, bf16[64,1024]{1,0:T(8,128)(2,1)S(1)}, u32[]{:S(2)}, u32[]{:S(2)}) collective-permute-start(bf16[64,1024]{1,0:T(8,128)(2,1)S(1)} %collective-permute-done.25.refs_4_), channel_id=1, source_target_pairs={{0,8},{2,10},{4,12},{6,14},{8,0},{10,2},{12,4},{14,6},{16,24},{18,... | collective-permute-start | bytes 393224 | tf_op jit(solution)/shard_map/ppermute | solution.py:34
  76.5 1.7 %collective-permute-start.26 = (bf16[64,1024]{1,0:T(8,128)(2,1)S(1)}, bf16[64,1024]{1,0:T(8,128)(2,1)S(1)}, u32[]{:S(2)}, u32[]{:S(2)}) collective-permute-start(bf16[64,1024]{1,0:T(8,128)(2,1)S(1)} %collective-permute-done.22.refs_1_), channel_id=1, source_target_pairs={{0,16},{2,18},{4,20},{6,22},{8,24},{10,26},{12,28},{14,30},{16,0},... | collective-permute-start | bytes 393224 | tf_op jit(solution)/shard_map/ppermute | solution.py:34
  78.1 1.3 %collective-permute-done.27.refs_6_ = bf16[64,1024]{1,0:T(8,128)(2,1)S(1)} collective-permute-done((bf16[64,1024]{1,0:T(8,128)(2,1)S(1)}, bf16[64,1024]{1,0:T(8,128)(2,1)S(1)}, u32[]{:S(2)}, u32[]{:S(2)}) %collective-permute-start.27) | collective-permute-done | bytes 131104 | tf_op jit(solution)/shard_map/ppermute | solution.py:34
  79.5 2.6 %collective-permute-done.24.refs_3_ = bf16[64,1024]{1,0:T(8,128)(2,1)S(1)} collective-permute-done((bf16[64,1024]{1,0:T(8,128)(2,1)S(1)}, bf16[64,1024]{1,0:T(8,128)(2,1)S(1)}, u32[]{:S(2)}, u32[]{:S(2)}) %collective-permute-start.24) | collective-permute-done | bytes 131104 | tf_op jit(solution)/shard_map/ppermute | solution.py:34
  82.1 2.3 %collective-permute-done.28.refs_7_ = bf16[64,1024]{1,0:T(8,128)(2,1)S(1)} collective-permute-done((bf16[64,1024]{1,0:T(8,128)(2,1)S(1)}, bf16[64,1024]{1,0:T(8,128)(2,1)S(1)}, u32[]{:S(2)}, u32[]{:S(2)}) %collective-permute-start.28) | collective-permute-done | bytes 131104 | tf_op jit(solution)/shard_map/ppermute | solution.py:34
  84.4 1.5 %shard_map.123 = (f32[256,512]{1,0:T(8,128)}, f32[256,512]{1,0:T(8,128)}, f32[256,512]{1,0:T(8,128)}, f32[256,512]{1,0:T(8,128)}) custom-call(bf16[64,1024]{1,0:T(8,128)(2,1)S(1)} %shard_map.122.refs_0_, bf16[64,1024]{1,0:T(8,128)(2,1)S(1)} %collective-permute-done.22.refs_1_, bf16[64,1024]{1,0:T(8,128)(2,1)S(1)} %collective-permute-done.23.refs_2_, ...), custom_call_target="tpu_custom_call" | custom-call | flops 1000000 | bytes 1000000 | tf_op jit(solution)/shard_map/pallas_call | solution.py:55
  (59 shorter events, 11.9 us)
Async XLA Ops:
  0.6 21.8 %copy-start.6 = (bf16[256,512]{1,0:T(8,128)(2,1)S(1)}, bf16[256,512]{1,0:T(8,128)(2,1)}, u32[]{:S(2)}) copy-start(bf16[256,512]{1,0:T(8,128)(2,1)} %wout.1) | copy-start | bytes 786436
  0.6 5.1 %collective-permute-start.2 = (bf16[256,512]{1,0:T(8,128)(2,1)}, bf16[256,512]{1,0:T(8,128)(2,1)S(1)}, u32[]{:S(2)}, u32[]{:S(2)}) collective-permute-start(bf16[256,512]{1,0:T(8,128)(2,1)} %wq0.3), channel_id=1, source_target_pairs={{0,1},{1,0},{2,3},{3,2},{4,5},{5,4},{6,7},{7,6},{8,9},{9,8},{10,11... | collective-permute-start | bytes 786440 | tf_op jit(solution)/shard_map/ppermute | solution.py:20
  1.2 4.6 %collective-permute-start.3 = (bf16[256,512]{1,0:T(8,128)(2,1)}, bf16[256,512]{1,0:T(8,128)(2,1)S(1)}, u32[]{:S(2)}, u32[]{:S(2)}) collective-permute-start(bf16[256,512]{1,0:T(8,128)(2,1)} %wk0.3), channel_id=1, source_target_pairs={{0,1},{1,0},{2,3},{3,2},{4,5},{5,4},{6,7},{7,6},{8,9},{9,8},{10,11... | collective-permute-start | bytes 786440 | tf_op jit(solution)/shard_map/ppermute | solution.py:20
  1.2 4.5 %collective-permute-start.4 = (bf16[256,512]{1,0:T(8,128)(2,1)}, bf16[256,512]{1,0:T(8,128)(2,1)S(1)}, u32[]{:S(2)}, u32[]{:S(2)}) collective-permute-start(bf16[256,512]{1,0:T(8,128)(2,1)} %wv0.3), channel_id=1, source_target_pairs={{0,1},{1,0},{2,3},{3,2},{4,5},{5,4},{6,7},{7,6},{8,9},{9,8},{10,11... | collective-permute-start | bytes 786440 | tf_op jit(solution)/shard_map/ppermute | solution.py:20
  2.6 6.1 %collective-permute-start.1 = (bf16[128,512]{1,0:T(8,128)(2,1)S(1)}, bf16[128,512]{1,0:T(8,128)(2,1)S(1)}, u32[]{:S(2)}, u32[]{:S(2)}) collective-permute-start(bf16[128,512]{1,0:T(8,128)(2,1)S(1)} %reshape.13.own.f_own), channel_id=1, source_target_pairs={{0,1},{1,0},{2,3},{3,2},{4,5},{5,4},{6,7},{7,6},{8,9},{9,8},{10,11... | collective-permute-start | bytes 393224 | tf_op jit(solution)/shard_map/ppermute | solution.py:20
  2.8 6.7 %collective-permute-start = (bf16[128,512]{1,0:T(8,128)(2,1)S(1)}, bf16[128,512]{1,0:T(8,128)(2,1)S(1)}, u32[]{:S(2)}, u32[]{:S(2)}) collective-permute-start(bf16[128,512]{1,0:T(8,128)(2,1)S(1)} %reshape.13.own.f_own), channel_id=1, source_target_pairs={{0,2},{2,0},{4,6},{6,4},{1,3},{3,1},{5,7},{7,5},{8,10},{10,8},{12,... | collective-permute-start | bytes 393224 | tf_op jit(solution)/shard_map/ppermute | solution.py:20
  9.5 1.3 %collective-permute-start.5 = (bf16[128,512]{1,0:T(8,128)(2,1)S(1)}, bf16[128,512]{1,0:T(8,128)(2,1)S(1)}, u32[]{:S(2)}, u32[]{:S(2)}) collective-permute-start(bf16[128,512]{1,0:T(8,128)(2,1)S(1)} %collective-permute-done.pair.f_pair), channel_id=1, source_target_pairs={{0,1},{1,0},{2,3},{3,2},{4,5},{5,4},{6,7},{7,6},{8,9},{9,8},{10,11... | collective-permute-start | bytes 393224 | tf_op jit(solution)/shard_map/ppermute | solution.py:20
  11.4 9.6 %collective-permute-start.7 = (bf16[128,768]{1,0:T(8,128)(2,1)S(1)}, bf16[128,768]{1,0:T(8,128)(2,1)S(1)}, u32[]{:S(2)}, u32[]{:S(2)}) collective-permute-start(bf16[128,768]{1,0:T(8,128)(2,1)S(1)} %get-tuple-element.53), channel_id=1, source_target_pairs={{0,2},{2,0},{4,6},{6,4},{1,3},{3,1},{5,7},{7,5},{8,10},{10,8},{12,... | collective-permute-start | bytes 589832 | tf_op jit(solution)/shard_map/ppermute | solution.py:20
  13.2 10.1 %collective-permute-start.9 = (bf16[512,256]{1,0:T(8,128)(2,1)S(1)}, bf16[512,256]{1,0:T(8,128)(2,1)S(1)}, u32[]{:S(2)}, u32[]{:S(2)}) collective-permute-start(bf16[512,256]{1,0:T(8,128)(2,1)S(1)} %get-tuple-element.56.refs_0_.refs_2_), channel_id=1, source_target_pairs={{0,8},{8,16},{16,24},{24,0},{1,9},{9,17},{17,25},{25,1},{2,10},{10... | collective-permute-start | bytes 786440 | tf_op jit(solution)/shard_map/ppermute | solution.py:25
  14.7 14.4 %collective-permute-start.11 = (bf16[512,256]{1,0:T(8,128)(2,1)S(1)}, bf16[512,256]{1,0:T(8,128)(2,1)S(1)}, u32[]{:S(2)}, u32[]{:S(2)}) collective-permute-start(bf16[512,256]{1,0:T(8,128)(2,1)S(1)} %get-tuple-element.56.refs_0_.refs_2_), channel_id=1, source_target_pairs={{0,4},{2,6},{4,0},{6,2},{1,5},{3,7},{5,1},{7,3},{8,12},{10,14},{12... | collective-permute-start | bytes 786440 | tf_op jit(solution)/shard_map/ppermute | solution.py:25
  17.3 11.8 %collective-permute-start.10 = (bf16[512,256]{1,0:T(8,128)(2,1)S(1)}, bf16[512,256]{1,0:T(8,128)(2,1)S(1)}, u32[]{:S(2)}, u32[]{:S(2)}) collective-permute-start(bf16[512,256]{1,0:T(8,128)(2,1)S(1)} %get-tuple-element.56.refs_0_.refs_2_), channel_id=1, source_target_pairs={{0,24},{8,0},{16,8},{24,16},{1,25},{9,1},{17,9},{25,17},{2,26},{10... | collective-permute-start | bytes 786440 | tf_op jit(solution)/shard_map/ppermute | solution.py:25
  18.7 2.3 %collective-permute-start.6 = (bf16[128,768]{1,0:T(8,128)(2,1)S(1)}, bf16[128,768]{1,0:T(8,128)(2,1)S(1)}, u32[]{:S(2)}, u32[]{:S(2)}) collective-permute-start(bf16[128,768]{1,0:T(8,128)(2,1)S(1)} %get-tuple-element.52.own), channel_id=1, source_target_pairs={{0,1},{1,0},{2,3},{3,2},{4,5},{5,4},{6,7},{7,6},{8,9},{9,8},{10,11... | collective-permute-start | bytes 589832 | tf_op jit(solution)/shard_map/ppermute | solution.py:20
  21.0 1.4 %collective-permute-start.8 = (bf16[128,768]{1,0:T(8,128)(2,1)S(1)}, bf16[128,768]{1,0:T(8,128)(2,1)S(1)}, u32[]{:S(2)}, u32[]{:S(2)}) collective-permute-start(bf16[128,768]{1,0:T(8,128)(2,1)S(1)} %collective-permute-done.7.pair), channel_id=1, source_target_pairs={{0,1},{1,0},{2,3},{3,2},{4,5},{5,4},{6,7},{7,6},{8,9},{9,8},{10,11... | collective-permute-start | bytes 589832 | tf_op jit(solution)/shard_map/ppermute | solution.py:20
  33.3 13.5 %collective-permute-start.12 = (bf16[512,256]{1,0:T(8,128)(2,1)S(1)}, bf16[512,256]{1,0:T(8,128)(2,1)S(1)}, u32[]{:S(2)}, u32[]{:S(2)}) collective-permute-start(bf16[512,256]{1,0:T(8,128)(2,1)S(1)} %get-tuple-element.65), channel_id=1, source_target_pairs={{0,4},{2,6},{4,0},{6,2},{1,5},{3,7},{5,1},{7,3},{8,12},{10,14},{12... | collective-permute-start | bytes 786440 | tf_op jit(solution)/shard_map/ppermute | solution.py:25
  34.8 12.1 %collective-permute-start.13 = (bf16[512,256]{1,0:T(8,128)(2,1)S(1)}, bf16[512,256]{1,0:T(8,128)(2,1)S(1)}, u32[]{:S(2)}, u32[]{:S(2)}) collective-permute-start(bf16[512,256]{1,0:T(8,128)(2,1)S(1)} %get-tuple-element.66), channel_id=1, source_target_pairs={{0,8},{8,16},{16,24},{24,0},{1,9},{9,17},{17,25},{25,1},{2,10},{10... | collective-permute-start | bytes 786440 | tf_op jit(solution)/shard_map/ppermute | solution.py:25
  36.3 11.0 %collective-permute-start.14 = (bf16[512,256]{1,0:T(8,128)(2,1)S(1)}, bf16[512,256]{1,0:T(8,128)(2,1)S(1)}, u32[]{:S(2)}, u32[]{:S(2)}) collective-permute-start(bf16[512,256]{1,0:T(8,128)(2,1)S(1)} %get-tuple-element.67), channel_id=1, source_target_pairs={{0,24},{8,0},{16,8},{24,16},{1,25},{9,1},{17,9},{25,17},{2,26},{10... | collective-permute-start | bytes 786440 | tf_op jit(solution)/shard_map/ppermute | solution.py:25
  39.6 21.6 %copy-start.1 = (bf16[256,512]{1,0:T(8,128)(2,1)S(1)}, bf16[256,512]{1,0:T(8,128)(2,1)}, u32[]{:S(2)}) copy-start(bf16[256,512]{1,0:T(8,128)(2,1)} %wq0.3) | copy-start | bytes 786436
  39.6 21.6 %copy-start.3 = (bf16[256,512]{1,0:T(8,128)(2,1)S(1)}, bf16[256,512]{1,0:T(8,128)(2,1)}, u32[]{:S(2)}) copy-start(bf16[256,512]{1,0:T(8,128)(2,1)} %wk0.3) | copy-start | bytes 786436
  47.6 2.7 %collective-permute-start.15 = (bf16[512,384]{1,0:T(8,128)(2,1)S(1)}, bf16[512,384]{1,0:T(8,128)(2,1)S(1)}, u32[]{:S(2)}, u32[]{:S(2)}) collective-permute-start(bf16[512,384]{1,0:T(8,128)(2,1)S(1)} %get-tuple-element.69.own), channel_id=1, source_target_pairs={{0,1},{1,0},{2,3},{3,2},{4,5},{5,4},{6,7},{7,6},{8,9},{9,8},{10,11... | collective-permute-start | bytes 1179656 | tf_op jit(solution)/shard_map/ppermute | solution.py:20
  47.7 12.0 %collective-permute-start.19 = (bf16[256,384]{1,0:T(8,128)(2,1)S(1)}, bf16[256,384]{1,0:T(8,128)(2,1)S(1)}, u32[]{:S(2)}, u32[]{:S(2)}) collective-permute-start(bf16[256,384]{1,0:T(8,128)(2,1)S(1)} %get-tuple-element.76), channel_id=1, source_target_pairs={{0,2},{2,0},{4,6},{6,4},{1,3},{3,1},{5,7},{7,5},{8,10},{10,8},{12,... | collective-permute-start | bytes 589832 | tf_op jit(solution)/shard_map/ppermute | solution.py:20
  50.8 6.4 %collective-permute-start.16 = (bf16[64,1024]{1,0:T(8,128)(2,1)S(1)}, bf16[64,1024]{1,0:T(8,128)(2,1)S(1)}, u32[]{:S(2)}, u32[]{:S(2)}) collective-permute-start(bf16[64,1024]{1,0:T(8,128)(2,1)S(1)} %get-tuple-element.73), channel_id=1, source_target_pairs={{0,8},{2,10},{4,12},{6,14},{8,0},{10,2},{12,4},{14,6},{16,24},{18,... | collective-permute-start | bytes 393224 | tf_op jit(solution)/shard_map/ppermute | solution.py:34
  51.5 8.1 %collective-permute-start.17 = (bf16[64,1024]{1,0:T(8,128)(2,1)S(1)}, bf16[64,1024]{1,0:T(8,128)(2,1)S(1)}, u32[]{:S(2)}, u32[]{:S(2)}) collective-permute-start(bf16[64,1024]{1,0:T(8,128)(2,1)S(1)} %get-tuple-element.74), channel_id=1, source_target_pairs={{0,16},{2,18},{4,20},{6,22},{8,24},{10,26},{12,28},{14,30},{16,0},... | collective-permute-start | bytes 393224 | tf_op jit(solution)/shard_map/ppermute | solution.py:34
  53.0 6.5 %collective-permute-start.18 = (bf16[64,1024]{1,0:T(8,128)(2,1)S(1)}, bf16[64,1024]{1,0:T(8,128)(2,1)S(1)}, u32[]{:S(2)}, u32[]{:S(2)}) collective-permute-start(bf16[64,1024]{1,0:T(8,128)(2,1)S(1)} %get-tuple-element.75), channel_id=1, source_target_pairs={{0,24},{2,26},{4,28},{6,30},{8,16},{10,18},{12,20},{14,22},{16,8},... | collective-permute-start | bytes 393224 | tf_op jit(solution)/shard_map/ppermute | solution.py:34
  59.6 1.5 %collective-permute-start.20 = (bf16[256,384]{1,0:T(8,128)(2,1)S(1)}, bf16[256,384]{1,0:T(8,128)(2,1)S(1)}, u32[]{:S(2)}, u32[]{:S(2)}) collective-permute-start(bf16[256,384]{1,0:T(8,128)(2,1)S(1)} %collective-permute-done.19.pair), channel_id=1, source_target_pairs={{0,1},{1,0},{2,3},{3,2},{4,5},{5,4},{6,7},{7,6},{8,9},{9,8},{10,11... | collective-permute-start | bytes 589832 | tf_op jit(solution)/shard_map/ppermute | solution.py:20
  59.7 9.6 %collective-permute-start.21 = (bf16[64,1024]{1,0:T(8,128)(2,1)S(1)}, bf16[64,1024]{1,0:T(8,128)(2,1)S(1)}, u32[]{:S(2)}, u32[]{:S(2)}) collective-permute-start(bf16[64,1024]{1,0:T(8,128)(2,1)S(1)} %shard_map.120.refs_0_), channel_id=1, source_target_pairs={{0,4},{2,6},{4,0},{6,2},{8,12},{10,14},{12,8},{14,10},{16,20},{18,... | collective-permute-start | bytes 393224 | tf_op jit(solution)/shard_map/ppermute | solution.py:34
  69.4 5.1 %collective-permute-start.25 = (bf16[64,1024]{1,0:T(8,128)(2,1)S(1)}, bf16[64,1024]{1,0:T(8,128)(2,1)S(1)}, u32[]{:S(2)}, u32[]{:S(2)}) collective-permute-start(bf16[64,1024]{1,0:T(8,128)(2,1)S(1)} %shard_map.122.refs_0_), channel_id=1, source_target_pairs={{0,16},{2,18},{4,20},{6,22},{8,24},{10,26},{12,28},{14,30},{16,0},... | collective-permute-start | bytes 393224 | tf_op jit(solution)/shard_map/ppermute | solution.py:34
  71.0 5.0 %collective-permute-start.23 = (bf16[64,1024]{1,0:T(8,128)(2,1)S(1)}, bf16[64,1024]{1,0:T(8,128)(2,1)S(1)}, u32[]{:S(2)}, u32[]{:S(2)}) collective-permute-start(bf16[64,1024]{1,0:T(8,128)(2,1)S(1)} %shard_map.122.refs_0_), channel_id=1, source_target_pairs={{0,8},{2,10},{4,12},{6,14},{8,0},{10,2},{12,4},{14,6},{16,24},{18,... | collective-permute-start | bytes 393224 | tf_op jit(solution)/shard_map/ppermute | solution.py:34
  71.5 5.0 %collective-permute-start.22 = (bf16[64,1024]{1,0:T(8,128)(2,1)S(1)}, bf16[64,1024]{1,0:T(8,128)(2,1)S(1)}, u32[]{:S(2)}, u32[]{:S(2)}) collective-permute-start(bf16[64,1024]{1,0:T(8,128)(2,1)S(1)} %shard_map.122.refs_0_), channel_id=1, source_target_pairs={{0,2},{2,0},{4,6},{6,4},{8,10},{10,8},{12,14},{14,12},{16,18},{18,... | collective-permute-start | bytes 393224 | tf_op jit(solution)/shard_map/ppermute | solution.py:34
  74.5 5.0 %collective-permute-start.27 = (bf16[64,1024]{1,0:T(8,128)(2,1)S(1)}, bf16[64,1024]{1,0:T(8,128)(2,1)S(1)}, u32[]{:S(2)}, u32[]{:S(2)}) collective-permute-start(bf16[64,1024]{1,0:T(8,128)(2,1)S(1)} %collective-permute-done.25.refs_4_), channel_id=1, source_target_pairs={{0,8},{2,10},{4,12},{6,14},{8,0},{10,2},{12,4},{14,6},{16,24},{18,... | collective-permute-start | bytes 393224 | tf_op jit(solution)/shard_map/ppermute | solution.py:34
  76.0 6.1 %collective-permute-start.24 = (bf16[64,1024]{1,0:T(8,128)(2,1)S(1)}, bf16[64,1024]{1,0:T(8,128)(2,1)S(1)}, u32[]{:S(2)}, u32[]{:S(2)}) collective-permute-start(bf16[64,1024]{1,0:T(8,128)(2,1)S(1)} %collective-permute-done.23.refs_2_), channel_id=1, source_target_pairs={{0,2},{2,0},{4,6},{6,4},{8,10},{10,8},{12,14},{14,12},{16,18},{18,... | collective-permute-start | bytes 393224 | tf_op jit(solution)/shard_map/ppermute | solution.py:34
  76.5 5.6 %collective-permute-start.26 = (bf16[64,1024]{1,0:T(8,128)(2,1)S(1)}, bf16[64,1024]{1,0:T(8,128)(2,1)S(1)}, u32[]{:S(2)}, u32[]{:S(2)}) collective-permute-start(bf16[64,1024]{1,0:T(8,128)(2,1)S(1)} %collective-permute-done.22.refs_1_), channel_id=1, source_target_pairs={{0,16},{2,18},{4,20},{6,22},{8,24},{10,26},{12,28},{14,30},{16,0},... | collective-permute-start | bytes 393224 | tf_op jit(solution)/shard_map/ppermute | solution.py:34
  79.5 5.0 %collective-permute-start.28 = (bf16[64,1024]{1,0:T(8,128)(2,1)S(1)}, bf16[64,1024]{1,0:T(8,128)(2,1)S(1)}, u32[]{:S(2)}, u32[]{:S(2)}) collective-permute-start(bf16[64,1024]{1,0:T(8,128)(2,1)S(1)} %collective-permute-done.27.refs_6_), channel_id=1, source_target_pairs={{0,2},{2,0},{4,6},{6,4},{8,10},{10,8},{12,14},{14,12},{16,18},{18,... | collective-permute-start | bytes 393224 | tf_op jit(solution)/shard_map/ppermute | solution.py:34
  (6 other events, 29.8 us)

commit v13 on v10

--- a/solution.py
+++ b/solution.py
@@ -460,7 +460,7 @@
         total, grad_x = lax.optimization_barrier((total, grad_x))
         total = call(sum_kernel, piece, [total, other])
         by_x, by_y, by_z = plane_swap(total, 1, 0), plane_swap(total, 2, 0), plane_swap(total, 0, 1)
-        by_xy, by_xz = plane_swap(by_y, 1, 0), plane_swap(by_x, 0, 1)
+        by_xy, by_xz = plane_swap(by_y, 1, 0), plane_swap(by_z, 1, 0)
         by_yz, by_xyz = plane_swap(by_z, 2, 0), plane_swap(by_xy, 0, 1)
         weights = call(
             spread_kernel,

time: 85.2 us -> 86.6 us (1.016)
  waiting for transfers between devices: 38.5 us -> 39.8 us
    ppermute x11, waiting for transfers between devices: 19.2 us -> 20.5 us  [plane_swap(): return lax.ppermute(value, ('gx', 'gy'), route)]
where the time goes in v13:
time: 86.6 us; the launch traced here: 86.4 us
  waiting for transfers between devices  39.8 us (46%)
  starting transfers between devices  29 us (33%)
  Pallas kernels  13 us (15%)
  local copies, waits for them, and re-layouts  3.81 us (4%)
    ppermute x11, waiting for transfers between devices, plane_swap(): return lax.ppermute(value, ('gx', 'gy'), route)  20.5 us
    pallas_call x14, Pallas kernels, call(): pl.pallas_call(kernel, out_shape=out_shape, in_specs=specs, scratch_shape...  13 us
    ppermute x6, waiting for transfers between devices, shifted(): lax.ppermute(value, axis, [(source, (source + steps) % count) for source...  11.7 us
    ppermute x11, starting transfers between devices, plane_swap(): return lax.ppermute(value, ('gx', 'gy'), route)  10.5 us
    ppermute x6, starting transfers between devices, shifted(): lax.ppermute(value, axis, [(source, (source + steps) % count) for source...  9.9 us
    ppermute x11, starting transfers between devices, from_partner(): return lax.ppermute(block, axis, route)  8.66 us
    ppermute x11, waiting for transfers between devices, from_partner(): return lax.ppermute(block, axis, route)  7.58 us
    unnamed x18, local copies, waits for them, and re-layouts  2.87 us
  transfers between devices with their start and end apart: 28, of which 17 were waited for; matrix products, arithmetic and copies ran while one was open for 1% of the time, Pallas kernels for 7%

profile of v13, /device:TPU:0, one launch (start us, length us, event | category | flops | bytes accessed | tf_op | source)
XLA Modules:
  0.0 86.4 jit_solution(17273252837066645782)
XLA Ops:
  2.8 3.0 %collective-permute-start = (bf16[128,512]{1,0:T(8,128)(2,1)S(1)}, bf16[128,512]{1,0:T(8,128)(2,1)S(1)}, u32[]{:S(2)}, u32[]{:S(2)}) collective-permute-start(bf16[128,512]{1,0:T(8,128)(2,1)S(1)} %reshape.13.own.f_own), channel_id=1, source_target_pairs={{0,2},{2,0},{4,6},{6,4},{1,3},{3,1},{5,7},{7,5},{8,10},{10,8},{12,... | collective-permute-start | bytes 393224 | tf_op jit(solution)/shard_map/ppermute | solution.py:20
  11.4 1.8 %collective-permute-start.7 = (bf16[128,768]{1,0:T(8,128)(2,1)S(1)}, bf16[128,768]{1,0:T(8,128)(2,1)S(1)}, u32[]{:S(2)}, u32[]{:S(2)}) collective-permute-start(bf16[128,768]{1,0:T(8,128)(2,1)S(1)} %get-tuple-element.53), channel_id=1, source_target_pairs={{0,2},{2,0},{4,6},{6,4},{1,3},{3,1},{5,7},{7,5},{8,10},{10,8},{12,... | collective-permute-start | bytes 589832 | tf_op jit(solution)/shard_map/ppermute | solution.py:20
  13.2 1.5 %collective-permute-start.9 = (bf16[512,256]{1,0:T(8,128)(2,1)S(1)}, bf16[512,256]{1,0:T(8,128)(2,1)S(1)}, u32[]{:S(2)}, u32[]{:S(2)}) collective-permute-start(bf16[512,256]{1,0:T(8,128)(2,1)S(1)} %get-tuple-element.56.refs_0_.refs_2_), channel_id=1, source_target_pairs={{0,8},{8,16},{16,24},{24,0},{1,9},{9,17},{17,25},{25,1},{2,10},{10... | collective-permute-start | bytes 786440 | tf_op jit(solution)/shard_map/ppermute | solution.py:25
  14.7 2.6 %collective-permute-start.11 = (bf16[512,256]{1,0:T(8,128)(2,1)S(1)}, bf16[512,256]{1,0:T(8,128)(2,1)S(1)}, u32[]{:S(2)}, u32[]{:S(2)}) collective-permute-start(bf16[512,256]{1,0:T(8,128)(2,1)S(1)} %get-tuple-element.56.refs_0_.refs_2_), channel_id=1, source_target_pairs={{0,4},{2,6},{4,0},{6,2},{1,5},{3,7},{5,1},{7,3},{8,12},{10,14},{12... | collective-permute-start | bytes 786440 | tf_op jit(solution)/shard_map/ppermute | solution.py:25
  17.3 1.4 %collective-permute-start.10 = (bf16[512,256]{1,0:T(8,128)(2,1)S(1)}, bf16[512,256]{1,0:T(8,128)(2,1)S(1)}, u32[]{:S(2)}, u32[]{:S(2)}) collective-permute-start(bf16[512,256]{1,0:T(8,128)(2,1)S(1)} %get-tuple-element.56.refs_0_.refs_2_), channel_id=1, source_target_pairs={{0,24},{8,0},{16,8},{24,16},{1,25},{9,1},{17,9},{25,17},{2,26},{10... | collective-permute-start | bytes 786440 | tf_op jit(solution)/shard_map/ppermute | solution.py:25
  18.7 2.3 %collective-permute-done.7.pair = bf16[128,768]{1,0:T(8,128)(2,1)S(1)} collective-permute-done((bf16[128,768]{1,0:T(8,128)(2,1)S(1)}, bf16[128,768]{1,0:T(8,128)(2,1)S(1)}, u32[]{:S(2)}, u32[]{:S(2)}) %collective-permute-start.7) | collective-permute-done | bytes 196640 | tf_op jit(solution)/shard_map/ppermute | solution.py:20
  21.0 1.4 %collective-permute-done.8.far = bf16[128,768]{1,0:T(8,128)(2,1)S(1)} collective-permute-done((bf16[128,768]{1,0:T(8,128)(2,1)S(1)}, bf16[128,768]{1,0:T(8,128)(2,1)S(1)}, u32[]{:S(2)}, u32[]{:S(2)}) %collective-permute-start.8) | collective-permute-done | bytes 196640 | tf_op jit(solution)/shard_map/ppermute | solution.py:20
  23.3 2.1 %shard_map.114 = (bf16[4,512,512]{2,1,0:T(8,128)(2,1)S(1)}, bf16[4,512,512]{2,1,0:T(8,128)(2,1)S(1)}, f32[16,512]{1,0:T(8,128)S(1)}) custom-call(bf16[512,128]{1,0:T(8,128)(2,1)S(1)} %get-tuple-element.49.q_ref, bf16[512,128]{1,0:T(8,128)(2,1)S(1)} %get-tuple-element.54.do_ref, f32[2,512]{1,0:T(2,128)S(1)} %get-tuple-element.55.delta_ref, ...), custom_call_target="tpu_custom_call" | custom-call | flops 536870912 | bytes 4194304 | tf_op jit(solution)/shard_map/pallas_call | solution.py:55
  25.4 3.7 %collective-permute-done.11.refs_1_.refs_5_ = bf16[512,256]{1,0:T(8,128)(2,1)S(1)} collective-permute-done((bf16[512,256]{1,0:T(8,128)(2,1)S(1)}, bf16[512,256]{1,0:T(8,128)(2,1)S(1)}, u32[]{:S(2)}, u32[]{:S(2)}) %collective-permute-start.11) | collective-permute-done | bytes 262176 | tf_op jit(solution)/shard_map/ppermute | solution.py:25
  29.0 2.1 %shard_map.115 = (bf16[4,512,512]{2,1,0:T(8,128)(2,1)S(1)}, bf16[4,512,512]{2,1,0:T(8,128)(2,1)S(1)}, f32[16,512]{1,0:T(8,128)S(1)}) custom-call(bf16[512,128]{1,0:T(8,128)(2,1)S(1)} %get-tuple-element.49.q_ref, bf16[512,128]{1,0:T(8,128)(2,1)S(1)} %get-tuple-element.54.do_ref, f32[2,512]{1,0:T(2,128)S(1)} %get-tuple-element.55.delta_ref, ...), custom_call_target="tpu_custom_call" | custom-call | flops 536870912 | bytes 4194304 | tf_op jit(solution)/shard_map/pallas_call | solution.py:55
  31.1 2.2 %shard_map.116 = (f32[8,512]{1,0:T(8,128)S(1)}, bf16[512,256]{1,0:T(8,128)(2,1)S(1)}, bf16[512,256]{1,0:T(8,128)(2,1)S(1)}, bf16[512,256]{1,0:T(8,128)(2,1)S(1)}) custom-call(bf16[512,128]{1,0:T(8,128)(2,1)S(1)} %get-tuple-element.49.q_ref, bf16[512,128]{1,0:T(8,128)(2,1)S(1)} %get-tuple-element.54.do_ref, ...), custom_call_target="tpu_custom_call" | custom-call | flops 1073741824 | bytes 8388608 | tf_op jit(solution)/shard_map/pallas_call | solution.py:55
  33.3 1.5 %collective-permute-start.12 = (bf16[512,256]{1,0:T(8,128)(2,1)S(1)}, bf16[512,256]{1,0:T(8,128)(2,1)S(1)}, u32[]{:S(2)}, u32[]{:S(2)}) collective-permute-start(bf16[512,256]{1,0:T(8,128)(2,1)S(1)} %get-tuple-element.65), channel_id=1, source_target_pairs={{0,4},{2,6},{4,0},{6,2},{1,5},{3,7},{5,1},{7,3},{8,12},{10,14},{12... | collective-permute-start | bytes 786440 | tf_op jit(solution)/shard_map/ppermute | solution.py:25
  34.8 1.5 %collective-permute-start.13 = (bf16[512,256]{1,0:T(8,128)(2,1)S(1)}, bf16[512,256]{1,0:T(8,128)(2,1)S(1)}, u32[]{:S(2)}, u32[]{:S(2)}) collective-permute-start(bf16[512,256]{1,0:T(8,128)(2,1)S(1)} %get-tuple-element.66), channel_id=1, source_target_pairs={{0,8},{8,16},{16,24},{24,0},{1,9},{9,17},{17,25},{25,1},{2,10},{10... | collective-permute-start | bytes 786440 | tf_op jit(solution)/shard_map/ppermute | solution.py:25
  36.3 1.4 %collective-permute-start.14 = (bf16[512,256]{1,0:T(8,128)(2,1)S(1)}, bf16[512,256]{1,0:T(8,128)(2,1)S(1)}, u32[]{:S(2)}, u32[]{:S(2)}) collective-permute-start(bf16[512,256]{1,0:T(8,128)(2,1)S(1)} %get-tuple-element.67), channel_id=1, source_target_pairs={{0,24},{8,0},{16,8},{24,16},{1,25},{9,1},{17,9},{25,17},{2,26},{10... | collective-permute-start | bytes 786440 | tf_op jit(solution)/shard_map/ppermute | solution.py:25
  37.7 1.8 %shard_map.117 = (bf16[512,128]{1,0:T(8,128)(2,1)S(1)}, bf16[512,256]{1,0:T(8,128)(2,1)S(1)}) custom-call(f32[8,512]{1,0:T(8,128)S(1)} %get-tuple-element.63.part_ref, bf16[512,128]{1,0:T(8,128)(2,1)S(1)} %get-tuple-element.49.q_ref, bf16[512,128]{1,0:T(8,128)(2,1)S(1)} %get-tuple-element.54.do_ref, ...), custom_call_target="tpu_custom_call" | custom-call | flops 536870912 | bytes 4194304 | tf_op jit(solution)/shard_map/pallas_call | solution.py:55
  39.6 7.2 %collective-permute-done.12.refs_0_ = bf16[512,256]{1,0:T(8,128)(2,1)S(1)} collective-permute-done((bf16[512,256]{1,0:T(8,128)(2,1)S(1)}, bf16[512,256]{1,0:T(8,128)(2,1)S(1)}, u32[]{:S(2)}, u32[]{:S(2)}) %collective-permute-start.12) | collective-permute-done | bytes 262176 | tf_op jit(solution)/shard_map/ppermute | solution.py:25
  47.6 1.7 %collective-permute-done.15.core = bf16[512,384]{1,0:T(8,128)(2,1)S(1)} collective-permute-done((bf16[512,384]{1,0:T(8,128)(2,1)S(1)}, bf16[512,384]{1,0:T(8,128)(2,1)S(1)}, u32[]{:S(2)}, u32[]{:S(2)}) %collective-permute-start.15) | collective-permute-done | bytes 393248 | tf_op jit(solution)/shard_map/ppermute | solution.py:20
  49.9 2.6 %collective-permute-start.19 = (bf16[128,768]{1,0:T(8,128)(2,1)S(1)}, bf16[128,768]{1,0:T(8,128)(2,1)S(1)}, u32[]{:S(2)}, u32[]{:S(2)}) collective-permute-start(bf16[128,768]{1,0:T(8,128)(2,1)S(1)} %get-tuple-element.75), channel_id=1, source_target_pairs={{0,2},{2,0},{4,6},{6,4},{1,3},{3,1},{5,7},{7,5},{8,10},{10,8},{12,... | collective-permute-start | bytes 589832 | tf_op jit(solution)/shard_map/ppermute | solution.py:20
  52.8 1.7 %collective-permute-start.17 = (bf16[64,1024]{1,0:T(8,128)(2,1)S(1)}, bf16[64,1024]{1,0:T(8,128)(2,1)S(1)}, u32[]{:S(2)}, u32[]{:S(2)}) collective-permute-start(bf16[64,1024]{1,0:T(8,128)(2,1)S(1)} %get-tuple-element.73), channel_id=1, source_target_pairs={{0,16},{2,18},{4,20},{6,22},{8,24},{10,26},{12,28},{14,30},{16,0},... | collective-permute-start | bytes 393224 | tf_op jit(solution)/shard_map/ppermute | solution.py:34
  54.5 1.5 %collective-permute-start.18 = (bf16[64,1024]{1,0:T(8,128)(2,1)S(1)}, bf16[64,1024]{1,0:T(8,128)(2,1)S(1)}, u32[]{:S(2)}, u32[]{:S(2)}) collective-permute-start(bf16[64,1024]{1,0:T(8,128)(2,1)S(1)} %get-tuple-element.74), channel_id=1, source_target_pairs={{0,24},{2,26},{4,28},{6,30},{8,16},{10,18},{12,20},{14,22},{16,8},... | collective-permute-start | bytes 393224 | tf_op jit(solution)/shard_map/ppermute | solution.py:34
  56.0 2.9 %collective-permute-done.16.refs_1_ = bf16[64,1024]{1,0:T(8,128)(2,1)S(1)} collective-permute-done((bf16[64,1024]{1,0:T(8,128)(2,1)S(1)}, bf16[64,1024]{1,0:T(8,128)(2,1)S(1)}, u32[]{:S(2)}, u32[]{:S(2)}) %collective-permute-start.16) | collective-permute-done | bytes 131104 | tf_op jit(solution)/shard_map/ppermute | solution.py:34
  58.8 1.7 %collective-permute-done.18.refs_3_ = bf16[64,1024]{1,0:T(8,128)(2,1)S(1)} collective-permute-done((bf16[64,1024]{1,0:T(8,128)(2,1)S(1)}, bf16[64,1024]{1,0:T(8,128)(2,1)S(1)}, u32[]{:S(2)}, u32[]{:S(2)}) %collective-permute-start.18) | collective-permute-done | bytes 131104 | tf_op jit(solution)/shard_map/ppermute | solution.py:34
  63.4 5.1 %collective-permute-done.20.refs_1_ = bf16[64,1024]{1,0:T(8,128)(2,1)S(1)} collective-permute-done((bf16[64,1024]{1,0:T(8,128)(2,1)S(1)}, bf16[64,1024]{1,0:T(8,128)(2,1)S(1)}, u32[]{:S(2)}, u32[]{:S(2)}) %collective-permute-start.20) | collective-permute-done | bytes 131104 | tf_op jit(solution)/shard_map/ppermute | solution.py:34
  68.5 1.8 %collective-permute-start.24 = (bf16[64,1024]{1,0:T(8,128)(2,1)S(1)}, bf16[64,1024]{1,0:T(8,128)(2,1)S(1)}, u32[]{:S(2)}, u32[]{:S(2)}) collective-permute-start(bf16[64,1024]{1,0:T(8,128)(2,1)S(1)} %shard_map.122.refs_0_), channel_id=1, source_target_pairs={{0,16},{2,18},{4,20},{6,22},{8,24},{10,26},{12,28},{14,30},{16,0},... | collective-permute-start | bytes 393224 | tf_op jit(solution)/shard_map/ppermute | solution.py:34
  70.3 3.2 %collective-permute-done.24.refs_4_ = bf16[64,1024]{1,0:T(8,128)(2,1)S(1)} collective-permute-done((bf16[64,1024]{1,0:T(8,128)(2,1)S(1)}, bf16[64,1024]{1,0:T(8,128)(2,1)S(1)}, u32[]{:S(2)}, u32[]{:S(2)}) %collective-permute-start.24) | collective-permute-done | bytes 131104 | tf_op jit(solution)/shard_map/ppermute | solution.py:34
  73.6 1.6 %collective-permute-start.26 = (bf16[64,1024]{1,0:T(8,128)(2,1)S(1)}, bf16[64,1024]{1,0:T(8,128)(2,1)S(1)}, u32[]{:S(2)}, u32[]{:S(2)}) collective-permute-start(bf16[64,1024]{1,0:T(8,128)(2,1)S(1)} %collective-permute-done.24.refs_4_), channel_id=1, source_target_pairs={{0,8},{2,10},{4,12},{6,14},{8,0},{10,2},{12,4},{14,6},{16,24},{18,... | collective-permute-start | bytes 393224 | tf_op jit(solution)/shard_map/ppermute | solution.py:34
  75.6 1.7 %collective-permute-start.25 = (bf16[64,1024]{1,0:T(8,128)(2,1)S(1)}, bf16[64,1024]{1,0:T(8,128)(2,1)S(1)}, u32[]{:S(2)}, u32[]{:S(2)}) collective-permute-start(bf16[64,1024]{1,0:T(8,128)(2,1)S(1)} %collective-permute-done.21.refs_1_), channel_id=1, source_target_pairs={{0,16},{2,18},{4,20},{6,22},{8,24},{10,26},{12,28},{14,30},{16,0},... | collective-permute-start | bytes 393224 | tf_op jit(solution)/shard_map/ppermute | solution.py:34
  77.4 2.5 %collective-permute-done.26.refs_6_ = bf16[64,1024]{1,0:T(8,128)(2,1)S(1)} collective-permute-done((bf16[64,1024]{1,0:T(8,128)(2,1)S(1)}, bf16[64,1024]{1,0:T(8,128)(2,1)S(1)}, u32[]{:S(2)}, u32[]{:S(2)}) %collective-permute-start.26) | collective-permute-done | bytes 131104 | tf_op jit(solution)/shard_map/ppermute | solution.py:34
  79.9 1.4 %collective-permute-done.22.refs_2_ = bf16[64,1024]{1,0:T(8,128)(2,1)S(1)} collective-permute-done((bf16[64,1024]{1,0:T(8,128)(2,1)S(1)}, bf16[64,1024]{1,0:T(8,128)(2,1)S(1)}, u32[]{:S(2)}, u32[]{:S(2)}) %collective-permute-start.22) | collective-permute-done | bytes 131104 | tf_op jit(solution)/shard_map/ppermute | solution.py:34
  81.4 1.4 %collective-permute-done.23.refs_3_ = bf16[64,1024]{1,0:T(8,128)(2,1)S(1)} collective-permute-done((bf16[64,1024]{1,0:T(8,128)(2,1)S(1)}, bf16[64,1024]{1,0:T(8,128)(2,1)S(1)}, u32[]{:S(2)}, u32[]{:S(2)}) %collective-permute-start.23) | collective-permute-done | bytes 131104 | tf_op jit(solution)/shard_map/ppermute | solution.py:34
  82.8 2.1 %collective-permute-done.27.refs_7_ = bf16[64,1024]{1,0:T(8,128)(2,1)S(1)} collective-permute-done((bf16[64,1024]{1,0:T(8,128)(2,1)S(1)}, bf16[64,1024]{1,0:T(8,128)(2,1)S(1)}, u32[]{:S(2)}, u32[]{:S(2)}) %collective-permute-start.27) | collective-permute-done | bytes 131104 | tf_op jit(solution)/shard_map/ppermute | solution.py:34
  84.9 1.5 %shard_map.123 = (f32[256,512]{1,0:T(8,128)}, f32[256,512]{1,0:T(8,128)}, f32[256,512]{1,0:T(8,128)}, f32[256,512]{1,0:T(8,128)}) custom-call(bf16[64,1024]{1,0:T(8,128)(2,1)S(1)} %shard_map.122.refs_0_, bf16[64,1024]{1,0:T(8,128)(2,1)S(1)} %collective-permute-done.21.refs_1_, bf16[64,1024]{1,0:T(8,128)(2,1)S(1)} %collective-permute-done.22.refs_2_, ...), custom_call_target="tpu_custom_call" | custom-call | flops 1000000 | bytes 1000000 | tf_op jit(solution)/shard_map/pallas_call | solution.py:55
  (57 shorter events, 13.4 us)
Async XLA Ops:
  0.6 21.8 %copy-start.6 = (bf16[256,512]{1,0:T(8,128)(2,1)S(1)}, bf16[256,512]{1,0:T(8,128)(2,1)}, u32[]{:S(2)}) copy-start(bf16[256,512]{1,0:T(8,128)(2,1)} %wout.1) | copy-start | bytes 786436
  0.6 5.1 %collective-permute-start.2 = (bf16[256,512]{1,0:T(8,128)(2,1)}, bf16[256,512]{1,0:T(8,128)(2,1)S(1)}, u32[]{:S(2)}, u32[]{:S(2)}) collective-permute-start(bf16[256,512]{1,0:T(8,128)(2,1)} %wq0.3), channel_id=1, source_target_pairs={{0,1},{1,0},{2,3},{3,2},{4,5},{5,4},{6,7},{7,6},{8,9},{9,8},{10,11... | collective-permute-start | bytes 786440 | tf_op jit(solution)/shard_map/ppermute | solution.py:20
  1.2 4.6 %collective-permute-start.3 = (bf16[256,512]{1,0:T(8,128)(2,1)}, bf16[256,512]{1,0:T(8,128)(2,1)S(1)}, u32[]{:S(2)}, u32[]{:S(2)}) collective-permute-start(bf16[256,512]{1,0:T(8,128)(2,1)} %wk0.3), channel_id=1, source_target_pairs={{0,1},{1,0},{2,3},{3,2},{4,5},{5,4},{6,7},{7,6},{8,9},{9,8},{10,11... | collective-permute-start | bytes 786440 | tf_op jit(solution)/shard_map/ppermute | solution.py:20
  1.2 4.5 %collective-permute-start.4 = (bf16[256,512]{1,0:T(8,128)(2,1)}, bf16[256,512]{1,0:T(8,128)(2,1)S(1)}, u32[]{:S(2)}, u32[]{:S(2)}) collective-permute-start(bf16[256,512]{1,0:T(8,128)(2,1)} %wv0.3), channel_id=1, source_target_pairs={{0,1},{1,0},{2,3},{3,2},{4,5},{5,4},{6,7},{7,6},{8,9},{9,8},{10,11... | collective-permute-start | bytes 786440 | tf_op jit(solution)/shard_map/ppermute | solution.py:20
  2.6 6.1 %collective-permute-start.1 = (bf16[128,512]{1,0:T(8,128)(2,1)S(1)}, bf16[128,512]{1,0:T(8,128)(2,1)S(1)}, u32[]{:S(2)}, u32[]{:S(2)}) collective-permute-start(bf16[128,512]{1,0:T(8,128)(2,1)S(1)} %reshape.13.own.f_own), channel_id=1, source_target_pairs={{0,1},{1,0},{2,3},{3,2},{4,5},{5,4},{6,7},{7,6},{8,9},{9,8},{10,11... | collective-permute-start | bytes 393224 | tf_op jit(solution)/shard_map/ppermute | solution.py:20
  2.8 6.7 %collective-permute-start = (bf16[128,512]{1,0:T(8,128)(2,1)S(1)}, bf16[128,512]{1,0:T(8,128)(2,1)S(1)}, u32[]{:S(2)}, u32[]{:S(2)}) collective-permute-start(bf16[128,512]{1,0:T(8,128)(2,1)S(1)} %reshape.13.own.f_own), channel_id=1, source_target_pairs={{0,2},{2,0},{4,6},{6,4},{1,3},{3,1},{5,7},{7,5},{8,10},{10,8},{12,... | collective-permute-start | bytes 393224 | tf_op jit(solution)/shard_map/ppermute | solution.py:20
  9.5 1.3 %collective-permute-start.5 = (bf16[128,512]{1,0:T(8,128)(2,1)S(1)}, bf16[128,512]{1,0:T(8,128)(2,1)S(1)}, u32[]{:S(2)}, u32[]{:S(2)}) collective-permute-start(bf16[128,512]{1,0:T(8,128)(2,1)S(1)} %collective-permute-done.pair.f_pair), channel_id=1, source_target_pairs={{0,1},{1,0},{2,3},{3,2},{4,5},{5,4},{6,7},{7,6},{8,9},{9,8},{10,11... | collective-permute-start | bytes 393224 | tf_op jit(solution)/shard_map/ppermute | solution.py:20
  11.4 9.6 %collective-permute-start.7 = (bf16[128,768]{1,0:T(8,128)(2,1)S(1)}, bf16[128,768]{1,0:T(8,128)(2,1)S(1)}, u32[]{:S(2)}, u32[]{:S(2)}) collective-permute-start(bf16[128,768]{1,0:T(8,128)(2,1)S(1)} %get-tuple-element.53), channel_id=1, source_target_pairs={{0,2},{2,0},{4,6},{6,4},{1,3},{3,1},{5,7},{7,5},{8,10},{10,8},{12,... | collective-permute-start | bytes 589832 | tf_op jit(solution)/shard_map/ppermute | solution.py:20
  13.2 10.1 %collective-permute-start.9 = (bf16[512,256]{1,0:T(8,128)(2,1)S(1)}, bf16[512,256]{1,0:T(8,128)(2,1)S(1)}, u32[]{:S(2)}, u32[]{:S(2)}) collective-permute-start(bf16[512,256]{1,0:T(8,128)(2,1)S(1)} %get-tuple-element.56.refs_0_.refs_2_), channel_id=1, source_target_pairs={{0,8},{8,16},{16,24},{24,0},{1,9},{9,17},{17,25},{25,1},{2,10},{10... | collective-permute-start | bytes 786440 | tf_op jit(solution)/shard_map/ppermute | solution.py:25
  14.7 14.4 %collective-permute-start.11 = (bf16[512,256]{1,0:T(8,128)(2,1)S(1)}, bf16[512,256]{1,0:T(8,128)(2,1)S(1)}, u32[]{:S(2)}, u32[]{:S(2)}) collective-permute-start(bf16[512,256]{1,0:T(8,128)(2,1)S(1)} %get-tuple-element.56.refs_0_.refs_2_), channel_id=1, source_target_pairs={{0,4},{2,6},{4,0},{6,2},{1,5},{3,7},{5,1},{7,3},{8,12},{10,14},{12... | collective-permute-start | bytes 786440 | tf_op jit(solution)/shard_map/ppermute | solution.py:25
  17.3 11.8 %collective-permute-start.10 = (bf16[512,256]{1,0:T(8,128)(2,1)S(1)}, bf16[512,256]{1,0:T(8,128)(2,1)S(1)}, u32[]{:S(2)}, u32[]{:S(2)}) collective-permute-start(bf16[512,256]{1,0:T(8,128)(2,1)S(1)} %get-tuple-element.56.refs_0_.refs_2_), channel_id=1, source_target_pairs={{0,24},{8,0},{16,8},{24,16},{1,25},{9,1},{17,9},{25,17},{2,26},{10... | collective-permute-start | bytes 786440 | tf_op jit(solution)/shard_map/ppermute | solution.py:25
  18.7 2.3 %collective-permute-start.6 = (bf16[128,768]{1,0:T(8,128)(2,1)S(1)}, bf16[128,768]{1,0:T(8,128)(2,1)S(1)}, u32[]{:S(2)}, u32[]{:S(2)}) collective-permute-start(bf16[128,768]{1,0:T(8,128)(2,1)S(1)} %get-tuple-element.52.own), channel_id=1, source_target_pairs={{0,1},{1,0},{2,3},{3,2},{4,5},{5,4},{6,7},{7,6},{8,9},{9,8},{10,11... | collective-permute-start | bytes 589832 | tf_op jit(solution)/shard_map/ppermute | solution.py:20
  21.0 1.4 %collective-permute-start.8 = (bf16[128,768]{1,0:T(8,128)(2,1)S(1)}, bf16[128,768]{1,0:T(8,128)(2,1)S(1)}, u32[]{:S(2)}, u32[]{:S(2)}) collective-permute-start(bf16[128,768]{1,0:T(8,128)(2,1)S(1)} %collective-permute-done.7.pair), channel_id=1, source_target_pairs={{0,1},{1,0},{2,3},{3,2},{4,5},{5,4},{6,7},{7,6},{8,9},{9,8},{10,11... | collective-permute-start | bytes 589832 | tf_op jit(solution)/shard_map/ppermute | solution.py:20
  33.3 13.5 %collective-permute-start.12 = (bf16[512,256]{1,0:T(8,128)(2,1)S(1)}, bf16[512,256]{1,0:T(8,128)(2,1)S(1)}, u32[]{:S(2)}, u32[]{:S(2)}) collective-permute-start(bf16[512,256]{1,0:T(8,128)(2,1)S(1)} %get-tuple-element.65), channel_id=1, source_target_pairs={{0,4},{2,6},{4,0},{6,2},{1,5},{3,7},{5,1},{7,3},{8,12},{10,14},{12... | collective-permute-start | bytes 786440 | tf_op jit(solution)/shard_map/ppermute | solution.py:25
  34.8 12.1 %collective-permute-start.13 = (bf16[512,256]{1,0:T(8,128)(2,1)S(1)}, bf16[512,256]{1,0:T(8,128)(2,1)S(1)}, u32[]{:S(2)}, u32[]{:S(2)}) collective-permute-start(bf16[512,256]{1,0:T(8,128)(2,1)S(1)} %get-tuple-element.66), channel_id=1, source_target_pairs={{0,8},{8,16},{16,24},{24,0},{1,9},{9,17},{17,25},{25,1},{2,10},{10... | collective-permute-start | bytes 786440 | tf_op jit(solution)/shard_map/ppermute | solution.py:25
  36.3 11.0 %collective-permute-start.14 = (bf16[512,256]{1,0:T(8,128)(2,1)S(1)}, bf16[512,256]{1,0:T(8,128)(2,1)S(1)}, u32[]{:S(2)}, u32[]{:S(2)}) collective-permute-start(bf16[512,256]{1,0:T(8,128)(2,1)S(1)} %get-tuple-element.67), channel_id=1, source_target_pairs={{0,24},{8,0},{16,8},{24,16},{1,25},{9,1},{17,9},{25,17},{2,26},{10... | collective-permute-start | bytes 786440 | tf_op jit(solution)/shard_map/ppermute | solution.py:25
  39.6 22.5 %copy-start.1 = (bf16[256,512]{1,0:T(8,128)(2,1)S(1)}, bf16[256,512]{1,0:T(8,128)(2,1)}, u32[]{:S(2)}) copy-start(bf16[256,512]{1,0:T(8,128)(2,1)} %wq0.3) | copy-start | bytes 786436
  39.6 22.5 %copy-start.3 = (bf16[256,512]{1,0:T(8,128)(2,1)S(1)}, bf16[256,512]{1,0:T(8,128)(2,1)}, u32[]{:S(2)}) copy-start(bf16[256,512]{1,0:T(8,128)(2,1)} %wk0.3) | copy-start | bytes 786436
  39.6 22.5 %copy-start.5 = (bf16[256,512]{1,0:T(8,128)(2,1)S(1)}, bf16[256,512]{1,0:T(8,128)(2,1)}, u32[]{:S(2)}) copy-start(bf16[256,512]{1,0:T(8,128)(2,1)} %wv0.3) | copy-start | bytes 786436
  47.5 1.8 %collective-permute-start.15 = (bf16[512,384]{1,0:T(8,128)(2,1)S(1)}, bf16[512,384]{1,0:T(8,128)(2,1)S(1)}, u32[]{:S(2)}, u32[]{:S(2)}) collective-permute-start(bf16[512,384]{1,0:T(8,128)(2,1)S(1)} %shard_map.118.own), channel_id=1, source_target_pairs={{0,1},{1,0},{2,3},{3,2},{4,5},{5,4},{6,7},{7,6},{8,9},{9,8},{10,11... | collective-permute-start | bytes 1179656 | tf_op jit(solution)/shard_map/ppermute | solution.py:20
  49.9 10.8 %collective-permute-start.19 = (bf16[128,768]{1,0:T(8,128)(2,1)S(1)}, bf16[128,768]{1,0:T(8,128)(2,1)S(1)}, u32[]{:S(2)}, u32[]{:S(2)}) collective-permute-start(bf16[128,768]{1,0:T(8,128)(2,1)S(1)} %get-tuple-element.75), channel_id=1, source_target_pairs={{0,2},{2,0},{4,6},{6,4},{1,3},{3,1},{5,7},{7,5},{8,10},{10,8},{12,... | collective-permute-start | bytes 589832 | tf_op jit(solution)/shard_map/ppermute | solution.py:20
  52.5 6.4 %collective-permute-start.16 = (bf16[64,1024]{1,0:T(8,128)(2,1)S(1)}, bf16[64,1024]{1,0:T(8,128)(2,1)S(1)}, u32[]{:S(2)}, u32[]{:S(2)}) collective-permute-start(bf16[64,1024]{1,0:T(8,128)(2,1)S(1)} %get-tuple-element.72), channel_id=1, source_target_pairs={{0,8},{2,10},{4,12},{6,14},{8,0},{10,2},{12,4},{14,6},{16,24},{18,... | collective-permute-start | bytes 393224 | tf_op jit(solution)/shard_map/ppermute | solution.py:34
  52.8 6.1 %collective-permute-start.17 = (bf16[64,1024]{1,0:T(8,128)(2,1)S(1)}, bf16[64,1024]{1,0:T(8,128)(2,1)S(1)}, u32[]{:S(2)}, u32[]{:S(2)}) collective-permute-start(bf16[64,1024]{1,0:T(8,128)(2,1)S(1)} %get-tuple-element.73), channel_id=1, source_target_pairs={{0,16},{2,18},{4,20},{6,22},{8,24},{10,26},{12,28},{14,30},{16,0},... | collective-permute-start | bytes 393224 | tf_op jit(solution)/shard_map/ppermute | solution.py:34
  54.5 6.1 %collective-permute-start.18 = (bf16[64,1024]{1,0:T(8,128)(2,1)S(1)}, bf16[64,1024]{1,0:T(8,128)(2,1)S(1)}, u32[]{:S(2)}, u32[]{:S(2)}) collective-permute-start(bf16[64,1024]{1,0:T(8,128)(2,1)S(1)} %get-tuple-element.74), channel_id=1, source_target_pairs={{0,24},{2,26},{4,28},{6,30},{8,16},{10,18},{12,20},{14,22},{16,8},... | collective-permute-start | bytes 393224 | tf_op jit(solution)/shard_map/ppermute | solution.py:34
  60.7 7.8 %collective-permute-start.20 = (bf16[64,1024]{1,0:T(8,128)(2,1)S(1)}, bf16[64,1024]{1,0:T(8,128)(2,1)S(1)}, u32[]{:S(2)}, u32[]{:S(2)}) collective-permute-start(bf16[64,1024]{1,0:T(8,128)(2,1)S(1)} %shard_map.120.refs_0_), channel_id=1, source_target_pairs={{0,4},{2,6},{4,0},{6,2},{8,12},{10,14},{12,8},{14,10},{16,20},{18,... | collective-permute-start | bytes 393224 | tf_op jit(solution)/shard_map/ppermute | solution.py:34
  68.5 5.0 %collective-permute-start.24 = (bf16[64,1024]{1,0:T(8,128)(2,1)S(1)}, bf16[64,1024]{1,0:T(8,128)(2,1)S(1)}, u32[]{:S(2)}, u32[]{:S(2)}) collective-permute-start(bf16[64,1024]{1,0:T(8,128)(2,1)S(1)} %shard_map.122.refs_0_), channel_id=1, source_target_pairs={{0,16},{2,18},{4,20},{6,22},{8,24},{10,26},{12,28},{14,30},{16,0},... | collective-permute-start | bytes 393224 | tf_op jit(solution)/shard_map/ppermute | solution.py:34
  70.3 5.3 %collective-permute-start.21 = (bf16[64,1024]{1,0:T(8,128)(2,1)S(1)}, bf16[64,1024]{1,0:T(8,128)(2,1)S(1)}, u32[]{:S(2)}, u32[]{:S(2)}) collective-permute-start(bf16[64,1024]{1,0:T(8,128)(2,1)S(1)} %shard_map.122.refs_0_), channel_id=1, source_target_pairs={{0,2},{2,0},{4,6},{6,4},{8,10},{10,8},{12,14},{14,12},{16,18},{18,... | collective-permute-start | bytes 393224 | tf_op jit(solution)/shard_map/ppermute | solution.py:34
  73.6 6.3 %collective-permute-start.26 = (bf16[64,1024]{1,0:T(8,128)(2,1)S(1)}, bf16[64,1024]{1,0:T(8,128)(2,1)S(1)}, u32[]{:S(2)}, u32[]{:S(2)}) collective-permute-start(bf16[64,1024]{1,0:T(8,128)(2,1)S(1)} %collective-permute-done.24.refs_4_), channel_id=1, source_target_pairs={{0,8},{2,10},{4,12},{6,14},{8,0},{10,2},{12,4},{14,6},{16,24},{18,... | collective-permute-start | bytes 393224 | tf_op jit(solution)/shard_map/ppermute | solution.py:34
  75.2 6.1 %collective-permute-start.22 = (bf16[64,1024]{1,0:T(8,128)(2,1)S(1)}, bf16[64,1024]{1,0:T(8,128)(2,1)S(1)}, u32[]{:S(2)}, u32[]{:S(2)}) collective-permute-start(bf16[64,1024]{1,0:T(8,128)(2,1)S(1)} %shard_map.122.refs_0_), channel_id=1, source_target_pairs={{0,8},{2,10},{4,12},{6,14},{8,0},{10,2},{12,4},{14,6},{16,24},{18,... | collective-permute-start | bytes 393224 | tf_op jit(solution)/shard_map/ppermute | solution.py:34
  75.6 5.8 %collective-permute-start.25 = (bf16[64,1024]{1,0:T(8,128)(2,1)S(1)}, bf16[64,1024]{1,0:T(8,128)(2,1)S(1)}, u32[]{:S(2)}, u32[]{:S(2)}) collective-permute-start(bf16[64,1024]{1,0:T(8,128)(2,1)S(1)} %collective-permute-done.21.refs_1_), channel_id=1, source_target_pairs={{0,16},{2,18},{4,20},{6,22},{8,24},{10,26},{12,28},{14,30},{16,0},... | collective-permute-start | bytes 393224 | tf_op jit(solution)/shard_map/ppermute | solution.py:34
  77.3 5.4 %collective-permute-start.23 = (bf16[64,1024]{1,0:T(8,128)(2,1)S(1)}, bf16[64,1024]{1,0:T(8,128)(2,1)S(1)}, u32[]{:S(2)}, u32[]{:S(2)}) collective-permute-start(bf16[64,1024]{1,0:T(8,128)(2,1)S(1)} %collective-permute-done.21.refs_1_), channel_id=1, source_target_pairs={{0,8},{2,10},{4,12},{6,14},{8,0},{10,2},{12,4},{14,6},{16,24},{18,... | collective-permute-start | bytes 393224 | tf_op jit(solution)/shard_map/ppermute | solution.py:34
  79.9 5.0 %collective-permute-start.27 = (bf16[64,1024]{1,0:T(8,128)(2,1)S(1)}, bf16[64,1024]{1,0:T(8,128)(2,1)S(1)}, u32[]{:S(2)}, u32[]{:S(2)}) collective-permute-start(bf16[64,1024]{1,0:T(8,128)(2,1)S(1)} %collective-permute-done.26.refs_6_), channel_id=1, source_target_pairs={{0,2},{2,0},{4,6},{6,4},{8,10},{10,8},{12,14},{14,12},{16,18},{18,... | collective-permute-start | bytes 393224 | tf_op jit(solution)/shard_map/ppermute | solution.py:34
  (5 other events, 8.2 us)
